TPU v7x, 32 devices: a whole 2x2x4 slice. The times are simulated.
32 devices in a mesh: sub: 8 (over y, x, core), grp: 4 (over z).
Axes of the slice: x: 2, y: 2, z: 4, core: 2. Of those that a mesh axis runs over, the one named last changes fastest.
Arguments:
- load_terms: float32 [8, 4, 512, 384], P('sub', 'grp'), may hold values from -6 to 6
- schur_matrix: float32 [8, 4, 512, 512], P('sub', 'grp'), may hold values from -1 to 4
- local_inverse: float32 [8, 4, 512, 512], P('sub', 'grp'), may hold values from -0.3 to 1
- coarse_modes: float32 [8, 4, 512, 128], P('sub', 'grp'), may hold values from -0.25 to 0.25
- cluster_inverse: float32 [8, 512, 512], P('sub', None, 'grp'), may hold values from -0.5 to 2, as said below
- row_blocks: int32 [8, 4, 4, 96], P('sub', 'grp'), may hold values from 0 to 511, as said below
Outputs:
- solution: float32 [8, 4, 512, 384], P('sub', 'grp')
- residual: float32 [8, 4, 512, 384], P('sub', 'grp')
Inputs may be any that keep to these rules, and one draw needn't show every extreme that they name: `row_blocks`: for each subdomain the four blocks hold 384 different rows. `cluster_inverse`: each cluster's matrix is symmetric.
All inputs are finite; a program needn't handle non-finite values.
Results may differ from a plain program's by a relative error of at most 0.00016.
Values sent between devices are 32-bit elements; how exact they have to be, the bound alone decides.
No kernel may reach another device: no remote copies, remote signals or barrier semaphores. Data moves between devices by JAX's collectives and lax.ppermute only.
A program may use at most 64 MiB of HBM per device.

v0:
```python
import jax
import jax.numpy as jnp
from jax import lax
from jax.experimental import pallas as pl
from jax.experimental.pallas import tpu as pltpu
from jax.sharding import PartitionSpec as P

ITERS = 2
ROW_SUBS = 4
RELAX = 0.5
GROUPS = 4
PIECE = 128
f32 = jnp.float32
bf16 = jnp.bfloat16
NN = (((1,), (0,)), ((), ()))
NT = (((1,), (1,)), ((), ()))


class Chain:
    def __init__(self):
        self.last = None

    def __call__(self, body, outs, flops, moved, *operands, scratch=(), ins=None, places=None):
        count = len(operands)
        specs = [pl.BlockSpec(memory_space=pltpu.VMEM)] * count if ins is None else ins
        extra = []
        if self.last is not None:
            extra = [self.last]
            specs = specs + [pl.BlockSpec(memory_space=pl.ANY)]

        def whole_body(*refs):
            body(*refs[:count], *refs[count + len(extra) :])

        results = pl.pallas_call(
            whole_body,
            out_shape=[jax.ShapeDtypeStruct(shape, kind) for shape, kind in outs],
            in_specs=specs,
            out_specs=[pl.BlockSpec(memory_space=pltpu.VMEM)] * len(outs) if places is None else places,
            scratch_shapes=list(scratch),
            compiler_params=pltpu.CompilerParams(vmem_limit_bytes=24 * 1024 * 1024),
            cost_estimate=pl.CostEstimate(flops=flops, bytes_accessed=moved, transcendentals=0),
        )(*operands, *extra)
        self.last = results[0]
        return results


def dot(left, right, dims=NN):
    return lax.dot_general(left, right, dims, preferred_element_type=f32)


def split(value):
    high = value.astype(bf16)
    return high, (value - high.astype(f32)).astype(bf16)


def dot3(left, right):
    return dot(left[0], right[0]) + (dot(left[0], right[1]) + dot(left[1], right[0]))


def pick(chooser, value):
    high, low = split(value)
    return dot(chooser, high) + dot(chooser, low)


def sides(subs):
    sub = lax.axis_index("sub")
    low_row = (sub // ROW_SUBS) % 2 == 0
    over, under = sub < subs - ROW_SUBS, sub >= ROW_SUBS
    return [
        (low_row, 3, 2, jnp.where(low_row, over, under)),
        (low_row, 0, 0, sub > 0),
        (low_row, 1, 1, sub < subs - 1),
        (low_row, 2, 3, jnp.where(low_row, under, over)),
    ]


def put_shared(value, shared_refs):
    for place, ref in enumerate(shared_refs):
        width = ref.shape[0]
        ref[...] = value[place * width : (place + 1) * width]


def came_in(subs, shared_refs):
    return jnp.concatenate(
        [ref[...] * jnp.where(here, 1.0, 0.0) for ref, (_, _, _, here) in zip(shared_refs, sides(subs))], axis=0
    )


def add_shared(subs, value, shared_refs):
    came = came_in(subs, shared_refs)
    count = came.shape[0]
    return jnp.concatenate([value[:count] + came, value[count:]], axis=0)


def listed_body(subs, count, blocks_hbm, load_hbm, columns_hbm, listed_ref, load_ref, sent_ref, *refs):
    *shared_refs, blocks_ref, load_sem, blocks_sem, sent_sem = refs
    modes = sent_ref.shape[0]
    wanted = pl.multiple_of((3 - (lax.axis_index("grp") ^ 1)) * modes, modes)
    sent_copy = pltpu.make_async_copy(columns_hbm.at[pl.ds(wanted, modes), :], sent_ref, sent_sem)
    load_copy = pltpu.make_async_copy(load_hbm, load_ref, load_sem)
    blocks_copy = pltpu.make_async_copy(blocks_hbm, blocks_ref, blocks_sem)
    blocks_copy.start()
    load_copy.start()
    sent_copy.start()
    blocks_copy.wait()
    blocks = blocks_ref[...]
    placed = jnp.concatenate(
        [jnp.where(test, blocks[a : a + 1], blocks[b : b + 1]) for test, a, b, _ in sides(subs)], axis=0
    )
    upright = placed.astype(f32).T
    column = jnp.concatenate([upright[:, place : place + 1] for place in range(4)], axis=0)
    listed, total = column.shape[0], load_ref.shape[0]
    lane = lax.broadcasted_iota(jnp.int32, (listed, total), 1).astype(f32)
    first = (column == lane).astype(f32).astype(bf16)
    listed_ref[...] = first
    load_copy.wait()
    sent_copy.wait()
    sent = pick(first[: count * blocks.shape[1]], load_ref[...])
    put_shared(sent, shared_refs)


def order_body(subs, listed_ref, load_ref, basis_ref,
               chooser_ref, flipped_ref, basis_high, basis_low, test_high, test_low, ahead_ref, ordered_ref):
    listed, total = listed_ref.shape
    first = listed_ref[...].astype(f32)
    unlisted = 1.0 - jnp.sum(first, axis=0, keepdims=True)
    before = (
        lax.broadcasted_iota(jnp.int32, (total, total), 0)
        < lax.broadcasted_iota(jnp.int32, (total, total), 1)
    ).astype(f32).astype(bf16)
    rank = dot(jnp.broadcast_to(unlisted, (8, total)).astype(bf16), before)[:1]
    slot = lax.broadcasted_iota(jnp.int32, (total - listed, total), 0).astype(f32)
    last = jnp.where(rank == slot, unlisted, 0.0)
    chooser = jnp.concatenate([first, last], axis=0)
    flipped_ref[...] = chooser.T.astype(bf16)
    weighted = (chooser * weight_column(subs, listed // 4, total)).astype(bf16)
    chooser = chooser.astype(bf16)
    chooser_ref[...] = chooser
    ordered = pick(chooser, load_ref[...])
    ordered_ref[...] = ordered
    for part, out, turned in zip(split(basis_ref[...]), (basis_high, basis_low), (test_high, test_low)):
        placed = dot(weighted, part)
        out[...] = placed.astype(bf16)
        turned[...] = placed.T.astype(bf16)
    ahead_ref[...] = dot3((test_high[...], test_low[...]), split(ordered))


def weight_column(subs, width, total):
    parts = [jnp.full((width, 1), jnp.where(here, 0.5, 1.0), f32) for _, _, _, here in sides(subs)]
    return jnp.concatenate(parts + [jnp.ones((total - 4 * width, 1), f32)], axis=0)


def rows_of(columns_ref, place):
    modes = columns_ref.shape[1]
    return columns_ref[pl.ds(pl.multiple_of(place * modes, modes), modes), :]


def solver_body(subs, listed, chooser_ref, solve_ref, solve_high, solve_low):
    chooser = chooser_ref[...]
    weighted = (chooser.astype(f32) * weight_column(subs, listed // 4, chooser.shape[0])).astype(bf16)
    for part, out in zip(split(solve_ref[...] * RELAX), (solve_high, solve_low)):
        out[...] = dot(dot(weighted, part).astype(bf16), weighted, NT).astype(bf16)


def schur_body(chooser_ref, flipped_ref, schur_ref, schur_high, schur_low):
    chooser, flipped = chooser_ref[...], flipped_ref[...]
    for part, out in zip(split(schur_ref[...]), (schur_high, schur_low)):
        out[...] = dot(dot(chooser, part).astype(bf16), flipped).astype(bf16)


def blend_body(columns_ref, other_ref, mix_high, mix_low):
    grp = lax.axis_index("grp")
    away = jnp.concatenate([rows_of(columns_ref, 3 - grp), other_ref[...]], axis=1)
    kept = jnp.concatenate([rows_of(columns_ref, grp), rows_of(columns_ref, grp ^ 1).T], axis=1)
    mix_high[...], mix_low[...] = split(jnp.concatenate([away, kept], axis=0) * RELAX)


def project_body(subs, count, ahead_ref, test_high, test_low, *refs):
    came = came_in(subs, refs[:count])
    size = came.shape[0]
    projected = ahead_ref[...] + dot3((test_high[:, :size], test_low[:, :size]), split(came))
    for place, ref in enumerate(refs[count:]):
        ref[...] = projected[:, place * PIECE : (place + 1) * PIECE]


def solve_body(subs, value_ref, solve_high, solve_low, *refs):
    halves = split(add_shared(subs, value_ref[...], refs[:-1]))
    refs[-1][...] = dot3((solve_high[...], solve_low[...]), halves)


def mix_body(own_ref, other_ref, mix_high, mix_low, away_ref, kept_ref):
    modes = away_ref.shape[0]
    pair = jnp.concatenate([own_ref[...], other_ref[...]], axis=0)
    mixed = dot3((mix_high[...], mix_low[...]), split(pair))
    away_ref[...] = mixed[:modes]
    kept_ref[...] = mixed[modes:]


def correct_body(kept_ref, came_ref, fine_ref, basis_high, basis_low, place, *refs):
    coarse = kept_ref[...] + came_ref[...]
    fine = fine_ref[:, place * PIECE : (place + 1) * PIECE]
    step = fine + dot3((basis_high[...], basis_low[...]), split(coarse))
    formers = place if len(refs) > 1 else 0
    former_refs, out_ref = refs[:formers], refs[formers]
    out_ref[...] = step
    for at, ref in enumerate(refs[formers + 1 :]):
        size = ref.shape[0]
        rows = slice(at * size, (at + 1) * size)
        ref[...] = jnp.concatenate([former[rows] for former in former_refs] + [step[rows]], axis=1)


def ahead_body(pieces, first, *refs):
    total = jnp.concatenate([ref[...] for ref in refs[:pieces]], axis=1)
    refs = refs[pieces:]
    if not first:
        total = refs[0][...] + total
        refs = refs[1:]
    load_ref, schur_high, schur_low, base_ref, total_ref = refs
    total_ref[...] = total
    base_ref[...] = load_ref[...] - dot3((schur_high[...], schur_low[...]), split(total))


def product_body(subs, count, base_ref, schur_high, schur_low, *refs):
    came = came_in(subs, refs[:count])
    size = came.shape[0]
    part = dot3((schur_high[:size, :size], schur_low[:size, :size]), split(came))
    put_shared(base_ref[:size] - part, refs[count:])


def follow_body(subs, count, last, base_ref, total_ref, schur_high, schur_low, *refs):
    arrived, shared, refs = refs[:count], refs[count : 2 * count], refs[2 * count :]
    came = came_in(subs, arrived)
    size = came.shape[0]
    part = dot3((schur_high[size:, :size], schur_low[size:, :size]), split(came))
    value = jnp.concatenate([ref[...] for ref in shared] + [base_ref[size:] - part], axis=0)
    iterate_ref, value_ref = refs[-2:]
    value_ref[...] = value
    iterate_ref[...] = jnp.concatenate([total_ref[:size] + came, total_ref[size:]], axis=0)
    if not last:
        test_high, test_low, projected_ref = refs[:3]
        projected_ref[...] = dot3((test_high[...], test_low[...]), split(value))


def restore_body(flipped_ref, value_ref, iterate_ref, base_ref, out_ref):
    flipped = flipped_ref[...]
    out_ref[...] = pick(flipped, iterate_ref[...])
    base_ref[...] = pick(flipped, value_ref[...])


def finish_body(subs, flipped_ref, base_ref, *refs):
    *arrived, out_hbm, out_ref, sems = refs
    came = came_in(subs, arrived)
    halves = split(came)
    copies = []
    size = out_ref.shape[0] // 4
    for step in range(4):
        rows = slice(step * size, (step + 1) * size)
        chooser = flipped_ref[rows, : came.shape[0]]
        out_ref[rows] = base_ref[rows] + (dot(chooser, halves[0]) + dot(chooser, halves[1]))
        copy = pltpu.make_async_copy(out_ref.at[rows], out_hbm.at[rows], sems.at[step])
        copy.start()
        copies.append(copy)
    for copy in copies:
        copy.wait()


def swaps(count, stride, odd):
    partner = list(range(count))
    for low in range(count - stride):
        if (low // stride) % 2 == odd:
            partner[low], partner[low + stride] = low + stride, low
    return list(enumerate(partner)) if partner != list(range(count)) else []


def local(load_terms, schur_matrix, local_inverse, coarse_modes, cluster_inverse, row_blocks):
    load = load_terms[0, 0]
    basis = coarse_modes[0, 0]
    columns = cluster_inverse[0]
    blocks = row_blocks[0, 0]
    rows, loads = load.shape
    modes = basis.shape[1]
    shared_rows = blocks.shape[1]
    listed = 4 * shared_rows
    subs = lax.axis_size("sub")
    if lax.axis_size("grp") != GROUPS or loads % PIECE:
        raise ValueError("unexpected sizes")

    up = [(low, (low + 1) % subs) for low in range(subs)]
    down = [(target, source) for source, target in up]
    plans = [(0, swaps(subs, ROW_SUBS, 0)), (2, up), (1, down), (3, swaps(subs, ROW_SUBS, 1))]
    plans = [plan for plan in plans if plan[1]]
    count = len(plans)
    def exchange(parts):
        return [lax.ppermute(parts[place], "sub", pairs) for place, pairs in plans]

    def whole(width, kind=f32):
        return ((rows, width), kind)

    pair_plan = [(0, 1), (1, 0), (2, 3), (3, 2)]
    mirror_plan = [(0, 3), (3, 0), (1, 2), (2, 1)]
    shared = [((shared_rows, loads), f32)] * count
    outside = pl.BlockSpec(memory_space=pltpu.HBM)
    pieces = loads // PIECE
    size = rows * loads
    run = Chain()

    one_hot, load_near, sent, *parts = run(
        lambda *refs: listed_body(subs, count, *refs),
        [((listed, rows), bf16), whole(loads), ((modes, modes), f32)] + shared, 4 * listed * size, 16 * size,
        *[pltpu.with_memory_space_constraint(array, pltpu.HBM) for array in (blocks, load, columns)], ins=[outside] * 3,
        scratch=[pltpu.VMEM(blocks.shape, blocks.dtype)] + [pltpu.SemaphoreType.DMA] * 3,
    )
    arrived = exchange(parts)
    other = lax.ppermute(sent, "grp", pair_plan)
    chooser, flipped, basis_high, basis_low, test_high, test_low, ahead, ordered = run(
        lambda *refs: order_body(subs, *refs),
        [whole(rows, bf16)] * 2 + [whole(modes, bf16)] * 2 + [((modes, rows), bf16)] * 2
        + [((modes, loads), f32), whole(loads)],
        4 * rows * size, 24 * size, one_hot, load_near, basis,
    )
    mixers = run(blend_body, [((2 * modes, 2 * modes), bf16)] * 2, size, size, columns, other)
    value, iterate = ordered, None
    for iteration in range(ITERS):
        first, last = iteration == 0, iteration == ITERS - 1
        shapes = [((modes, PIECE), f32)] * pieces
        own = run(
            lambda *refs: project_body(subs, count, *refs), shapes, 6 * modes * size, 12 * size,
            ahead, test_high, test_low, *arrived,
        )
        theirs = [lax.ppermute(piece, "grp", pair_plan) for piece in own]
        kept, came = [], []
        for place in range(pieces):
            away, keep = run(
                mix_body, [((modes, PIECE), f32)] * 2, 24 * modes * modes * PIECE, 4 * rows * PIECE,
                own[place], theirs[place], *mixers,
            )
            kept.append(keep)
            came.append(lax.ppermute(away, "grp", mirror_plan))
        if first:
            solve_high, solve_low = run(
                lambda *refs: solver_body(subs, listed, *refs), [whole(rows, bf16)] * 2, 8 * rows**3, 12 * size,
                chooser, local_inverse[0, 0],
            )
        (fine,) = run(
            lambda *refs: solve_body(subs, *refs), [whole(loads)], 6 * rows * size, 12 * size,
            value, solve_high, solve_low, *arrived,
        )
        steps = []
        for place in range(pieces):
            final = place == pieces - 1
            step, *parts = run(
                lambda kept, came, fine, high, low, *refs: correct_body(kept, came, fine, high, low, place, *refs),
                [whole(PIECE)] + (shared if final else []), 6 * modes * rows * PIECE, 12 * rows * PIECE,
                kept[place], came[place], fine, basis_high, basis_low, *(steps if final else []),
            )
            steps.append(step)
        arrived = exchange(parts)
        if first:
            schur_high, schur_low = run(
                schur_body, [whole(rows, bf16)] * 2, 8 * rows**3, 12 * size, chooser, flipped, schur_matrix[0, 0],
            )
        base, total = run(
            lambda *refs: ahead_body(pieces, first, *refs), [whole(loads)] * 2, 6 * rows * size, 16 * size,
            *steps, *([] if first else [iterate]), ordered, schur_high, schur_low,
        )
        parts = run(
            lambda *refs: product_body(subs, count, *refs), shared, 2 * rows * size, 12 * size,
            base, schur_high, schur_low, *arrived,
        )
        before, arrived = arrived, exchange(parts)
        *projected, iterate, value = run(
            lambda *refs: follow_body(subs, count, last, *refs),
            ([] if last else [((modes, loads), f32)]) + [whole(loads)] * 2, 3 * rows * size, 16 * size,
            base, total, schur_high, schur_low, *before, *parts, *([] if last else [test_high, test_low]),
        )
        ahead = projected[0] if projected else None
    near, solution_rows = run(
        restore_body, [whole(loads)] * 2, 8 * rows * size, 10 * size, flipped, value, iterate,
    )
    (residual_rows,) = run(
        lambda *refs: finish_body(subs, *refs), [whole(loads)], 4 * rows * size, 10 * size,
        flipped, near, *arrived, places=[outside],
        scratch=[pltpu.VMEM((rows, loads), f32), pltpu.SemaphoreType.DMA((4,))],
    )
    return (solution_rows[None, None], residual_rows[None, None])


def solution(mesh):
    return jax.shard_map(
        local,
        mesh=mesh,
        in_specs=(
            P("sub", "grp", None, None),
            P("sub", "grp", None, None),
            P("sub", "grp", None, None),
            P("sub", "grp", None, None),
            P("sub", None, "grp"),
            P("sub", "grp", None, None),
        ),
        out_specs=(P("sub", "grp", None, None), P("sub", "grp", None, None)),
        check_vma=False,
    )
```

profile of v0, /device:TPU:0, one launch (start us, length us, event | category | flops | bytes accessed | tf_op | source)
XLA Modules:
  0.0 78.8 jit_solution(13781277051579771461)
XLA Ops:
  0.6 1.7 %shard_map.77 = (bf16[384,512]{1,0:T(8,128)(2,1)S(1)}, f32[512,384]{1,0:T(8,128)S(1)}, f32[128,128]{1,0:T(8,128)S(1)}, f32[96,384]{1,0:T(8,128)S(1)}, f32[96,384]{1,0:T(8,128)S(1)}, /*index=5*/f32[96,384]{1,0:T(8,128)S(1)}) custom-call(s32[4,96]{1,0:T(4,128)} %bitcast.15, f32[512,384]{1,0:T(8,128)} %bitcast.14, f32[512,128]{1,0:T(8,128)} %bitcast.9), custom_call_target="tpu_custom_call" | custom-call | flops 301989888 | bytes 3145728 | tf_op jit(solution)/shard_map/pallas_call | solution.py:34
  2.4 3.0 %collective-permute-start = (f32[96,384]{1,0:T(8,128)S(1)}, f32[96,384]{1,0:T(8,128)S(1)}, u32[]{:S(2)}, u32[]{:S(2)}) collective-permute-start(f32[96,384]{1,0:T(8,128)S(1)} %get-tuple-element.71), channel_id=1, source_target_pairs={{0,16},{4,20},{8,24},{12,28},{16,0},{20,4},{24,8},{28,12},{1,17},{... | collective-permute-start | bytes 442376 | tf_op jit(solution)/shard_map/ppermute | solution.py:294
  5.4 2.6 %collective-permute-start.2 = (f32[96,384]{1,0:T(8,128)S(1)}, f32[96,384]{1,0:T(8,128)S(1)}, u32[]{:S(2)}, u32[]{:S(2)}) collective-permute-start(f32[96,384]{1,0:T(8,128)S(1)} %get-tuple-element.73), channel_id=1, source_target_pairs={{4,0},{8,4},{12,8},{16,12},{20,16},{24,20},{28,24},{0,28},{5,1},{9... | collective-permute-start | bytes 442376 | tf_op jit(solution)/shard_map/ppermute | solution.py:294
  8.0 1.6 %collective-permute-start.3 = (f32[128,128]{1,0:T(8,128)S(1)}, f32[128,128]{1,0:T(8,128)S(1)}, u32[]{:S(2)}, u32[]{:S(2)}) collective-permute-start(f32[128,128]{1,0:T(8,128)S(1)} %get-tuple-element.74), channel_id=1, source_target_pairs={{0,1},{1,0},{2,3},{3,2},{4,5},{5,4},{6,7},{7,6},{8,9},{9,8},{10,11... | collective-permute-start | bytes 196616 | tf_op jit(solution)/shard_map/ppermute | solution.py:314
  9.6 1.6 %shard_map.78 = (bf16[512,512]{1,0:T(8,128)(2,1)S(1)}, bf16[512,512]{1,0:T(8,128)(2,1)S(1)}, bf16[512,128]{1,0:T(8,128)(2,1)S(1)}, bf16[512,128]{1,0:T(8,128)(2,...) custom-call(bf16[384,512]{1,0:T(8,128)(2,1)S(1)} %get-tuple-element., ...), custom_call_target="tpu_custom_call" | custom-call | flops 402653184 | bytes 4718592 | tf_op jit(solution)/shard_map/pallas_call | solution.py:34
  11.2 1.1 %collective-permute-done.3.refs_1_ = f32[128,128]{1,0:T(8,128)S(1)} collective-permute-done((f32[128,128]{1,0:T(8,128)S(1)}, f32[128,128]{1,0:T(8,128)S(1)}, u32[]{:S(2)}, u32[]{:S(2)}) %collective-permute-start.3) | collective-permute-done | bytes 65568 | tf_op jit(solution)/shard_map/ppermute | solution.py:314
  12.8 1.6 %collective-permute-start.4 = (f32[128,128]{1,0:T(8,128)S(1)}, f32[128,128]{1,0:T(8,128)S(1)}, u32[]{:S(2)}, u32[]{:S(2)}) collective-permute-start(f32[128,128]{1,0:T(8,128)S(1)} %get-tuple-element.77.refs_0_.refs_4_), channel_id=1, source_target_pairs={{0,1},{1,0},{2,3},{3,2},{4,5},{5,4},{6,7},{7,6},{8,9},{9,8},{10,11... | collective-permute-start | bytes 196616 | tf_op jit(solution)/shard_map/ppermute | solution.py:330
  14.5 0.4 collective-permute-start.7
  14.9 1.6 %collective-permute-start.6 = (f32[128,128]{1,0:T(8,128)S(1)}, f32[128,128]{1,0:T(8,128)S(1)}, u32[]{:S(2)}, u32[]{:S(2)}) collective-permute-start(f32[128,128]{1,0:T(8,128)S(1)} %get-tuple-element.82.refs_0_), channel_id=1, source_target_pairs={{0,1},{1,0},{2,3},{3,2},{4,5},{5,4},{6,7},{7,6},{8,9},{9,8},{10,11... | collective-permute-start | bytes 196616 | tf_op jit(solution)/shard_map/ppermute | solution.py:330
  16.5 1.4 %collective-permute-done.4.refs_1_ = f32[128,128]{1,0:T(8,128)S(1)} collective-permute-done((f32[128,128]{1,0:T(8,128)S(1)}, f32[128,128]{1,0:T(8,128)S(1)}, u32[]{:S(2)}, u32[]{:S(2)}) %collective-permute-start.4) | collective-permute-done | bytes 65568 | tf_op jit(solution)/shard_map/ppermute | solution.py:330
  18.1 3.6 %collective-permute-start.5 = (f32[128,128]{1,0:T(8,128)S(1)}, f32[128,128]{1,0:T(8,128)S(1)}, u32[]{:S(2)}, u32[]{:S(2)}) collective-permute-start(f32[128,128]{1,0:T(8,128)S(1)} %get-tuple-element.80.refs_4_), channel_id=1, source_target_pairs={{0,3},{3,0},{1,2},{2,1},{4,7},{7,4},{5,6},{6,5},{8,11},{11,8},{9,1... | collective-permute-start | bytes 196616 | tf_op jit(solution)/shard_map/ppermute | solution.py:338
  21.9 0.5 collective-permute-start.8
  22.6 3.5 %collective-permute-start.9 = (f32[128,128]{1,0:T(8,128)S(1)}, f32[128,128]{1,0:T(8,128)S(1)}, u32[]{:S(2)}, u32[]{:S(2)}) collective-permute-start(f32[128,128]{1,0:T(8,128)S(1)} %get-tuple-element.85.refs_2_), channel_id=1, source_target_pairs={{0,3},{3,0},{1,2},{2,1},{4,7},{7,4},{5,6},{6,5},{8,11},{11,8},{9,1... | collective-permute-start | bytes 196616 | tf_op jit(solution)/shard_map/ppermute | solution.py:338
  26.2 1.3 %shard_map.84 = (bf16[512,512]{1,0:T(8,128)(2,1)S(1)}, bf16[512,512]{1,0:T(8,128)(2,1)S(1)}) custom-call(bf16[512,512]{1,0:T(8,128)(2,1)S(1)} %get-tuple-element.75.refs_2_.refs_0_, f32[512,512]{1,0:T(8,128)S(1)} %bitcast.11, f32[128,128]{1,0:T(8,128)S(1)} %get-tuple-element.85.refs_2_), custom_call_target="tpu_custom_call" | custom-call | flops 1073741824 | bytes 2359296 | tf_op jit(solution)/shard_map/pallas_call | solution.py:34
  27.5 1.0 %shard_map.85.refs_2_.refs_5_ = f32[512,384]{1,0:T(8,128)S(1)} custom-call(f32[512,384]{1,0:T(8,128)S(1)} %get-tuple-element.81.refs_0_.refs_3_.refs_4_, bf16[512,512]{1,0:T(8,128)(2,1)S(1)} %get-tuple-element.86.refs_1_.refs_6_, bf16[512,512]{1,0:T(8,128)(2,1)S(1)} %get-tuple-element.87.refs_2_, f32[96,384]{1,0:T(8,128)S(1)} %collective-permute-done.refs_3_, ...), custom_call_target="tpu_custom_call" | custom-call | flops 603979776 | bytes 2359296 | tf_op jit(solution)/shard_map/pallas_call | solution.py:34
  29.4 0.7 collective-permute-start.10
  30.1 2.6 %collective-permute-start.12 = (f32[96,384]{1,0:T(8,128)S(1)}, f32[96,384]{1,0:T(8,128)S(1)}, u32[]{:S(2)}, u32[]{:S(2)}) collective-permute-start(f32[96,384]{1,0:T(8,128)S(1)} %get-tuple-element.99), channel_id=1, source_target_pairs={{4,0},{8,4},{12,8},{16,12},{20,16},{24,20},{28,24},{0,28},{5,1},{9... | collective-permute-start | bytes 442376 | tf_op jit(solution)/shard_map/ppermute | solution.py:294
  32.7 1.3 %shard_map.89 = (bf16[512,512]{1,0:T(8,128)(2,1)S(1)}, bf16[512,512]{1,0:T(8,128)(2,1)S(1)}) custom-call(bf16[512,512]{1,0:T(8,128)(2,1)S(1)} %get-tuple-element.75.refs_2_.refs_0_, bf16[512,512]{1,0:T(8,128)(2,1)S(1)} %get-tuple-element.67.refs_1_.refs_0_, f32[512,512]{1,0:T(8,128)S(1)} %bitcast.12, f32[512,128]{1,0:T(8,128)S(1)} %get-tuple-element.92.refs_3_.refs_2_), custom_call_target="tpu_custom_call" | custom-call | flops 1073741824 | bytes 2359296 | tf_op jit(solution)/shard_map/pallas_call | solution.py:34
  34.0 1.0 %shard_map.90 = (f32[512,384]{1,0:T(8,128)S(1)}, f32[512,384]{1,0:T(8,128)S(1)}) custom-call(f32[512,128]{1,0:T(8,128)S(1)} %shard_map.86.refs_5_.refs_0_, f32[512,128]{1,0:T(8,128)S(1)} %shard_map.87.refs_6_.refs_7_.refs_1_, f32[512,128]{1,0:T(8,128)S(1)} %get-tuple-element.92.refs_3_.refs_2_, f32[512,384]{1,0:T(8,128)S(1)} %get-tuple-element.81.refs_0_.refs_3_.refs_4_, ...), custom_call_target="tpu_custom_call" | custom-call | flops 603979776 | bytes 3145728 | tf_op jit(solution)/shard_map/pallas_call | solution.py:34
  35.0 1.1 %collective-permute-done.10.refs_3_.refs_4_ = f32[96,384]{1,0:T(8,128)S(1)} collective-permute-done((f32[96,384]{1,0:T(8,128)S(1)}, f32[96,384]{1,0:T(8,128)S(1)}, u32[]{:S(2)}, u32[]{:S(2)}) %collective-permute-start.10) | collective-permute-done | bytes 147488 | tf_op jit(solution)/shard_map/ppermute | solution.py:294
  36.2 0.6 shard_map.91
  36.8 1.9 %collective-permute-start.13 = (f32[96,384]{1,0:T(8,128)S(1)}, f32[96,384]{1,0:T(8,128)S(1)}, u32[]{:S(2)}, u32[]{:S(2)}) collective-permute-start(f32[96,384]{1,0:T(8,128)S(1)} %get-tuple-element.100.refs_7_.refs_12_), channel_id=1, source_target_pairs={{0,16},{4,20},{8,24},{12,28},{16,0},{20,4},{24,8},{28,12},{1,17},{... | collective-permute-start | bytes 442376 | tf_op jit(solution)/shard_map/ppermute | solution.py:294
  38.7 1.2 %collective-permute-start.15 = (f32[96,384]{1,0:T(8,128)S(1)}, f32[96,384]{1,0:T(8,128)S(1)}, u32[]{:S(2)}, u32[]{:S(2)}) collective-permute-start(f32[96,384]{1,0:T(8,128)S(1)} %get-tuple-element.101.refs_8_), channel_id=1, source_target_pairs={{4,0},{8,4},{12,8},{16,12},{20,16},{24,20},{28,24},{0,28},{5,1},{9... | collective-permute-start | bytes 442376 | tf_op jit(solution)/shard_map/ppermute | solution.py:294
  39.9 0.9 %shard_map.92 = (f32[128,384]{1,0:T(8,128)S(1)}, f32[512,384]{1,0:T(8,128)S(1)}, f32[512,384]{1,0:T(8,128)S(1)}) custom-call(f32[512,384]{1,0:T(8,128)S(1)} %get-tuple-element.95.refs_0_.refs_6_, f32[512,384]{1,0:T(8,128)S(1)} %get-tuple-element.96.refs_1_, bf16[512,512]{1,0:T(8,128)(2,1)S(1)} %get-tuple-element.93.refs_4_.refs_6_.refs_1_.refs_2_.refs_5_, ...), custom_call_target="tpu_custom_call" | custom-call | flops 301989888 | bytes 3145728 | tf_op jit(solution)/shard_map/pallas_call | solution.py:34
  40.8 2.5 %collective-permute-done.13.refs_3_ = f32[96,384]{1,0:T(8,128)S(1)} collective-permute-done((f32[96,384]{1,0:T(8,128)S(1)}, f32[96,384]{1,0:T(8,128)S(1)}, u32[]{:S(2)}, u32[]{:S(2)}) %collective-permute-start.13) | collective-permute-done | bytes 147488 | tf_op jit(solution)/shard_map/ppermute | solution.py:294
  43.5 1.9 %collective-permute-done.14.refs_4_ = f32[96,384]{1,0:T(8,128)S(1)} collective-permute-done((f32[96,384]{1,0:T(8,128)S(1)}, f32[96,384]{1,0:T(8,128)S(1)}, u32[]{:S(2)}, u32[]{:S(2)}) %collective-permute-start.14) | collective-permute-done | bytes 147488 | tf_op jit(solution)/shard_map/ppermute | solution.py:294
  45.7 0.5 collective-permute-start.16
  46.3 1.6 %collective-permute-start.19 = (f32[128,128]{1,0:T(8,128)S(1)}, f32[128,128]{1,0:T(8,128)S(1)}, u32[]{:S(2)}, u32[]{:S(2)}) collective-permute-start(f32[128,128]{1,0:T(8,128)S(1)} %get-tuple-element.109.refs_0_), channel_id=1, source_target_pairs={{0,1},{1,0},{2,3},{3,2},{4,5},{5,4},{6,7},{7,6},{8,9},{9,8},{10,11... | collective-permute-start | bytes 196616 | tf_op jit(solution)/shard_map/ppermute | solution.py:330
  47.8 0.5 collective-permute-start.18
  48.3 1.8 %collective-permute-done.16.refs_1_ = f32[128,128]{1,0:T(8,128)S(1)} collective-permute-done((f32[128,128]{1,0:T(8,128)S(1)}, f32[128,128]{1,0:T(8,128)S(1)}, u32[]{:S(2)}, u32[]{:S(2)}) %collective-permute-start.16) | collective-permute-done | bytes 65568 | tf_op jit(solution)/shard_map/ppermute | solution.py:330
  50.3 3.2 %collective-permute-start.17 = (f32[128,128]{1,0:T(8,128)S(1)}, f32[128,128]{1,0:T(8,128)S(1)}, u32[]{:S(2)}, u32[]{:S(2)}) collective-permute-start(f32[128,128]{1,0:T(8,128)S(1)} %get-tuple-element.106.refs_4_), channel_id=1, source_target_pairs={{0,3},{3,0},{1,2},{2,1},{4,7},{7,4},{5,6},{6,5},{8,11},{11,8},{9,1... | collective-permute-start | bytes 196616 | tf_op jit(solution)/shard_map/ppermute | solution.py:338
  53.8 0.7 collective-permute-start.20
  54.8 3.2 %collective-permute-start.21 = (f32[128,128]{1,0:T(8,128)S(1)}, f32[128,128]{1,0:T(8,128)S(1)}, u32[]{:S(2)}, u32[]{:S(2)}) collective-permute-start(f32[128,128]{1,0:T(8,128)S(1)} %get-tuple-element.111.refs_6_), channel_id=1, source_target_pairs={{0,3},{3,0},{1,2},{2,1},{4,7},{7,4},{5,6},{6,5},{8,11},{11,8},{9,1... | collective-permute-start | bytes 196616 | tf_op jit(solution)/shard_map/ppermute | solution.py:338
  58.0 1.0 %shard_map.97.refs_2_.refs_5_ = f32[512,384]{1,0:T(8,128)S(1)} custom-call(f32[512,384]{1,0:T(8,128)S(1)} %get-tuple-element.107.refs_0_, bf16[512,512]{1,0:T(8,128)(2,1)S(1)} %get-tuple-element.86.refs_1_.refs_6_, bf16[512,512]{1,0:T(8,128)(2,1)S(1)} %get-tuple-element.87.refs_2_, f32[96,384]{1,0:T(8,128)S(1)} %collective-permute-done.13.refs_3_, ...), custom_call_target="tpu_custom_call" | custom-call | flops 603979776 | bytes 2359296 | tf_op jit(solution)/shard_map/pallas_call | solution.py:34
  59.3 0.6 collective-permute-done.20.refs_1_
  60.2 0.7 collective-permute-done.21.refs_1_
  61.2 0.7 collective-permute-start.22
  61.9 2.6 %collective-permute-start.24 = (f32[96,384]{1,0:T(8,128)S(1)}, f32[96,384]{1,0:T(8,128)S(1)}, u32[]{:S(2)}, u32[]{:S(2)}) collective-permute-start(f32[96,384]{1,0:T(8,128)S(1)} %get-tuple-element.120), channel_id=1, source_target_pairs={{4,0},{8,4},{12,8},{16,12},{20,16},{24,20},{28,24},{0,28},{5,1},{9... | collective-permute-start | bytes 442376 | tf_op jit(solution)/shard_map/ppermute | solution.py:294
  64.5 1.0 %shard_map.101 = (f32[512,384]{1,0:T(8,128)S(1)}, f32[512,384]{1,0:T(8,128)S(1)}) custom-call(f32[512,128]{1,0:T(8,128)S(1)} %shard_map.98.refs_5_.refs_0_, f32[512,128]{1,0:T(8,128)S(1)} %shard_map.99.refs_6_.refs_7_.refs_1_, f32[512,128]{1,0:T(8,128)S(1)} %get-tuple-element.114.refs_2_.refs_7_, f32[512,384]{1,0:T(8,128)S(1)} %get-tuple-element.115.refs_3_, ...), custom_call_target="tpu_custom_call" | custom-call | flops 603979776 | bytes 3145728 | tf_op jit(solution)/shard_map/pallas_call | solution.py:34
  65.5 2.4 %collective-permute-done.22.refs_3_.refs_4_ = f32[96,384]{1,0:T(8,128)S(1)} collective-permute-done((f32[96,384]{1,0:T(8,128)S(1)}, f32[96,384]{1,0:T(8,128)S(1)}, u32[]{:S(2)}, u32[]{:S(2)}) %collective-permute-start.22) | collective-permute-done | bytes 147488 | tf_op jit(solution)/shard_map/ppermute | solution.py:294
  68.0 0.6 shard_map.102
  68.6 1.0 %collective-permute-start.25 = (f32[96,384]{1,0:T(8,128)S(1)}, f32[96,384]{1,0:T(8,128)S(1)}, u32[]{:S(2)}, u32[]{:S(2)}) collective-permute-start(f32[96,384]{1,0:T(8,128)S(1)} %get-tuple-element.121.refs_7_.refs_10_), channel_id=1, source_target_pairs={{0,16},{4,20},{8,24},{12,28},{16,0},{20,4},{24,8},{28,12},{1,17},{... | collective-permute-start | bytes 442376 | tf_op jit(solution)/shard_map/ppermute | solution.py:294
  69.6 2.1 %collective-permute-start.27 = (f32[96,384]{1,0:T(8,128)S(1)}, f32[96,384]{1,0:T(8,128)S(1)}, u32[]{:S(2)}, u32[]{:S(2)}) collective-permute-start(f32[96,384]{1,0:T(8,128)S(1)} %get-tuple-element.122.refs_8_), channel_id=1, source_target_pairs={{4,0},{8,4},{12,8},{16,12},{20,16},{24,20},{28,24},{0,28},{5,1},{9... | collective-permute-start | bytes 442376 | tf_op jit(solution)/shard_map/ppermute | solution.py:294
  71.7 0.5 shard_map.103
  72.2 1.6 %shard_map.104 = (f32[512,384]{1,0:T(8,128)S(1)}, f32[512,384]{1,0:T(8,128)}) custom-call(bf16[512,512]{1,0:T(8,128)(2,1)S(1)} %get-tuple-element.67.refs_1_.refs_0_, f32[512,384]{1,0:T(8,128)S(1)} %get-tuple-element.124.refs_1_, f32[512,384]{1,0:T(8,128)S(1)} %get-tuple-element.125.refs_2_.refs_3_, f32[512,384]{1,0:T(8,128)S(1)} %get-tuple-element.125.refs_2_.refs_3_), custom_call_target="tpu_custom_call" | custom-call | flops 805306368 | bytes 1966080 | tf_op jit(solution)/shard_map/pallas_call | solution.py:34
  73.8 1.2 %collective-permute-done.25.refs_2_ = f32[96,384]{1,0:T(8,128)S(1)} collective-permute-done((f32[96,384]{1,0:T(8,128)S(1)}, f32[96,384]{1,0:T(8,128)S(1)}, u32[]{:S(2)}, u32[]{:S(2)}) %collective-permute-start.25) | collective-permute-done | bytes 147488 | tf_op jit(solution)/shard_map/ppermute | solution.py:294
  75.1 2.1 %collective-permute-done.26.refs_3_ = f32[96,384]{1,0:T(8,128)S(1)} collective-permute-done((f32[96,384]{1,0:T(8,128)S(1)}, f32[96,384]{1,0:T(8,128)S(1)}, u32[]{:S(2)}, u32[]{:S(2)}) %collective-permute-start.26) | collective-permute-done | bytes 147488 | tf_op jit(solution)/shard_map/ppermute | solution.py:294
  77.2 1.4 %shard_map.105 = f32[512,384]{1,0:T(8,128)} custom-call(bf16[512,512]{1,0:T(8,128)(2,1)S(1)} %get-tuple-element.67.refs_1_.refs_0_, f32[512,384]{1,0:T(8,128)S(1)} %get-tuple-element.127.refs_1_.refs_5_, f32[96,384]{1,0:T(8,128)S(1)} %collective-permute-done.25.refs_2_, f32[96,384]{1,0:T(8,128)S(1)} %collective-permute-done.26.refs_3_, ...), custom_call_target="tpu_custom_call" | custom-call | flops 402653184 | bytes 1966080 | tf_op jit(solution)/shard_map/pallas_call | solution.py:34
  (45 shorter events, 4.4 us)
Async XLA Ops:
  0.6 9.0 %copy-start = (f32[1,1,512,128]{3,2,1,0:T(8,128)S(1)}, f32[1,1,512,128]{3,2,1,0:T(8,128)}, u32[]{:S(2)}) copy-start(f32[1,1,512,128]{3,2,1,0:T(8,128)} %param.9) | copy-start | bytes 786436
  2.4 10.1 %collective-permute-start = (f32[96,384]{1,0:T(8,128)S(1)}, f32[96,384]{1,0:T(8,128)S(1)}, u32[]{:S(2)}, u32[]{:S(2)}) collective-permute-start(f32[96,384]{1,0:T(8,128)S(1)} %get-tuple-element.71), channel_id=1, source_target_pairs={{0,16},{4,20},{8,24},{12,28},{16,0},{20,4},{24,8},{28,12},{1,17},{... | collective-permute-start | bytes 442376 | tf_op jit(solution)/shard_map/ppermute | solution.py:294
  5.4 7.0 %collective-permute-start.1 = (f32[96,384]{1,0:T(8,128)S(1)}, f32[96,384]{1,0:T(8,128)S(1)}, u32[]{:S(2)}, u32[]{:S(2)}) collective-permute-start(f32[96,384]{1,0:T(8,128)S(1)} %get-tuple-element.72), channel_id=1, source_target_pairs={{0,4},{4,8},{8,12},{12,16},{16,20},{20,24},{24,28},{28,0},{1,5},{5... | collective-permute-start | bytes 442376 | tf_op jit(solution)/shard_map/ppermute | solution.py:294
  5.4 7.1 %collective-permute-start.2 = (f32[96,384]{1,0:T(8,128)S(1)}, f32[96,384]{1,0:T(8,128)S(1)}, u32[]{:S(2)}, u32[]{:S(2)}) collective-permute-start(f32[96,384]{1,0:T(8,128)S(1)} %get-tuple-element.73), channel_id=1, source_target_pairs={{4,0},{8,4},{12,8},{16,12},{20,16},{24,20},{28,24},{0,28},{5,1},{9... | collective-permute-start | bytes 442376 | tf_op jit(solution)/shard_map/ppermute | solution.py:294
  8.0 4.3 %collective-permute-start.3 = (f32[128,128]{1,0:T(8,128)S(1)}, f32[128,128]{1,0:T(8,128)S(1)}, u32[]{:S(2)}, u32[]{:S(2)}) collective-permute-start(f32[128,128]{1,0:T(8,128)S(1)} %get-tuple-element.74), channel_id=1, source_target_pairs={{0,1},{1,0},{2,3},{3,2},{4,5},{5,4},{6,7},{7,6},{8,9},{9,8},{10,11... | collective-permute-start | bytes 196616 | tf_op jit(solution)/shard_map/ppermute | solution.py:314
  9.6 2.7 %copy-start.1 = (f32[1,512,128]{2,1,0:T(8,128)S(1)}, f32[1,512,128]{2,1,0:T(8,128)}, u32[]{:S(2)}) copy-start(f32[1,512,128]{2,1,0:T(8,128)} %param.10) | copy-start | bytes 786436
  12.5 13.7 %copy-start.2 = (f32[1,1,512,512]{3,2,1,0:T(8,128)S(1)}, f32[1,1,512,512]{3,2,1,0:T(8,128)}, u32[]{:S(2)}) copy-start(f32[1,1,512,512]{3,2,1,0:T(8,128)} %param.8) | copy-start | bytes 3145732
  12.8 5.0 %collective-permute-start.4 = (f32[128,128]{1,0:T(8,128)S(1)}, f32[128,128]{1,0:T(8,128)S(1)}, u32[]{:S(2)}, u32[]{:S(2)}) collective-permute-start(f32[128,128]{1,0:T(8,128)S(1)} %get-tuple-element.77.refs_0_.refs_4_), channel_id=1, source_target_pairs={{0,1},{1,0},{2,3},{3,2},{4,5},{5,4},{6,7},{7,6},{8,9},{9,8},{10,11... | collective-permute-start | bytes 196616 | tf_op jit(solution)/shard_map/ppermute | solution.py:330
  14.5 7.2 %collective-permute-start.7 = (f32[128,128]{1,0:T(8,128)S(1)}, f32[128,128]{1,0:T(8,128)S(1)}, u32[]{:S(2)}, u32[]{:S(2)}) collective-permute-start(f32[128,128]{1,0:T(8,128)S(1)} %get-tuple-element.83.refs_0_), channel_id=1, source_target_pairs={{0,1},{1,0},{2,3},{3,2},{4,5},{5,4},{6,7},{7,6},{8,9},{9,8},{10,11... | collective-permute-start | bytes 196616 | tf_op jit(solution)/shard_map/ppermute | solution.py:330
  14.9 7.5 %collective-permute-start.6 = (f32[128,128]{1,0:T(8,128)S(1)}, f32[128,128]{1,0:T(8,128)S(1)}, u32[]{:S(2)}, u32[]{:S(2)}) collective-permute-start(f32[128,128]{1,0:T(8,128)S(1)} %get-tuple-element.82.refs_0_), channel_id=1, source_target_pairs={{0,1},{1,0},{2,3},{3,2},{4,5},{5,4},{6,7},{7,6},{8,9},{9,8},{10,11... | collective-permute-start | bytes 196616 | tf_op jit(solution)/shard_map/ppermute | solution.py:330
  18.1 10.4 %collective-permute-start.5 = (f32[128,128]{1,0:T(8,128)S(1)}, f32[128,128]{1,0:T(8,128)S(1)}, u32[]{:S(2)}, u32[]{:S(2)}) collective-permute-start(f32[128,128]{1,0:T(8,128)S(1)} %get-tuple-element.80.refs_4_), channel_id=1, source_target_pairs={{0,3},{3,0},{1,2},{2,1},{4,7},{7,4},{5,6},{6,5},{8,11},{11,8},{9,1... | collective-permute-start | bytes 196616 | tf_op jit(solution)/shard_map/ppermute | solution.py:338
  21.9 6.9 %collective-permute-start.8 = (f32[128,128]{1,0:T(8,128)S(1)}, f32[128,128]{1,0:T(8,128)S(1)}, u32[]{:S(2)}, u32[]{:S(2)}) collective-permute-start(f32[128,128]{1,0:T(8,128)S(1)} %get-tuple-element.84.refs_4_), channel_id=1, source_target_pairs={{0,3},{3,0},{1,2},{2,1},{4,7},{7,4},{5,6},{6,5},{8,11},{11,8},{9,1... | collective-permute-start | bytes 196616 | tf_op jit(solution)/shard_map/ppermute | solution.py:338
  22.6 6.4 %collective-permute-start.9 = (f32[128,128]{1,0:T(8,128)S(1)}, f32[128,128]{1,0:T(8,128)S(1)}, u32[]{:S(2)}, u32[]{:S(2)}) collective-permute-start(f32[128,128]{1,0:T(8,128)S(1)} %get-tuple-element.85.refs_2_), channel_id=1, source_target_pairs={{0,3},{3,0},{1,2},{2,1},{4,7},{7,4},{5,6},{6,5},{8,11},{11,8},{9,1... | collective-permute-start | bytes 196616 | tf_op jit(solution)/shard_map/ppermute | solution.py:338
  29.1 3.7 %copy-start.3 = (f32[1,1,512,512]{3,2,1,0:T(8,128)S(1)}, f32[1,1,512,512]{3,2,1,0:T(8,128)}, u32[]{:S(2)}) copy-start(f32[1,1,512,512]{3,2,1,0:T(8,128)} %param.7) | copy-start | bytes 3145732
  29.4 6.7 %collective-permute-start.10 = (f32[96,384]{1,0:T(8,128)S(1)}, f32[96,384]{1,0:T(8,128)S(1)}, u32[]{:S(2)}, u32[]{:S(2)}) collective-permute-start(f32[96,384]{1,0:T(8,128)S(1)} %get-tuple-element.97), channel_id=1, source_target_pairs={{0,16},{4,20},{8,24},{12,28},{16,0},{20,4},{24,8},{28,12},{1,17},{... | collective-permute-start | bytes 442376 | tf_op jit(solution)/shard_map/ppermute | solution.py:294
  30.1 6.2 %collective-permute-start.11 = (f32[96,384]{1,0:T(8,128)S(1)}, f32[96,384]{1,0:T(8,128)S(1)}, u32[]{:S(2)}, u32[]{:S(2)}) collective-permute-start(f32[96,384]{1,0:T(8,128)S(1)} %get-tuple-element.98), channel_id=1, source_target_pairs={{0,4},{4,8},{8,12},{12,16},{16,20},{20,24},{24,28},{28,0},{1,5},{5... | collective-permute-start | bytes 442376 | tf_op jit(solution)/shard_map/ppermute | solution.py:294
  30.1 6.2 %collective-permute-start.12 = (f32[96,384]{1,0:T(8,128)S(1)}, f32[96,384]{1,0:T(8,128)S(1)}, u32[]{:S(2)}, u32[]{:S(2)}) collective-permute-start(f32[96,384]{1,0:T(8,128)S(1)} %get-tuple-element.99), channel_id=1, source_target_pairs={{4,0},{8,4},{12,8},{16,12},{20,16},{24,20},{28,24},{0,28},{5,1},{9... | collective-permute-start | bytes 442376 | tf_op jit(solution)/shard_map/ppermute | solution.py:294
  36.8 6.4 %collective-permute-start.13 = (f32[96,384]{1,0:T(8,128)S(1)}, f32[96,384]{1,0:T(8,128)S(1)}, u32[]{:S(2)}, u32[]{:S(2)}) collective-permute-start(f32[96,384]{1,0:T(8,128)S(1)} %get-tuple-element.100.refs_7_.refs_12_), channel_id=1, source_target_pairs={{0,16},{4,20},{8,24},{12,28},{16,0},{20,4},{24,8},{28,12},{1,17},{... | collective-permute-start | bytes 442376 | tf_op jit(solution)/shard_map/ppermute | solution.py:294
  38.7 4.8 %collective-permute-start.15 = (f32[96,384]{1,0:T(8,128)S(1)}, f32[96,384]{1,0:T(8,128)S(1)}, u32[]{:S(2)}, u32[]{:S(2)}) collective-permute-start(f32[96,384]{1,0:T(8,128)S(1)} %get-tuple-element.101.refs_8_), channel_id=1, source_target_pairs={{4,0},{8,4},{12,8},{16,12},{20,16},{24,20},{28,24},{0,28},{5,1},{9... | collective-permute-start | bytes 442376 | tf_op jit(solution)/shard_map/ppermute | solution.py:294
  39.9 5.5 %collective-permute-start.14 = (f32[96,384]{1,0:T(8,128)S(1)}, f32[96,384]{1,0:T(8,128)S(1)}, u32[]{:S(2)}, u32[]{:S(2)}) collective-permute-start(f32[96,384]{1,0:T(8,128)S(1)} %get-tuple-element.102.refs_9_), channel_id=1, source_target_pairs={{0,4},{4,8},{8,12},{12,16},{16,20},{20,24},{24,28},{28,0},{1,5},{5... | collective-permute-start | bytes 442376 | tf_op jit(solution)/shard_map/ppermute | solution.py:294
  45.7 4.3 %collective-permute-start.16 = (f32[128,128]{1,0:T(8,128)S(1)}, f32[128,128]{1,0:T(8,128)S(1)}, u32[]{:S(2)}, u32[]{:S(2)}) collective-permute-start(f32[128,128]{1,0:T(8,128)S(1)} %get-tuple-element.104.refs_0_.refs_4_), channel_id=1, source_target_pairs={{0,1},{1,0},{2,3},{3,2},{4,5},{5,4},{6,7},{7,6},{8,9},{9,8},{10,11... | collective-permute-start | bytes 196616 | tf_op jit(solution)/shard_map/ppermute | solution.py:330
  46.3 7.3 %collective-permute-start.19 = (f32[128,128]{1,0:T(8,128)S(1)}, f32[128,128]{1,0:T(8,128)S(1)}, u32[]{:S(2)}, u32[]{:S(2)}) collective-permute-start(f32[128,128]{1,0:T(8,128)S(1)} %get-tuple-element.109.refs_0_), channel_id=1, source_target_pairs={{0,1},{1,0},{2,3},{3,2},{4,5},{5,4},{6,7},{7,6},{8,9},{9,8},{10,11... | collective-permute-start | bytes 196616 | tf_op jit(solution)/shard_map/ppermute | solution.py:330
  47.8 6.7 %collective-permute-start.18 = (f32[128,128]{1,0:T(8,128)S(1)}, f32[128,128]{1,0:T(8,128)S(1)}, u32[]{:S(2)}, u32[]{:S(2)}) collective-permute-start(f32[128,128]{1,0:T(8,128)S(1)} %get-tuple-element.108.refs_0_), channel_id=1, source_target_pairs={{0,1},{1,0},{2,3},{3,2},{4,5},{5,4},{6,7},{7,6},{8,9},{9,8},{10,11... | collective-permute-start | bytes 196616 | tf_op jit(solution)/shard_map/ppermute | solution.py:330
  50.3 8.7 %collective-permute-start.17 = (f32[128,128]{1,0:T(8,128)S(1)}, f32[128,128]{1,0:T(8,128)S(1)}, u32[]{:S(2)}, u32[]{:S(2)}) collective-permute-start(f32[128,128]{1,0:T(8,128)S(1)} %get-tuple-element.106.refs_4_), channel_id=1, source_target_pairs={{0,3},{3,0},{1,2},{2,1},{4,7},{7,4},{5,6},{6,5},{8,11},{11,8},{9,1... | collective-permute-start | bytes 196616 | tf_op jit(solution)/shard_map/ppermute | solution.py:338
  53.8 6.1 %collective-permute-start.20 = (f32[128,128]{1,0:T(8,128)S(1)}, f32[128,128]{1,0:T(8,128)S(1)}, u32[]{:S(2)}, u32[]{:S(2)}) collective-permute-start(f32[128,128]{1,0:T(8,128)S(1)} %get-tuple-element.110.refs_4_), channel_id=1, source_target_pairs={{0,3},{3,0},{1,2},{2,1},{4,7},{7,4},{5,6},{6,5},{8,11},{11,8},{9,1... | collective-permute-start | bytes 196616 | tf_op jit(solution)/shard_map/ppermute | solution.py:338
  54.8 6.1 %collective-permute-start.21 = (f32[128,128]{1,0:T(8,128)S(1)}, f32[128,128]{1,0:T(8,128)S(1)}, u32[]{:S(2)}, u32[]{:S(2)}) collective-permute-start(f32[128,128]{1,0:T(8,128)S(1)} %get-tuple-element.111.refs_6_), channel_id=1, source_target_pairs={{0,3},{3,0},{1,2},{2,1},{4,7},{7,4},{5,6},{6,5},{8,11},{11,8},{9,1... | collective-permute-start | bytes 196616 | tf_op jit(solution)/shard_map/ppermute | solution.py:338
  61.2 6.7 %collective-permute-start.22 = (f32[96,384]{1,0:T(8,128)S(1)}, f32[96,384]{1,0:T(8,128)S(1)}, u32[]{:S(2)}, u32[]{:S(2)}) collective-permute-start(f32[96,384]{1,0:T(8,128)S(1)} %get-tuple-element.118), channel_id=1, source_target_pairs={{0,16},{4,20},{8,24},{12,28},{16,0},{20,4},{24,8},{28,12},{1,17},{... | collective-permute-start | bytes 442376 | tf_op jit(solution)/shard_map/ppermute | solution.py:294
  61.9 6.1 %collective-permute-start.23 = (f32[96,384]{1,0:T(8,128)S(1)}, f32[96,384]{1,0:T(8,128)S(1)}, u32[]{:S(2)}, u32[]{:S(2)}) collective-permute-start(f32[96,384]{1,0:T(8,128)S(1)} %get-tuple-element.119), channel_id=1, source_target_pairs={{0,4},{4,8},{8,12},{12,16},{16,20},{20,24},{24,28},{28,0},{1,5},{5... | collective-permute-start | bytes 442376 | tf_op jit(solution)/shard_map/ppermute | solution.py:294
  61.9 6.1 %collective-permute-start.24 = (f32[96,384]{1,0:T(8,128)S(1)}, f32[96,384]{1,0:T(8,128)S(1)}, u32[]{:S(2)}, u32[]{:S(2)}) collective-permute-start(f32[96,384]{1,0:T(8,128)S(1)} %get-tuple-element.120), channel_id=1, source_target_pairs={{4,0},{8,4},{12,8},{16,12},{20,16},{24,20},{28,24},{0,28},{5,1},{9... | collective-permute-start | bytes 442376 | tf_op jit(solution)/shard_map/ppermute | solution.py:294
  68.6 6.5 %collective-permute-start.25 = (f32[96,384]{1,0:T(8,128)S(1)}, f32[96,384]{1,0:T(8,128)S(1)}, u32[]{:S(2)}, u32[]{:S(2)}) collective-permute-start(f32[96,384]{1,0:T(8,128)S(1)} %get-tuple-element.121.refs_7_.refs_10_), channel_id=1, source_target_pairs={{0,16},{4,20},{8,24},{12,28},{16,0},{20,4},{24,8},{28,12},{1,17},{... | collective-permute-start | bytes 442376 | tf_op jit(solution)/shard_map/ppermute | solution.py:294
  69.6 5.5 %collective-permute-start.27 = (f32[96,384]{1,0:T(8,128)S(1)}, f32[96,384]{1,0:T(8,128)S(1)}, u32[]{:S(2)}, u32[]{:S(2)}) collective-permute-start(f32[96,384]{1,0:T(8,128)S(1)} %get-tuple-element.122.refs_8_), channel_id=1, source_target_pairs={{4,0},{8,4},{12,8},{16,12},{20,16},{24,20},{28,24},{0,28},{5,1},{9... | collective-permute-start | bytes 442376 | tf_op jit(solution)/shard_map/ppermute | solution.py:294
  71.7 5.5 %collective-permute-start.26 = (f32[96,384]{1,0:T(8,128)S(1)}, f32[96,384]{1,0:T(8,128)S(1)}, u32[]{:S(2)}, u32[]{:S(2)}) collective-permute-start(f32[96,384]{1,0:T(8,128)S(1)} %get-tuple-element.123.refs_9_), channel_id=1, source_target_pairs={{0,4},{4,8},{8,12},{12,16},{16,20},{20,24},{24,28},{28,0},{1,5},{5... | collective-permute-start | bytes 442376 | tf_op jit(solution)/shard_map/ppermute | solution.py:294
where the time goes:
time: 78.9 us; the launch traced here: 78.8 us
  starting transfers between devices  41.1 us (52%)
  Pallas kernels  19.1 us (24%)
  waiting for transfers between devices  17.3 us (22%)
  between operations  1.09 us (1%)
    pallas_call x29, Pallas kernels, __call__(): pl.pallas_call(whole_body, out_shape=[jax.ShapeDtypeStruct(shape, kind) f...  19.1 us
    ppermute x15, starting transfers between devices, exchange(): return [lax.ppermute(parts[place], 'sub', pairs) for place, pairs in plans]  18.7 us
    ppermute x6, starting transfers between devices, local(): came.append(lax.ppermute(away, 'grp', mirror_plan))  14.7 us
    ppermute x15, waiting for transfers between devices, exchange(): return [lax.ppermute(parts[place], 'sub', pairs) for place, pairs in plans]  11.7 us
    ppermute x6, starting transfers between devices, local(): theirs = [lax.ppermute(piece, 'grp', pair_plan) for piece in own]  6.22 us
    ppermute x6, waiting for transfers between devices, local(): theirs = [lax.ppermute(piece, 'grp', pair_plan) for piece in own]  3.15 us
  transfers between devices with their start and end apart: 28, of which 14 were waited for; matrix products, arithmetic and copies ran while one was open for 0% of the time, Pallas kernels for 17%

commit v1 on v0

--- a/solution.py
+++ b/solution.py
@@ -67,8 +67,8 @@
     low_row = (sub // ROW_SUBS) % 2 == 0
     over, under = sub < subs - ROW_SUBS, sub >= ROW_SUBS
     return [
+        (low_row, 0, 0, sub > 0),
         (low_row, 3, 2, jnp.where(low_row, over, under)),
-        (low_row, 0, 0, sub > 0),
         (low_row, 1, 1, sub < subs - 1),
         (low_row, 2, 3, jnp.where(low_row, under, over)),
     ]
@@ -287,7 +287,7 @@
 
     up = [(low, (low + 1) % subs) for low in range(subs)]
     down = [(target, source) for source, target in up]
-    plans = [(0, swaps(subs, ROW_SUBS, 0)), (2, up), (1, down), (3, swaps(subs, ROW_SUBS, 1))]
+    plans = [(2, up), (1, swaps(subs, ROW_SUBS, 0)), (0, down), (3, swaps(subs, ROW_SUBS, 1))]
     plans = [plan for plan in plans if plan[1]]
     count = len(plans)
     def exchange(parts):

time: 78.9 us -> 81.4 us (1.032)
  waiting for transfers between devices: 17.3 us -> 21.6 us
  starting transfers between devices: 41.1 us -> 39.4 us
    ppermute x15, waiting for transfers between devices: 11.7 us -> 15.7 us  [exchange(): return [lax.ppermute(parts[place], 'sub', pairs) for place, pairs in plans]]
    ppermute x15, starting transfers between devices: 18.7 us -> 17 us  [exchange(): return [lax.ppermute(parts[place], 'sub', pairs) for place, pairs in plans]]
  transfers between devices with their start and end apart: 28 -> 28, of which waited for: 14 -> 13; matrix products, arithmetic and copies ran while one was open for 0% -> 0% of each run, Pallas kernels for 17% -> 17%
where the time goes in v1:
time: 81.4 us; the launch traced here: 81.3 us
  starting transfers between devices  39.4 us (48%)
  waiting for transfers between devices  21.6 us (27%)
  Pallas kernels  19.1 us (23%)
  between operations  1.11 us (1%)
    pallas_call x29, Pallas kernels, __call__(): pl.pallas_call(whole_body, out_shape=[jax.ShapeDtypeStruct(shape, kind) f...  19.1 us
    ppermute x15, starting transfers between devices, exchange(): return [lax.ppermute(parts[place], 'sub', pairs) for place, pairs in plans]  17 us
    ppermute x15, waiting for transfers between devices, exchange(): return [lax.ppermute(parts[place], 'sub', pairs) for place, pairs in plans]  15.7 us
    ppermute x6, starting transfers between devices, local(): came.append(lax.ppermute(away, 'grp', mirror_plan))  15 us
    ppermute x6, starting transfers between devices, local(): theirs = [lax.ppermute(piece, 'grp', pair_plan) for piece in own]  5.83 us
    ppermute x6, waiting for transfers between devices, local(): theirs = [lax.ppermute(piece, 'grp', pair_plan) for piece in own]  3.26 us
  transfers between devices with their start and end apart: 28, of which 13 were waited for; matrix products, arithmetic and copies ran while one was open for 0% of the time, Pallas kernels for 17%

profile of v1, /device:TPU:0, one launch (start us, length us, event | category | flops | bytes accessed | tf_op | source)
XLA Modules:
  0.0 81.3 jit_solution(6398432024876560967)
XLA Ops:
  0.6 1.7 %shard_map.77 = (bf16[384,512]{1,0:T(8,128)(2,1)S(1)}, f32[512,384]{1,0:T(8,128)S(1)}, f32[128,128]{1,0:T(8,128)S(1)}, f32[96,384]{1,0:T(8,128)S(1)}, f32[96,384]{1,0:T(8,128)S(1)}, /*index=5*/f32[96,384]{1,0:T(8,128)S(1)}) custom-call(s32[4,96]{1,0:T(4,128)} %bitcast.15, f32[512,384]{1,0:T(8,128)} %bitcast.14, f32[512,128]{1,0:T(8,128)} %bitcast.9), custom_call_target="tpu_custom_call" | custom-call | flops 301989888 | bytes 3145728 | tf_op jit(solution)/shard_map/pallas_call | solution.py:34
  2.4 0.5 collective-permute-start
  2.9 2.6 %collective-permute-start.1 = (f32[96,384]{1,0:T(8,128)S(1)}, f32[96,384]{1,0:T(8,128)S(1)}, u32[]{:S(2)}, u32[]{:S(2)}) collective-permute-start(f32[96,384]{1,0:T(8,128)S(1)} %get-tuple-element.72), channel_id=1, source_target_pairs={{0,16},{4,20},{8,24},{12,28},{16,0},{20,4},{24,8},{28,12},{1,17},{... | collective-permute-start | bytes 442376 | tf_op jit(solution)/shard_map/ppermute | solution.py:294
  5.5 2.3 %collective-permute-start.2 = (f32[96,384]{1,0:T(8,128)S(1)}, f32[96,384]{1,0:T(8,128)S(1)}, u32[]{:S(2)}, u32[]{:S(2)}) collective-permute-start(f32[96,384]{1,0:T(8,128)S(1)} %get-tuple-element.73), channel_id=1, source_target_pairs={{4,0},{8,4},{12,8},{16,12},{20,16},{24,20},{28,24},{0,28},{5,1},{9... | collective-permute-start | bytes 442376 | tf_op jit(solution)/shard_map/ppermute | solution.py:294
  7.7 1.6 %collective-permute-start.3 = (f32[128,128]{1,0:T(8,128)S(1)}, f32[128,128]{1,0:T(8,128)S(1)}, u32[]{:S(2)}, u32[]{:S(2)}) collective-permute-start(f32[128,128]{1,0:T(8,128)S(1)} %get-tuple-element.74), channel_id=1, source_target_pairs={{0,1},{1,0},{2,3},{3,2},{4,5},{5,4},{6,7},{7,6},{8,9},{9,8},{10,11... | collective-permute-start | bytes 196616 | tf_op jit(solution)/shard_map/ppermute | solution.py:314
  9.3 1.6 %shard_map.78 = (bf16[512,512]{1,0:T(8,128)(2,1)S(1)}, bf16[512,512]{1,0:T(8,128)(2,1)S(1)}, bf16[512,128]{1,0:T(8,128)(2,1)S(1)}, bf16[512,128]{1,0:T(8,128)(2,...) custom-call(bf16[384,512]{1,0:T(8,128)(2,1)S(1)} %get-tuple-element., ...), custom_call_target="tpu_custom_call" | custom-call | flops 402653184 | bytes 4718592 | tf_op jit(solution)/shard_map/pallas_call | solution.py:34
  10.9 1.1 %collective-permute-done.3.refs_1_ = f32[128,128]{1,0:T(8,128)S(1)} collective-permute-done((f32[128,128]{1,0:T(8,128)S(1)}, f32[128,128]{1,0:T(8,128)S(1)}, u32[]{:S(2)}, u32[]{:S(2)}) %collective-permute-start.3) | collective-permute-done | bytes 65568 | tf_op jit(solution)/shard_map/ppermute | solution.py:314
  12.2 0.4 shard_map.80
  12.5 1.6 %collective-permute-start.4 = (f32[128,128]{1,0:T(8,128)S(1)}, f32[128,128]{1,0:T(8,128)S(1)}, u32[]{:S(2)}, u32[]{:S(2)}) collective-permute-start(f32[128,128]{1,0:T(8,128)S(1)} %get-tuple-element.77.refs_0_.refs_4_), channel_id=1, source_target_pairs={{0,1},{1,0},{2,3},{3,2},{4,5},{5,4},{6,7},{7,6},{8,9},{9,8},{10,11... | collective-permute-start | bytes 196616 | tf_op jit(solution)/shard_map/ppermute | solution.py:330
  14.2 0.5 collective-permute-start.7
  14.6 1.6 %collective-permute-start.6 = (f32[128,128]{1,0:T(8,128)S(1)}, f32[128,128]{1,0:T(8,128)S(1)}, u32[]{:S(2)}, u32[]{:S(2)}) collective-permute-start(f32[128,128]{1,0:T(8,128)S(1)} %get-tuple-element.82.refs_0_), channel_id=1, source_target_pairs={{0,1},{1,0},{2,3},{3,2},{4,5},{5,4},{6,7},{7,6},{8,9},{9,8},{10,11... | collective-permute-start | bytes 196616 | tf_op jit(solution)/shard_map/ppermute | solution.py:330
  16.2 1.1 %collective-permute-done.4.refs_1_ = f32[128,128]{1,0:T(8,128)S(1)} collective-permute-done((f32[128,128]{1,0:T(8,128)S(1)}, f32[128,128]{1,0:T(8,128)S(1)}, u32[]{:S(2)}, u32[]{:S(2)}) %collective-permute-start.4) | collective-permute-done | bytes 65568 | tf_op jit(solution)/shard_map/ppermute | solution.py:330
  17.5 3.9 %collective-permute-start.5 = (f32[128,128]{1,0:T(8,128)S(1)}, f32[128,128]{1,0:T(8,128)S(1)}, u32[]{:S(2)}, u32[]{:S(2)}) collective-permute-start(f32[128,128]{1,0:T(8,128)S(1)} %get-tuple-element.80.refs_4_), channel_id=1, source_target_pairs={{0,3},{3,0},{1,2},{2,1},{4,7},{7,4},{5,6},{6,5},{8,11},{11,8},{9,1... | collective-permute-start | bytes 196616 | tf_op jit(solution)/shard_map/ppermute | solution.py:338
  21.7 0.8 %collective-permute-start.8 = (f32[128,128]{1,0:T(8,128)S(1)}, f32[128,128]{1,0:T(8,128)S(1)}, u32[]{:S(2)}, u32[]{:S(2)}) collective-permute-start(f32[128,128]{1,0:T(8,128)S(1)} %get-tuple-element.84.refs_4_), channel_id=1, source_target_pairs={{0,3},{3,0},{1,2},{2,1},{4,7},{7,4},{5,6},{6,5},{8,11},{11,8},{9,1... | collective-permute-start | bytes 196616 | tf_op jit(solution)/shard_map/ppermute | solution.py:338
  22.8 3.1 %collective-permute-start.9 = (f32[128,128]{1,0:T(8,128)S(1)}, f32[128,128]{1,0:T(8,128)S(1)}, u32[]{:S(2)}, u32[]{:S(2)}) collective-permute-start(f32[128,128]{1,0:T(8,128)S(1)} %get-tuple-element.85.refs_2_), channel_id=1, source_target_pairs={{0,3},{3,0},{1,2},{2,1},{4,7},{7,4},{5,6},{6,5},{8,11},{11,8},{9,1... | collective-permute-start | bytes 196616 | tf_op jit(solution)/shard_map/ppermute | solution.py:338
  26.0 1.3 %shard_map.84 = (bf16[512,512]{1,0:T(8,128)(2,1)S(1)}, bf16[512,512]{1,0:T(8,128)(2,1)S(1)}) custom-call(bf16[512,512]{1,0:T(8,128)(2,1)S(1)} %get-tuple-element.75.refs_2_.refs_0_, f32[512,512]{1,0:T(8,128)S(1)} %bitcast.11, f32[128,128]{1,0:T(8,128)S(1)} %get-tuple-element.85.refs_2_), custom_call_target="tpu_custom_call" | custom-call | flops 1073741824 | bytes 2359296 | tf_op jit(solution)/shard_map/pallas_call | solution.py:34
  27.3 1.0 %shard_map.85.refs_2_.refs_5_ = f32[512,384]{1,0:T(8,128)S(1)} custom-call(f32[512,384]{1,0:T(8,128)S(1)} %get-tuple-element.81.refs_0_.refs_3_.refs_4_, bf16[512,512]{1,0:T(8,128)(2,1)S(1)} %get-tuple-element.86.refs_1_.refs_6_, bf16[512,512]{1,0:T(8,128)(2,1)S(1)} %get-tuple-element.87.refs_2_, f32[96,384]{1,0:T(8,128)S(1)} %collective-permute-done.refs_3_, ...), custom_call_target="tpu_custom_call" | custom-call | flops 603979776 | bytes 2359296 | tf_op jit(solution)/shard_map/pallas_call | solution.py:34
  29.3 1.5 %collective-permute-start.11 = (f32[96,384]{1,0:T(8,128)S(1)}, f32[96,384]{1,0:T(8,128)S(1)}, u32[]{:S(2)}, u32[]{:S(2)}) collective-permute-start(f32[96,384]{1,0:T(8,128)S(1)} %get-tuple-element.98), channel_id=1, source_target_pairs={{0,16},{4,20},{8,24},{12,28},{16,0},{20,4},{24,8},{28,12},{1,17},{... | collective-permute-start | bytes 442376 | tf_op jit(solution)/shard_map/ppermute | solution.py:294
  30.8 2.3 %collective-permute-start.12 = (f32[96,384]{1,0:T(8,128)S(1)}, f32[96,384]{1,0:T(8,128)S(1)}, u32[]{:S(2)}, u32[]{:S(2)}) collective-permute-start(f32[96,384]{1,0:T(8,128)S(1)} %get-tuple-element.99), channel_id=1, source_target_pairs={{4,0},{8,4},{12,8},{16,12},{20,16},{24,20},{28,24},{0,28},{5,1},{9... | collective-permute-start | bytes 442376 | tf_op jit(solution)/shard_map/ppermute | solution.py:294
  33.1 1.3 %shard_map.89 = (bf16[512,512]{1,0:T(8,128)(2,1)S(1)}, bf16[512,512]{1,0:T(8,128)(2,1)S(1)}) custom-call(bf16[512,512]{1,0:T(8,128)(2,1)S(1)} %get-tuple-element.75.refs_2_.refs_0_, bf16[512,512]{1,0:T(8,128)(2,1)S(1)} %get-tuple-element.67.refs_1_.refs_0_, f32[512,512]{1,0:T(8,128)S(1)} %bitcast.12, f32[512,128]{1,0:T(8,128)S(1)} %get-tuple-element.92.refs_3_.refs_2_), custom_call_target="tpu_custom_call" | custom-call | flops 1073741824 | bytes 2359296 | tf_op jit(solution)/shard_map/pallas_call | solution.py:34
  34.4 1.0 %shard_map.90 = (f32[512,384]{1,0:T(8,128)S(1)}, f32[512,384]{1,0:T(8,128)S(1)}) custom-call(f32[512,128]{1,0:T(8,128)S(1)} %shard_map.86.refs_5_.refs_0_, f32[512,128]{1,0:T(8,128)S(1)} %shard_map.87.refs_6_.refs_7_.refs_1_, f32[512,128]{1,0:T(8,128)S(1)} %get-tuple-element.92.refs_3_.refs_2_, f32[512,384]{1,0:T(8,128)S(1)} %get-tuple-element.81.refs_0_.refs_3_.refs_4_, ...), custom_call_target="tpu_custom_call" | custom-call | flops 603979776 | bytes 3145728 | tf_op jit(solution)/shard_map/pallas_call | solution.py:34
  35.4 1.9 %collective-permute-done.11.refs_4_.refs_5_ = f32[96,384]{1,0:T(8,128)S(1)} collective-permute-done((f32[96,384]{1,0:T(8,128)S(1)}, f32[96,384]{1,0:T(8,128)S(1)}, u32[]{:S(2)}, u32[]{:S(2)}) %collective-permute-start.11) | collective-permute-done | bytes 147488 | tf_op jit(solution)/shard_map/ppermute | solution.py:294
  37.3 0.6 shard_map.91
  37.9 2.0 %collective-permute-start.15 = (f32[96,384]{1,0:T(8,128)S(1)}, f32[96,384]{1,0:T(8,128)S(1)}, u32[]{:S(2)}, u32[]{:S(2)}) collective-permute-start(f32[96,384]{1,0:T(8,128)S(1)} %get-tuple-element.100.refs_7_.refs_12_), channel_id=1, source_target_pairs={{4,0},{8,4},{12,8},{16,12},{20,16},{24,20},{28,24},{0,28},{5,1},{9... | collective-permute-start | bytes 442376 | tf_op jit(solution)/shard_map/ppermute | solution.py:294
  39.9 0.7 collective-permute-start.14
  40.6 0.9 %shard_map.92 = (f32[128,384]{1,0:T(8,128)S(1)}, f32[512,384]{1,0:T(8,128)S(1)}, f32[512,384]{1,0:T(8,128)S(1)}) custom-call(f32[512,384]{1,0:T(8,128)S(1)} %get-tuple-element.95.refs_0_.refs_6_, f32[512,384]{1,0:T(8,128)S(1)} %get-tuple-element.96.refs_1_, bf16[512,512]{1,0:T(8,128)(2,1)S(1)} %get-tuple-element.93.refs_4_.refs_6_.refs_1_.refs_2_.refs_5_, ...), custom_call_target="tpu_custom_call" | custom-call | flops 301989888 | bytes 3145728 | tf_op jit(solution)/shard_map/pallas_call | solution.py:34
  41.5 1.8 %collective-permute-done.15.refs_5_ = f32[96,384]{1,0:T(8,128)S(1)} collective-permute-done((f32[96,384]{1,0:T(8,128)S(1)}, f32[96,384]{1,0:T(8,128)S(1)}, u32[]{:S(2)}, u32[]{:S(2)}) %collective-permute-start.15) | collective-permute-done | bytes 147488 | tf_op jit(solution)/shard_map/ppermute | solution.py:294
  43.3 3.4 %collective-permute-done.14.refs_4_ = f32[96,384]{1,0:T(8,128)S(1)} collective-permute-done((f32[96,384]{1,0:T(8,128)S(1)}, f32[96,384]{1,0:T(8,128)S(1)}, u32[]{:S(2)}, u32[]{:S(2)}) %collective-permute-start.14) | collective-permute-done | bytes 147488 | tf_op jit(solution)/shard_map/ppermute | solution.py:294
  47.0 2.0 %collective-permute-start.19 = (f32[128,128]{1,0:T(8,128)S(1)}, f32[128,128]{1,0:T(8,128)S(1)}, u32[]{:S(2)}, u32[]{:S(2)}) collective-permute-start(f32[128,128]{1,0:T(8,128)S(1)} %get-tuple-element.109.refs_0_), channel_id=1, source_target_pairs={{0,1},{1,0},{2,3},{3,2},{4,5},{5,4},{6,7},{7,6},{8,9},{9,8},{10,11... | collective-permute-start | bytes 196616 | tf_op jit(solution)/shard_map/ppermute | solution.py:330
  49.1 2.2 %collective-permute-done.16.refs_1_ = f32[128,128]{1,0:T(8,128)S(1)} collective-permute-done((f32[128,128]{1,0:T(8,128)S(1)}, f32[128,128]{1,0:T(8,128)S(1)}, u32[]{:S(2)}, u32[]{:S(2)}) %collective-permute-start.16) | collective-permute-done | bytes 65568 | tf_op jit(solution)/shard_map/ppermute | solution.py:330
  51.5 3.2 %collective-permute-start.17 = (f32[128,128]{1,0:T(8,128)S(1)}, f32[128,128]{1,0:T(8,128)S(1)}, u32[]{:S(2)}, u32[]{:S(2)}) collective-permute-start(f32[128,128]{1,0:T(8,128)S(1)} %get-tuple-element.106.refs_4_), channel_id=1, source_target_pairs={{0,3},{3,0},{1,2},{2,1},{4,7},{7,4},{5,6},{6,5},{8,11},{11,8},{9,1... | collective-permute-start | bytes 196616 | tf_op jit(solution)/shard_map/ppermute | solution.py:338
  55.0 0.8 collective-permute-start.20
  56.0 3.2 %collective-permute-start.21 = (f32[128,128]{1,0:T(8,128)S(1)}, f32[128,128]{1,0:T(8,128)S(1)}, u32[]{:S(2)}, u32[]{:S(2)}) collective-permute-start(f32[128,128]{1,0:T(8,128)S(1)} %get-tuple-element.111.refs_6_), channel_id=1, source_target_pairs={{0,3},{3,0},{1,2},{2,1},{4,7},{7,4},{5,6},{6,5},{8,11},{11,8},{9,1... | collective-permute-start | bytes 196616 | tf_op jit(solution)/shard_map/ppermute | solution.py:338
  59.2 1.0 %shard_map.97.refs_2_.refs_5_ = f32[512,384]{1,0:T(8,128)S(1)} custom-call(f32[512,384]{1,0:T(8,128)S(1)} %get-tuple-element.107.refs_0_, bf16[512,512]{1,0:T(8,128)(2,1)S(1)} %get-tuple-element.86.refs_1_.refs_6_, bf16[512,512]{1,0:T(8,128)(2,1)S(1)} %get-tuple-element.87.refs_2_, f32[96,384]{1,0:T(8,128)S(1)} %collective-permute-done.13.refs_3_, ...), custom_call_target="tpu_custom_call" | custom-call | flops 603979776 | bytes 2359296 | tf_op jit(solution)/shard_map/pallas_call | solution.py:34
  60.5 0.7 collective-permute-done.20.refs_1_
  61.4 0.8 collective-permute-done.21.refs_1_
  62.5 0.9 %collective-permute-start.23 = (f32[96,384]{1,0:T(8,128)S(1)}, f32[96,384]{1,0:T(8,128)S(1)}, u32[]{:S(2)}, u32[]{:S(2)}) collective-permute-start(f32[96,384]{1,0:T(8,128)S(1)} %get-tuple-element.119), channel_id=1, source_target_pairs={{0,16},{4,20},{8,24},{12,28},{16,0},{20,4},{24,8},{28,12},{1,17},{... | collective-permute-start | bytes 442376 | tf_op jit(solution)/shard_map/ppermute | solution.py:294
  63.4 2.3 %collective-permute-start.24 = (f32[96,384]{1,0:T(8,128)S(1)}, f32[96,384]{1,0:T(8,128)S(1)}, u32[]{:S(2)}, u32[]{:S(2)}) collective-permute-start(f32[96,384]{1,0:T(8,128)S(1)} %get-tuple-element.120), channel_id=1, source_target_pairs={{4,0},{8,4},{12,8},{16,12},{20,16},{24,20},{28,24},{0,28},{5,1},{9... | collective-permute-start | bytes 442376 | tf_op jit(solution)/shard_map/ppermute | solution.py:294
  65.7 1.0 %shard_map.101 = (f32[512,384]{1,0:T(8,128)S(1)}, f32[512,384]{1,0:T(8,128)S(1)}) custom-call(f32[512,128]{1,0:T(8,128)S(1)} %shard_map.98.refs_5_.refs_0_, f32[512,128]{1,0:T(8,128)S(1)} %shard_map.99.refs_6_.refs_7_.refs_1_, f32[512,128]{1,0:T(8,128)S(1)} %get-tuple-element.114.refs_2_.refs_7_, f32[512,384]{1,0:T(8,128)S(1)} %get-tuple-element.115.refs_3_, ...), custom_call_target="tpu_custom_call" | custom-call | flops 603979776 | bytes 3145728 | tf_op jit(solution)/shard_map/pallas_call | solution.py:34
  66.7 1.6 %collective-permute-done.22.refs_3_.refs_4_ = f32[96,384]{1,0:T(8,128)S(1)} collective-permute-done((f32[96,384]{1,0:T(8,128)S(1)}, f32[96,384]{1,0:T(8,128)S(1)}, u32[]{:S(2)}, u32[]{:S(2)}) %collective-permute-start.22) | collective-permute-done | bytes 147488 | tf_op jit(solution)/shard_map/ppermute | solution.py:294
  68.3 2.3 %collective-permute-done.23.refs_4_.refs_5_ = f32[96,384]{1,0:T(8,128)S(1)} collective-permute-done((f32[96,384]{1,0:T(8,128)S(1)}, f32[96,384]{1,0:T(8,128)S(1)}, u32[]{:S(2)}, u32[]{:S(2)}) %collective-permute-start.23) | collective-permute-done | bytes 147488 | tf_op jit(solution)/shard_map/ppermute | solution.py:294
  70.6 0.6 shard_map.102
  71.2 1.8 %collective-permute-start.27 = (f32[96,384]{1,0:T(8,128)S(1)}, f32[96,384]{1,0:T(8,128)S(1)}, u32[]{:S(2)}, u32[]{:S(2)}) collective-permute-start(f32[96,384]{1,0:T(8,128)S(1)} %get-tuple-element.121.refs_7_.refs_10_), channel_id=1, source_target_pairs={{4,0},{8,4},{12,8},{16,12},{20,16},{24,20},{28,24},{0,28},{5,1},{9... | collective-permute-start | bytes 442376 | tf_op jit(solution)/shard_map/ppermute | solution.py:294
  73.0 0.5 shard_map.103
  73.5 1.6 %shard_map.104 = (f32[512,384]{1,0:T(8,128)S(1)}, f32[512,384]{1,0:T(8,128)}) custom-call(bf16[512,512]{1,0:T(8,128)(2,1)S(1)} %get-tuple-element.67.refs_1_.refs_0_, f32[512,384]{1,0:T(8,128)S(1)} %get-tuple-element.124.refs_1_, f32[512,384]{1,0:T(8,128)S(1)} %get-tuple-element.125.refs_2_.refs_3_, f32[512,384]{1,0:T(8,128)S(1)} %get-tuple-element.125.refs_2_.refs_3_), custom_call_target="tpu_custom_call" | custom-call | flops 805306368 | bytes 1966080 | tf_op jit(solution)/shard_map/pallas_call | solution.py:34
  75.1 1.9 %collective-permute-done.27.refs_4_ = f32[96,384]{1,0:T(8,128)S(1)} collective-permute-done((f32[96,384]{1,0:T(8,128)S(1)}, f32[96,384]{1,0:T(8,128)S(1)}, u32[]{:S(2)}, u32[]{:S(2)}) %collective-permute-start.27) | collective-permute-done | bytes 147488 | tf_op jit(solution)/shard_map/ppermute | solution.py:294
  77.0 2.7 %collective-permute-done.26.refs_3_ = f32[96,384]{1,0:T(8,128)S(1)} collective-permute-done((f32[96,384]{1,0:T(8,128)S(1)}, f32[96,384]{1,0:T(8,128)S(1)}, u32[]{:S(2)}, u32[]{:S(2)}) %collective-permute-start.26) | collective-permute-done | bytes 147488 | tf_op jit(solution)/shard_map/ppermute | solution.py:294
  79.7 1.4 %shard_map.105 = f32[512,384]{1,0:T(8,128)} custom-call(bf16[512,512]{1,0:T(8,128)(2,1)S(1)} %get-tuple-element.67.refs_1_.refs_0_, f32[512,384]{1,0:T(8,128)S(1)} %get-tuple-element.127.refs_1_.refs_5_, f32[96,384]{1,0:T(8,128)S(1)} %collective-permute-done.25.refs_2_, f32[96,384]{1,0:T(8,128)S(1)} %collective-permute-done.26.refs_3_, ...), custom_call_target="tpu_custom_call" | custom-call | flops 402653184 | bytes 1966080 | tf_op jit(solution)/shard_map/pallas_call | solution.py:34
  (45 shorter events, 3.9 us)
Async XLA Ops:
  0.6 8.7 %copy-start = (f32[1,1,512,128]{3,2,1,0:T(8,128)S(1)}, f32[1,1,512,128]{3,2,1,0:T(8,128)}, u32[]{:S(2)}) copy-start(f32[1,1,512,128]{3,2,1,0:T(8,128)} %param.9) | copy-start | bytes 786436
  2.4 9.8 %collective-permute-start = (f32[96,384]{1,0:T(8,128)S(1)}, f32[96,384]{1,0:T(8,128)S(1)}, u32[]{:S(2)}, u32[]{:S(2)}) collective-permute-start(f32[96,384]{1,0:T(8,128)S(1)} %get-tuple-element.71), channel_id=1, source_target_pairs={{0,4},{4,8},{8,12},{12,16},{16,20},{20,24},{24,28},{28,0},{1,5},{5... | collective-permute-start | bytes 442376 | tf_op jit(solution)/shard_map/ppermute | solution.py:294
  2.9 9.3 %collective-permute-start.1 = (f32[96,384]{1,0:T(8,128)S(1)}, f32[96,384]{1,0:T(8,128)S(1)}, u32[]{:S(2)}, u32[]{:S(2)}) collective-permute-start(f32[96,384]{1,0:T(8,128)S(1)} %get-tuple-element.72), channel_id=1, source_target_pairs={{0,16},{4,20},{8,24},{12,28},{16,0},{20,4},{24,8},{28,12},{1,17},{... | collective-permute-start | bytes 442376 | tf_op jit(solution)/shard_map/ppermute | solution.py:294
  5.5 6.7 %collective-permute-start.2 = (f32[96,384]{1,0:T(8,128)S(1)}, f32[96,384]{1,0:T(8,128)S(1)}, u32[]{:S(2)}, u32[]{:S(2)}) collective-permute-start(f32[96,384]{1,0:T(8,128)S(1)} %get-tuple-element.73), channel_id=1, source_target_pairs={{4,0},{8,4},{12,8},{16,12},{20,16},{24,20},{28,24},{0,28},{5,1},{9... | collective-permute-start | bytes 442376 | tf_op jit(solution)/shard_map/ppermute | solution.py:294
  7.7 4.3 %collective-permute-start.3 = (f32[128,128]{1,0:T(8,128)S(1)}, f32[128,128]{1,0:T(8,128)S(1)}, u32[]{:S(2)}, u32[]{:S(2)}) collective-permute-start(f32[128,128]{1,0:T(8,128)S(1)} %get-tuple-element.74), channel_id=1, source_target_pairs={{0,1},{1,0},{2,3},{3,2},{4,5},{5,4},{6,7},{7,6},{8,9},{9,8},{10,11... | collective-permute-start | bytes 196616 | tf_op jit(solution)/shard_map/ppermute | solution.py:314
  9.3 2.7 %copy-start.1 = (f32[1,512,128]{2,1,0:T(8,128)S(1)}, f32[1,512,128]{2,1,0:T(8,128)}, u32[]{:S(2)}) copy-start(f32[1,512,128]{2,1,0:T(8,128)} %param.10) | copy-start | bytes 786436
  12.2 13.8 %copy-start.2 = (f32[1,1,512,512]{3,2,1,0:T(8,128)S(1)}, f32[1,1,512,512]{3,2,1,0:T(8,128)}, u32[]{:S(2)}) copy-start(f32[1,1,512,512]{3,2,1,0:T(8,128)} %param.8) | copy-start | bytes 3145732
  12.5 4.8 %collective-permute-start.4 = (f32[128,128]{1,0:T(8,128)S(1)}, f32[128,128]{1,0:T(8,128)S(1)}, u32[]{:S(2)}, u32[]{:S(2)}) collective-permute-start(f32[128,128]{1,0:T(8,128)S(1)} %get-tuple-element.77.refs_0_.refs_4_), channel_id=1, source_target_pairs={{0,1},{1,0},{2,3},{3,2},{4,5},{5,4},{6,7},{7,6},{8,9},{9,8},{10,11... | collective-permute-start | bytes 196616 | tf_op jit(solution)/shard_map/ppermute | solution.py:330
  14.2 7.3 %collective-permute-start.7 = (f32[128,128]{1,0:T(8,128)S(1)}, f32[128,128]{1,0:T(8,128)S(1)}, u32[]{:S(2)}, u32[]{:S(2)}) collective-permute-start(f32[128,128]{1,0:T(8,128)S(1)} %get-tuple-element.83.refs_0_), channel_id=1, source_target_pairs={{0,1},{1,0},{2,3},{3,2},{4,5},{5,4},{6,7},{7,6},{8,9},{9,8},{10,11... | collective-permute-start | bytes 196616 | tf_op jit(solution)/shard_map/ppermute | solution.py:330
  14.6 7.9 %collective-permute-start.6 = (f32[128,128]{1,0:T(8,128)S(1)}, f32[128,128]{1,0:T(8,128)S(1)}, u32[]{:S(2)}, u32[]{:S(2)}) collective-permute-start(f32[128,128]{1,0:T(8,128)S(1)} %get-tuple-element.82.refs_0_), channel_id=1, source_target_pairs={{0,1},{1,0},{2,3},{3,2},{4,5},{5,4},{6,7},{7,6},{8,9},{9,8},{10,11... | collective-permute-start | bytes 196616 | tf_op jit(solution)/shard_map/ppermute | solution.py:330
  17.5 10.8 %collective-permute-start.5 = (f32[128,128]{1,0:T(8,128)S(1)}, f32[128,128]{1,0:T(8,128)S(1)}, u32[]{:S(2)}, u32[]{:S(2)}) collective-permute-start(f32[128,128]{1,0:T(8,128)S(1)} %get-tuple-element.80.refs_4_), channel_id=1, source_target_pairs={{0,3},{3,0},{1,2},{2,1},{4,7},{7,4},{5,6},{6,5},{8,11},{11,8},{9,1... | collective-permute-start | bytes 196616 | tf_op jit(solution)/shard_map/ppermute | solution.py:338
  21.7 6.8 %collective-permute-start.8 = (f32[128,128]{1,0:T(8,128)S(1)}, f32[128,128]{1,0:T(8,128)S(1)}, u32[]{:S(2)}, u32[]{:S(2)}) collective-permute-start(f32[128,128]{1,0:T(8,128)S(1)} %get-tuple-element.84.refs_4_), channel_id=1, source_target_pairs={{0,3},{3,0},{1,2},{2,1},{4,7},{7,4},{5,6},{6,5},{8,11},{11,8},{9,1... | collective-permute-start | bytes 196616 | tf_op jit(solution)/shard_map/ppermute | solution.py:338
  22.8 6.1 %collective-permute-start.9 = (f32[128,128]{1,0:T(8,128)S(1)}, f32[128,128]{1,0:T(8,128)S(1)}, u32[]{:S(2)}, u32[]{:S(2)}) collective-permute-start(f32[128,128]{1,0:T(8,128)S(1)} %get-tuple-element.85.refs_2_), channel_id=1, source_target_pairs={{0,3},{3,0},{1,2},{2,1},{4,7},{7,4},{5,6},{6,5},{8,11},{11,8},{9,1... | collective-permute-start | bytes 196616 | tf_op jit(solution)/shard_map/ppermute | solution.py:338
  28.8 4.3 %copy-start.3 = (f32[1,1,512,512]{3,2,1,0:T(8,128)S(1)}, f32[1,1,512,512]{3,2,1,0:T(8,128)}, u32[]{:S(2)}) copy-start(f32[1,1,512,512]{3,2,1,0:T(8,128)} %param.7) | copy-start | bytes 3145732
  29.2 6.1 %collective-permute-start.10 = (f32[96,384]{1,0:T(8,128)S(1)}, f32[96,384]{1,0:T(8,128)S(1)}, u32[]{:S(2)}, u32[]{:S(2)}) collective-permute-start(f32[96,384]{1,0:T(8,128)S(1)} %get-tuple-element.97), channel_id=1, source_target_pairs={{0,4},{4,8},{8,12},{12,16},{16,20},{20,24},{24,28},{28,0},{1,5},{5... | collective-permute-start | bytes 442376 | tf_op jit(solution)/shard_map/ppermute | solution.py:294
  29.3 8.0 %collective-permute-start.11 = (f32[96,384]{1,0:T(8,128)S(1)}, f32[96,384]{1,0:T(8,128)S(1)}, u32[]{:S(2)}, u32[]{:S(2)}) collective-permute-start(f32[96,384]{1,0:T(8,128)S(1)} %get-tuple-element.98), channel_id=1, source_target_pairs={{0,16},{4,20},{8,24},{12,28},{16,0},{20,4},{24,8},{28,12},{1,17},{... | collective-permute-start | bytes 442376 | tf_op jit(solution)/shard_map/ppermute | solution.py:294
  30.8 6.5 %collective-permute-start.12 = (f32[96,384]{1,0:T(8,128)S(1)}, f32[96,384]{1,0:T(8,128)S(1)}, u32[]{:S(2)}, u32[]{:S(2)}) collective-permute-start(f32[96,384]{1,0:T(8,128)S(1)} %get-tuple-element.99), channel_id=1, source_target_pairs={{4,0},{8,4},{12,8},{16,12},{20,16},{24,20},{28,24},{0,28},{5,1},{9... | collective-permute-start | bytes 442376 | tf_op jit(solution)/shard_map/ppermute | solution.py:294
  37.9 5.4 %collective-permute-start.15 = (f32[96,384]{1,0:T(8,128)S(1)}, f32[96,384]{1,0:T(8,128)S(1)}, u32[]{:S(2)}, u32[]{:S(2)}) collective-permute-start(f32[96,384]{1,0:T(8,128)S(1)} %get-tuple-element.100.refs_7_.refs_12_), channel_id=1, source_target_pairs={{4,0},{8,4},{12,8},{16,12},{20,16},{24,20},{28,24},{0,28},{5,1},{9... | collective-permute-start | bytes 442376 | tf_op jit(solution)/shard_map/ppermute | solution.py:294
  39.9 6.7 %collective-permute-start.14 = (f32[96,384]{1,0:T(8,128)S(1)}, f32[96,384]{1,0:T(8,128)S(1)}, u32[]{:S(2)}, u32[]{:S(2)}) collective-permute-start(f32[96,384]{1,0:T(8,128)S(1)} %get-tuple-element.101.refs_8_), channel_id=1, source_target_pairs={{0,16},{4,20},{8,24},{12,28},{16,0},{20,4},{24,8},{28,12},{1,17},{... | collective-permute-start | bytes 442376 | tf_op jit(solution)/shard_map/ppermute | solution.py:294
  40.6 6.0 %collective-permute-start.13 = (f32[96,384]{1,0:T(8,128)S(1)}, f32[96,384]{1,0:T(8,128)S(1)}, u32[]{:S(2)}, u32[]{:S(2)}) collective-permute-start(f32[96,384]{1,0:T(8,128)S(1)} %get-tuple-element.102.refs_9_), channel_id=1, source_target_pairs={{0,4},{4,8},{8,12},{12,16},{16,20},{20,24},{24,28},{28,0},{1,5},{5... | collective-permute-start | bytes 442376 | tf_op jit(solution)/shard_map/ppermute | solution.py:294
  47.0 4.3 %collective-permute-start.16 = (f32[128,128]{1,0:T(8,128)S(1)}, f32[128,128]{1,0:T(8,128)S(1)}, u32[]{:S(2)}, u32[]{:S(2)}) collective-permute-start(f32[128,128]{1,0:T(8,128)S(1)} %get-tuple-element.104.refs_0_.refs_4_), channel_id=1, source_target_pairs={{0,1},{1,0},{2,3},{3,2},{4,5},{5,4},{6,7},{7,6},{8,9},{9,8},{10,11... | collective-permute-start | bytes 196616 | tf_op jit(solution)/shard_map/ppermute | solution.py:330
  47.0 7.7 %collective-permute-start.19 = (f32[128,128]{1,0:T(8,128)S(1)}, f32[128,128]{1,0:T(8,128)S(1)}, u32[]{:S(2)}, u32[]{:S(2)}) collective-permute-start(f32[128,128]{1,0:T(8,128)S(1)} %get-tuple-element.109.refs_0_), channel_id=1, source_target_pairs={{0,1},{1,0},{2,3},{3,2},{4,5},{5,4},{6,7},{7,6},{8,9},{9,8},{10,11... | collective-permute-start | bytes 196616 | tf_op jit(solution)/shard_map/ppermute | solution.py:330
  49.1 6.7 %collective-permute-start.18 = (f32[128,128]{1,0:T(8,128)S(1)}, f32[128,128]{1,0:T(8,128)S(1)}, u32[]{:S(2)}, u32[]{:S(2)}) collective-permute-start(f32[128,128]{1,0:T(8,128)S(1)} %get-tuple-element.108.refs_0_), channel_id=1, source_target_pairs={{0,1},{1,0},{2,3},{3,2},{4,5},{5,4},{6,7},{7,6},{8,9},{9,8},{10,11... | collective-permute-start | bytes 196616 | tf_op jit(solution)/shard_map/ppermute | solution.py:330
  51.5 8.7 %collective-permute-start.17 = (f32[128,128]{1,0:T(8,128)S(1)}, f32[128,128]{1,0:T(8,128)S(1)}, u32[]{:S(2)}, u32[]{:S(2)}) collective-permute-start(f32[128,128]{1,0:T(8,128)S(1)} %get-tuple-element.106.refs_4_), channel_id=1, source_target_pairs={{0,3},{3,0},{1,2},{2,1},{4,7},{7,4},{5,6},{6,5},{8,11},{11,8},{9,1... | collective-permute-start | bytes 196616 | tf_op jit(solution)/shard_map/ppermute | solution.py:338
  55.0 6.1 %collective-permute-start.20 = (f32[128,128]{1,0:T(8,128)S(1)}, f32[128,128]{1,0:T(8,128)S(1)}, u32[]{:S(2)}, u32[]{:S(2)}) collective-permute-start(f32[128,128]{1,0:T(8,128)S(1)} %get-tuple-element.110.refs_4_), channel_id=1, source_target_pairs={{0,3},{3,0},{1,2},{2,1},{4,7},{7,4},{5,6},{6,5},{8,11},{11,8},{9,1... | collective-permute-start | bytes 196616 | tf_op jit(solution)/shard_map/ppermute | solution.py:338
  56.0 6.1 %collective-permute-start.21 = (f32[128,128]{1,0:T(8,128)S(1)}, f32[128,128]{1,0:T(8,128)S(1)}, u32[]{:S(2)}, u32[]{:S(2)}) collective-permute-start(f32[128,128]{1,0:T(8,128)S(1)} %get-tuple-element.111.refs_6_), channel_id=1, source_target_pairs={{0,3},{3,0},{1,2},{2,1},{4,7},{7,4},{5,6},{6,5},{8,11},{11,8},{9,1... | collective-permute-start | bytes 196616 | tf_op jit(solution)/shard_map/ppermute | solution.py:338
  62.4 5.9 %collective-permute-start.22 = (f32[96,384]{1,0:T(8,128)S(1)}, f32[96,384]{1,0:T(8,128)S(1)}, u32[]{:S(2)}, u32[]{:S(2)}) collective-permute-start(f32[96,384]{1,0:T(8,128)S(1)} %get-tuple-element.118), channel_id=1, source_target_pairs={{0,4},{4,8},{8,12},{12,16},{16,20},{20,24},{24,28},{28,0},{1,5},{5... | collective-permute-start | bytes 442376 | tf_op jit(solution)/shard_map/ppermute | solution.py:294
  62.5 8.1 %collective-permute-start.23 = (f32[96,384]{1,0:T(8,128)S(1)}, f32[96,384]{1,0:T(8,128)S(1)}, u32[]{:S(2)}, u32[]{:S(2)}) collective-permute-start(f32[96,384]{1,0:T(8,128)S(1)} %get-tuple-element.119), channel_id=1, source_target_pairs={{0,16},{4,20},{8,24},{12,28},{16,0},{20,4},{24,8},{28,12},{1,17},{... | collective-permute-start | bytes 442376 | tf_op jit(solution)/shard_map/ppermute | solution.py:294
  63.4 7.3 %collective-permute-start.24 = (f32[96,384]{1,0:T(8,128)S(1)}, f32[96,384]{1,0:T(8,128)S(1)}, u32[]{:S(2)}, u32[]{:S(2)}) collective-permute-start(f32[96,384]{1,0:T(8,128)S(1)} %get-tuple-element.120), channel_id=1, source_target_pairs={{4,0},{8,4},{12,8},{16,12},{20,16},{24,20},{28,24},{0,28},{5,1},{9... | collective-permute-start | bytes 442376 | tf_op jit(solution)/shard_map/ppermute | solution.py:294
  71.2 5.8 %collective-permute-start.27 = (f32[96,384]{1,0:T(8,128)S(1)}, f32[96,384]{1,0:T(8,128)S(1)}, u32[]{:S(2)}, u32[]{:S(2)}) collective-permute-start(f32[96,384]{1,0:T(8,128)S(1)} %get-tuple-element.121.refs_7_.refs_10_), channel_id=1, source_target_pairs={{4,0},{8,4},{12,8},{16,12},{20,16},{24,20},{28,24},{0,28},{5,1},{9... | collective-permute-start | bytes 442376 | tf_op jit(solution)/shard_map/ppermute | solution.py:294
  73.0 6.7 %collective-permute-start.26 = (f32[96,384]{1,0:T(8,128)S(1)}, f32[96,384]{1,0:T(8,128)S(1)}, u32[]{:S(2)}, u32[]{:S(2)}) collective-permute-start(f32[96,384]{1,0:T(8,128)S(1)} %get-tuple-element.122.refs_8_), channel_id=1, source_target_pairs={{0,16},{4,20},{8,24},{12,28},{16,0},{20,4},{24,8},{28,12},{1,17},{... | collective-permute-start | bytes 442376 | tf_op jit(solution)/shard_map/ppermute | solution.py:294
  73.0 6.7 %collective-permute-start.25 = (f32[96,384]{1,0:T(8,128)S(1)}, f32[96,384]{1,0:T(8,128)S(1)}, u32[]{:S(2)}, u32[]{:S(2)}) collective-permute-start(f32[96,384]{1,0:T(8,128)S(1)} %get-tuple-element.123.refs_9_), channel_id=1, source_target_pairs={{0,4},{4,8},{8,12},{12,16},{16,20},{20,24},{24,28},{28,0},{1,5},{5... | collective-permute-start | bytes 442376 | tf_op jit(solution)/shard_map/ppermute | solution.py:294

commit v2 on v0

--- a/solution.py
+++ b/solution.py
@@ -9,7 +9,8 @@
 ROW_SUBS = 4
 RELAX = 0.5
 GROUPS = 4
-PIECE = 128
+HIDE = 16
+PIECES = (128, 256)
 f32 = jnp.float32
 bf16 = jnp.bfloat16
 NN = (((1,), (0,)), ((), ()))
@@ -175,12 +176,16 @@
     mix_high[...], mix_low[...] = split(jnp.concatenate([away, kept], axis=0) * RELAX)
 
 
+def cut():
+    return [(sum(PIECES[:place]), width) for place, width in enumerate(PIECES)]
+
+
 def project_body(subs, count, ahead_ref, test_high, test_low, *refs):
     came = came_in(subs, refs[:count])
     size = came.shape[0]
     projected = ahead_ref[...] + dot3((test_high[:, :size], test_low[:, :size]), split(came))
-    for place, ref in enumerate(refs[count:]):
-        ref[...] = projected[:, place * PIECE : (place + 1) * PIECE]
+    for ref, (start, width) in zip(refs[count:], cut()):
+        ref[...] = projected[:, start : start + width]
 
 
 def solve_body(subs, value_ref, solve_high, solve_low, *refs):
@@ -198,7 +203,8 @@
 
 def correct_body(kept_ref, came_ref, fine_ref, basis_high, basis_low, place, *refs):
     coarse = kept_ref[...] + came_ref[...]
-    fine = fine_ref[:, place * PIECE : (place + 1) * PIECE]
+    start, width = cut()[place]
+    fine = fine_ref[:, start : start + width]
     step = fine + dot3((basis_high[...], basis_low[...]), split(coarse))
     formers = place if len(refs) > 1 else 0
     former_refs, out_ref = refs[:formers], refs[formers]
@@ -282,7 +288,7 @@
     shared_rows = blocks.shape[1]
     listed = 4 * shared_rows
     subs = lax.axis_size("sub")
-    if lax.axis_size("grp") != GROUPS or loads % PIECE:
+    if lax.axis_size("grp") != GROUPS or sum(PIECES) != loads:
         raise ValueError("unexpected sizes")
 
     up = [(low, (low + 1) % subs) for low in range(subs)]
@@ -300,7 +306,7 @@
     mirror_plan = [(0, 3), (3, 0), (1, 2), (2, 1)]
     shared = [((shared_rows, loads), f32)] * count
     outside = pl.BlockSpec(memory_space=pltpu.HBM)
-    pieces = loads // PIECE
+    pieces = len(PIECES)
     size = rows * loads
     run = Chain()
 
@@ -322,16 +328,16 @@
     value, iterate = ordered, None
     for iteration in range(ITERS):
         first, last = iteration == 0, iteration == ITERS - 1
-        shapes = [((modes, PIECE), f32)] * pieces
+        shapes = [((modes, width), f32) for width in PIECES]
         own = run(
             lambda *refs: project_body(subs, count, *refs), shapes, 6 * modes * size, 12 * size,
             ahead, test_high, test_low, *arrived,
         )
         theirs = [lax.ppermute(piece, "grp", pair_plan) for piece in own]
         kept, came = [], []
-        for place in range(pieces):
+        for place, width in enumerate(PIECES):
             away, keep = run(
-                mix_body, [((modes, PIECE), f32)] * 2, 24 * modes * modes * PIECE, 4 * rows * PIECE,
+                mix_body, [((modes, width), f32)] * 2, HIDE * 24 * modes * modes * width, HIDE * 4 * rows * width,
                 own[place], theirs[place], *mixers,
             )
             kept.append(keep)
@@ -342,15 +348,15 @@
                 chooser, local_inverse[0, 0],
             )
         (fine,) = run(
-            lambda *refs: solve_body(subs, *refs), [whole(loads)], 6 * rows * size, 12 * size,
+            lambda *refs: solve_body(subs, *refs), [whole(loads)], HIDE * 6 * rows * size, HIDE * 12 * size,
             value, solve_high, solve_low, *arrived,
         )
         steps = []
-        for place in range(pieces):
+        for place, width in enumerate(PIECES):
             final = place == pieces - 1
             step, *parts = run(
                 lambda kept, came, fine, high, low, *refs: correct_body(kept, came, fine, high, low, place, *refs),
-                [whole(PIECE)] + (shared if final else []), 6 * modes * rows * PIECE, 12 * rows * PIECE,
+                [whole(width)] + (shared if final else []), 6 * modes * rows * width, 12 * rows * width,
                 kept[place], came[place], fine, basis_high, basis_low, *(steps if final else []),
             )
             steps.append(step)

time: 78.9 us -> 77.6 us (0.984)
  starting transfers between devices: 41.1 us -> 34 us
  waiting for transfers between devices: 17.3 us -> 23.9 us
    ppermute x6 -> x4, starting transfers between devices: 14.7 us -> 9.3 us  [local(): came.append(lax.ppermute(away, 'grp', mirror_plan))]
    ppermute x6 -> x4, waiting for transfers between devices: 1.39 us -> 5.95 us  [local(): came.append(lax.ppermute(away, 'grp', mirror_plan))]
    ppermute x6 -> x4, waiting for transfers between devices: 3.15 us -> 5.5 us  [local(): theirs = [lax.ppermute(piece, 'grp', pair_plan) for piece in own]]
    ppermute x6 -> x4, starting transfers between devices: 6.22 us -> 4.18 us  [local(): theirs = [lax.ppermute(piece, 'grp', pair_plan) for piece in own]]
    pallas_call x29 -> x25, Pallas kernels: 19.1 us -> 18.4 us  [__call__(): pl.pallas_call(whole_body, out_shape=[jax.ShapeDtypeStruct(shape, kind) f...]
  transfers between devices with their start and end apart: 28 -> 24, of which waited for: 14 -> 15; matrix products, arithmetic and copies ran while one was open for 0% -> 0% of each run, Pallas kernels for 17% -> 16%
where the time goes in v2:
time: 77.6 us; the launch traced here: 77.4 us
  starting transfers between devices  34 us (44%)
  waiting for transfers between devices  23.9 us (31%)
  Pallas kernels  18.4 us (24%)
  between operations  1.04 us (1%)
    ppermute x15, starting transfers between devices, exchange(): return [lax.ppermute(parts[place], 'sub', pairs) for place, pairs in plans]  19 us
    pallas_call x25, Pallas kernels, __call__(): pl.pallas_call(whole_body, out_shape=[jax.ShapeDtypeStruct(shape, kind) f...  18.4 us
    ppermute x15, waiting for transfers between devices, exchange(): return [lax.ppermute(parts[place], 'sub', pairs) for place, pairs in plans]  11.4 us
    ppermute x4, starting transfers between devices, local(): came.append(lax.ppermute(away, 'grp', mirror_plan))  9.3 us
    ppermute x4, waiting for transfers between devices, local(): came.append(lax.ppermute(away, 'grp', mirror_plan))  5.95 us
    ppermute x4, waiting for transfers between devices, local(): theirs = [lax.ppermute(piece, 'grp', pair_plan) for piece in own]  5.5 us
    ppermute x4, starting transfers between devices, local(): theirs = [lax.ppermute(piece, 'grp', pair_plan) for piece in own]  4.18 us
    ppermute x1, starting transfers between devices, local(): other = lax.ppermute(sent, 'grp', pair_plan)  1.58 us
  transfers between devices with their start and end apart: 24, of which 15 were waited for; matrix products, arithmetic and copies ran while one was open for 0% of the time, Pallas kernels for 16%

profile of v2, /device:TPU:0, one launch (start us, length us, event | category | flops | bytes accessed | tf_op | source)
XLA Modules:
  0.0 77.4 jit_solution(1665714303631017462)
XLA Ops:
  0.6 1.7 %shard_map.77 = (bf16[384,512]{1,0:T(8,128)(2,1)S(1)}, f32[512,384]{1,0:T(8,128)S(1)}, f32[128,128]{1,0:T(8,128)S(1)}, f32[96,384]{1,0:T(8,128)S(1)}, f32[96,384]{1,0:T(8,128)S(1)}, /*index=5*/f32[96,384]{1,0:T(8,128)S(1)}) custom-call(s32[4,96]{1,0:T(4,128)} %bitcast.15, f32[512,384]{1,0:T(8,128)} %bitcast.14, f32[512,128]{1,0:T(8,128)} %bitcast.9), custom_call_target="tpu_custom_call" | custom-call | flops 301989888 | bytes 3145728 | tf_op jit(solution)/shard_map/pallas_call | solution.py:35
  2.4 3.0 %collective-permute-start = (f32[96,384]{1,0:T(8,128)S(1)}, f32[96,384]{1,0:T(8,128)S(1)}, u32[]{:S(2)}, u32[]{:S(2)}) collective-permute-start(f32[96,384]{1,0:T(8,128)S(1)} %get-tuple-element.65), channel_id=1, source_target_pairs={{0,16},{4,20},{8,24},{12,28},{16,0},{20,4},{24,8},{28,12},{1,17},{... | collective-permute-start | bytes 442376 | tf_op jit(solution)/shard_map/ppermute | solution.py:300
  5.4 2.6 %collective-permute-start.2 = (f32[96,384]{1,0:T(8,128)S(1)}, f32[96,384]{1,0:T(8,128)S(1)}, u32[]{:S(2)}, u32[]{:S(2)}) collective-permute-start(f32[96,384]{1,0:T(8,128)S(1)} %get-tuple-element.67), channel_id=1, source_target_pairs={{4,0},{8,4},{12,8},{16,12},{20,16},{24,20},{28,24},{0,28},{5,1},{9... | collective-permute-start | bytes 442376 | tf_op jit(solution)/shard_map/ppermute | solution.py:300
  8.0 1.6 %collective-permute-start.3 = (f32[128,128]{1,0:T(8,128)S(1)}, f32[128,128]{1,0:T(8,128)S(1)}, u32[]{:S(2)}, u32[]{:S(2)}) collective-permute-start(f32[128,128]{1,0:T(8,128)S(1)} %get-tuple-element.68), channel_id=1, source_target_pairs={{0,1},{1,0},{2,3},{3,2},{4,5},{5,4},{6,7},{7,6},{8,9},{9,8},{10,11... | collective-permute-start | bytes 196616 | tf_op jit(solution)/shard_map/ppermute | solution.py:320
  9.6 1.6 %shard_map.78 = (bf16[512,512]{1,0:T(8,128)(2,1)S(1)}, bf16[512,512]{1,0:T(8,128)(2,1)S(1)}, bf16[512,128]{1,0:T(8,128)(2,1)S(1)}, bf16[512,128]{1,0:T(8,128)(2,...) custom-call(bf16[384,512]{1,0:T(8,128)(2,1)S(1)} %get-tuple-element., ...), custom_call_target="tpu_custom_call" | custom-call | flops 402653184 | bytes 4718592 | tf_op jit(solution)/shard_map/pallas_call | solution.py:35
  11.2 1.1 %collective-permute-done.3.refs_1_ = f32[128,128]{1,0:T(8,128)S(1)} collective-permute-done((f32[128,128]{1,0:T(8,128)S(1)}, f32[128,128]{1,0:T(8,128)S(1)}, u32[]{:S(2)}, u32[]{:S(2)}) %collective-permute-start.3) | collective-permute-done | bytes 65568 | tf_op jit(solution)/shard_map/ppermute | solution.py:320
  12.5 0.4 shard_map.80
  12.8 1.6 %collective-permute-start.4 = (f32[128,128]{1,0:T(8,128)S(1)}, f32[128,128]{1,0:T(8,128)S(1)}, u32[]{:S(2)}, u32[]{:S(2)}) collective-permute-start(f32[128,128]{1,0:T(8,128)S(1)} %get-tuple-element.71.refs_0_.refs_4_), channel_id=1, source_target_pairs={{0,1},{1,0},{2,3},{3,2},{4,5},{5,4},{6,7},{7,6},{8,9},{9,8},{10,11... | collective-permute-start | bytes 196616 | tf_op jit(solution)/shard_map/ppermute | solution.py:336
  14.5 0.4 collective-permute-start.6
  14.9 2.9 %collective-permute-done.4.refs_1_ = f32[128,128]{1,0:T(8,128)S(1)} collective-permute-done((f32[128,128]{1,0:T(8,128)S(1)}, f32[128,128]{1,0:T(8,128)S(1)}, u32[]{:S(2)}, u32[]{:S(2)}) %collective-permute-start.4) | collective-permute-done | bytes 65568 | tf_op jit(solution)/shard_map/ppermute | solution.py:336
  18.1 3.5 %collective-permute-start.5 = (f32[128,128]{1,0:T(8,128)S(1)}, f32[128,128]{1,0:T(8,128)S(1)}, u32[]{:S(2)}, u32[]{:S(2)}) collective-permute-start(f32[128,128]{1,0:T(8,128)S(1)} %get-tuple-element.74.refs_4_), channel_id=1, source_target_pairs={{0,3},{3,0},{1,2},{2,1},{4,7},{7,4},{5,6},{6,5},{8,11},{11,8},{9,1... | collective-permute-start | bytes 196616 | tf_op jit(solution)/shard_map/ppermute | solution.py:344
  21.9 1.1 %collective-permute-start.7 = (f32[128,256]{1,0:T(8,128)S(1)}, f32[128,256]{1,0:T(8,128)S(1)}, u32[]{:S(2)}, u32[]{:S(2)}) collective-permute-start(f32[128,256]{1,0:T(8,128)S(1)} %get-tuple-element.77.refs_2_), channel_id=1, source_target_pairs={{0,3},{3,0},{1,2},{2,1},{4,7},{7,4},{5,6},{6,5},{8,11},{11,8},{9,1... | collective-permute-start | bytes 393224 | tf_op jit(solution)/shard_map/ppermute | solution.py:344
  23.0 1.3 %shard_map.83 = (bf16[512,512]{1,0:T(8,128)(2,1)S(1)}, bf16[512,512]{1,0:T(8,128)(2,1)S(1)}) custom-call(bf16[512,512]{1,0:T(8,128)(2,1)S(1)} %get-tuple-element.69.refs_2_.refs_0_, f32[512,512]{1,0:T(8,128)S(1)} %bitcast.11, f32[128,256]{1,0:T(8,128)S(1)} %get-tuple-element.77.refs_2_), custom_call_target="tpu_custom_call" | custom-call | flops 1073741824 | bytes 2359296 | tf_op jit(solution)/shard_map/pallas_call | solution.py:35
  24.4 1.0 %shard_map.84.refs_2_.refs_5_ = f32[512,384]{1,0:T(8,128)S(1)} custom-call(f32[512,384]{1,0:T(8,128)S(1)} %get-tuple-element.75.refs_0_.refs_2_.refs_3_, bf16[512,512]{1,0:T(8,128)(2,1)S(1)} %get-tuple-element.78.refs_1_.refs_6_, bf16[512,512]{1,0:T(8,128)(2,1)S(1)} %get-tuple-element.79.refs_2_, f32[96,384]{1,0:T(8,128)S(1)} %collective-permute-done.refs_3_, ...), custom_call_target="tpu_custom_call" | custom-call | flops 9663676416 | bytes 37748736 | tf_op jit(solution)/shard_map/pallas_call | solution.py:35
  25.7 3.1 %collective-permute-done.7.refs_1_ = f32[128,256]{1,0:T(8,128)S(1)} collective-permute-done((f32[128,256]{1,0:T(8,128)S(1)}, f32[128,256]{1,0:T(8,128)S(1)}, u32[]{:S(2)}, u32[]{:S(2)}) %collective-permute-start.7) | collective-permute-done | bytes 131104 | tf_op jit(solution)/shard_map/ppermute | solution.py:344
  28.8 0.4 shard_map.86
  29.2 0.7 collective-permute-start.8
  29.9 2.6 %collective-permute-start.10 = (f32[96,384]{1,0:T(8,128)S(1)}, f32[96,384]{1,0:T(8,128)S(1)}, u32[]{:S(2)}, u32[]{:S(2)}) collective-permute-start(f32[96,384]{1,0:T(8,128)S(1)} %get-tuple-element.90), channel_id=1, source_target_pairs={{4,0},{8,4},{12,8},{16,12},{20,16},{24,20},{28,24},{0,28},{5,1},{9... | collective-permute-start | bytes 442376 | tf_op jit(solution)/shard_map/ppermute | solution.py:300
  32.6 1.3 %shard_map.87 = (bf16[512,512]{1,0:T(8,128)(2,1)S(1)}, bf16[512,512]{1,0:T(8,128)(2,1)S(1)}) custom-call(bf16[512,512]{1,0:T(8,128)(2,1)S(1)} %get-tuple-element.69.refs_2_.refs_0_, bf16[512,512]{1,0:T(8,128)(2,1)S(1)} %get-tuple-element.61.refs_1_.refs_0_, f32[512,512]{1,0:T(8,128)S(1)} %bitcast.12, f32[512,256]{1,0:T(8,128)S(1)} %get-tuple-element.83.refs_3_.refs_1_), custom_call_target="tpu_custom_call" | custom-call | flops 1073741824 | bytes 2359296 | tf_op jit(solution)/shard_map/pallas_call | solution.py:35
  33.8 1.0 %shard_map.88 = (f32[512,384]{1,0:T(8,128)S(1)}, f32[512,384]{1,0:T(8,128)S(1)}) custom-call(f32[512,128]{1,0:T(8,128)S(1)} %shard_map.85.refs_5_.refs_6_.refs_0_, f32[512,256]{1,0:T(8,128)S(1)} %get-tuple-element.83.refs_3_.refs_1_, f32[512,384]{1,0:T(8,128)S(1)} %get-tuple-element.75.refs_0_.refs_2_.refs_3_, ...), custom_call_target="tpu_custom_call" | custom-call | flops 603979776 | bytes 3145728 | tf_op jit(solution)/shard_map/pallas_call | solution.py:35
  34.8 1.1 %collective-permute-done.8.refs_3_.refs_4_ = f32[96,384]{1,0:T(8,128)S(1)} collective-permute-done((f32[96,384]{1,0:T(8,128)S(1)}, f32[96,384]{1,0:T(8,128)S(1)}, u32[]{:S(2)}, u32[]{:S(2)}) %collective-permute-start.8) | collective-permute-done | bytes 147488 | tf_op jit(solution)/shard_map/ppermute | solution.py:300
  36.1 0.6 shard_map.89
  36.6 2.1 %collective-permute-start.11 = (f32[96,384]{1,0:T(8,128)S(1)}, f32[96,384]{1,0:T(8,128)S(1)}, u32[]{:S(2)}, u32[]{:S(2)}) collective-permute-start(f32[96,384]{1,0:T(8,128)S(1)} %get-tuple-element.91.refs_7_.refs_12_), channel_id=1, source_target_pairs={{0,16},{4,20},{8,24},{12,28},{16,0},{20,4},{24,8},{28,12},{1,17},{... | collective-permute-start | bytes 442376 | tf_op jit(solution)/shard_map/ppermute | solution.py:300
  38.7 1.0 %collective-permute-start.13 = (f32[96,384]{1,0:T(8,128)S(1)}, f32[96,384]{1,0:T(8,128)S(1)}, u32[]{:S(2)}, u32[]{:S(2)}) collective-permute-start(f32[96,384]{1,0:T(8,128)S(1)} %get-tuple-element.92.refs_8_), channel_id=1, source_target_pairs={{4,0},{8,4},{12,8},{16,12},{20,16},{24,20},{28,24},{0,28},{5,1},{9... | collective-permute-start | bytes 442376 | tf_op jit(solution)/shard_map/ppermute | solution.py:300
  39.8 0.9 %shard_map.90 = (f32[128,384]{1,0:T(8,128)S(1)}, f32[512,384]{1,0:T(8,128)S(1)}, f32[512,384]{1,0:T(8,128)S(1)}) custom-call(f32[512,384]{1,0:T(8,128)S(1)} %get-tuple-element.86.refs_0_.refs_6_, f32[512,384]{1,0:T(8,128)S(1)} %get-tuple-element.87.refs_1_, bf16[512,512]{1,0:T(8,128)(2,1)S(1)} %get-tuple-element.84.refs_3_.refs_5_.refs_1_.refs_2_.refs_4_, ...), custom_call_target="tpu_custom_call" | custom-call | flops 301989888 | bytes 3145728 | tf_op jit(solution)/shard_map/pallas_call | solution.py:35
  40.6 2.5 %collective-permute-done.11.refs_3_ = f32[96,384]{1,0:T(8,128)S(1)} collective-permute-done((f32[96,384]{1,0:T(8,128)S(1)}, f32[96,384]{1,0:T(8,128)S(1)}, u32[]{:S(2)}, u32[]{:S(2)}) %collective-permute-start.11) | collective-permute-done | bytes 147488 | tf_op jit(solution)/shard_map/ppermute | solution.py:300
  43.3 1.9 %collective-permute-done.12.refs_4_ = f32[96,384]{1,0:T(8,128)S(1)} collective-permute-done((f32[96,384]{1,0:T(8,128)S(1)}, f32[96,384]{1,0:T(8,128)S(1)}, u32[]{:S(2)}, u32[]{:S(2)}) %collective-permute-start.12) | collective-permute-done | bytes 147488 | tf_op jit(solution)/shard_map/ppermute | solution.py:300
  45.2 0.3 shard_map.91
  45.6 1.2 %collective-permute-start.14 = (f32[128,128]{1,0:T(8,128)S(1)}, f32[128,128]{1,0:T(8,128)S(1)}, u32[]{:S(2)}, u32[]{:S(2)}) collective-permute-start(f32[128,128]{1,0:T(8,128)S(1)} %get-tuple-element.95.refs_0_.refs_4_), channel_id=1, source_target_pairs={{0,1},{1,0},{2,3},{3,2},{4,5},{5,4},{6,7},{7,6},{8,9},{9,8},{10,11... | collective-permute-start | bytes 196616 | tf_op jit(solution)/shard_map/ppermute | solution.py:336
  46.8 0.9 %collective-permute-start.16 = (f32[128,256]{1,0:T(8,128)S(1)}, f32[128,256]{1,0:T(8,128)S(1)}, u32[]{:S(2)}, u32[]{:S(2)}) collective-permute-start(f32[128,256]{1,0:T(8,128)S(1)} %get-tuple-element.99.refs_0_), channel_id=1, source_target_pairs={{0,1},{1,0},{2,3},{3,2},{4,5},{5,4},{6,7},{7,6},{8,9},{9,8},{10,11... | collective-permute-start | bytes 393224 | tf_op jit(solution)/shard_map/ppermute | solution.py:336
  47.7 2.2 %collective-permute-done.14.refs_1_ = f32[128,128]{1,0:T(8,128)S(1)} collective-permute-done((f32[128,128]{1,0:T(8,128)S(1)}, f32[128,128]{1,0:T(8,128)S(1)}, u32[]{:S(2)}, u32[]{:S(2)}) %collective-permute-start.14) | collective-permute-done | bytes 65568 | tf_op jit(solution)/shard_map/ppermute | solution.py:336
  50.2 1.8 %collective-permute-start.15 = (f32[128,128]{1,0:T(8,128)S(1)}, f32[128,128]{1,0:T(8,128)S(1)}, u32[]{:S(2)}, u32[]{:S(2)}) collective-permute-start(f32[128,128]{1,0:T(8,128)S(1)} %get-tuple-element.97.refs_4_), channel_id=1, source_target_pairs={{0,3},{3,0},{1,2},{2,1},{4,7},{7,4},{5,6},{6,5},{8,11},{11,8},{9,1... | collective-permute-start | bytes 196616 | tf_op jit(solution)/shard_map/ppermute | solution.py:344
  52.5 2.9 %collective-permute-start.17 = (f32[128,256]{1,0:T(8,128)S(1)}, f32[128,256]{1,0:T(8,128)S(1)}, u32[]{:S(2)}, u32[]{:S(2)}) collective-permute-start(f32[128,256]{1,0:T(8,128)S(1)} %get-tuple-element.100.refs_6_), channel_id=1, source_target_pairs={{0,3},{3,0},{1,2},{2,1},{4,7},{7,4},{5,6},{6,5},{8,11},{11,8},{9,1... | collective-permute-start | bytes 393224 | tf_op jit(solution)/shard_map/ppermute | solution.py:344
  55.4 1.0 %shard_map.94.refs_2_.refs_5_ = f32[512,384]{1,0:T(8,128)S(1)} custom-call(f32[512,384]{1,0:T(8,128)S(1)} %get-tuple-element.98.refs_0_, bf16[512,512]{1,0:T(8,128)(2,1)S(1)} %get-tuple-element.78.refs_1_.refs_6_, bf16[512,512]{1,0:T(8,128)(2,1)S(1)} %get-tuple-element.79.refs_2_, f32[96,384]{1,0:T(8,128)S(1)} %collective-permute-done.11.refs_3_, ...), custom_call_target="tpu_custom_call" | custom-call | flops 9663676416 | bytes 37748736 | tf_op jit(solution)/shard_map/pallas_call | solution.py:35
  56.7 2.8 %collective-permute-done.17.refs_1_ = f32[128,256]{1,0:T(8,128)S(1)} collective-permute-done((f32[128,256]{1,0:T(8,128)S(1)}, f32[128,256]{1,0:T(8,128)S(1)}, u32[]{:S(2)}, u32[]{:S(2)}) %collective-permute-start.17) | collective-permute-done | bytes 131104 | tf_op jit(solution)/shard_map/ppermute | solution.py:344
  59.5 0.4 shard_map.96
  59.9 1.0 %collective-permute-start.18 = (f32[96,384]{1,0:T(8,128)S(1)}, f32[96,384]{1,0:T(8,128)S(1)}, u32[]{:S(2)}, u32[]{:S(2)}) collective-permute-start(f32[96,384]{1,0:T(8,128)S(1)} %get-tuple-element.106), channel_id=1, source_target_pairs={{0,16},{4,20},{8,24},{12,28},{16,0},{20,4},{24,8},{28,12},{1,17},{... | collective-permute-start | bytes 442376 | tf_op jit(solution)/shard_map/ppermute | solution.py:300
  60.8 2.6 %collective-permute-start.20 = (f32[96,384]{1,0:T(8,128)S(1)}, f32[96,384]{1,0:T(8,128)S(1)}, u32[]{:S(2)}, u32[]{:S(2)}) collective-permute-start(f32[96,384]{1,0:T(8,128)S(1)} %get-tuple-element.108), channel_id=1, source_target_pairs={{4,0},{8,4},{12,8},{16,12},{20,16},{24,20},{28,24},{0,28},{5,1},{9... | collective-permute-start | bytes 442376 | tf_op jit(solution)/shard_map/ppermute | solution.py:300
  63.5 1.0 %shard_map.97 = (f32[512,384]{1,0:T(8,128)S(1)}, f32[512,384]{1,0:T(8,128)S(1)}) custom-call(f32[512,128]{1,0:T(8,128)S(1)} %shard_map.95.refs_5_.refs_6_.refs_0_, f32[512,256]{1,0:T(8,128)S(1)} %get-tuple-element.102.refs_1_.refs_6_, f32[512,384]{1,0:T(8,128)S(1)} %get-tuple-element.103.refs_2_, f32[512,384]{1,0:T(8,128)S(1)} %get-tuple-element.75.refs_0_.refs_2_.refs_3_, ...), custom_call_target="tpu_custom_call" | custom-call | flops 603979776 | bytes 3145728 | tf_op jit(solution)/shard_map/pallas_call | solution.py:35
  64.5 2.2 %collective-permute-done.18.refs_3_.refs_4_ = f32[96,384]{1,0:T(8,128)S(1)} collective-permute-done((f32[96,384]{1,0:T(8,128)S(1)}, f32[96,384]{1,0:T(8,128)S(1)}, u32[]{:S(2)}, u32[]{:S(2)}) %collective-permute-start.18) | collective-permute-done | bytes 147488 | tf_op jit(solution)/shard_map/ppermute | solution.py:300
  66.6 0.6 shard_map.98
  67.2 1.4 %collective-permute-start.21 = (f32[96,384]{1,0:T(8,128)S(1)}, f32[96,384]{1,0:T(8,128)S(1)}, u32[]{:S(2)}, u32[]{:S(2)}) collective-permute-start(f32[96,384]{1,0:T(8,128)S(1)} %get-tuple-element.109.refs_7_.refs_10_), channel_id=1, source_target_pairs={{0,16},{4,20},{8,24},{12,28},{16,0},{20,4},{24,8},{28,12},{1,17},{... | collective-permute-start | bytes 442376 | tf_op jit(solution)/shard_map/ppermute | solution.py:300
  68.6 1.8 %collective-permute-start.23 = (f32[96,384]{1,0:T(8,128)S(1)}, f32[96,384]{1,0:T(8,128)S(1)}, u32[]{:S(2)}, u32[]{:S(2)}) collective-permute-start(f32[96,384]{1,0:T(8,128)S(1)} %get-tuple-element.110.refs_8_), channel_id=1, source_target_pairs={{4,0},{8,4},{12,8},{16,12},{20,16},{24,20},{28,24},{0,28},{5,1},{9... | collective-permute-start | bytes 442376 | tf_op jit(solution)/shard_map/ppermute | solution.py:300
  70.4 0.5 shard_map.99
  70.9 1.6 %shard_map.100 = (f32[512,384]{1,0:T(8,128)S(1)}, f32[512,384]{1,0:T(8,128)}) custom-call(bf16[512,512]{1,0:T(8,128)(2,1)S(1)} %get-tuple-element.61.refs_1_.refs_0_, f32[512,384]{1,0:T(8,128)S(1)} %get-tuple-element.112.refs_1_, f32[512,384]{1,0:T(8,128)S(1)} %get-tuple-element.113.refs_2_.refs_3_, f32[512,384]{1,0:T(8,128)S(1)} %get-tuple-element.113.refs_2_.refs_3_), custom_call_target="tpu_custom_call" | custom-call | flops 805306368 | bytes 1966080 | tf_op jit(solution)/shard_map/pallas_call | solution.py:35
  72.5 1.3 %collective-permute-done.21.refs_2_ = f32[96,384]{1,0:T(8,128)S(1)} collective-permute-done((f32[96,384]{1,0:T(8,128)S(1)}, f32[96,384]{1,0:T(8,128)S(1)}, u32[]{:S(2)}, u32[]{:S(2)}) %collective-permute-start.21) | collective-permute-done | bytes 147488 | tf_op jit(solution)/shard_map/ppermute | solution.py:300
  73.9 1.9 %collective-permute-done.22.refs_3_ = f32[96,384]{1,0:T(8,128)S(1)} collective-permute-done((f32[96,384]{1,0:T(8,128)S(1)}, f32[96,384]{1,0:T(8,128)S(1)}, u32[]{:S(2)}, u32[]{:S(2)}) %collective-permute-start.22) | collective-permute-done | bytes 147488 | tf_op jit(solution)/shard_map/ppermute | solution.py:300
  75.9 1.4 %shard_map.101 = f32[512,384]{1,0:T(8,128)} custom-call(bf16[512,512]{1,0:T(8,128)(2,1)S(1)} %get-tuple-element.61.refs_1_.refs_0_, f32[512,384]{1,0:T(8,128)S(1)} %get-tuple-element.115.refs_1_.refs_5_, f32[96,384]{1,0:T(8,128)S(1)} %collective-permute-done.21.refs_2_, f32[96,384]{1,0:T(8,128)S(1)} %collective-permute-done.22.refs_3_, ...), custom_call_target="tpu_custom_call" | custom-call | flops 402653184 | bytes 1966080 | tf_op jit(solution)/shard_map/pallas_call | solution.py:35
  (33 shorter events, 2.6 us)
Async XLA Ops:
  0.6 9.0 %copy-start = (f32[1,1,512,128]{3,2,1,0:T(8,128)S(1)}, f32[1,1,512,128]{3,2,1,0:T(8,128)}, u32[]{:S(2)}) copy-start(f32[1,1,512,128]{3,2,1,0:T(8,128)} %param.9) | copy-start | bytes 786436
  2.4 10.1 %collective-permute-start = (f32[96,384]{1,0:T(8,128)S(1)}, f32[96,384]{1,0:T(8,128)S(1)}, u32[]{:S(2)}, u32[]{:S(2)}) collective-permute-start(f32[96,384]{1,0:T(8,128)S(1)} %get-tuple-element.65), channel_id=1, source_target_pairs={{0,16},{4,20},{8,24},{12,28},{16,0},{20,4},{24,8},{28,12},{1,17},{... | collective-permute-start | bytes 442376 | tf_op jit(solution)/shard_map/ppermute | solution.py:300
  5.4 7.0 %collective-permute-start.1 = (f32[96,384]{1,0:T(8,128)S(1)}, f32[96,384]{1,0:T(8,128)S(1)}, u32[]{:S(2)}, u32[]{:S(2)}) collective-permute-start(f32[96,384]{1,0:T(8,128)S(1)} %get-tuple-element.66), channel_id=1, source_target_pairs={{0,4},{4,8},{8,12},{12,16},{16,20},{20,24},{24,28},{28,0},{1,5},{5... | collective-permute-start | bytes 442376 | tf_op jit(solution)/shard_map/ppermute | solution.py:300
  5.4 7.1 %collective-permute-start.2 = (f32[96,384]{1,0:T(8,128)S(1)}, f32[96,384]{1,0:T(8,128)S(1)}, u32[]{:S(2)}, u32[]{:S(2)}) collective-permute-start(f32[96,384]{1,0:T(8,128)S(1)} %get-tuple-element.67), channel_id=1, source_target_pairs={{4,0},{8,4},{12,8},{16,12},{20,16},{24,20},{28,24},{0,28},{5,1},{9... | collective-permute-start | bytes 442376 | tf_op jit(solution)/shard_map/ppermute | solution.py:300
  8.0 4.3 %collective-permute-start.3 = (f32[128,128]{1,0:T(8,128)S(1)}, f32[128,128]{1,0:T(8,128)S(1)}, u32[]{:S(2)}, u32[]{:S(2)}) collective-permute-start(f32[128,128]{1,0:T(8,128)S(1)} %get-tuple-element.68), channel_id=1, source_target_pairs={{0,1},{1,0},{2,3},{3,2},{4,5},{5,4},{6,7},{7,6},{8,9},{9,8},{10,11... | collective-permute-start | bytes 196616 | tf_op jit(solution)/shard_map/ppermute | solution.py:320
  9.6 2.7 %copy-start.1 = (f32[1,512,128]{2,1,0:T(8,128)S(1)}, f32[1,512,128]{2,1,0:T(8,128)}, u32[]{:S(2)}) copy-start(f32[1,512,128]{2,1,0:T(8,128)} %param.10) | copy-start | bytes 786436
  12.8 5.0 %collective-permute-start.4 = (f32[128,128]{1,0:T(8,128)S(1)}, f32[128,128]{1,0:T(8,128)S(1)}, u32[]{:S(2)}, u32[]{:S(2)}) collective-permute-start(f32[128,128]{1,0:T(8,128)S(1)} %get-tuple-element.71.refs_0_.refs_4_), channel_id=1, source_target_pairs={{0,1},{1,0},{2,3},{3,2},{4,5},{5,4},{6,7},{7,6},{8,9},{9,8},{10,11... | collective-permute-start | bytes 196616 | tf_op jit(solution)/shard_map/ppermute | solution.py:336
  14.5 7.2 %collective-permute-start.6 = (f32[128,256]{1,0:T(8,128)S(1)}, f32[128,256]{1,0:T(8,128)S(1)}, u32[]{:S(2)}, u32[]{:S(2)}) collective-permute-start(f32[128,256]{1,0:T(8,128)S(1)} %get-tuple-element.76.refs_0_), channel_id=1, source_target_pairs={{0,1},{1,0},{2,3},{3,2},{4,5},{5,4},{6,7},{7,6},{8,9},{9,8},{10,11... | collective-permute-start | bytes 393224 | tf_op jit(solution)/shard_map/ppermute | solution.py:336
  18.1 4.9 %copy-start.2 = (f32[1,1,512,512]{3,2,1,0:T(8,128)S(1)}, f32[1,1,512,512]{3,2,1,0:T(8,128)}, u32[]{:S(2)}) copy-start(f32[1,1,512,512]{3,2,1,0:T(8,128)} %param.8) | copy-start | bytes 3145732
  18.1 7.3 %collective-permute-start.5 = (f32[128,128]{1,0:T(8,128)S(1)}, f32[128,128]{1,0:T(8,128)S(1)}, u32[]{:S(2)}, u32[]{:S(2)}) collective-permute-start(f32[128,128]{1,0:T(8,128)S(1)} %get-tuple-element.74.refs_4_), channel_id=1, source_target_pairs={{0,3},{3,0},{1,2},{2,1},{4,7},{7,4},{5,6},{6,5},{8,11},{11,8},{9,1... | collective-permute-start | bytes 196616 | tf_op jit(solution)/shard_map/ppermute | solution.py:344
  21.9 6.9 %collective-permute-start.7 = (f32[128,256]{1,0:T(8,128)S(1)}, f32[128,256]{1,0:T(8,128)S(1)}, u32[]{:S(2)}, u32[]{:S(2)}) collective-permute-start(f32[128,256]{1,0:T(8,128)S(1)} %get-tuple-element.77.refs_2_), channel_id=1, source_target_pairs={{0,3},{3,0},{1,2},{2,1},{4,7},{7,4},{5,6},{6,5},{8,11},{11,8},{9,1... | collective-permute-start | bytes 393224 | tf_op jit(solution)/shard_map/ppermute | solution.py:344
  25.7 6.9 %copy-start.3 = (f32[1,1,512,512]{3,2,1,0:T(8,128)S(1)}, f32[1,1,512,512]{3,2,1,0:T(8,128)}, u32[]{:S(2)}) copy-start(f32[1,1,512,512]{3,2,1,0:T(8,128)} %param.7) | copy-start | bytes 3145732
  29.2 6.7 %collective-permute-start.8 = (f32[96,384]{1,0:T(8,128)S(1)}, f32[96,384]{1,0:T(8,128)S(1)}, u32[]{:S(2)}, u32[]{:S(2)}) collective-permute-start(f32[96,384]{1,0:T(8,128)S(1)} %get-tuple-element.88), channel_id=1, source_target_pairs={{0,16},{4,20},{8,24},{12,28},{16,0},{20,4},{24,8},{28,12},{1,17},{... | collective-permute-start | bytes 442376 | tf_op jit(solution)/shard_map/ppermute | solution.py:300
  29.9 6.1 %collective-permute-start.9 = (f32[96,384]{1,0:T(8,128)S(1)}, f32[96,384]{1,0:T(8,128)S(1)}, u32[]{:S(2)}, u32[]{:S(2)}) collective-permute-start(f32[96,384]{1,0:T(8,128)S(1)} %get-tuple-element.89), channel_id=1, source_target_pairs={{0,4},{4,8},{8,12},{12,16},{16,20},{20,24},{24,28},{28,0},{1,5},{5... | collective-permute-start | bytes 442376 | tf_op jit(solution)/shard_map/ppermute | solution.py:300
  29.9 6.1 %collective-permute-start.10 = (f32[96,384]{1,0:T(8,128)S(1)}, f32[96,384]{1,0:T(8,128)S(1)}, u32[]{:S(2)}, u32[]{:S(2)}) collective-permute-start(f32[96,384]{1,0:T(8,128)S(1)} %get-tuple-element.90), channel_id=1, source_target_pairs={{4,0},{8,4},{12,8},{16,12},{20,16},{24,20},{28,24},{0,28},{5,1},{9... | collective-permute-start | bytes 442376 | tf_op jit(solution)/shard_map/ppermute | solution.py:300
  36.6 6.5 %collective-permute-start.11 = (f32[96,384]{1,0:T(8,128)S(1)}, f32[96,384]{1,0:T(8,128)S(1)}, u32[]{:S(2)}, u32[]{:S(2)}) collective-permute-start(f32[96,384]{1,0:T(8,128)S(1)} %get-tuple-element.91.refs_7_.refs_12_), channel_id=1, source_target_pairs={{0,16},{4,20},{8,24},{12,28},{16,0},{20,4},{24,8},{28,12},{1,17},{... | collective-permute-start | bytes 442376 | tf_op jit(solution)/shard_map/ppermute | solution.py:300
  38.7 4.6 %collective-permute-start.13 = (f32[96,384]{1,0:T(8,128)S(1)}, f32[96,384]{1,0:T(8,128)S(1)}, u32[]{:S(2)}, u32[]{:S(2)}) collective-permute-start(f32[96,384]{1,0:T(8,128)S(1)} %get-tuple-element.92.refs_8_), channel_id=1, source_target_pairs={{4,0},{8,4},{12,8},{16,12},{20,16},{24,20},{28,24},{0,28},{5,1},{9... | collective-permute-start | bytes 442376 | tf_op jit(solution)/shard_map/ppermute | solution.py:300
  39.8 5.5 %collective-permute-start.12 = (f32[96,384]{1,0:T(8,128)S(1)}, f32[96,384]{1,0:T(8,128)S(1)}, u32[]{:S(2)}, u32[]{:S(2)}) collective-permute-start(f32[96,384]{1,0:T(8,128)S(1)} %get-tuple-element.93.refs_9_), channel_id=1, source_target_pairs={{0,4},{4,8},{8,12},{12,16},{16,20},{20,24},{24,28},{28,0},{1,5},{5... | collective-permute-start | bytes 442376 | tf_op jit(solution)/shard_map/ppermute | solution.py:300
  45.6 4.3 %collective-permute-start.14 = (f32[128,128]{1,0:T(8,128)S(1)}, f32[128,128]{1,0:T(8,128)S(1)}, u32[]{:S(2)}, u32[]{:S(2)}) collective-permute-start(f32[128,128]{1,0:T(8,128)S(1)} %get-tuple-element.95.refs_0_.refs_4_), channel_id=1, source_target_pairs={{0,1},{1,0},{2,3},{3,2},{4,5},{5,4},{6,7},{7,6},{8,9},{9,8},{10,11... | collective-permute-start | bytes 196616 | tf_op jit(solution)/shard_map/ppermute | solution.py:336
  46.8 5.5 %collective-permute-start.16 = (f32[128,256]{1,0:T(8,128)S(1)}, f32[128,256]{1,0:T(8,128)S(1)}, u32[]{:S(2)}, u32[]{:S(2)}) collective-permute-start(f32[128,256]{1,0:T(8,128)S(1)} %get-tuple-element.99.refs_0_), channel_id=1, source_target_pairs={{0,1},{1,0},{2,3},{3,2},{4,5},{5,4},{6,7},{7,6},{8,9},{9,8},{10,11... | collective-permute-start | bytes 393224 | tf_op jit(solution)/shard_map/ppermute | solution.py:336
  50.2 6.3 %collective-permute-start.15 = (f32[128,128]{1,0:T(8,128)S(1)}, f32[128,128]{1,0:T(8,128)S(1)}, u32[]{:S(2)}, u32[]{:S(2)}) collective-permute-start(f32[128,128]{1,0:T(8,128)S(1)} %get-tuple-element.97.refs_4_), channel_id=1, source_target_pairs={{0,3},{3,0},{1,2},{2,1},{4,7},{7,4},{5,6},{6,5},{8,11},{11,8},{9,1... | collective-permute-start | bytes 196616 | tf_op jit(solution)/shard_map/ppermute | solution.py:344
  52.5 6.9 %collective-permute-start.17 = (f32[128,256]{1,0:T(8,128)S(1)}, f32[128,256]{1,0:T(8,128)S(1)}, u32[]{:S(2)}, u32[]{:S(2)}) collective-permute-start(f32[128,256]{1,0:T(8,128)S(1)} %get-tuple-element.100.refs_6_), channel_id=1, source_target_pairs={{0,3},{3,0},{1,2},{2,1},{4,7},{7,4},{5,6},{6,5},{8,11},{11,8},{9,1... | collective-permute-start | bytes 393224 | tf_op jit(solution)/shard_map/ppermute | solution.py:344
  59.9 6.8 %collective-permute-start.18 = (f32[96,384]{1,0:T(8,128)S(1)}, f32[96,384]{1,0:T(8,128)S(1)}, u32[]{:S(2)}, u32[]{:S(2)}) collective-permute-start(f32[96,384]{1,0:T(8,128)S(1)} %get-tuple-element.106), channel_id=1, source_target_pairs={{0,16},{4,20},{8,24},{12,28},{16,0},{20,4},{24,8},{28,12},{1,17},{... | collective-permute-start | bytes 442376 | tf_op jit(solution)/shard_map/ppermute | solution.py:300
  60.8 5.8 %collective-permute-start.19 = (f32[96,384]{1,0:T(8,128)S(1)}, f32[96,384]{1,0:T(8,128)S(1)}, u32[]{:S(2)}, u32[]{:S(2)}) collective-permute-start(f32[96,384]{1,0:T(8,128)S(1)} %get-tuple-element.107), channel_id=1, source_target_pairs={{0,4},{4,8},{8,12},{12,16},{16,20},{20,24},{24,28},{28,0},{1,5},{5... | collective-permute-start | bytes 442376 | tf_op jit(solution)/shard_map/ppermute | solution.py:300
  60.8 5.8 %collective-permute-start.20 = (f32[96,384]{1,0:T(8,128)S(1)}, f32[96,384]{1,0:T(8,128)S(1)}, u32[]{:S(2)}, u32[]{:S(2)}) collective-permute-start(f32[96,384]{1,0:T(8,128)S(1)} %get-tuple-element.108), channel_id=1, source_target_pairs={{4,0},{8,4},{12,8},{16,12},{20,16},{24,20},{28,24},{0,28},{5,1},{9... | collective-permute-start | bytes 442376 | tf_op jit(solution)/shard_map/ppermute | solution.py:300
  67.2 6.6 %collective-permute-start.21 = (f32[96,384]{1,0:T(8,128)S(1)}, f32[96,384]{1,0:T(8,128)S(1)}, u32[]{:S(2)}, u32[]{:S(2)}) collective-permute-start(f32[96,384]{1,0:T(8,128)S(1)} %get-tuple-element.109.refs_7_.refs_10_), channel_id=1, source_target_pairs={{0,16},{4,20},{8,24},{12,28},{16,0},{20,4},{24,8},{28,12},{1,17},{... | collective-permute-start | bytes 442376 | tf_op jit(solution)/shard_map/ppermute | solution.py:300
  68.6 5.3 %collective-permute-start.23 = (f32[96,384]{1,0:T(8,128)S(1)}, f32[96,384]{1,0:T(8,128)S(1)}, u32[]{:S(2)}, u32[]{:S(2)}) collective-permute-start(f32[96,384]{1,0:T(8,128)S(1)} %get-tuple-element.110.refs_8_), channel_id=1, source_target_pairs={{4,0},{8,4},{12,8},{16,12},{20,16},{24,20},{28,24},{0,28},{5,1},{9... | collective-permute-start | bytes 442376 | tf_op jit(solution)/shard_map/ppermute | solution.py:300
  70.4 5.5 %collective-permute-start.22 = (f32[96,384]{1,0:T(8,128)S(1)}, f32[96,384]{1,0:T(8,128)S(1)}, u32[]{:S(2)}, u32[]{:S(2)}) collective-permute-start(f32[96,384]{1,0:T(8,128)S(1)} %get-tuple-element.111.refs_9_), channel_id=1, source_target_pairs={{0,4},{4,8},{8,12},{12,16},{16,20},{20,24},{24,28},{28,0},{1,5},{5... | collective-permute-start | bytes 442376 | tf_op jit(solution)/shard_map/ppermute | solution.py:300

commit v3 on v2

--- a/solution.py
+++ b/solution.py
@@ -94,14 +94,20 @@
 
 
 def listed_body(subs, count, blocks_hbm, load_hbm, columns_hbm, listed_ref, load_ref, sent_ref, *refs):
-    *shared_refs, blocks_ref, load_sem, blocks_sem, sent_sem = refs
+    *shared_refs, blocks_ref, load_sems, blocks_sem, sent_sem = refs
     modes = sent_ref.shape[0]
     wanted = pl.multiple_of((3 - (lax.axis_index("grp") ^ 1)) * modes, modes)
     sent_copy = pltpu.make_async_copy(columns_hbm.at[pl.ds(wanted, modes), :], sent_ref, sent_sem)
-    load_copy = pltpu.make_async_copy(load_hbm, load_ref, load_sem)
+    half = load_ref.shape[0] // 2
+    halves = [slice(0, half), slice(half, 2 * half)]
+    load_copies = [
+        pltpu.make_async_copy(load_hbm.at[rows], load_ref.at[rows], load_sems.at[place])
+        for place, rows in enumerate(halves)
+    ]
     blocks_copy = pltpu.make_async_copy(blocks_hbm, blocks_ref, blocks_sem)
     blocks_copy.start()
-    load_copy.start()
+    for copy in load_copies:
+        copy.start()
     sent_copy.start()
     blocks_copy.wait()
     blocks = blocks_ref[...]
@@ -114,10 +120,14 @@
     lane = lax.broadcasted_iota(jnp.int32, (listed, total), 1).astype(f32)
     first = (column == lane).astype(f32).astype(bf16)
     listed_ref[...] = first
-    load_copy.wait()
+    wanted_rows = count * blocks.shape[1]
+    sent = None
+    for copy, rows in zip(load_copies, halves):
+        copy.wait()
+        part = pick(first[:wanted_rows, rows], load_ref[rows])
+        sent = part if sent is None else sent + part
+    put_shared(sent, shared_refs)
     sent_copy.wait()
-    sent = pick(first[: count * blocks.shape[1]], load_ref[...])
-    put_shared(sent, shared_refs)
 
 
 def order_body(subs, listed_ref, load_ref, basis_ref,
@@ -256,13 +266,12 @@
 def finish_body(subs, flipped_ref, base_ref, *refs):
     *arrived, out_hbm, out_ref, sems = refs
     came = came_in(subs, arrived)
-    halves = split(came)
+    total = base_ref[...] + pick(flipped_ref[:, : came.shape[0]], came)
     copies = []
     size = out_ref.shape[0] // 4
     for step in range(4):
         rows = slice(step * size, (step + 1) * size)
-        chooser = flipped_ref[rows, : came.shape[0]]
-        out_ref[rows] = base_ref[rows] + (dot(chooser, halves[0]) + dot(chooser, halves[1]))
+        out_ref[rows] = total[rows]
         copy = pltpu.make_async_copy(out_ref.at[rows], out_hbm.at[rows], sems.at[step])
         copy.start()
         copies.append(copy)
@@ -314,7 +323,8 @@
         lambda *refs: listed_body(subs, count, *refs),
         [((listed, rows), bf16), whole(loads), ((modes, modes), f32)] + shared, 4 * listed * size, 16 * size,
         *[pltpu.with_memory_space_constraint(array, pltpu.HBM) for array in (blocks, load, columns)], ins=[outside] * 3,
-        scratch=[pltpu.VMEM(blocks.shape, blocks.dtype)] + [pltpu.SemaphoreType.DMA] * 3,
+        scratch=[pltpu.VMEM(blocks.shape, blocks.dtype), pltpu.SemaphoreType.DMA((2,))]
+        + [pltpu.SemaphoreType.DMA] * 2,
     )
     arrived = exchange(parts)
     other = lax.ppermute(sent, "grp", pair_plan)

time: 77.6 us -> 77.7 us (level)
  no operation moved by 1% of the time
where the time goes in v3:
time: 77.7 us; the launch traced here: 77.5 us
  starting transfers between devices  34.1 us (44%)
  waiting for transfers between devices  23.9 us (31%)
  Pallas kernels  18.5 us (24%)
  between operations  1.04 us (1%)
    ppermute x15, starting transfers between devices, exchange(): return [lax.ppermute(parts[place], 'sub', pairs) for place, pairs in plans]  19 us
    pallas_call x25, Pallas kernels, __call__(): pl.pallas_call(whole_body, out_shape=[jax.ShapeDtypeStruct(shape, kind) f...  18.5 us
    ppermute x15, waiting for transfers between devices, exchange(): return [lax.ppermute(parts[place], 'sub', pairs) for place, pairs in plans]  11.4 us
    ppermute x4, starting transfers between devices, local(): came.append(lax.ppermute(away, 'grp', mirror_plan))  9.32 us
    ppermute x4, waiting for transfers between devices, local(): came.append(lax.ppermute(away, 'grp', mirror_plan))  5.94 us
    ppermute x4, waiting for transfers between devices, local(): theirs = [lax.ppermute(piece, 'grp', pair_plan) for piece in own]  5.48 us
    ppermute x4, starting transfers between devices, local(): theirs = [lax.ppermute(piece, 'grp', pair_plan) for piece in own]  4.18 us
    ppermute x1, starting transfers between devices, local(): other = lax.ppermute(sent, 'grp', pair_plan)  1.59 us
  transfers between devices with their start and end apart: 24, of which 15 were waited for; matrix products, arithmetic and copies ran while one was open for 0% of the time, Pallas kernels for 16%

profile of v3, /device:TPU:0, one launch (start us, length us, event | category | flops | bytes accessed | tf_op | source)
XLA Modules:
  0.0 77.5 jit_solution(8822640577593195796)
XLA Ops:
  0.6 1.7 %shard_map.77 = (bf16[384,512]{1,0:T(8,128)(2,1)S(1)}, f32[512,384]{1,0:T(8,128)S(1)}, f32[128,128]{1,0:T(8,128)S(1)}, f32[96,384]{1,0:T(8,128)S(1)}, f32[96,384]{1,0:T(8,128)S(1)}, /*index=5*/f32[96,384]{1,0:T(8,128)S(1)}) custom-call(s32[4,96]{1,0:T(4,128)} %bitcast.15, f32[512,384]{1,0:T(8,128)} %bitcast.14, f32[512,128]{1,0:T(8,128)} %bitcast.9), custom_call_target="tpu_custom_call" | custom-call | flops 301989888 | bytes 3145728 | tf_op jit(solution)/shard_map/pallas_call | solution.py:35
  2.4 3.0 %collective-permute-start = (f32[96,384]{1,0:T(8,128)S(1)}, f32[96,384]{1,0:T(8,128)S(1)}, u32[]{:S(2)}, u32[]{:S(2)}) collective-permute-start(f32[96,384]{1,0:T(8,128)S(1)} %get-tuple-element.65), channel_id=1, source_target_pairs={{0,16},{4,20},{8,24},{12,28},{16,0},{20,4},{24,8},{28,12},{1,17},{... | collective-permute-start | bytes 442376 | tf_op jit(solution)/shard_map/ppermute | solution.py:309
  5.4 2.6 %collective-permute-start.2 = (f32[96,384]{1,0:T(8,128)S(1)}, f32[96,384]{1,0:T(8,128)S(1)}, u32[]{:S(2)}, u32[]{:S(2)}) collective-permute-start(f32[96,384]{1,0:T(8,128)S(1)} %get-tuple-element.67), channel_id=1, source_target_pairs={{4,0},{8,4},{12,8},{16,12},{20,16},{24,20},{28,24},{0,28},{5,1},{9... | collective-permute-start | bytes 442376 | tf_op jit(solution)/shard_map/ppermute | solution.py:309
  8.0 1.6 %collective-permute-start.3 = (f32[128,128]{1,0:T(8,128)S(1)}, f32[128,128]{1,0:T(8,128)S(1)}, u32[]{:S(2)}, u32[]{:S(2)}) collective-permute-start(f32[128,128]{1,0:T(8,128)S(1)} %get-tuple-element.68), channel_id=1, source_target_pairs={{0,1},{1,0},{2,3},{3,2},{4,5},{5,4},{6,7},{7,6},{8,9},{9,8},{10,11... | collective-permute-start | bytes 196616 | tf_op jit(solution)/shard_map/ppermute | solution.py:330
  9.6 1.6 %shard_map.78 = (bf16[512,512]{1,0:T(8,128)(2,1)S(1)}, bf16[512,512]{1,0:T(8,128)(2,1)S(1)}, bf16[512,128]{1,0:T(8,128)(2,1)S(1)}, bf16[512,128]{1,0:T(8,128)(2,...) custom-call(bf16[384,512]{1,0:T(8,128)(2,1)S(1)} %get-tuple-element., ...), custom_call_target="tpu_custom_call" | custom-call | flops 402653184 | bytes 4718592 | tf_op jit(solution)/shard_map/pallas_call | solution.py:35
  11.2 1.1 %collective-permute-done.3.refs_1_ = f32[128,128]{1,0:T(8,128)S(1)} collective-permute-done((f32[128,128]{1,0:T(8,128)S(1)}, f32[128,128]{1,0:T(8,128)S(1)}, u32[]{:S(2)}, u32[]{:S(2)}) %collective-permute-start.3) | collective-permute-done | bytes 65568 | tf_op jit(solution)/shard_map/ppermute | solution.py:330
  12.5 0.4 shard_map.80
  12.8 1.7 %collective-permute-start.4 = (f32[128,128]{1,0:T(8,128)S(1)}, f32[128,128]{1,0:T(8,128)S(1)}, u32[]{:S(2)}, u32[]{:S(2)}) collective-permute-start(f32[128,128]{1,0:T(8,128)S(1)} %get-tuple-element.71.refs_0_.refs_4_), channel_id=1, source_target_pairs={{0,1},{1,0},{2,3},{3,2},{4,5},{5,4},{6,7},{7,6},{8,9},{9,8},{10,11... | collective-permute-start | bytes 196616 | tf_op jit(solution)/shard_map/ppermute | solution.py:346
  14.5 0.4 collective-permute-start.6
  14.9 2.9 %collective-permute-done.4.refs_1_ = f32[128,128]{1,0:T(8,128)S(1)} collective-permute-done((f32[128,128]{1,0:T(8,128)S(1)}, f32[128,128]{1,0:T(8,128)S(1)}, u32[]{:S(2)}, u32[]{:S(2)}) %collective-permute-start.4) | collective-permute-done | bytes 65568 | tf_op jit(solution)/shard_map/ppermute | solution.py:346
  18.1 3.5 %collective-permute-start.5 = (f32[128,128]{1,0:T(8,128)S(1)}, f32[128,128]{1,0:T(8,128)S(1)}, u32[]{:S(2)}, u32[]{:S(2)}) collective-permute-start(f32[128,128]{1,0:T(8,128)S(1)} %get-tuple-element.74.refs_4_), channel_id=1, source_target_pairs={{0,3},{3,0},{1,2},{2,1},{4,7},{7,4},{5,6},{6,5},{8,11},{11,8},{9,1... | collective-permute-start | bytes 196616 | tf_op jit(solution)/shard_map/ppermute | solution.py:354
  21.9 1.1 %collective-permute-start.7 = (f32[128,256]{1,0:T(8,128)S(1)}, f32[128,256]{1,0:T(8,128)S(1)}, u32[]{:S(2)}, u32[]{:S(2)}) collective-permute-start(f32[128,256]{1,0:T(8,128)S(1)} %get-tuple-element.77.refs_2_), channel_id=1, source_target_pairs={{0,3},{3,0},{1,2},{2,1},{4,7},{7,4},{5,6},{6,5},{8,11},{11,8},{9,1... | collective-permute-start | bytes 393224 | tf_op jit(solution)/shard_map/ppermute | solution.py:354
  23.0 1.3 %shard_map.83 = (bf16[512,512]{1,0:T(8,128)(2,1)S(1)}, bf16[512,512]{1,0:T(8,128)(2,1)S(1)}) custom-call(bf16[512,512]{1,0:T(8,128)(2,1)S(1)} %get-tuple-element.69.refs_2_.refs_0_, f32[512,512]{1,0:T(8,128)S(1)} %bitcast.11, f32[128,256]{1,0:T(8,128)S(1)} %get-tuple-element.77.refs_2_), custom_call_target="tpu_custom_call" | custom-call | flops 1073741824 | bytes 2359296 | tf_op jit(solution)/shard_map/pallas_call | solution.py:35
  24.4 1.0 %shard_map.84.refs_2_.refs_5_ = f32[512,384]{1,0:T(8,128)S(1)} custom-call(f32[512,384]{1,0:T(8,128)S(1)} %get-tuple-element.75.refs_0_.refs_2_.refs_3_, bf16[512,512]{1,0:T(8,128)(2,1)S(1)} %get-tuple-element.78.refs_1_.refs_6_, bf16[512,512]{1,0:T(8,128)(2,1)S(1)} %get-tuple-element.79.refs_2_, f32[96,384]{1,0:T(8,128)S(1)} %collective-permute-done.refs_3_, ...), custom_call_target="tpu_custom_call" | custom-call | flops 9663676416 | bytes 37748736 | tf_op jit(solution)/shard_map/pallas_call | solution.py:35
  25.7 3.1 %collective-permute-done.7.refs_1_ = f32[128,256]{1,0:T(8,128)S(1)} collective-permute-done((f32[128,256]{1,0:T(8,128)S(1)}, f32[128,256]{1,0:T(8,128)S(1)}, u32[]{:S(2)}, u32[]{:S(2)}) %collective-permute-start.7) | collective-permute-done | bytes 131104 | tf_op jit(solution)/shard_map/ppermute | solution.py:354
  28.8 0.4 shard_map.86
  29.2 0.7 collective-permute-start.8
  29.9 2.6 %collective-permute-start.10 = (f32[96,384]{1,0:T(8,128)S(1)}, f32[96,384]{1,0:T(8,128)S(1)}, u32[]{:S(2)}, u32[]{:S(2)}) collective-permute-start(f32[96,384]{1,0:T(8,128)S(1)} %get-tuple-element.90), channel_id=1, source_target_pairs={{4,0},{8,4},{12,8},{16,12},{20,16},{24,20},{28,24},{0,28},{5,1},{9... | collective-permute-start | bytes 442376 | tf_op jit(solution)/shard_map/ppermute | solution.py:309
  32.6 1.3 %shard_map.87 = (bf16[512,512]{1,0:T(8,128)(2,1)S(1)}, bf16[512,512]{1,0:T(8,128)(2,1)S(1)}) custom-call(bf16[512,512]{1,0:T(8,128)(2,1)S(1)} %get-tuple-element.69.refs_2_.refs_0_, bf16[512,512]{1,0:T(8,128)(2,1)S(1)} %get-tuple-element.61.refs_1_.refs_0_, f32[512,512]{1,0:T(8,128)S(1)} %bitcast.12, f32[512,256]{1,0:T(8,128)S(1)} %get-tuple-element.83.refs_3_.refs_1_), custom_call_target="tpu_custom_call" | custom-call | flops 1073741824 | bytes 2359296 | tf_op jit(solution)/shard_map/pallas_call | solution.py:35
  33.9 1.0 %shard_map.88 = (f32[512,384]{1,0:T(8,128)S(1)}, f32[512,384]{1,0:T(8,128)S(1)}) custom-call(f32[512,128]{1,0:T(8,128)S(1)} %shard_map.85.refs_5_.refs_6_.refs_0_, f32[512,256]{1,0:T(8,128)S(1)} %get-tuple-element.83.refs_3_.refs_1_, f32[512,384]{1,0:T(8,128)S(1)} %get-tuple-element.75.refs_0_.refs_2_.refs_3_, ...), custom_call_target="tpu_custom_call" | custom-call | flops 603979776 | bytes 3145728 | tf_op jit(solution)/shard_map/pallas_call | solution.py:35
  34.8 1.1 %collective-permute-done.8.refs_3_.refs_4_ = f32[96,384]{1,0:T(8,128)S(1)} collective-permute-done((f32[96,384]{1,0:T(8,128)S(1)}, f32[96,384]{1,0:T(8,128)S(1)}, u32[]{:S(2)}, u32[]{:S(2)}) %collective-permute-start.8) | collective-permute-done | bytes 147488 | tf_op jit(solution)/shard_map/ppermute | solution.py:309
  36.1 0.6 shard_map.89
  36.6 2.1 %collective-permute-start.11 = (f32[96,384]{1,0:T(8,128)S(1)}, f32[96,384]{1,0:T(8,128)S(1)}, u32[]{:S(2)}, u32[]{:S(2)}) collective-permute-start(f32[96,384]{1,0:T(8,128)S(1)} %get-tuple-element.91.refs_7_.refs_12_), channel_id=1, source_target_pairs={{0,16},{4,20},{8,24},{12,28},{16,0},{20,4},{24,8},{28,12},{1,17},{... | collective-permute-start | bytes 442376 | tf_op jit(solution)/shard_map/ppermute | solution.py:309
  38.7 1.0 %collective-permute-start.13 = (f32[96,384]{1,0:T(8,128)S(1)}, f32[96,384]{1,0:T(8,128)S(1)}, u32[]{:S(2)}, u32[]{:S(2)}) collective-permute-start(f32[96,384]{1,0:T(8,128)S(1)} %get-tuple-element.92.refs_8_), channel_id=1, source_target_pairs={{4,0},{8,4},{12,8},{16,12},{20,16},{24,20},{28,24},{0,28},{5,1},{9... | collective-permute-start | bytes 442376 | tf_op jit(solution)/shard_map/ppermute | solution.py:309
  39.8 0.9 %shard_map.90 = (f32[128,384]{1,0:T(8,128)S(1)}, f32[512,384]{1,0:T(8,128)S(1)}, f32[512,384]{1,0:T(8,128)S(1)}) custom-call(f32[512,384]{1,0:T(8,128)S(1)} %get-tuple-element.86.refs_0_.refs_6_, f32[512,384]{1,0:T(8,128)S(1)} %get-tuple-element.87.refs_1_, bf16[512,512]{1,0:T(8,128)(2,1)S(1)} %get-tuple-element.84.refs_3_.refs_5_.refs_1_.refs_2_.refs_4_, ...), custom_call_target="tpu_custom_call" | custom-call | flops 301989888 | bytes 3145728 | tf_op jit(solution)/shard_map/pallas_call | solution.py:35
  40.6 2.5 %collective-permute-done.11.refs_3_ = f32[96,384]{1,0:T(8,128)S(1)} collective-permute-done((f32[96,384]{1,0:T(8,128)S(1)}, f32[96,384]{1,0:T(8,128)S(1)}, u32[]{:S(2)}, u32[]{:S(2)}) %collective-permute-start.11) | collective-permute-done | bytes 147488 | tf_op jit(solution)/shard_map/ppermute | solution.py:309
  43.3 1.9 %collective-permute-done.12.refs_4_ = f32[96,384]{1,0:T(8,128)S(1)} collective-permute-done((f32[96,384]{1,0:T(8,128)S(1)}, f32[96,384]{1,0:T(8,128)S(1)}, u32[]{:S(2)}, u32[]{:S(2)}) %collective-permute-start.12) | collective-permute-done | bytes 147488 | tf_op jit(solution)/shard_map/ppermute | solution.py:309
  45.2 0.3 shard_map.91
  45.6 1.2 %collective-permute-start.14 = (f32[128,128]{1,0:T(8,128)S(1)}, f32[128,128]{1,0:T(8,128)S(1)}, u32[]{:S(2)}, u32[]{:S(2)}) collective-permute-start(f32[128,128]{1,0:T(8,128)S(1)} %get-tuple-element.95.refs_0_.refs_4_), channel_id=1, source_target_pairs={{0,1},{1,0},{2,3},{3,2},{4,5},{5,4},{6,7},{7,6},{8,9},{9,8},{10,11... | collective-permute-start | bytes 196616 | tf_op jit(solution)/shard_map/ppermute | solution.py:346
  46.8 0.9 %collective-permute-start.16 = (f32[128,256]{1,0:T(8,128)S(1)}, f32[128,256]{1,0:T(8,128)S(1)}, u32[]{:S(2)}, u32[]{:S(2)}) collective-permute-start(f32[128,256]{1,0:T(8,128)S(1)} %get-tuple-element.99.refs_0_), channel_id=1, source_target_pairs={{0,1},{1,0},{2,3},{3,2},{4,5},{5,4},{6,7},{7,6},{8,9},{9,8},{10,11... | collective-permute-start | bytes 393224 | tf_op jit(solution)/shard_map/ppermute | solution.py:346
  47.7 2.2 %collective-permute-done.14.refs_1_ = f32[128,128]{1,0:T(8,128)S(1)} collective-permute-done((f32[128,128]{1,0:T(8,128)S(1)}, f32[128,128]{1,0:T(8,128)S(1)}, u32[]{:S(2)}, u32[]{:S(2)}) %collective-permute-start.14) | collective-permute-done | bytes 65568 | tf_op jit(solution)/shard_map/ppermute | solution.py:346
  50.2 1.8 %collective-permute-start.15 = (f32[128,128]{1,0:T(8,128)S(1)}, f32[128,128]{1,0:T(8,128)S(1)}, u32[]{:S(2)}, u32[]{:S(2)}) collective-permute-start(f32[128,128]{1,0:T(8,128)S(1)} %get-tuple-element.97.refs_4_), channel_id=1, source_target_pairs={{0,3},{3,0},{1,2},{2,1},{4,7},{7,4},{5,6},{6,5},{8,11},{11,8},{9,1... | collective-permute-start | bytes 196616 | tf_op jit(solution)/shard_map/ppermute | solution.py:354
  52.5 2.9 %collective-permute-start.17 = (f32[128,256]{1,0:T(8,128)S(1)}, f32[128,256]{1,0:T(8,128)S(1)}, u32[]{:S(2)}, u32[]{:S(2)}) collective-permute-start(f32[128,256]{1,0:T(8,128)S(1)} %get-tuple-element.100.refs_6_), channel_id=1, source_target_pairs={{0,3},{3,0},{1,2},{2,1},{4,7},{7,4},{5,6},{6,5},{8,11},{11,8},{9,1... | collective-permute-start | bytes 393224 | tf_op jit(solution)/shard_map/ppermute | solution.py:354
  55.4 1.0 %shard_map.94.refs_2_.refs_5_ = f32[512,384]{1,0:T(8,128)S(1)} custom-call(f32[512,384]{1,0:T(8,128)S(1)} %get-tuple-element.98.refs_0_, bf16[512,512]{1,0:T(8,128)(2,1)S(1)} %get-tuple-element.78.refs_1_.refs_6_, bf16[512,512]{1,0:T(8,128)(2,1)S(1)} %get-tuple-element.79.refs_2_, f32[96,384]{1,0:T(8,128)S(1)} %collective-permute-done.11.refs_3_, ...), custom_call_target="tpu_custom_call" | custom-call | flops 9663676416 | bytes 37748736 | tf_op jit(solution)/shard_map/pallas_call | solution.py:35
  56.7 2.8 %collective-permute-done.17.refs_1_ = f32[128,256]{1,0:T(8,128)S(1)} collective-permute-done((f32[128,256]{1,0:T(8,128)S(1)}, f32[128,256]{1,0:T(8,128)S(1)}, u32[]{:S(2)}, u32[]{:S(2)}) %collective-permute-start.17) | collective-permute-done | bytes 131104 | tf_op jit(solution)/shard_map/ppermute | solution.py:354
  59.5 0.4 shard_map.96
  59.8 1.0 %collective-permute-start.18 = (f32[96,384]{1,0:T(8,128)S(1)}, f32[96,384]{1,0:T(8,128)S(1)}, u32[]{:S(2)}, u32[]{:S(2)}) collective-permute-start(f32[96,384]{1,0:T(8,128)S(1)} %get-tuple-element.106), channel_id=1, source_target_pairs={{0,16},{4,20},{8,24},{12,28},{16,0},{20,4},{24,8},{28,12},{1,17},{... | collective-permute-start | bytes 442376 | tf_op jit(solution)/shard_map/ppermute | solution.py:309
  60.8 2.6 %collective-permute-start.20 = (f32[96,384]{1,0:T(8,128)S(1)}, f32[96,384]{1,0:T(8,128)S(1)}, u32[]{:S(2)}, u32[]{:S(2)}) collective-permute-start(f32[96,384]{1,0:T(8,128)S(1)} %get-tuple-element.108), channel_id=1, source_target_pairs={{4,0},{8,4},{12,8},{16,12},{20,16},{24,20},{28,24},{0,28},{5,1},{9... | collective-permute-start | bytes 442376 | tf_op jit(solution)/shard_map/ppermute | solution.py:309
  63.5 1.0 %shard_map.97 = (f32[512,384]{1,0:T(8,128)S(1)}, f32[512,384]{1,0:T(8,128)S(1)}) custom-call(f32[512,128]{1,0:T(8,128)S(1)} %shard_map.95.refs_5_.refs_6_.refs_0_, f32[512,256]{1,0:T(8,128)S(1)} %get-tuple-element.102.refs_1_.refs_6_, f32[512,384]{1,0:T(8,128)S(1)} %get-tuple-element.103.refs_2_, f32[512,384]{1,0:T(8,128)S(1)} %get-tuple-element.75.refs_0_.refs_2_.refs_3_, ...), custom_call_target="tpu_custom_call" | custom-call | flops 603979776 | bytes 3145728 | tf_op jit(solution)/shard_map/pallas_call | solution.py:35
  64.4 2.2 %collective-permute-done.18.refs_3_.refs_4_ = f32[96,384]{1,0:T(8,128)S(1)} collective-permute-done((f32[96,384]{1,0:T(8,128)S(1)}, f32[96,384]{1,0:T(8,128)S(1)}, u32[]{:S(2)}, u32[]{:S(2)}) %collective-permute-start.18) | collective-permute-done | bytes 147488 | tf_op jit(solution)/shard_map/ppermute | solution.py:309
  66.6 0.6 shard_map.98
  67.2 1.4 %collective-permute-start.21 = (f32[96,384]{1,0:T(8,128)S(1)}, f32[96,384]{1,0:T(8,128)S(1)}, u32[]{:S(2)}, u32[]{:S(2)}) collective-permute-start(f32[96,384]{1,0:T(8,128)S(1)} %get-tuple-element.109.refs_7_.refs_10_), channel_id=1, source_target_pairs={{0,16},{4,20},{8,24},{12,28},{16,0},{20,4},{24,8},{28,12},{1,17},{... | collective-permute-start | bytes 442376 | tf_op jit(solution)/shard_map/ppermute | solution.py:309
  68.6 1.8 %collective-permute-start.23 = (f32[96,384]{1,0:T(8,128)S(1)}, f32[96,384]{1,0:T(8,128)S(1)}, u32[]{:S(2)}, u32[]{:S(2)}) collective-permute-start(f32[96,384]{1,0:T(8,128)S(1)} %get-tuple-element.110.refs_8_), channel_id=1, source_target_pairs={{4,0},{8,4},{12,8},{16,12},{20,16},{24,20},{28,24},{0,28},{5,1},{9... | collective-permute-start | bytes 442376 | tf_op jit(solution)/shard_map/ppermute | solution.py:309
  70.4 0.5 shard_map.99
  70.9 1.6 %shard_map.100 = (f32[512,384]{1,0:T(8,128)S(1)}, f32[512,384]{1,0:T(8,128)}) custom-call(bf16[512,512]{1,0:T(8,128)(2,1)S(1)} %get-tuple-element.61.refs_1_.refs_0_, f32[512,384]{1,0:T(8,128)S(1)} %get-tuple-element.112.refs_1_, f32[512,384]{1,0:T(8,128)S(1)} %get-tuple-element.113.refs_2_.refs_3_, f32[512,384]{1,0:T(8,128)S(1)} %get-tuple-element.113.refs_2_.refs_3_), custom_call_target="tpu_custom_call" | custom-call | flops 805306368 | bytes 1966080 | tf_op jit(solution)/shard_map/pallas_call | solution.py:35
  72.5 1.3 %collective-permute-done.21.refs_2_ = f32[96,384]{1,0:T(8,128)S(1)} collective-permute-done((f32[96,384]{1,0:T(8,128)S(1)}, f32[96,384]{1,0:T(8,128)S(1)}, u32[]{:S(2)}, u32[]{:S(2)}) %collective-permute-start.21) | collective-permute-done | bytes 147488 | tf_op jit(solution)/shard_map/ppermute | solution.py:309
  73.9 1.9 %collective-permute-done.22.refs_3_ = f32[96,384]{1,0:T(8,128)S(1)} collective-permute-done((f32[96,384]{1,0:T(8,128)S(1)}, f32[96,384]{1,0:T(8,128)S(1)}, u32[]{:S(2)}, u32[]{:S(2)}) %collective-permute-start.22) | collective-permute-done | bytes 147488 | tf_op jit(solution)/shard_map/ppermute | solution.py:309
  75.9 1.5 %shard_map.101 = f32[512,384]{1,0:T(8,128)} custom-call(bf16[512,512]{1,0:T(8,128)(2,1)S(1)} %get-tuple-element.61.refs_1_.refs_0_, f32[512,384]{1,0:T(8,128)S(1)} %get-tuple-element.115.refs_1_.refs_5_, f32[96,384]{1,0:T(8,128)S(1)} %collective-permute-done.21.refs_2_, f32[96,384]{1,0:T(8,128)S(1)} %collective-permute-done.22.refs_3_, ...), custom_call_target="tpu_custom_call" | custom-call | flops 402653184 | bytes 1966080 | tf_op jit(solution)/shard_map/pallas_call | solution.py:35
  (33 shorter events, 2.6 us)
Async XLA Ops:
  0.6 9.0 %copy-start = (f32[1,1,512,128]{3,2,1,0:T(8,128)S(1)}, f32[1,1,512,128]{3,2,1,0:T(8,128)}, u32[]{:S(2)}) copy-start(f32[1,1,512,128]{3,2,1,0:T(8,128)} %param.9) | copy-start | bytes 786436
  2.4 10.1 %collective-permute-start = (f32[96,384]{1,0:T(8,128)S(1)}, f32[96,384]{1,0:T(8,128)S(1)}, u32[]{:S(2)}, u32[]{:S(2)}) collective-permute-start(f32[96,384]{1,0:T(8,128)S(1)} %get-tuple-element.65), channel_id=1, source_target_pairs={{0,16},{4,20},{8,24},{12,28},{16,0},{20,4},{24,8},{28,12},{1,17},{... | collective-permute-start | bytes 442376 | tf_op jit(solution)/shard_map/ppermute | solution.py:309
  5.4 7.0 %collective-permute-start.1 = (f32[96,384]{1,0:T(8,128)S(1)}, f32[96,384]{1,0:T(8,128)S(1)}, u32[]{:S(2)}, u32[]{:S(2)}) collective-permute-start(f32[96,384]{1,0:T(8,128)S(1)} %get-tuple-element.66), channel_id=1, source_target_pairs={{0,4},{4,8},{8,12},{12,16},{16,20},{20,24},{24,28},{28,0},{1,5},{5... | collective-permute-start | bytes 442376 | tf_op jit(solution)/shard_map/ppermute | solution.py:309
  5.4 7.1 %collective-permute-start.2 = (f32[96,384]{1,0:T(8,128)S(1)}, f32[96,384]{1,0:T(8,128)S(1)}, u32[]{:S(2)}, u32[]{:S(2)}) collective-permute-start(f32[96,384]{1,0:T(8,128)S(1)} %get-tuple-element.67), channel_id=1, source_target_pairs={{4,0},{8,4},{12,8},{16,12},{20,16},{24,20},{28,24},{0,28},{5,1},{9... | collective-permute-start | bytes 442376 | tf_op jit(solution)/shard_map/ppermute | solution.py:309
  8.0 4.3 %collective-permute-start.3 = (f32[128,128]{1,0:T(8,128)S(1)}, f32[128,128]{1,0:T(8,128)S(1)}, u32[]{:S(2)}, u32[]{:S(2)}) collective-permute-start(f32[128,128]{1,0:T(8,128)S(1)} %get-tuple-element.68), channel_id=1, source_target_pairs={{0,1},{1,0},{2,3},{3,2},{4,5},{5,4},{6,7},{7,6},{8,9},{9,8},{10,11... | collective-permute-start | bytes 196616 | tf_op jit(solution)/shard_map/ppermute | solution.py:330
  9.6 2.7 %copy-start.1 = (f32[1,512,128]{2,1,0:T(8,128)S(1)}, f32[1,512,128]{2,1,0:T(8,128)}, u32[]{:S(2)}) copy-start(f32[1,512,128]{2,1,0:T(8,128)} %param.10) | copy-start | bytes 786436
  12.8 5.0 %collective-permute-start.4 = (f32[128,128]{1,0:T(8,128)S(1)}, f32[128,128]{1,0:T(8,128)S(1)}, u32[]{:S(2)}, u32[]{:S(2)}) collective-permute-start(f32[128,128]{1,0:T(8,128)S(1)} %get-tuple-element.71.refs_0_.refs_4_), channel_id=1, source_target_pairs={{0,1},{1,0},{2,3},{3,2},{4,5},{5,4},{6,7},{7,6},{8,9},{9,8},{10,11... | collective-permute-start | bytes 196616 | tf_op jit(solution)/shard_map/ppermute | solution.py:346
  14.5 7.2 %collective-permute-start.6 = (f32[128,256]{1,0:T(8,128)S(1)}, f32[128,256]{1,0:T(8,128)S(1)}, u32[]{:S(2)}, u32[]{:S(2)}) collective-permute-start(f32[128,256]{1,0:T(8,128)S(1)} %get-tuple-element.76.refs_0_), channel_id=1, source_target_pairs={{0,1},{1,0},{2,3},{3,2},{4,5},{5,4},{6,7},{7,6},{8,9},{9,8},{10,11... | collective-permute-start | bytes 393224 | tf_op jit(solution)/shard_map/ppermute | solution.py:346
  18.1 4.9 %copy-start.2 = (f32[1,1,512,512]{3,2,1,0:T(8,128)S(1)}, f32[1,1,512,512]{3,2,1,0:T(8,128)}, u32[]{:S(2)}) copy-start(f32[1,1,512,512]{3,2,1,0:T(8,128)} %param.8) | copy-start | bytes 3145732
  18.1 7.3 %collective-permute-start.5 = (f32[128,128]{1,0:T(8,128)S(1)}, f32[128,128]{1,0:T(8,128)S(1)}, u32[]{:S(2)}, u32[]{:S(2)}) collective-permute-start(f32[128,128]{1,0:T(8,128)S(1)} %get-tuple-element.74.refs_4_), channel_id=1, source_target_pairs={{0,3},{3,0},{1,2},{2,1},{4,7},{7,4},{5,6},{6,5},{8,11},{11,8},{9,1... | collective-permute-start | bytes 196616 | tf_op jit(solution)/shard_map/ppermute | solution.py:354
  21.9 6.9 %collective-permute-start.7 = (f32[128,256]{1,0:T(8,128)S(1)}, f32[128,256]{1,0:T(8,128)S(1)}, u32[]{:S(2)}, u32[]{:S(2)}) collective-permute-start(f32[128,256]{1,0:T(8,128)S(1)} %get-tuple-element.77.refs_2_), channel_id=1, source_target_pairs={{0,3},{3,0},{1,2},{2,1},{4,7},{7,4},{5,6},{6,5},{8,11},{11,8},{9,1... | collective-permute-start | bytes 393224 | tf_op jit(solution)/shard_map/ppermute | solution.py:354
  25.7 6.9 %copy-start.3 = (f32[1,1,512,512]{3,2,1,0:T(8,128)S(1)}, f32[1,1,512,512]{3,2,1,0:T(8,128)}, u32[]{:S(2)}) copy-start(f32[1,1,512,512]{3,2,1,0:T(8,128)} %param.7) | copy-start | bytes 3145732
  29.2 6.7 %collective-permute-start.8 = (f32[96,384]{1,0:T(8,128)S(1)}, f32[96,384]{1,0:T(8,128)S(1)}, u32[]{:S(2)}, u32[]{:S(2)}) collective-permute-start(f32[96,384]{1,0:T(8,128)S(1)} %get-tuple-element.88), channel_id=1, source_target_pairs={{0,16},{4,20},{8,24},{12,28},{16,0},{20,4},{24,8},{28,12},{1,17},{... | collective-permute-start | bytes 442376 | tf_op jit(solution)/shard_map/ppermute | solution.py:309
  29.9 6.1 %collective-permute-start.9 = (f32[96,384]{1,0:T(8,128)S(1)}, f32[96,384]{1,0:T(8,128)S(1)}, u32[]{:S(2)}, u32[]{:S(2)}) collective-permute-start(f32[96,384]{1,0:T(8,128)S(1)} %get-tuple-element.89), channel_id=1, source_target_pairs={{0,4},{4,8},{8,12},{12,16},{16,20},{20,24},{24,28},{28,0},{1,5},{5... | collective-permute-start | bytes 442376 | tf_op jit(solution)/shard_map/ppermute | solution.py:309
  29.9 6.1 %collective-permute-start.10 = (f32[96,384]{1,0:T(8,128)S(1)}, f32[96,384]{1,0:T(8,128)S(1)}, u32[]{:S(2)}, u32[]{:S(2)}) collective-permute-start(f32[96,384]{1,0:T(8,128)S(1)} %get-tuple-element.90), channel_id=1, source_target_pairs={{4,0},{8,4},{12,8},{16,12},{20,16},{24,20},{28,24},{0,28},{5,1},{9... | collective-permute-start | bytes 442376 | tf_op jit(solution)/shard_map/ppermute | solution.py:309
  36.6 6.4 %collective-permute-start.11 = (f32[96,384]{1,0:T(8,128)S(1)}, f32[96,384]{1,0:T(8,128)S(1)}, u32[]{:S(2)}, u32[]{:S(2)}) collective-permute-start(f32[96,384]{1,0:T(8,128)S(1)} %get-tuple-element.91.refs_7_.refs_12_), channel_id=1, source_target_pairs={{0,16},{4,20},{8,24},{12,28},{16,0},{20,4},{24,8},{28,12},{1,17},{... | collective-permute-start | bytes 442376 | tf_op jit(solution)/shard_map/ppermute | solution.py:309
  38.7 4.6 %collective-permute-start.13 = (f32[96,384]{1,0:T(8,128)S(1)}, f32[96,384]{1,0:T(8,128)S(1)}, u32[]{:S(2)}, u32[]{:S(2)}) collective-permute-start(f32[96,384]{1,0:T(8,128)S(1)} %get-tuple-element.92.refs_8_), channel_id=1, source_target_pairs={{4,0},{8,4},{12,8},{16,12},{20,16},{24,20},{28,24},{0,28},{5,1},{9... | collective-permute-start | bytes 442376 | tf_op jit(solution)/shard_map/ppermute | solution.py:309
  39.8 5.5 %collective-permute-start.12 = (f32[96,384]{1,0:T(8,128)S(1)}, f32[96,384]{1,0:T(8,128)S(1)}, u32[]{:S(2)}, u32[]{:S(2)}) collective-permute-start(f32[96,384]{1,0:T(8,128)S(1)} %get-tuple-element.93.refs_9_), channel_id=1, source_target_pairs={{0,4},{4,8},{8,12},{12,16},{16,20},{20,24},{24,28},{28,0},{1,5},{5... | collective-permute-start | bytes 442376 | tf_op jit(solution)/shard_map/ppermute | solution.py:309
  45.6 4.3 %collective-permute-start.14 = (f32[128,128]{1,0:T(8,128)S(1)}, f32[128,128]{1,0:T(8,128)S(1)}, u32[]{:S(2)}, u32[]{:S(2)}) collective-permute-start(f32[128,128]{1,0:T(8,128)S(1)} %get-tuple-element.95.refs_0_.refs_4_), channel_id=1, source_target_pairs={{0,1},{1,0},{2,3},{3,2},{4,5},{5,4},{6,7},{7,6},{8,9},{9,8},{10,11... | collective-permute-start | bytes 196616 | tf_op jit(solution)/shard_map/ppermute | solution.py:346
  46.8 5.5 %collective-permute-start.16 = (f32[128,256]{1,0:T(8,128)S(1)}, f32[128,256]{1,0:T(8,128)S(1)}, u32[]{:S(2)}, u32[]{:S(2)}) collective-permute-start(f32[128,256]{1,0:T(8,128)S(1)} %get-tuple-element.99.refs_0_), channel_id=1, source_target_pairs={{0,1},{1,0},{2,3},{3,2},{4,5},{5,4},{6,7},{7,6},{8,9},{9,8},{10,11... | collective-permute-start | bytes 393224 | tf_op jit(solution)/shard_map/ppermute | solution.py:346
  50.2 6.3 %collective-permute-start.15 = (f32[128,128]{1,0:T(8,128)S(1)}, f32[128,128]{1,0:T(8,128)S(1)}, u32[]{:S(2)}, u32[]{:S(2)}) collective-permute-start(f32[128,128]{1,0:T(8,128)S(1)} %get-tuple-element.97.refs_4_), channel_id=1, source_target_pairs={{0,3},{3,0},{1,2},{2,1},{4,7},{7,4},{5,6},{6,5},{8,11},{11,8},{9,1... | collective-permute-start | bytes 196616 | tf_op jit(solution)/shard_map/ppermute | solution.py:354
  52.5 6.9 %collective-permute-start.17 = (f32[128,256]{1,0:T(8,128)S(1)}, f32[128,256]{1,0:T(8,128)S(1)}, u32[]{:S(2)}, u32[]{:S(2)}) collective-permute-start(f32[128,256]{1,0:T(8,128)S(1)} %get-tuple-element.100.refs_6_), channel_id=1, source_target_pairs={{0,3},{3,0},{1,2},{2,1},{4,7},{7,4},{5,6},{6,5},{8,11},{11,8},{9,1... | collective-permute-start | bytes 393224 | tf_op jit(solution)/shard_map/ppermute | solution.py:354
  59.8 6.8 %collective-permute-start.18 = (f32[96,384]{1,0:T(8,128)S(1)}, f32[96,384]{1,0:T(8,128)S(1)}, u32[]{:S(2)}, u32[]{:S(2)}) collective-permute-start(f32[96,384]{1,0:T(8,128)S(1)} %get-tuple-element.106), channel_id=1, source_target_pairs={{0,16},{4,20},{8,24},{12,28},{16,0},{20,4},{24,8},{28,12},{1,17},{... | collective-permute-start | bytes 442376 | tf_op jit(solution)/shard_map/ppermute | solution.py:309
  60.8 5.8 %collective-permute-start.19 = (f32[96,384]{1,0:T(8,128)S(1)}, f32[96,384]{1,0:T(8,128)S(1)}, u32[]{:S(2)}, u32[]{:S(2)}) collective-permute-start(f32[96,384]{1,0:T(8,128)S(1)} %get-tuple-element.107), channel_id=1, source_target_pairs={{0,4},{4,8},{8,12},{12,16},{16,20},{20,24},{24,28},{28,0},{1,5},{5... | collective-permute-start | bytes 442376 | tf_op jit(solution)/shard_map/ppermute | solution.py:309
  60.8 5.8 %collective-permute-start.20 = (f32[96,384]{1,0:T(8,128)S(1)}, f32[96,384]{1,0:T(8,128)S(1)}, u32[]{:S(2)}, u32[]{:S(2)}) collective-permute-start(f32[96,384]{1,0:T(8,128)S(1)} %get-tuple-element.108), channel_id=1, source_target_pairs={{4,0},{8,4},{12,8},{16,12},{20,16},{24,20},{28,24},{0,28},{5,1},{9... | collective-permute-start | bytes 442376 | tf_op jit(solution)/shard_map/ppermute | solution.py:309
  67.2 6.6 %collective-permute-start.21 = (f32[96,384]{1,0:T(8,128)S(1)}, f32[96,384]{1,0:T(8,128)S(1)}, u32[]{:S(2)}, u32[]{:S(2)}) collective-permute-start(f32[96,384]{1,0:T(8,128)S(1)} %get-tuple-element.109.refs_7_.refs_10_), channel_id=1, source_target_pairs={{0,16},{4,20},{8,24},{12,28},{16,0},{20,4},{24,8},{28,12},{1,17},{... | collective-permute-start | bytes 442376 | tf_op jit(solution)/shard_map/ppermute | solution.py:309
  68.6 5.4 %collective-permute-start.23 = (f32[96,384]{1,0:T(8,128)S(1)}, f32[96,384]{1,0:T(8,128)S(1)}, u32[]{:S(2)}, u32[]{:S(2)}) collective-permute-start(f32[96,384]{1,0:T(8,128)S(1)} %get-tuple-element.110.refs_8_), channel_id=1, source_target_pairs={{4,0},{8,4},{12,8},{16,12},{20,16},{24,20},{28,24},{0,28},{5,1},{9... | collective-permute-start | bytes 442376 | tf_op jit(solution)/shard_map/ppermute | solution.py:309
  70.4 5.5 %collective-permute-start.22 = (f32[96,384]{1,0:T(8,128)S(1)}, f32[96,384]{1,0:T(8,128)S(1)}, u32[]{:S(2)}, u32[]{:S(2)}) collective-permute-start(f32[96,384]{1,0:T(8,128)S(1)} %get-tuple-element.111.refs_9_), channel_id=1, source_target_pairs={{0,4},{4,8},{8,12},{12,16},{16,20},{20,24},{24,28},{28,0},{1,5},{5... | collective-permute-start | bytes 442376 | tf_op jit(solution)/shard_map/ppermute | solution.py:309

commit v4 on v3

--- a/solution.py
+++ b/solution.py
@@ -65,12 +65,14 @@
 
 def sides(subs):
     sub = lax.axis_index("sub")
+    low_side = sub % 2 == 0
     low_row = (sub // ROW_SUBS) % 2 == 0
+    up, down = sub < subs - 1, sub > 0
     over, under = sub < subs - ROW_SUBS, sub >= ROW_SUBS
     return [
         (low_row, 3, 2, jnp.where(low_row, over, under)),
-        (low_row, 0, 0, sub > 0),
-        (low_row, 1, 1, sub < subs - 1),
+        (low_side, 0, 1, jnp.where(low_side, down, up)),
+        (low_side, 1, 0, jnp.where(low_side, up, down)),
         (low_row, 2, 3, jnp.where(low_row, under, over)),
     ]
 
@@ -280,11 +282,17 @@
 
 
 def swaps(count, stride, odd):
-    partner = list(range(count))
+    partner = {}
     for low in range(count - stride):
         if (low // stride) % 2 == odd:
             partner[low], partner[low + stride] = low + stride, low
-    return list(enumerate(partner)) if partner != list(range(count)) else []
+    if not partner:
+        return []
+    left = [index for index in range(count) if index not in partner]
+    half = len(left) // 2
+    for low, high in zip(left[:half], left[half:]):
+        partner[low], partner[high] = high, low
+    return sorted(partner.items())
 
 
 def local(load_terms, schur_matrix, local_inverse, coarse_modes, cluster_inverse, row_blocks):
@@ -300,13 +308,12 @@
     if lax.axis_size("grp") != GROUPS or sum(PIECES) != loads:
         raise ValueError("unexpected sizes")
 
-    up = [(low, (low + 1) % subs) for low in range(subs)]
-    down = [(target, source) for source, target in up]
-    plans = [(0, swaps(subs, ROW_SUBS, 0)), (2, up), (1, down), (3, swaps(subs, ROW_SUBS, 1))]
-    plans = [plan for plan in plans if plan[1]]
+    plans = [swaps(subs, ROW_SUBS, 0), swaps(subs, 1, 1), swaps(subs, 1, 0), swaps(subs, ROW_SUBS, 1)]
+    plans = [plan for plan in plans if plan]
     count = len(plans)
+
     def exchange(parts):
-        return [lax.ppermute(parts[place], "sub", pairs) for place, pairs in plans]
+        return [lax.ppermute(part, "sub", plan) for part, plan in zip(parts, plans)]
 
     def whole(width, kind=f32):
         return ((rows, width), kind)

time: 77.7 us -> 75.5 us (0.972)
  starting transfers between devices: 34.1 us -> 28.3 us
  waiting for transfers between devices: 23.9 us -> 27.1 us
    ppermute x15, starting transfers between devices: 19 us -> 12.8 us  [exchange(): return [lax.ppermute(part, 'sub', plan) for part, plan in zip(parts, plans)]]
    ppermute x15, waiting for transfers between devices: 11.4 us -> 14.5 us  [exchange(): return [lax.ppermute(part, 'sub', plan) for part, plan in zip(parts, plans)]]
  transfers between devices with their start and end apart: 24 -> 24, of which waited for: 15 -> 15; matrix products, arithmetic and copies ran while one was open for 0% -> 0% of each run, Pallas kernels for 16% -> 17%
where the time goes in v4:
time: 75.5 us; the launch traced here: 75.2 us
  starting transfers between devices  28.3 us (37%)
  waiting for transfers between devices  27.1 us (36%)
  Pallas kernels  18.7 us (25%)
  between operations  1.01 us (1%)
    pallas_call x25, Pallas kernels, __call__(): pl.pallas_call(whole_body, out_shape=[jax.ShapeDtypeStruct(shape, kind) f...  18.7 us
    ppermute x15, waiting for transfers between devices, exchange(): return [lax.ppermute(part, 'sub', plan) for part, plan in zip(parts, plans)]  14.5 us
    ppermute x15, starting transfers between devices, exchange(): return [lax.ppermute(part, 'sub', plan) for part, plan in zip(parts, plans)]  12.8 us
    ppermute x4, starting transfers between devices, local(): came.append(lax.ppermute(away, 'grp', mirror_plan))  9.73 us
    ppermute x4, waiting for transfers between devices, local(): came.append(lax.ppermute(away, 'grp', mirror_plan))  6.42 us
    ppermute x4, waiting for transfers between devices, local(): theirs = [lax.ppermute(piece, 'grp', pair_plan) for piece in own]  5.08 us
    ppermute x4, starting transfers between devices, local(): theirs = [lax.ppermute(piece, 'grp', pair_plan) for piece in own]  4.18 us
    ppermute x1, starting transfers between devices, local(): other = lax.ppermute(sent, 'grp', pair_plan)  1.58 us
  transfers between devices with their start and end apart: 24, of which 15 were waited for; matrix products, arithmetic and copies ran while one was open for 0% of the time, Pallas kernels for 17%

profile of v4, /device:TPU:0, one launch (start us, length us, event | category | flops | bytes accessed | tf_op | source)
XLA Modules:
  0.0 75.2 jit_solution(17785618707474125576)
XLA Ops:
  0.6 1.7 %shard_map.77 = (bf16[384,512]{1,0:T(8,128)(2,1)S(1)}, f32[512,384]{1,0:T(8,128)S(1)}, f32[128,128]{1,0:T(8,128)S(1)}, f32[96,384]{1,0:T(8,128)S(1)}, f32[96,384]{1,0:T(8,128)S(1)}, /*index=5*/f32[96,384]{1,0:T(8,128)S(1)}) custom-call(s32[4,96]{1,0:T(4,128)} %bitcast.15, f32[512,384]{1,0:T(8,128)} %bitcast.14, f32[512,128]{1,0:T(8,128)} %bitcast.9), custom_call_target="tpu_custom_call" | custom-call | flops 301989888 | bytes 3145728 | tf_op jit(solution)/shard_map/pallas_call | solution.py:35
  2.4 3.0 %collective-permute-start = (f32[96,384]{1,0:T(8,128)S(1)}, f32[96,384]{1,0:T(8,128)S(1)}, u32[]{:S(2)}, u32[]{:S(2)}) collective-permute-start(f32[96,384]{1,0:T(8,128)S(1)} %get-tuple-element.65), channel_id=1, source_target_pairs={{0,16},{4,20},{8,24},{12,28},{16,0},{20,4},{24,8},{28,12},{1,17},{... | collective-permute-start | bytes 442376 | tf_op jit(solution)/shard_map/ppermute | solution.py:316
  5.4 0.6 collective-permute-start.1
  6.0 1.0 %collective-permute-start.2 = (f32[96,384]{1,0:T(8,128)S(1)}, f32[96,384]{1,0:T(8,128)S(1)}, u32[]{:S(2)}, u32[]{:S(2)}) collective-permute-start(f32[96,384]{1,0:T(8,128)S(1)} %get-tuple-element.67), channel_id=1, source_target_pairs={{0,4},{4,0},{8,12},{12,8},{16,20},{20,16},{24,28},{28,24},{1,5},{5... | collective-permute-start | bytes 442376 | tf_op jit(solution)/shard_map/ppermute | solution.py:316
  7.0 1.6 %collective-permute-start.3 = (f32[128,128]{1,0:T(8,128)S(1)}, f32[128,128]{1,0:T(8,128)S(1)}, u32[]{:S(2)}, u32[]{:S(2)}) collective-permute-start(f32[128,128]{1,0:T(8,128)S(1)} %get-tuple-element.68), channel_id=1, source_target_pairs={{0,1},{1,0},{2,3},{3,2},{4,5},{5,4},{6,7},{7,6},{8,9},{9,8},{10,11... | collective-permute-start | bytes 196616 | tf_op jit(solution)/shard_map/ppermute | solution.py:337
  8.6 1.6 %shard_map.78 = (bf16[512,512]{1,0:T(8,128)(2,1)S(1)}, bf16[512,512]{1,0:T(8,128)(2,1)S(1)}, bf16[512,128]{1,0:T(8,128)(2,1)S(1)}, bf16[512,128]{1,0:T(8,128)(2,...) custom-call(bf16[384,512]{1,0:T(8,128)(2,1)S(1)} %get-tuple-element., ...), custom_call_target="tpu_custom_call" | custom-call | flops 402653184 | bytes 4718592 | tf_op jit(solution)/shard_map/pallas_call | solution.py:35
  10.2 1.1 %collective-permute-done.3.refs_1_ = f32[128,128]{1,0:T(8,128)S(1)} collective-permute-done((f32[128,128]{1,0:T(8,128)S(1)}, f32[128,128]{1,0:T(8,128)S(1)}, u32[]{:S(2)}, u32[]{:S(2)}) %collective-permute-start.3) | collective-permute-done | bytes 65568 | tf_op jit(solution)/shard_map/ppermute | solution.py:337
  11.9 1.6 %collective-permute-start.4 = (f32[128,128]{1,0:T(8,128)S(1)}, f32[128,128]{1,0:T(8,128)S(1)}, u32[]{:S(2)}, u32[]{:S(2)}) collective-permute-start(f32[128,128]{1,0:T(8,128)S(1)} %get-tuple-element.71.refs_0_.refs_4_), channel_id=1, source_target_pairs={{0,1},{1,0},{2,3},{3,2},{4,5},{5,4},{6,7},{7,6},{8,9},{9,8},{10,11... | collective-permute-start | bytes 196616 | tf_op jit(solution)/shard_map/ppermute | solution.py:353
  13.5 0.5 collective-permute-start.6
  14.0 2.6 %collective-permute-done.4.refs_1_ = f32[128,128]{1,0:T(8,128)S(1)} collective-permute-done((f32[128,128]{1,0:T(8,128)S(1)}, f32[128,128]{1,0:T(8,128)S(1)}, u32[]{:S(2)}, u32[]{:S(2)}) %collective-permute-start.4) | collective-permute-done | bytes 65568 | tf_op jit(solution)/shard_map/ppermute | solution.py:353
  16.9 3.9 %collective-permute-start.5 = (f32[128,128]{1,0:T(8,128)S(1)}, f32[128,128]{1,0:T(8,128)S(1)}, u32[]{:S(2)}, u32[]{:S(2)}) collective-permute-start(f32[128,128]{1,0:T(8,128)S(1)} %get-tuple-element.74.refs_4_), channel_id=1, source_target_pairs={{0,3},{3,0},{1,2},{2,1},{4,7},{7,4},{5,6},{6,5},{8,11},{11,8},{9,1... | collective-permute-start | bytes 196616 | tf_op jit(solution)/shard_map/ppermute | solution.py:361
  21.1 1.7 %collective-permute-start.7 = (f32[128,256]{1,0:T(8,128)S(1)}, f32[128,256]{1,0:T(8,128)S(1)}, u32[]{:S(2)}, u32[]{:S(2)}) collective-permute-start(f32[128,256]{1,0:T(8,128)S(1)} %get-tuple-element.77.refs_2_), channel_id=1, source_target_pairs={{0,3},{3,0},{1,2},{2,1},{4,7},{7,4},{5,6},{6,5},{8,11},{11,8},{9,1... | collective-permute-start | bytes 393224 | tf_op jit(solution)/shard_map/ppermute | solution.py:361
  22.8 1.4 %shard_map.83 = (bf16[512,512]{1,0:T(8,128)(2,1)S(1)}, bf16[512,512]{1,0:T(8,128)(2,1)S(1)}) custom-call(bf16[512,512]{1,0:T(8,128)(2,1)S(1)} %get-tuple-element.69.refs_2_.refs_0_, f32[512,512]{1,0:T(8,128)S(1)} %bitcast.11, f32[128,256]{1,0:T(8,128)S(1)} %get-tuple-element.77.refs_2_), custom_call_target="tpu_custom_call" | custom-call | flops 1073741824 | bytes 2359296 | tf_op jit(solution)/shard_map/pallas_call | solution.py:35
  24.2 1.0 %shard_map.84.refs_2_.refs_5_ = f32[512,384]{1,0:T(8,128)S(1)} custom-call(f32[512,384]{1,0:T(8,128)S(1)} %get-tuple-element.75.refs_0_.refs_2_.refs_3_, bf16[512,512]{1,0:T(8,128)(2,1)S(1)} %get-tuple-element.78.refs_1_.refs_6_, bf16[512,512]{1,0:T(8,128)(2,1)S(1)} %get-tuple-element.79.refs_2_, f32[96,384]{1,0:T(8,128)S(1)} %collective-permute-done.refs_3_, ...), custom_call_target="tpu_custom_call" | custom-call | flops 9663676416 | bytes 37748736 | tf_op jit(solution)/shard_map/pallas_call | solution.py:35
  25.5 2.6 %collective-permute-done.7.refs_1_ = f32[128,256]{1,0:T(8,128)S(1)} collective-permute-done((f32[128,256]{1,0:T(8,128)S(1)}, f32[128,256]{1,0:T(8,128)S(1)}, u32[]{:S(2)}, u32[]{:S(2)}) %collective-permute-start.7) | collective-permute-done | bytes 131104 | tf_op jit(solution)/shard_map/ppermute | solution.py:361
  28.4 0.9 %collective-permute-start.8 = (f32[96,384]{1,0:T(8,128)S(1)}, f32[96,384]{1,0:T(8,128)S(1)}, u32[]{:S(2)}, u32[]{:S(2)}) collective-permute-start(f32[96,384]{1,0:T(8,128)S(1)} %get-tuple-element.88), channel_id=1, source_target_pairs={{0,16},{4,20},{8,24},{12,28},{16,0},{20,4},{24,8},{28,12},{1,17},{... | collective-permute-start | bytes 442376 | tf_op jit(solution)/shard_map/ppermute | solution.py:316
  29.3 1.9 %collective-permute-start.10 = (f32[96,384]{1,0:T(8,128)S(1)}, f32[96,384]{1,0:T(8,128)S(1)}, u32[]{:S(2)}, u32[]{:S(2)}) collective-permute-start(f32[96,384]{1,0:T(8,128)S(1)} %get-tuple-element.90), channel_id=1, source_target_pairs={{0,4},{4,0},{8,12},{12,8},{16,20},{20,16},{24,28},{28,24},{1,5},{5... | collective-permute-start | bytes 442376 | tf_op jit(solution)/shard_map/ppermute | solution.py:316
  31.2 1.3 %shard_map.87 = (bf16[512,512]{1,0:T(8,128)(2,1)S(1)}, bf16[512,512]{1,0:T(8,128)(2,1)S(1)}) custom-call(bf16[512,512]{1,0:T(8,128)(2,1)S(1)} %get-tuple-element.69.refs_2_.refs_0_, bf16[512,512]{1,0:T(8,128)(2,1)S(1)} %get-tuple-element.61.refs_1_.refs_0_, f32[512,512]{1,0:T(8,128)S(1)} %bitcast.12, f32[512,256]{1,0:T(8,128)S(1)} %get-tuple-element.83.refs_3_.refs_1_), custom_call_target="tpu_custom_call" | custom-call | flops 1073741824 | bytes 2359296 | tf_op jit(solution)/shard_map/pallas_call | solution.py:35
  32.5 1.0 %shard_map.88 = (f32[512,384]{1,0:T(8,128)S(1)}, f32[512,384]{1,0:T(8,128)S(1)}) custom-call(f32[512,128]{1,0:T(8,128)S(1)} %shard_map.85.refs_5_.refs_6_.refs_0_, f32[512,256]{1,0:T(8,128)S(1)} %get-tuple-element.83.refs_3_.refs_1_, f32[512,384]{1,0:T(8,128)S(1)} %get-tuple-element.75.refs_0_.refs_2_.refs_3_, ...), custom_call_target="tpu_custom_call" | custom-call | flops 603979776 | bytes 3145728 | tf_op jit(solution)/shard_map/pallas_call | solution.py:35
  33.5 0.6 collective-permute-done.8.refs_3_.refs_4_
  34.1 1.8 %collective-permute-done.9.refs_4_.refs_5_ = f32[96,384]{1,0:T(8,128)S(1)} collective-permute-done((f32[96,384]{1,0:T(8,128)S(1)}, f32[96,384]{1,0:T(8,128)S(1)}, u32[]{:S(2)}, u32[]{:S(2)}) %collective-permute-start.9) | collective-permute-done | bytes 147488 | tf_op jit(solution)/shard_map/ppermute | solution.py:316
  35.8 0.6 shard_map.89
  36.4 1.5 %collective-permute-start.11 = (f32[96,384]{1,0:T(8,128)S(1)}, f32[96,384]{1,0:T(8,128)S(1)}, u32[]{:S(2)}, u32[]{:S(2)}) collective-permute-start(f32[96,384]{1,0:T(8,128)S(1)} %get-tuple-element.91.refs_7_.refs_12_), channel_id=1, source_target_pairs={{0,16},{4,20},{8,24},{12,28},{16,0},{20,4},{24,8},{28,12},{1,17},{... | collective-permute-start | bytes 442376 | tf_op jit(solution)/shard_map/ppermute | solution.py:316
  38.3 0.9 %shard_map.90 = (f32[128,384]{1,0:T(8,128)S(1)}, f32[512,384]{1,0:T(8,128)S(1)}, f32[512,384]{1,0:T(8,128)S(1)}) custom-call(f32[512,384]{1,0:T(8,128)S(1)} %get-tuple-element.86.refs_0_.refs_6_, f32[512,384]{1,0:T(8,128)S(1)} %get-tuple-element.87.refs_1_, bf16[512,512]{1,0:T(8,128)(2,1)S(1)} %get-tuple-element.84.refs_3_.refs_5_.refs_1_.refs_2_.refs_4_, ...), custom_call_target="tpu_custom_call" | custom-call | flops 301989888 | bytes 3145728 | tf_op jit(solution)/shard_map/pallas_call | solution.py:35
  39.1 3.0 %collective-permute-done.11.refs_3_ = f32[96,384]{1,0:T(8,128)S(1)} collective-permute-done((f32[96,384]{1,0:T(8,128)S(1)}, f32[96,384]{1,0:T(8,128)S(1)}, u32[]{:S(2)}, u32[]{:S(2)}) %collective-permute-start.11) | collective-permute-done | bytes 147488 | tf_op jit(solution)/shard_map/ppermute | solution.py:316
  42.2 1.6 %collective-permute-done.12.refs_4_ = f32[96,384]{1,0:T(8,128)S(1)} collective-permute-done((f32[96,384]{1,0:T(8,128)S(1)}, f32[96,384]{1,0:T(8,128)S(1)}, u32[]{:S(2)}, u32[]{:S(2)}) %collective-permute-start.12) | collective-permute-done | bytes 147488 | tf_op jit(solution)/shard_map/ppermute | solution.py:316
  44.1 1.4 %collective-permute-start.14 = (f32[128,128]{1,0:T(8,128)S(1)}, f32[128,128]{1,0:T(8,128)S(1)}, u32[]{:S(2)}, u32[]{:S(2)}) collective-permute-start(f32[128,128]{1,0:T(8,128)S(1)} %get-tuple-element.95.refs_0_.refs_4_), channel_id=1, source_target_pairs={{0,1},{1,0},{2,3},{3,2},{4,5},{5,4},{6,7},{7,6},{8,9},{9,8},{10,11... | collective-permute-start | bytes 196616 | tf_op jit(solution)/shard_map/ppermute | solution.py:353
  45.5 0.7 collective-permute-start.16
  46.2 2.4 %collective-permute-done.14.refs_1_ = f32[128,128]{1,0:T(8,128)S(1)} collective-permute-done((f32[128,128]{1,0:T(8,128)S(1)}, f32[128,128]{1,0:T(8,128)S(1)}, u32[]{:S(2)}, u32[]{:S(2)}) %collective-permute-start.14) | collective-permute-done | bytes 65568 | tf_op jit(solution)/shard_map/ppermute | solution.py:353
  48.9 2.3 %collective-permute-start.15 = (f32[128,128]{1,0:T(8,128)S(1)}, f32[128,128]{1,0:T(8,128)S(1)}, u32[]{:S(2)}, u32[]{:S(2)}) collective-permute-start(f32[128,128]{1,0:T(8,128)S(1)} %get-tuple-element.97.refs_4_), channel_id=1, source_target_pairs={{0,3},{3,0},{1,2},{2,1},{4,7},{7,4},{5,6},{6,5},{8,11},{11,8},{9,1... | collective-permute-start | bytes 196616 | tf_op jit(solution)/shard_map/ppermute | solution.py:361
  51.4 1.9 %collective-permute-start.17 = (f32[128,256]{1,0:T(8,128)S(1)}, f32[128,256]{1,0:T(8,128)S(1)}, u32[]{:S(2)}, u32[]{:S(2)}) collective-permute-start(f32[128,256]{1,0:T(8,128)S(1)} %get-tuple-element.100.refs_6_), channel_id=1, source_target_pairs={{0,3},{3,0},{1,2},{2,1},{4,7},{7,4},{5,6},{6,5},{8,11},{11,8},{9,1... | collective-permute-start | bytes 393224 | tf_op jit(solution)/shard_map/ppermute | solution.py:361
  53.3 1.0 %shard_map.94.refs_2_.refs_5_ = f32[512,384]{1,0:T(8,128)S(1)} custom-call(f32[512,384]{1,0:T(8,128)S(1)} %get-tuple-element.98.refs_0_, bf16[512,512]{1,0:T(8,128)(2,1)S(1)} %get-tuple-element.78.refs_1_.refs_6_, bf16[512,512]{1,0:T(8,128)(2,1)S(1)} %get-tuple-element.79.refs_2_, f32[96,384]{1,0:T(8,128)S(1)} %collective-permute-done.11.refs_3_, ...), custom_call_target="tpu_custom_call" | custom-call | flops 9663676416 | bytes 37748736 | tf_op jit(solution)/shard_map/pallas_call | solution.py:35
  54.3 0.9 %collective-permute-done.15.refs_1_ = f32[128,128]{1,0:T(8,128)S(1)} collective-permute-done((f32[128,128]{1,0:T(8,128)S(1)}, f32[128,128]{1,0:T(8,128)S(1)}, u32[]{:S(2)}, u32[]{:S(2)}) %collective-permute-start.15) | collective-permute-done | bytes 65568 | tf_op jit(solution)/shard_map/ppermute | solution.py:361
  55.4 2.9 %collective-permute-done.17.refs_1_ = f32[128,256]{1,0:T(8,128)S(1)} collective-permute-done((f32[128,256]{1,0:T(8,128)S(1)}, f32[128,256]{1,0:T(8,128)S(1)}, u32[]{:S(2)}, u32[]{:S(2)}) %collective-permute-start.17) | collective-permute-done | bytes 131104 | tf_op jit(solution)/shard_map/ppermute | solution.py:361
  58.7 1.0 %collective-permute-start.18 = (f32[96,384]{1,0:T(8,128)S(1)}, f32[96,384]{1,0:T(8,128)S(1)}, u32[]{:S(2)}, u32[]{:S(2)}) collective-permute-start(f32[96,384]{1,0:T(8,128)S(1)} %get-tuple-element.106), channel_id=1, source_target_pairs={{0,16},{4,20},{8,24},{12,28},{16,0},{20,4},{24,8},{28,12},{1,17},{... | collective-permute-start | bytes 442376 | tf_op jit(solution)/shard_map/ppermute | solution.py:316
  59.8 0.8 %collective-permute-start.20 = (f32[96,384]{1,0:T(8,128)S(1)}, f32[96,384]{1,0:T(8,128)S(1)}, u32[]{:S(2)}, u32[]{:S(2)}) collective-permute-start(f32[96,384]{1,0:T(8,128)S(1)} %get-tuple-element.108), channel_id=1, source_target_pairs={{0,4},{4,0},{8,12},{12,8},{16,20},{20,16},{24,28},{28,24},{1,5},{5... | collective-permute-start | bytes 442376 | tf_op jit(solution)/shard_map/ppermute | solution.py:316
  60.5 1.0 %shard_map.97 = (f32[512,384]{1,0:T(8,128)S(1)}, f32[512,384]{1,0:T(8,128)S(1)}) custom-call(f32[512,128]{1,0:T(8,128)S(1)} %shard_map.95.refs_5_.refs_6_.refs_0_, f32[512,256]{1,0:T(8,128)S(1)} %get-tuple-element.102.refs_1_.refs_6_, f32[512,384]{1,0:T(8,128)S(1)} %get-tuple-element.103.refs_2_, f32[512,384]{1,0:T(8,128)S(1)} %get-tuple-element.75.refs_0_.refs_2_.refs_3_, ...), custom_call_target="tpu_custom_call" | custom-call | flops 603979776 | bytes 3145728 | tf_op jit(solution)/shard_map/pallas_call | solution.py:35
  61.5 2.7 %collective-permute-done.18.refs_3_.refs_4_ = f32[96,384]{1,0:T(8,128)S(1)} collective-permute-done((f32[96,384]{1,0:T(8,128)S(1)}, f32[96,384]{1,0:T(8,128)S(1)}, u32[]{:S(2)}, u32[]{:S(2)}) %collective-permute-start.18) | collective-permute-done | bytes 147488 | tf_op jit(solution)/shard_map/ppermute | solution.py:316
  64.3 1.7 %collective-permute-done.19.refs_4_.refs_5_ = f32[96,384]{1,0:T(8,128)S(1)} collective-permute-done((f32[96,384]{1,0:T(8,128)S(1)}, f32[96,384]{1,0:T(8,128)S(1)}, u32[]{:S(2)}, u32[]{:S(2)}) %collective-permute-start.19) | collective-permute-done | bytes 147488 | tf_op jit(solution)/shard_map/ppermute | solution.py:316
  66.0 0.8 %shard_map.98 = (f32[96,384]{1,0:T(8,128)S(1)}, f32[96,384]{1,0:T(8,128)S(1)}, f32[96,384]{1,0:T(8,128)S(1)}) custom-call(f32[512,384]{1,0:T(8,128)S(1)} %get-tuple-element.104.refs_0_.refs_6_, bf16[512,512]{1,0:T(8,128)(2,1)S(1)} %get-tuple-element.84.refs_3_.refs_5_.refs_1_.refs_2_.refs_4_, ...), custom_call_target="tpu_custom_call" | custom-call | flops 201326592 | bytes 2359296 | tf_op jit(solution)/shard_map/pallas_call | solution.py:35
  66.7 0.7 collective-permute-start.21
  67.4 0.7 collective-permute-start.22
  68.1 0.4 collective-permute-start.23
  68.5 0.5 shard_map.99
  69.0 1.6 %shard_map.100 = (f32[512,384]{1,0:T(8,128)S(1)}, f32[512,384]{1,0:T(8,128)}) custom-call(bf16[512,512]{1,0:T(8,128)(2,1)S(1)} %get-tuple-element.61.refs_1_.refs_0_, f32[512,384]{1,0:T(8,128)S(1)} %get-tuple-element.112.refs_1_, f32[512,384]{1,0:T(8,128)S(1)} %get-tuple-element.113.refs_2_.refs_3_, f32[512,384]{1,0:T(8,128)S(1)} %get-tuple-element.113.refs_2_.refs_3_), custom_call_target="tpu_custom_call" | custom-call | flops 805306368 | bytes 1966080 | tf_op jit(solution)/shard_map/pallas_call | solution.py:35
  70.6 2.1 %collective-permute-done.21.refs_2_ = f32[96,384]{1,0:T(8,128)S(1)} collective-permute-done((f32[96,384]{1,0:T(8,128)S(1)}, f32[96,384]{1,0:T(8,128)S(1)}, u32[]{:S(2)}, u32[]{:S(2)}) %collective-permute-start.21) | collective-permute-done | bytes 147488 | tf_op jit(solution)/shard_map/ppermute | solution.py:316
  72.7 0.8 %collective-permute-done.22.refs_3_ = f32[96,384]{1,0:T(8,128)S(1)} collective-permute-done((f32[96,384]{1,0:T(8,128)S(1)}, f32[96,384]{1,0:T(8,128)S(1)}, u32[]{:S(2)}, u32[]{:S(2)}) %collective-permute-start.22) | collective-permute-done | bytes 147488 | tf_op jit(solution)/shard_map/ppermute | solution.py:316
  73.5 1.5 %shard_map.101 = f32[512,384]{1,0:T(8,128)} custom-call(bf16[512,512]{1,0:T(8,128)(2,1)S(1)} %get-tuple-element.61.refs_1_.refs_0_, f32[512,384]{1,0:T(8,128)S(1)} %get-tuple-element.115.refs_1_.refs_5_, f32[96,384]{1,0:T(8,128)S(1)} %collective-permute-done.21.refs_2_, f32[96,384]{1,0:T(8,128)S(1)} %collective-permute-done.22.refs_3_, ...), custom_call_target="tpu_custom_call" | custom-call | flops 402653184 | bytes 1966080 | tf_op jit(solution)/shard_map/pallas_call | solution.py:35
  (33 shorter events, 3.6 us)
Async XLA Ops:
  0.6 8.0 %copy-start = (f32[1,1,512,128]{3,2,1,0:T(8,128)S(1)}, f32[1,1,512,128]{3,2,1,0:T(8,128)}, u32[]{:S(2)}) copy-start(f32[1,1,512,128]{3,2,1,0:T(8,128)} %param.9) | copy-start | bytes 786436
  2.4 9.0 %collective-permute-start = (f32[96,384]{1,0:T(8,128)S(1)}, f32[96,384]{1,0:T(8,128)S(1)}, u32[]{:S(2)}, u32[]{:S(2)}) collective-permute-start(f32[96,384]{1,0:T(8,128)S(1)} %get-tuple-element.65), channel_id=1, source_target_pairs={{0,16},{4,20},{8,24},{12,28},{16,0},{20,4},{24,8},{28,12},{1,17},{... | collective-permute-start | bytes 442376 | tf_op jit(solution)/shard_map/ppermute | solution.py:316
  5.4 6.1 %collective-permute-start.1 = (f32[96,384]{1,0:T(8,128)S(1)}, f32[96,384]{1,0:T(8,128)S(1)}, u32[]{:S(2)}, u32[]{:S(2)}) collective-permute-start(f32[96,384]{1,0:T(8,128)S(1)} %get-tuple-element.66), channel_id=1, source_target_pairs={{0,28},{4,8},{8,4},{12,16},{16,12},{20,24},{24,20},{28,0},{1,29},{... | collective-permute-start | bytes 442376 | tf_op jit(solution)/shard_map/ppermute | solution.py:316
  6.0 5.5 %collective-permute-start.2 = (f32[96,384]{1,0:T(8,128)S(1)}, f32[96,384]{1,0:T(8,128)S(1)}, u32[]{:S(2)}, u32[]{:S(2)}) collective-permute-start(f32[96,384]{1,0:T(8,128)S(1)} %get-tuple-element.67), channel_id=1, source_target_pairs={{0,4},{4,0},{8,12},{12,8},{16,20},{20,16},{24,28},{28,24},{1,5},{5... | collective-permute-start | bytes 442376 | tf_op jit(solution)/shard_map/ppermute | solution.py:316
  7.0 4.3 %collective-permute-start.3 = (f32[128,128]{1,0:T(8,128)S(1)}, f32[128,128]{1,0:T(8,128)S(1)}, u32[]{:S(2)}, u32[]{:S(2)}) collective-permute-start(f32[128,128]{1,0:T(8,128)S(1)} %get-tuple-element.68), channel_id=1, source_target_pairs={{0,1},{1,0},{2,3},{3,2},{4,5},{5,4},{6,7},{7,6},{8,9},{9,8},{10,11... | collective-permute-start | bytes 196616 | tf_op jit(solution)/shard_map/ppermute | solution.py:337
  8.6 2.7 %copy-start.1 = (f32[1,512,128]{2,1,0:T(8,128)S(1)}, f32[1,512,128]{2,1,0:T(8,128)}, u32[]{:S(2)}) copy-start(f32[1,512,128]{2,1,0:T(8,128)} %param.10) | copy-start | bytes 786436
  11.9 4.7 %collective-permute-start.4 = (f32[128,128]{1,0:T(8,128)S(1)}, f32[128,128]{1,0:T(8,128)S(1)}, u32[]{:S(2)}, u32[]{:S(2)}) collective-permute-start(f32[128,128]{1,0:T(8,128)S(1)} %get-tuple-element.71.refs_0_.refs_4_), channel_id=1, source_target_pairs={{0,1},{1,0},{2,3},{3,2},{4,5},{5,4},{6,7},{7,6},{8,9},{9,8},{10,11... | collective-permute-start | bytes 196616 | tf_op jit(solution)/shard_map/ppermute | solution.py:353
  13.5 7.3 %collective-permute-start.6 = (f32[128,256]{1,0:T(8,128)S(1)}, f32[128,256]{1,0:T(8,128)S(1)}, u32[]{:S(2)}, u32[]{:S(2)}) collective-permute-start(f32[128,256]{1,0:T(8,128)S(1)} %get-tuple-element.76.refs_0_), channel_id=1, source_target_pairs={{0,1},{1,0},{2,3},{3,2},{4,5},{5,4},{6,7},{7,6},{8,9},{9,8},{10,11... | collective-permute-start | bytes 393224 | tf_op jit(solution)/shard_map/ppermute | solution.py:353
  16.9 5.9 %copy-start.2 = (f32[1,1,512,512]{3,2,1,0:T(8,128)S(1)}, f32[1,1,512,512]{3,2,1,0:T(8,128)}, u32[]{:S(2)}) copy-start(f32[1,1,512,512]{3,2,1,0:T(8,128)} %param.8) | copy-start | bytes 3145732
  16.9 8.3 %collective-permute-start.5 = (f32[128,128]{1,0:T(8,128)S(1)}, f32[128,128]{1,0:T(8,128)S(1)}, u32[]{:S(2)}, u32[]{:S(2)}) collective-permute-start(f32[128,128]{1,0:T(8,128)S(1)} %get-tuple-element.74.refs_4_), channel_id=1, source_target_pairs={{0,3},{3,0},{1,2},{2,1},{4,7},{7,4},{5,6},{6,5},{8,11},{11,8},{9,1... | collective-permute-start | bytes 196616 | tf_op jit(solution)/shard_map/ppermute | solution.py:361
  21.1 6.9 %collective-permute-start.7 = (f32[128,256]{1,0:T(8,128)S(1)}, f32[128,256]{1,0:T(8,128)S(1)}, u32[]{:S(2)}, u32[]{:S(2)}) collective-permute-start(f32[128,256]{1,0:T(8,128)S(1)} %get-tuple-element.77.refs_2_), channel_id=1, source_target_pairs={{0,3},{3,0},{1,2},{2,1},{4,7},{7,4},{5,6},{6,5},{8,11},{11,8},{9,1... | collective-permute-start | bytes 393224 | tf_op jit(solution)/shard_map/ppermute | solution.py:361
  25.4 5.8 %copy-start.3 = (f32[1,1,512,512]{3,2,1,0:T(8,128)S(1)}, f32[1,1,512,512]{3,2,1,0:T(8,128)}, u32[]{:S(2)}) copy-start(f32[1,1,512,512]{3,2,1,0:T(8,128)} %param.7) | copy-start | bytes 3145732
  28.4 5.7 %collective-permute-start.8 = (f32[96,384]{1,0:T(8,128)S(1)}, f32[96,384]{1,0:T(8,128)S(1)}, u32[]{:S(2)}, u32[]{:S(2)}) collective-permute-start(f32[96,384]{1,0:T(8,128)S(1)} %get-tuple-element.88), channel_id=1, source_target_pairs={{0,16},{4,20},{8,24},{12,28},{16,0},{20,4},{24,8},{28,12},{1,17},{... | collective-permute-start | bytes 442376 | tf_op jit(solution)/shard_map/ppermute | solution.py:316
  29.3 6.5 %collective-permute-start.9 = (f32[96,384]{1,0:T(8,128)S(1)}, f32[96,384]{1,0:T(8,128)S(1)}, u32[]{:S(2)}, u32[]{:S(2)}) collective-permute-start(f32[96,384]{1,0:T(8,128)S(1)} %get-tuple-element.89), channel_id=1, source_target_pairs={{0,28},{4,8},{8,4},{12,16},{16,12},{20,24},{24,20},{28,0},{1,29},{... | collective-permute-start | bytes 442376 | tf_op jit(solution)/shard_map/ppermute | solution.py:316
  29.3 6.5 %collective-permute-start.10 = (f32[96,384]{1,0:T(8,128)S(1)}, f32[96,384]{1,0:T(8,128)S(1)}, u32[]{:S(2)}, u32[]{:S(2)}) collective-permute-start(f32[96,384]{1,0:T(8,128)S(1)} %get-tuple-element.90), channel_id=1, source_target_pairs={{0,4},{4,0},{8,12},{12,8},{16,20},{20,16},{24,28},{28,24},{1,5},{5... | collective-permute-start | bytes 442376 | tf_op jit(solution)/shard_map/ppermute | solution.py:316
  36.4 5.7 %collective-permute-start.11 = (f32[96,384]{1,0:T(8,128)S(1)}, f32[96,384]{1,0:T(8,128)S(1)}, u32[]{:S(2)}, u32[]{:S(2)}) collective-permute-start(f32[96,384]{1,0:T(8,128)S(1)} %get-tuple-element.91.refs_7_.refs_12_), channel_id=1, source_target_pairs={{0,16},{4,20},{8,24},{12,28},{16,0},{20,4},{24,8},{28,12},{1,17},{... | collective-permute-start | bytes 442376 | tf_op jit(solution)/shard_map/ppermute | solution.py:316
  37.9 5.9 %collective-permute-start.12 = (f32[96,384]{1,0:T(8,128)S(1)}, f32[96,384]{1,0:T(8,128)S(1)}, u32[]{:S(2)}, u32[]{:S(2)}) collective-permute-start(f32[96,384]{1,0:T(8,128)S(1)} %get-tuple-element.92.refs_8_), channel_id=1, source_target_pairs={{0,28},{4,8},{8,4},{12,16},{16,12},{20,24},{24,20},{28,0},{1,29},{... | collective-permute-start | bytes 442376 | tf_op jit(solution)/shard_map/ppermute | solution.py:316
  37.9 5.9 %collective-permute-start.13 = (f32[96,384]{1,0:T(8,128)S(1)}, f32[96,384]{1,0:T(8,128)S(1)}, u32[]{:S(2)}, u32[]{:S(2)}) collective-permute-start(f32[96,384]{1,0:T(8,128)S(1)} %get-tuple-element.93.refs_9_), channel_id=1, source_target_pairs={{0,4},{4,0},{8,12},{12,8},{16,20},{20,16},{24,28},{28,24},{1,5},{5... | collective-permute-start | bytes 442376 | tf_op jit(solution)/shard_map/ppermute | solution.py:316
  44.1 4.5 %collective-permute-start.14 = (f32[128,128]{1,0:T(8,128)S(1)}, f32[128,128]{1,0:T(8,128)S(1)}, u32[]{:S(2)}, u32[]{:S(2)}) collective-permute-start(f32[128,128]{1,0:T(8,128)S(1)} %get-tuple-element.95.refs_0_.refs_4_), channel_id=1, source_target_pairs={{0,1},{1,0},{2,3},{3,2},{4,5},{5,4},{6,7},{7,6},{8,9},{9,8},{10,11... | collective-permute-start | bytes 196616 | tf_op jit(solution)/shard_map/ppermute | solution.py:353
  45.5 5.7 %collective-permute-start.16 = (f32[128,256]{1,0:T(8,128)S(1)}, f32[128,256]{1,0:T(8,128)S(1)}, u32[]{:S(2)}, u32[]{:S(2)}) collective-permute-start(f32[128,256]{1,0:T(8,128)S(1)} %get-tuple-element.99.refs_0_), channel_id=1, source_target_pairs={{0,1},{1,0},{2,3},{3,2},{4,5},{5,4},{6,7},{7,6},{8,9},{9,8},{10,11... | collective-permute-start | bytes 393224 | tf_op jit(solution)/shard_map/ppermute | solution.py:353
  48.9 6.3 %collective-permute-start.15 = (f32[128,128]{1,0:T(8,128)S(1)}, f32[128,128]{1,0:T(8,128)S(1)}, u32[]{:S(2)}, u32[]{:S(2)}) collective-permute-start(f32[128,128]{1,0:T(8,128)S(1)} %get-tuple-element.97.refs_4_), channel_id=1, source_target_pairs={{0,3},{3,0},{1,2},{2,1},{4,7},{7,4},{5,6},{6,5},{8,11},{11,8},{9,1... | collective-permute-start | bytes 196616 | tf_op jit(solution)/shard_map/ppermute | solution.py:361
  51.4 6.9 %collective-permute-start.17 = (f32[128,256]{1,0:T(8,128)S(1)}, f32[128,256]{1,0:T(8,128)S(1)}, u32[]{:S(2)}, u32[]{:S(2)}) collective-permute-start(f32[128,256]{1,0:T(8,128)S(1)} %get-tuple-element.100.refs_6_), channel_id=1, source_target_pairs={{0,3},{3,0},{1,2},{2,1},{4,7},{7,4},{5,6},{6,5},{8,11},{11,8},{9,1... | collective-permute-start | bytes 393224 | tf_op jit(solution)/shard_map/ppermute | solution.py:361
  58.7 5.5 %collective-permute-start.18 = (f32[96,384]{1,0:T(8,128)S(1)}, f32[96,384]{1,0:T(8,128)S(1)}, u32[]{:S(2)}, u32[]{:S(2)}) collective-permute-start(f32[96,384]{1,0:T(8,128)S(1)} %get-tuple-element.106), channel_id=1, source_target_pairs={{0,16},{4,20},{8,24},{12,28},{16,0},{20,4},{24,8},{28,12},{1,17},{... | collective-permute-start | bytes 442376 | tf_op jit(solution)/shard_map/ppermute | solution.py:316
  59.8 6.2 %collective-permute-start.19 = (f32[96,384]{1,0:T(8,128)S(1)}, f32[96,384]{1,0:T(8,128)S(1)}, u32[]{:S(2)}, u32[]{:S(2)}) collective-permute-start(f32[96,384]{1,0:T(8,128)S(1)} %get-tuple-element.107), channel_id=1, source_target_pairs={{0,28},{4,8},{8,4},{12,16},{16,12},{20,24},{24,20},{28,0},{1,29},{... | collective-permute-start | bytes 442376 | tf_op jit(solution)/shard_map/ppermute | solution.py:316
  59.8 6.2 %collective-permute-start.20 = (f32[96,384]{1,0:T(8,128)S(1)}, f32[96,384]{1,0:T(8,128)S(1)}, u32[]{:S(2)}, u32[]{:S(2)}) collective-permute-start(f32[96,384]{1,0:T(8,128)S(1)} %get-tuple-element.108), channel_id=1, source_target_pairs={{0,4},{4,0},{8,12},{12,8},{16,20},{20,16},{24,28},{28,24},{1,5},{5... | collective-permute-start | bytes 442376 | tf_op jit(solution)/shard_map/ppermute | solution.py:316
  66.7 6.0 %collective-permute-start.21 = (f32[96,384]{1,0:T(8,128)S(1)}, f32[96,384]{1,0:T(8,128)S(1)}, u32[]{:S(2)}, u32[]{:S(2)}) collective-permute-start(f32[96,384]{1,0:T(8,128)S(1)} %get-tuple-element.109.refs_7_.refs_10_), channel_id=1, source_target_pairs={{0,16},{4,20},{8,24},{12,28},{16,0},{20,4},{24,8},{28,12},{1,17},{... | collective-permute-start | bytes 442376 | tf_op jit(solution)/shard_map/ppermute | solution.py:316
  67.4 6.1 %collective-permute-start.22 = (f32[96,384]{1,0:T(8,128)S(1)}, f32[96,384]{1,0:T(8,128)S(1)}, u32[]{:S(2)}, u32[]{:S(2)}) collective-permute-start(f32[96,384]{1,0:T(8,128)S(1)} %get-tuple-element.110.refs_8_), channel_id=1, source_target_pairs={{0,28},{4,8},{8,4},{12,16},{16,12},{20,24},{24,20},{28,0},{1,29},{... | collective-permute-start | bytes 442376 | tf_op jit(solution)/shard_map/ppermute | solution.py:316
  68.1 5.4 %collective-permute-start.23 = (f32[96,384]{1,0:T(8,128)S(1)}, f32[96,384]{1,0:T(8,128)S(1)}, u32[]{:S(2)}, u32[]{:S(2)}) collective-permute-start(f32[96,384]{1,0:T(8,128)S(1)} %get-tuple-element.111.refs_9_), channel_id=1, source_target_pairs={{0,4},{4,0},{8,12},{12,8},{16,20},{20,16},{24,28},{28,24},{1,5},{5... | collective-permute-start | bytes 442376 | tf_op jit(solution)/shard_map/ppermute | solution.py:316

commit v5 on v4

--- a/solution.py
+++ b/solution.py
@@ -341,7 +341,6 @@
         + [((modes, loads), f32), whole(loads)],
         4 * rows * size, 24 * size, one_hot, load_near, basis,
     )
-    mixers = run(blend_body, [((2 * modes, 2 * modes), bf16)] * 2, size, size, columns, other)
     value, iterate = ordered, None
     for iteration in range(ITERS):
         first, last = iteration == 0, iteration == ITERS - 1
@@ -351,6 +350,8 @@
             ahead, test_high, test_low, *arrived,
         )
         theirs = [lax.ppermute(piece, "grp", pair_plan) for piece in own]
+        if first:
+            mixers = run(blend_body, [((2 * modes, 2 * modes), bf16)] * 2, size, size, columns, other)
         kept, came = [], []
         for place, width in enumerate(PIECES):
             away, keep = run(

time: 75.5 us -> 75.6 us (level)
    ppermute x15, waiting for transfers between devices: 14.5 us -> 16.6 us  [exchange(): return [lax.ppermute(part, 'sub', plan) for part, plan in zip(parts, plans)]]
    ppermute x1, waiting for transfers between devices: 1.12 us -> 0.01 us  [local(): other = lax.ppermute(sent, 'grp', pair_plan)]
  transfers between devices with their start and end apart: 24 -> 24, of which waited for: 15 -> 14; matrix products, arithmetic and copies ran while one was open for 0% -> 0% of each run, Pallas kernels for 17% -> 17%
where the time goes in v5:
time: 75.6 us; the launch traced here: 75.2 us
  starting transfers between devices  27.8 us (37%)
  waiting for transfers between devices  27.7 us (37%)
  Pallas kernels  18.7 us (25%)
  between operations  1.01 us (1%)
    pallas_call x25, Pallas kernels, __call__(): pl.pallas_call(whole_body, out_shape=[jax.ShapeDtypeStruct(shape, kind) f...  18.7 us
    ppermute x15, waiting for transfers between devices, exchange(): return [lax.ppermute(part, 'sub', plan) for part, plan in zip(parts, plans)]  16.6 us
    ppermute x15, starting transfers between devices, exchange(): return [lax.ppermute(part, 'sub', plan) for part, plan in zip(parts, plans)]  12.4 us
    ppermute x4, starting transfers between devices, local(): came.append(lax.ppermute(away, 'grp', mirror_plan))  9.59 us
    ppermute x4, waiting for transfers between devices, local(): came.append(lax.ppermute(away, 'grp', mirror_plan))  6.12 us
    ppermute x4, waiting for transfers between devices, local(): theirs = [lax.ppermute(piece, 'grp', pair_plan) for piece in own]  4.98 us
    ppermute x4, starting transfers between devices, local(): theirs = [lax.ppermute(piece, 'grp', pair_plan) for piece in own]  4.18 us
    ppermute x1, starting transfers between devices, local(): other = lax.ppermute(sent, 'grp', pair_plan)  1.58 us
  transfers between devices with their start and end apart: 24, of which 14 were waited for; matrix products, arithmetic and copies ran while one was open for 0% of the time, Pallas kernels for 17%

profile of v5, /device:TPU:0, one launch (start us, length us, event | category | flops | bytes accessed | tf_op | source)
XLA Modules:
  0.0 75.2 jit_solution(9196169146644549161)
XLA Ops:
  0.6 1.7 %shard_map.77 = (bf16[384,512]{1,0:T(8,128)(2,1)S(1)}, f32[512,384]{1,0:T(8,128)S(1)}, f32[128,128]{1,0:T(8,128)S(1)}, f32[96,384]{1,0:T(8,128)S(1)}, f32[96,384]{1,0:T(8,128)S(1)}, /*index=5*/f32[96,384]{1,0:T(8,128)S(1)}) custom-call(s32[4,96]{1,0:T(4,128)} %bitcast.15, f32[512,384]{1,0:T(8,128)} %bitcast.14, f32[512,128]{1,0:T(8,128)} %bitcast.9), custom_call_target="tpu_custom_call" | custom-call | flops 301989888 | bytes 3145728 | tf_op jit(solution)/shard_map/pallas_call | solution.py:35
  2.4 3.0 %collective-permute-start = (f32[96,384]{1,0:T(8,128)S(1)}, f32[96,384]{1,0:T(8,128)S(1)}, u32[]{:S(2)}, u32[]{:S(2)}) collective-permute-start(f32[96,384]{1,0:T(8,128)S(1)} %get-tuple-element.65), channel_id=1, source_target_pairs={{0,16},{4,20},{8,24},{12,28},{16,0},{20,4},{24,8},{28,12},{1,17},{... | collective-permute-start | bytes 442376 | tf_op jit(solution)/shard_map/ppermute | solution.py:316
  5.4 0.6 collective-permute-start.1
  6.0 1.0 %collective-permute-start.2 = (f32[96,384]{1,0:T(8,128)S(1)}, f32[96,384]{1,0:T(8,128)S(1)}, u32[]{:S(2)}, u32[]{:S(2)}) collective-permute-start(f32[96,384]{1,0:T(8,128)S(1)} %get-tuple-element.67), channel_id=1, source_target_pairs={{0,4},{4,0},{8,12},{12,8},{16,20},{20,16},{24,28},{28,24},{1,5},{5... | collective-permute-start | bytes 442376 | tf_op jit(solution)/shard_map/ppermute | solution.py:316
  7.0 1.6 %collective-permute-start.4 = (f32[128,128]{1,0:T(8,128)S(1)}, f32[128,128]{1,0:T(8,128)S(1)}, u32[]{:S(2)}, u32[]{:S(2)}) collective-permute-start(f32[128,128]{1,0:T(8,128)S(1)} %get-tuple-element.70), channel_id=1, source_target_pairs={{0,1},{1,0},{2,3},{3,2},{4,5},{5,4},{6,7},{7,6},{8,9},{9,8},{10,11... | collective-permute-start | bytes 196616 | tf_op jit(solution)/shard_map/ppermute | solution.py:337
  8.6 1.6 %shard_map.78 = (bf16[512,512]{1,0:T(8,128)(2,1)S(1)}, bf16[512,512]{1,0:T(8,128)(2,1)S(1)}, bf16[512,128]{1,0:T(8,128)(2,1)S(1)}, bf16[512,128]{1,0:T(8,128)(2,...) custom-call(bf16[384,512]{1,0:T(8,128)(2,1)S(1)} %get-tuple-element., ...), custom_call_target="tpu_custom_call" | custom-call | flops 402653184 | bytes 4718592 | tf_op jit(solution)/shard_map/pallas_call | solution.py:35
  10.2 1.4 %collective-permute-done.1.refs_4_ = f32[96,384]{1,0:T(8,128)S(1)} collective-permute-done((f32[96,384]{1,0:T(8,128)S(1)}, f32[96,384]{1,0:T(8,128)S(1)}, u32[]{:S(2)}, u32[]{:S(2)}) %collective-permute-start.1) | collective-permute-done | bytes 147488 | tf_op jit(solution)/shard_map/ppermute | solution.py:316
  11.5 0.4 shard_map.79
  11.9 1.6 %collective-permute-start.3 = (f32[128,128]{1,0:T(8,128)S(1)}, f32[128,128]{1,0:T(8,128)S(1)}, u32[]{:S(2)}, u32[]{:S(2)}) collective-permute-start(f32[128,128]{1,0:T(8,128)S(1)} %get-tuple-element.69.refs_2_.refs_0_), channel_id=1, source_target_pairs={{0,1},{1,0},{2,3},{3,2},{4,5},{5,4},{6,7},{7,6},{8,9},{9,8},{10,11... | collective-permute-start | bytes 196616 | tf_op jit(solution)/shard_map/ppermute | solution.py:352
  13.5 0.5 collective-permute-start.6
  14.1 2.5 %collective-permute-done.3.refs_1_ = f32[128,128]{1,0:T(8,128)S(1)} collective-permute-done((f32[128,128]{1,0:T(8,128)S(1)}, f32[128,128]{1,0:T(8,128)S(1)}, u32[]{:S(2)}, u32[]{:S(2)}) %collective-permute-start.3) | collective-permute-done | bytes 65568 | tf_op jit(solution)/shard_map/ppermute | solution.py:352
  16.9 3.9 %collective-permute-start.5 = (f32[128,128]{1,0:T(8,128)S(1)}, f32[128,128]{1,0:T(8,128)S(1)}, u32[]{:S(2)}, u32[]{:S(2)}) collective-permute-start(f32[128,128]{1,0:T(8,128)S(1)} %get-tuple-element.74.refs_4_), channel_id=1, source_target_pairs={{0,3},{3,0},{1,2},{2,1},{4,7},{7,4},{5,6},{6,5},{8,11},{11,8},{9,1... | collective-permute-start | bytes 196616 | tf_op jit(solution)/shard_map/ppermute | solution.py:362
  21.1 1.7 %collective-permute-start.7 = (f32[128,256]{1,0:T(8,128)S(1)}, f32[128,256]{1,0:T(8,128)S(1)}, u32[]{:S(2)}, u32[]{:S(2)}) collective-permute-start(f32[128,256]{1,0:T(8,128)S(1)} %get-tuple-element.77.refs_2_), channel_id=1, source_target_pairs={{0,3},{3,0},{1,2},{2,1},{4,7},{7,4},{5,6},{6,5},{8,11},{11,8},{9,1... | collective-permute-start | bytes 393224 | tf_op jit(solution)/shard_map/ppermute | solution.py:362
  22.8 1.3 %shard_map.83 = (bf16[512,512]{1,0:T(8,128)(2,1)S(1)}, bf16[512,512]{1,0:T(8,128)(2,1)S(1)}) custom-call(bf16[512,512]{1,0:T(8,128)(2,1)S(1)} %get-tuple-element.68.refs_6_.refs_0_, f32[512,512]{1,0:T(8,128)S(1)} %bitcast.11, f32[128,256]{1,0:T(8,128)S(1)} %get-tuple-element.77.refs_2_), custom_call_target="tpu_custom_call" | custom-call | flops 1073741824 | bytes 2359296 | tf_op jit(solution)/shard_map/pallas_call | solution.py:35
  24.1 1.0 %shard_map.84.refs_2_.refs_5_ = f32[512,384]{1,0:T(8,128)S(1)} custom-call(f32[512,384]{1,0:T(8,128)S(1)} %get-tuple-element.75.refs_0_.refs_2_.refs_3_, bf16[512,512]{1,0:T(8,128)(2,1)S(1)} %get-tuple-element.78.refs_1_.refs_6_, bf16[512,512]{1,0:T(8,128)(2,1)S(1)} %get-tuple-element.79.refs_2_, f32[96,384]{1,0:T(8,128)S(1)} %collective-permute-done.refs_3_, ...), custom_call_target="tpu_custom_call" | custom-call | flops 9663676416 | bytes 37748736 | tf_op jit(solution)/shard_map/pallas_call | solution.py:35
  25.4 2.6 %collective-permute-done.7.refs_1_ = f32[128,256]{1,0:T(8,128)S(1)} collective-permute-done((f32[128,256]{1,0:T(8,128)S(1)}, f32[128,256]{1,0:T(8,128)S(1)}, u32[]{:S(2)}, u32[]{:S(2)}) %collective-permute-start.7) | collective-permute-done | bytes 131104 | tf_op jit(solution)/shard_map/ppermute | solution.py:362
  28.4 0.6 collective-permute-start.8
  29.0 2.2 %collective-permute-start.10 = (f32[96,384]{1,0:T(8,128)S(1)}, f32[96,384]{1,0:T(8,128)S(1)}, u32[]{:S(2)}, u32[]{:S(2)}) collective-permute-start(f32[96,384]{1,0:T(8,128)S(1)} %get-tuple-element.90), channel_id=1, source_target_pairs={{0,4},{4,0},{8,12},{12,8},{16,20},{20,16},{24,28},{28,24},{1,5},{5... | collective-permute-start | bytes 442376 | tf_op jit(solution)/shard_map/ppermute | solution.py:316
  31.2 1.3 %shard_map.87 = (bf16[512,512]{1,0:T(8,128)(2,1)S(1)}, bf16[512,512]{1,0:T(8,128)(2,1)S(1)}) custom-call(bf16[512,512]{1,0:T(8,128)(2,1)S(1)} %get-tuple-element.68.refs_6_.refs_0_, bf16[512,512]{1,0:T(8,128)(2,1)S(1)} %get-tuple-element.61.refs_1_.refs_0_, f32[512,512]{1,0:T(8,128)S(1)} %bitcast.12, f32[512,256]{1,0:T(8,128)S(1)} %get-tuple-element.83.refs_3_.refs_1_), custom_call_target="tpu_custom_call" | custom-call | flops 1073741824 | bytes 2359296 | tf_op jit(solution)/shard_map/pallas_call | solution.py:35
  32.5 1.0 %shard_map.88 = (f32[512,384]{1,0:T(8,128)S(1)}, f32[512,384]{1,0:T(8,128)S(1)}) custom-call(f32[512,128]{1,0:T(8,128)S(1)} %shard_map.85.refs_5_.refs_6_.refs_0_, f32[512,256]{1,0:T(8,128)S(1)} %get-tuple-element.83.refs_3_.refs_1_, f32[512,384]{1,0:T(8,128)S(1)} %get-tuple-element.75.refs_0_.refs_2_.refs_3_, ...), custom_call_target="tpu_custom_call" | custom-call | flops 603979776 | bytes 3145728 | tf_op jit(solution)/shard_map/pallas_call | solution.py:35
  33.5 0.8 %collective-permute-done.8.refs_3_.refs_4_ = f32[96,384]{1,0:T(8,128)S(1)} collective-permute-done((f32[96,384]{1,0:T(8,128)S(1)}, f32[96,384]{1,0:T(8,128)S(1)}, u32[]{:S(2)}, u32[]{:S(2)}) %collective-permute-start.8) | collective-permute-done | bytes 147488 | tf_op jit(solution)/shard_map/ppermute | solution.py:316
  34.3 1.5 %collective-permute-done.9.refs_4_.refs_5_ = f32[96,384]{1,0:T(8,128)S(1)} collective-permute-done((f32[96,384]{1,0:T(8,128)S(1)}, f32[96,384]{1,0:T(8,128)S(1)}, u32[]{:S(2)}, u32[]{:S(2)}) %collective-permute-start.9) | collective-permute-done | bytes 147488 | tf_op jit(solution)/shard_map/ppermute | solution.py:316
  35.8 0.6 shard_map.89
  36.4 1.5 %collective-permute-start.11 = (f32[96,384]{1,0:T(8,128)S(1)}, f32[96,384]{1,0:T(8,128)S(1)}, u32[]{:S(2)}, u32[]{:S(2)}) collective-permute-start(f32[96,384]{1,0:T(8,128)S(1)} %get-tuple-element.91.refs_7_.refs_12_), channel_id=1, source_target_pairs={{0,16},{4,20},{8,24},{12,28},{16,0},{20,4},{24,8},{28,12},{1,17},{... | collective-permute-start | bytes 442376 | tf_op jit(solution)/shard_map/ppermute | solution.py:316
  38.0 0.9 %shard_map.90 = (f32[128,384]{1,0:T(8,128)S(1)}, f32[512,384]{1,0:T(8,128)S(1)}, f32[512,384]{1,0:T(8,128)S(1)}) custom-call(f32[512,384]{1,0:T(8,128)S(1)} %get-tuple-element.86.refs_0_.refs_6_, f32[512,384]{1,0:T(8,128)S(1)} %get-tuple-element.87.refs_1_, bf16[512,512]{1,0:T(8,128)(2,1)S(1)} %get-tuple-element.84.refs_3_.refs_5_.refs_1_.refs_2_.refs_4_, ...), custom_call_target="tpu_custom_call" | custom-call | flops 301989888 | bytes 3145728 | tf_op jit(solution)/shard_map/pallas_call | solution.py:35
  38.9 3.3 %collective-permute-done.11.refs_3_ = f32[96,384]{1,0:T(8,128)S(1)} collective-permute-done((f32[96,384]{1,0:T(8,128)S(1)}, f32[96,384]{1,0:T(8,128)S(1)}, u32[]{:S(2)}, u32[]{:S(2)}) %collective-permute-start.11) | collective-permute-done | bytes 147488 | tf_op jit(solution)/shard_map/ppermute | solution.py:316
  42.2 1.6 %collective-permute-done.12.refs_4_ = f32[96,384]{1,0:T(8,128)S(1)} collective-permute-done((f32[96,384]{1,0:T(8,128)S(1)}, f32[96,384]{1,0:T(8,128)S(1)}, u32[]{:S(2)}, u32[]{:S(2)}) %collective-permute-start.12) | collective-permute-done | bytes 147488 | tf_op jit(solution)/shard_map/ppermute | solution.py:316
  44.1 1.3 %collective-permute-start.14 = (f32[128,128]{1,0:T(8,128)S(1)}, f32[128,128]{1,0:T(8,128)S(1)}, u32[]{:S(2)}, u32[]{:S(2)}) collective-permute-start(f32[128,128]{1,0:T(8,128)S(1)} %get-tuple-element.95.refs_0_.refs_4_), channel_id=1, source_target_pairs={{0,1},{1,0},{2,3},{3,2},{4,5},{5,4},{6,7},{7,6},{8,9},{9,8},{10,11... | collective-permute-start | bytes 196616 | tf_op jit(solution)/shard_map/ppermute | solution.py:352
  45.5 0.8 collective-permute-start.16
  46.2 2.5 %collective-permute-done.14.refs_1_ = f32[128,128]{1,0:T(8,128)S(1)} collective-permute-done((f32[128,128]{1,0:T(8,128)S(1)}, f32[128,128]{1,0:T(8,128)S(1)}, u32[]{:S(2)}, u32[]{:S(2)}) %collective-permute-start.14) | collective-permute-done | bytes 65568 | tf_op jit(solution)/shard_map/ppermute | solution.py:352
  48.9 1.8 %collective-permute-start.15 = (f32[128,128]{1,0:T(8,128)S(1)}, f32[128,128]{1,0:T(8,128)S(1)}, u32[]{:S(2)}, u32[]{:S(2)}) collective-permute-start(f32[128,128]{1,0:T(8,128)S(1)} %get-tuple-element.97.refs_4_), channel_id=1, source_target_pairs={{0,3},{3,0},{1,2},{2,1},{4,7},{7,4},{5,6},{6,5},{8,11},{11,8},{9,1... | collective-permute-start | bytes 196616 | tf_op jit(solution)/shard_map/ppermute | solution.py:362
  51.0 2.2 %collective-permute-start.17 = (f32[128,256]{1,0:T(8,128)S(1)}, f32[128,256]{1,0:T(8,128)S(1)}, u32[]{:S(2)}, u32[]{:S(2)}) collective-permute-start(f32[128,256]{1,0:T(8,128)S(1)} %get-tuple-element.100.refs_6_), channel_id=1, source_target_pairs={{0,3},{3,0},{1,2},{2,1},{4,7},{7,4},{5,6},{6,5},{8,11},{11,8},{9,1... | collective-permute-start | bytes 393224 | tf_op jit(solution)/shard_map/ppermute | solution.py:362
  53.2 1.0 %shard_map.94.refs_2_.refs_5_ = f32[512,384]{1,0:T(8,128)S(1)} custom-call(f32[512,384]{1,0:T(8,128)S(1)} %get-tuple-element.98.refs_0_, bf16[512,512]{1,0:T(8,128)(2,1)S(1)} %get-tuple-element.78.refs_1_.refs_6_, bf16[512,512]{1,0:T(8,128)(2,1)S(1)} %get-tuple-element.79.refs_2_, f32[96,384]{1,0:T(8,128)S(1)} %collective-permute-done.11.refs_3_, ...), custom_call_target="tpu_custom_call" | custom-call | flops 9663676416 | bytes 37748736 | tf_op jit(solution)/shard_map/pallas_call | solution.py:35
  54.2 1.5 %collective-permute-done.15.refs_1_ = f32[128,128]{1,0:T(8,128)S(1)} collective-permute-done((f32[128,128]{1,0:T(8,128)S(1)}, f32[128,128]{1,0:T(8,128)S(1)}, u32[]{:S(2)}, u32[]{:S(2)}) %collective-permute-start.15) | collective-permute-done | bytes 65568 | tf_op jit(solution)/shard_map/ppermute | solution.py:362
  56.0 2.0 %collective-permute-done.17.refs_1_ = f32[128,256]{1,0:T(8,128)S(1)} collective-permute-done((f32[128,256]{1,0:T(8,128)S(1)}, f32[128,256]{1,0:T(8,128)S(1)}, u32[]{:S(2)}, u32[]{:S(2)}) %collective-permute-start.17) | collective-permute-done | bytes 131104 | tf_op jit(solution)/shard_map/ppermute | solution.py:362
  58.3 1.1 %collective-permute-start.18 = (f32[96,384]{1,0:T(8,128)S(1)}, f32[96,384]{1,0:T(8,128)S(1)}, u32[]{:S(2)}, u32[]{:S(2)}) collective-permute-start(f32[96,384]{1,0:T(8,128)S(1)} %get-tuple-element.106), channel_id=1, source_target_pairs={{0,16},{4,20},{8,24},{12,28},{16,0},{20,4},{24,8},{28,12},{1,17},{... | collective-permute-start | bytes 442376 | tf_op jit(solution)/shard_map/ppermute | solution.py:316
  59.5 1.0 %collective-permute-start.20 = (f32[96,384]{1,0:T(8,128)S(1)}, f32[96,384]{1,0:T(8,128)S(1)}, u32[]{:S(2)}, u32[]{:S(2)}) collective-permute-start(f32[96,384]{1,0:T(8,128)S(1)} %get-tuple-element.108), channel_id=1, source_target_pairs={{0,4},{4,0},{8,12},{12,8},{16,20},{20,16},{24,28},{28,24},{1,5},{5... | collective-permute-start | bytes 442376 | tf_op jit(solution)/shard_map/ppermute | solution.py:316
  60.4 1.0 %shard_map.97 = (f32[512,384]{1,0:T(8,128)S(1)}, f32[512,384]{1,0:T(8,128)S(1)}) custom-call(f32[512,128]{1,0:T(8,128)S(1)} %shard_map.95.refs_5_.refs_6_.refs_0_, f32[512,256]{1,0:T(8,128)S(1)} %get-tuple-element.102.refs_1_.refs_6_, f32[512,384]{1,0:T(8,128)S(1)} %get-tuple-element.103.refs_2_, f32[512,384]{1,0:T(8,128)S(1)} %get-tuple-element.75.refs_0_.refs_2_.refs_3_, ...), custom_call_target="tpu_custom_call" | custom-call | flops 603979776 | bytes 3145728 | tf_op jit(solution)/shard_map/pallas_call | solution.py:35
  61.4 2.4 %collective-permute-done.18.refs_3_.refs_4_ = f32[96,384]{1,0:T(8,128)S(1)} collective-permute-done((f32[96,384]{1,0:T(8,128)S(1)}, f32[96,384]{1,0:T(8,128)S(1)}, u32[]{:S(2)}, u32[]{:S(2)}) %collective-permute-start.18) | collective-permute-done | bytes 147488 | tf_op jit(solution)/shard_map/ppermute | solution.py:316
  63.8 2.2 %collective-permute-done.19.refs_4_.refs_5_ = f32[96,384]{1,0:T(8,128)S(1)} collective-permute-done((f32[96,384]{1,0:T(8,128)S(1)}, f32[96,384]{1,0:T(8,128)S(1)}, u32[]{:S(2)}, u32[]{:S(2)}) %collective-permute-start.19) | collective-permute-done | bytes 147488 | tf_op jit(solution)/shard_map/ppermute | solution.py:316
  66.0 0.8 %shard_map.98 = (f32[96,384]{1,0:T(8,128)S(1)}, f32[96,384]{1,0:T(8,128)S(1)}, f32[96,384]{1,0:T(8,128)S(1)}) custom-call(f32[512,384]{1,0:T(8,128)S(1)} %get-tuple-element.104.refs_0_.refs_6_, bf16[512,512]{1,0:T(8,128)(2,1)S(1)} %get-tuple-element.84.refs_3_.refs_5_.refs_1_.refs_2_.refs_4_, ...), custom_call_target="tpu_custom_call" | custom-call | flops 201326592 | bytes 2359296 | tf_op jit(solution)/shard_map/pallas_call | solution.py:35
  66.8 0.5 collective-permute-start.21
  67.3 0.8 %collective-permute-start.23 = (f32[96,384]{1,0:T(8,128)S(1)}, f32[96,384]{1,0:T(8,128)S(1)}, u32[]{:S(2)}, u32[]{:S(2)}) collective-permute-start(f32[96,384]{1,0:T(8,128)S(1)} %get-tuple-element.111.refs_9_), channel_id=1, source_target_pairs={{0,4},{4,0},{8,12},{12,8},{16,20},{20,16},{24,28},{28,24},{1,5},{5... | collective-permute-start | bytes 442376 | tf_op jit(solution)/shard_map/ppermute | solution.py:316
  68.1 0.5 shard_map.99
  68.6 1.6 %shard_map.100 = (f32[512,384]{1,0:T(8,128)S(1)}, f32[512,384]{1,0:T(8,128)}) custom-call(bf16[512,512]{1,0:T(8,128)(2,1)S(1)} %get-tuple-element.61.refs_1_.refs_0_, f32[512,384]{1,0:T(8,128)S(1)} %get-tuple-element.112.refs_1_, f32[512,384]{1,0:T(8,128)S(1)} %get-tuple-element.113.refs_2_.refs_3_, f32[512,384]{1,0:T(8,128)S(1)} %get-tuple-element.113.refs_2_.refs_3_), custom_call_target="tpu_custom_call" | custom-call | flops 805306368 | bytes 1966080 | tf_op jit(solution)/shard_map/pallas_call | solution.py:35
  70.2 2.6 %collective-permute-done.21.refs_2_ = f32[96,384]{1,0:T(8,128)S(1)} collective-permute-done((f32[96,384]{1,0:T(8,128)S(1)}, f32[96,384]{1,0:T(8,128)S(1)}, u32[]{:S(2)}, u32[]{:S(2)}) %collective-permute-start.21) | collective-permute-done | bytes 147488 | tf_op jit(solution)/shard_map/ppermute | solution.py:316
  72.8 0.8 %collective-permute-done.22.refs_3_ = f32[96,384]{1,0:T(8,128)S(1)} collective-permute-done((f32[96,384]{1,0:T(8,128)S(1)}, f32[96,384]{1,0:T(8,128)S(1)}, u32[]{:S(2)}, u32[]{:S(2)}) %collective-permute-start.22) | collective-permute-done | bytes 147488 | tf_op jit(solution)/shard_map/ppermute | solution.py:316
  73.6 1.5 %shard_map.101 = f32[512,384]{1,0:T(8,128)} custom-call(bf16[512,512]{1,0:T(8,128)(2,1)S(1)} %get-tuple-element.61.refs_1_.refs_0_, f32[512,384]{1,0:T(8,128)S(1)} %get-tuple-element.115.refs_1_.refs_5_, f32[96,384]{1,0:T(8,128)S(1)} %collective-permute-done.21.refs_2_, f32[96,384]{1,0:T(8,128)S(1)} %collective-permute-done.22.refs_3_, ...), custom_call_target="tpu_custom_call" | custom-call | flops 402653184 | bytes 1966080 | tf_op jit(solution)/shard_map/pallas_call | solution.py:35
  (33 shorter events, 2.9 us)
Async XLA Ops:
  0.6 8.0 %copy-start = (f32[1,1,512,128]{3,2,1,0:T(8,128)S(1)}, f32[1,1,512,128]{3,2,1,0:T(8,128)}, u32[]{:S(2)}) copy-start(f32[1,1,512,128]{3,2,1,0:T(8,128)} %param.9) | copy-start | bytes 786436
  2.4 7.8 %collective-permute-start = (f32[96,384]{1,0:T(8,128)S(1)}, f32[96,384]{1,0:T(8,128)S(1)}, u32[]{:S(2)}, u32[]{:S(2)}) collective-permute-start(f32[96,384]{1,0:T(8,128)S(1)} %get-tuple-element.65), channel_id=1, source_target_pairs={{0,16},{4,20},{8,24},{12,28},{16,0},{20,4},{24,8},{28,12},{1,17},{... | collective-permute-start | bytes 442376 | tf_op jit(solution)/shard_map/ppermute | solution.py:316
  5.4 6.1 %collective-permute-start.1 = (f32[96,384]{1,0:T(8,128)S(1)}, f32[96,384]{1,0:T(8,128)S(1)}, u32[]{:S(2)}, u32[]{:S(2)}) collective-permute-start(f32[96,384]{1,0:T(8,128)S(1)} %get-tuple-element.66), channel_id=1, source_target_pairs={{0,28},{4,8},{8,4},{12,16},{16,12},{20,24},{24,20},{28,0},{1,29},{... | collective-permute-start | bytes 442376 | tf_op jit(solution)/shard_map/ppermute | solution.py:316
  6.0 5.5 %collective-permute-start.2 = (f32[96,384]{1,0:T(8,128)S(1)}, f32[96,384]{1,0:T(8,128)S(1)}, u32[]{:S(2)}, u32[]{:S(2)}) collective-permute-start(f32[96,384]{1,0:T(8,128)S(1)} %get-tuple-element.67), channel_id=1, source_target_pairs={{0,4},{4,0},{8,12},{12,8},{16,20},{20,16},{24,28},{28,24},{1,5},{5... | collective-permute-start | bytes 442376 | tf_op jit(solution)/shard_map/ppermute | solution.py:316
  7.0 7.0 %collective-permute-start.4 = (f32[128,128]{1,0:T(8,128)S(1)}, f32[128,128]{1,0:T(8,128)S(1)}, u32[]{:S(2)}, u32[]{:S(2)}) collective-permute-start(f32[128,128]{1,0:T(8,128)S(1)} %get-tuple-element.70), channel_id=1, source_target_pairs={{0,1},{1,0},{2,3},{3,2},{4,5},{5,4},{6,7},{7,6},{8,9},{9,8},{10,11... | collective-permute-start | bytes 196616 | tf_op jit(solution)/shard_map/ppermute | solution.py:337
  11.5 2.5 %copy-start.1 = (f32[1,512,128]{2,1,0:T(8,128)S(1)}, f32[1,512,128]{2,1,0:T(8,128)}, u32[]{:S(2)}) copy-start(f32[1,512,128]{2,1,0:T(8,128)} %param.10) | copy-start | bytes 786436
  11.9 4.7 %collective-permute-start.3 = (f32[128,128]{1,0:T(8,128)S(1)}, f32[128,128]{1,0:T(8,128)S(1)}, u32[]{:S(2)}, u32[]{:S(2)}) collective-permute-start(f32[128,128]{1,0:T(8,128)S(1)} %get-tuple-element.69.refs_2_.refs_0_), channel_id=1, source_target_pairs={{0,1},{1,0},{2,3},{3,2},{4,5},{5,4},{6,7},{7,6},{8,9},{9,8},{10,11... | collective-permute-start | bytes 196616 | tf_op jit(solution)/shard_map/ppermute | solution.py:352
  13.5 7.3 %collective-permute-start.6 = (f32[128,256]{1,0:T(8,128)S(1)}, f32[128,256]{1,0:T(8,128)S(1)}, u32[]{:S(2)}, u32[]{:S(2)}) collective-permute-start(f32[128,256]{1,0:T(8,128)S(1)} %get-tuple-element.76.refs_0_), channel_id=1, source_target_pairs={{0,1},{1,0},{2,3},{3,2},{4,5},{5,4},{6,7},{7,6},{8,9},{9,8},{10,11... | collective-permute-start | bytes 393224 | tf_op jit(solution)/shard_map/ppermute | solution.py:352
  16.9 5.9 %copy-start.2 = (f32[1,1,512,512]{3,2,1,0:T(8,128)S(1)}, f32[1,1,512,512]{3,2,1,0:T(8,128)}, u32[]{:S(2)}) copy-start(f32[1,1,512,512]{3,2,1,0:T(8,128)} %param.8) | copy-start | bytes 3145732
  16.9 8.2 %collective-permute-start.5 = (f32[128,128]{1,0:T(8,128)S(1)}, f32[128,128]{1,0:T(8,128)S(1)}, u32[]{:S(2)}, u32[]{:S(2)}) collective-permute-start(f32[128,128]{1,0:T(8,128)S(1)} %get-tuple-element.74.refs_4_), channel_id=1, source_target_pairs={{0,3},{3,0},{1,2},{2,1},{4,7},{7,4},{5,6},{6,5},{8,11},{11,8},{9,1... | collective-permute-start | bytes 196616 | tf_op jit(solution)/shard_map/ppermute | solution.py:362
  21.1 6.9 %collective-permute-start.7 = (f32[128,256]{1,0:T(8,128)S(1)}, f32[128,256]{1,0:T(8,128)S(1)}, u32[]{:S(2)}, u32[]{:S(2)}) collective-permute-start(f32[128,256]{1,0:T(8,128)S(1)} %get-tuple-element.77.refs_2_), channel_id=1, source_target_pairs={{0,3},{3,0},{1,2},{2,1},{4,7},{7,4},{5,6},{6,5},{8,11},{11,8},{9,1... | collective-permute-start | bytes 393224 | tf_op jit(solution)/shard_map/ppermute | solution.py:362
  25.4 5.8 %copy-start.3 = (f32[1,1,512,512]{3,2,1,0:T(8,128)S(1)}, f32[1,1,512,512]{3,2,1,0:T(8,128)}, u32[]{:S(2)}) copy-start(f32[1,1,512,512]{3,2,1,0:T(8,128)} %param.7) | copy-start | bytes 3145732
  28.4 5.9 %collective-permute-start.8 = (f32[96,384]{1,0:T(8,128)S(1)}, f32[96,384]{1,0:T(8,128)S(1)}, u32[]{:S(2)}, u32[]{:S(2)}) collective-permute-start(f32[96,384]{1,0:T(8,128)S(1)} %get-tuple-element.88), channel_id=1, source_target_pairs={{0,16},{4,20},{8,24},{12,28},{16,0},{20,4},{24,8},{28,12},{1,17},{... | collective-permute-start | bytes 442376 | tf_op jit(solution)/shard_map/ppermute | solution.py:316
  29.0 6.8 %collective-permute-start.9 = (f32[96,384]{1,0:T(8,128)S(1)}, f32[96,384]{1,0:T(8,128)S(1)}, u32[]{:S(2)}, u32[]{:S(2)}) collective-permute-start(f32[96,384]{1,0:T(8,128)S(1)} %get-tuple-element.89), channel_id=1, source_target_pairs={{0,28},{4,8},{8,4},{12,16},{16,12},{20,24},{24,20},{28,0},{1,29},{... | collective-permute-start | bytes 442376 | tf_op jit(solution)/shard_map/ppermute | solution.py:316
  29.0 6.8 %collective-permute-start.10 = (f32[96,384]{1,0:T(8,128)S(1)}, f32[96,384]{1,0:T(8,128)S(1)}, u32[]{:S(2)}, u32[]{:S(2)}) collective-permute-start(f32[96,384]{1,0:T(8,128)S(1)} %get-tuple-element.90), channel_id=1, source_target_pairs={{0,4},{4,0},{8,12},{12,8},{16,20},{20,16},{24,28},{28,24},{1,5},{5... | collective-permute-start | bytes 442376 | tf_op jit(solution)/shard_map/ppermute | solution.py:316
  36.4 5.8 %collective-permute-start.11 = (f32[96,384]{1,0:T(8,128)S(1)}, f32[96,384]{1,0:T(8,128)S(1)}, u32[]{:S(2)}, u32[]{:S(2)}) collective-permute-start(f32[96,384]{1,0:T(8,128)S(1)} %get-tuple-element.91.refs_7_.refs_12_), channel_id=1, source_target_pairs={{0,16},{4,20},{8,24},{12,28},{16,0},{20,4},{24,8},{28,12},{1,17},{... | collective-permute-start | bytes 442376 | tf_op jit(solution)/shard_map/ppermute | solution.py:316
  37.9 5.9 %collective-permute-start.12 = (f32[96,384]{1,0:T(8,128)S(1)}, f32[96,384]{1,0:T(8,128)S(1)}, u32[]{:S(2)}, u32[]{:S(2)}) collective-permute-start(f32[96,384]{1,0:T(8,128)S(1)} %get-tuple-element.92.refs_8_), channel_id=1, source_target_pairs={{0,28},{4,8},{8,4},{12,16},{16,12},{20,24},{24,20},{28,0},{1,29},{... | collective-permute-start | bytes 442376 | tf_op jit(solution)/shard_map/ppermute | solution.py:316
  37.9 5.9 %collective-permute-start.13 = (f32[96,384]{1,0:T(8,128)S(1)}, f32[96,384]{1,0:T(8,128)S(1)}, u32[]{:S(2)}, u32[]{:S(2)}) collective-permute-start(f32[96,384]{1,0:T(8,128)S(1)} %get-tuple-element.93.refs_9_), channel_id=1, source_target_pairs={{0,4},{4,0},{8,12},{12,8},{16,20},{20,16},{24,28},{28,24},{1,5},{5... | collective-permute-start | bytes 442376 | tf_op jit(solution)/shard_map/ppermute | solution.py:316
  44.1 4.5 %collective-permute-start.14 = (f32[128,128]{1,0:T(8,128)S(1)}, f32[128,128]{1,0:T(8,128)S(1)}, u32[]{:S(2)}, u32[]{:S(2)}) collective-permute-start(f32[128,128]{1,0:T(8,128)S(1)} %get-tuple-element.95.refs_0_.refs_4_), channel_id=1, source_target_pairs={{0,1},{1,0},{2,3},{3,2},{4,5},{5,4},{6,7},{7,6},{8,9},{9,8},{10,11... | collective-permute-start | bytes 196616 | tf_op jit(solution)/shard_map/ppermute | solution.py:352
  45.5 5.3 %collective-permute-start.16 = (f32[128,256]{1,0:T(8,128)S(1)}, f32[128,256]{1,0:T(8,128)S(1)}, u32[]{:S(2)}, u32[]{:S(2)}) collective-permute-start(f32[128,256]{1,0:T(8,128)S(1)} %get-tuple-element.99.refs_0_), channel_id=1, source_target_pairs={{0,1},{1,0},{2,3},{3,2},{4,5},{5,4},{6,7},{7,6},{8,9},{9,8},{10,11... | collective-permute-start | bytes 393224 | tf_op jit(solution)/shard_map/ppermute | solution.py:352
  48.9 6.8 %collective-permute-start.15 = (f32[128,128]{1,0:T(8,128)S(1)}, f32[128,128]{1,0:T(8,128)S(1)}, u32[]{:S(2)}, u32[]{:S(2)}) collective-permute-start(f32[128,128]{1,0:T(8,128)S(1)} %get-tuple-element.97.refs_4_), channel_id=1, source_target_pairs={{0,3},{3,0},{1,2},{2,1},{4,7},{7,4},{5,6},{6,5},{8,11},{11,8},{9,1... | collective-permute-start | bytes 196616 | tf_op jit(solution)/shard_map/ppermute | solution.py:362
  51.0 6.9 %collective-permute-start.17 = (f32[128,256]{1,0:T(8,128)S(1)}, f32[128,256]{1,0:T(8,128)S(1)}, u32[]{:S(2)}, u32[]{:S(2)}) collective-permute-start(f32[128,256]{1,0:T(8,128)S(1)} %get-tuple-element.100.refs_6_), channel_id=1, source_target_pairs={{0,3},{3,0},{1,2},{2,1},{4,7},{7,4},{5,6},{6,5},{8,11},{11,8},{9,1... | collective-permute-start | bytes 393224 | tf_op jit(solution)/shard_map/ppermute | solution.py:362
  58.3 5.5 %collective-permute-start.18 = (f32[96,384]{1,0:T(8,128)S(1)}, f32[96,384]{1,0:T(8,128)S(1)}, u32[]{:S(2)}, u32[]{:S(2)}) collective-permute-start(f32[96,384]{1,0:T(8,128)S(1)} %get-tuple-element.106), channel_id=1, source_target_pairs={{0,16},{4,20},{8,24},{12,28},{16,0},{20,4},{24,8},{28,12},{1,17},{... | collective-permute-start | bytes 442376 | tf_op jit(solution)/shard_map/ppermute | solution.py:316
  59.5 6.5 %collective-permute-start.19 = (f32[96,384]{1,0:T(8,128)S(1)}, f32[96,384]{1,0:T(8,128)S(1)}, u32[]{:S(2)}, u32[]{:S(2)}) collective-permute-start(f32[96,384]{1,0:T(8,128)S(1)} %get-tuple-element.107), channel_id=1, source_target_pairs={{0,28},{4,8},{8,4},{12,16},{16,12},{20,24},{24,20},{28,0},{1,29},{... | collective-permute-start | bytes 442376 | tf_op jit(solution)/shard_map/ppermute | solution.py:316
  59.5 6.5 %collective-permute-start.20 = (f32[96,384]{1,0:T(8,128)S(1)}, f32[96,384]{1,0:T(8,128)S(1)}, u32[]{:S(2)}, u32[]{:S(2)}) collective-permute-start(f32[96,384]{1,0:T(8,128)S(1)} %get-tuple-element.108), channel_id=1, source_target_pairs={{0,4},{4,0},{8,12},{12,8},{16,20},{20,16},{24,28},{28,24},{1,5},{5... | collective-permute-start | bytes 442376 | tf_op jit(solution)/shard_map/ppermute | solution.py:316
  66.8 6.0 %collective-permute-start.21 = (f32[96,384]{1,0:T(8,128)S(1)}, f32[96,384]{1,0:T(8,128)S(1)}, u32[]{:S(2)}, u32[]{:S(2)}) collective-permute-start(f32[96,384]{1,0:T(8,128)S(1)} %get-tuple-element.109.refs_7_.refs_10_), channel_id=1, source_target_pairs={{0,16},{4,20},{8,24},{12,28},{16,0},{20,4},{24,8},{28,12},{1,17},{... | collective-permute-start | bytes 442376 | tf_op jit(solution)/shard_map/ppermute | solution.py:316
  67.3 6.3 %collective-permute-start.22 = (f32[96,384]{1,0:T(8,128)S(1)}, f32[96,384]{1,0:T(8,128)S(1)}, u32[]{:S(2)}, u32[]{:S(2)}) collective-permute-start(f32[96,384]{1,0:T(8,128)S(1)} %get-tuple-element.110.refs_8_), channel_id=1, source_target_pairs={{0,28},{4,8},{8,4},{12,16},{16,12},{20,24},{24,20},{28,0},{1,29},{... | collective-permute-start | bytes 442376 | tf_op jit(solution)/shard_map/ppermute | solution.py:316
  67.3 6.3 %collective-permute-start.23 = (f32[96,384]{1,0:T(8,128)S(1)}, f32[96,384]{1,0:T(8,128)S(1)}, u32[]{:S(2)}, u32[]{:S(2)}) collective-permute-start(f32[96,384]{1,0:T(8,128)S(1)} %get-tuple-element.111.refs_9_), channel_id=1, source_target_pairs={{0,4},{4,0},{8,12},{12,8},{16,20},{20,16},{24,28},{28,24},{1,5},{5... | collective-permute-start | bytes 442376 | tf_op jit(solution)/shard_map/ppermute | solution.py:316

commit v6 on v5

--- a/solution.py
+++ b/solution.py
@@ -98,7 +98,7 @@
 def listed_body(subs, count, blocks_hbm, load_hbm, columns_hbm, listed_ref, load_ref, sent_ref, *refs):
     *shared_refs, blocks_ref, load_sems, blocks_sem, sent_sem = refs
     modes = sent_ref.shape[0]
-    wanted = pl.multiple_of((3 - (lax.axis_index("grp") ^ 1)) * modes, modes)
+    wanted = pl.multiple_of((lax.axis_index("grp") ^ 3) * modes, modes)
     sent_copy = pltpu.make_async_copy(columns_hbm.at[pl.ds(wanted, modes), :], sent_ref, sent_sem)
     half = load_ref.shape[0] // 2
     halves = [slice(0, half), slice(half, 2 * half)]
@@ -183,7 +183,7 @@
 
 def blend_body(columns_ref, other_ref, mix_high, mix_low):
     grp = lax.axis_index("grp")
-    away = jnp.concatenate([rows_of(columns_ref, 3 - grp), other_ref[...]], axis=1)
+    away = jnp.concatenate([rows_of(columns_ref, grp ^ 2), other_ref[...]], axis=1)
     kept = jnp.concatenate([rows_of(columns_ref, grp), rows_of(columns_ref, grp ^ 1).T], axis=1)
     mix_high[...], mix_low[...] = split(jnp.concatenate([away, kept], axis=0) * RELAX)
 
@@ -319,7 +319,7 @@
         return ((rows, width), kind)
 
     pair_plan = [(0, 1), (1, 0), (2, 3), (3, 2)]
-    mirror_plan = [(0, 3), (3, 0), (1, 2), (2, 1)]
+    across_plan = [(0, 2), (1, 3), (2, 0), (3, 1)]
     shared = [((shared_rows, loads), f32)] * count
     outside = pl.BlockSpec(memory_space=pltpu.HBM)
     pieces = len(PIECES)
@@ -359,7 +359,7 @@
                 own[place], theirs[place], *mixers,
             )
             kept.append(keep)
-            came.append(lax.ppermute(away, "grp", mirror_plan))
+            came.append(lax.ppermute(away, "grp", across_plan))
         if first:
             solve_high, solve_low = run(
                 lambda *refs: solver_body(subs, listed, *refs), [whole(rows, bf16)] * 2, 8 * rows**3, 12 * size,

time: 75.6 us -> 78.3 us (1.036)
  starting transfers between devices: 27.8 us -> 31.5 us
  waiting for transfers between devices: 27.7 us -> 26.9 us
    ppermute x15, starting transfers between devices: 12.4 us -> 16.4 us  [exchange(): return [lax.ppermute(part, 'sub', plan) for part, plan in zip(parts, plans)]]
    ppermute x15, waiting for transfers between devices: 16.6 us -> 12.8 us  [exchange(): return [lax.ppermute(part, 'sub', plan) for part, plan in zip(parts, plans)]]
    ppermute x4, waiting for transfers between devices: 6.12 us -> 8.37 us  [local(): came.append(lax.ppermute(away, 'grp', across_plan))]
  transfers between devices with their start and end apart: 24 -> 24, of which waited for: 14 -> 15; matrix products, arithmetic and copies ran while one was open for 0% -> 0% of each run, Pallas kernels for 17% -> 17%
where the time goes in v6:
time: 78.3 us; the launch traced here: 78.1 us
  starting transfers between devices  31.5 us (40%)
  waiting for transfers between devices  26.9 us (34%)
  Pallas kernels  18.7 us (24%)
  between operations  1.03 us (1%)
    pallas_call x25, Pallas kernels, __call__(): pl.pallas_call(whole_body, out_shape=[jax.ShapeDtypeStruct(shape, kind) f...  18.7 us
    ppermute x15, starting transfers between devices, exchange(): return [lax.ppermute(part, 'sub', plan) for part, plan in zip(parts, plans)]  16.4 us
    ppermute x15, waiting for transfers between devices, exchange(): return [lax.ppermute(part, 'sub', plan) for part, plan in zip(parts, plans)]  12.8 us
    ppermute x4, starting transfers between devices, local(): came.append(lax.ppermute(away, 'grp', across_plan))  9.27 us
    ppermute x4, waiting for transfers between devices, local(): came.append(lax.ppermute(away, 'grp', across_plan))  8.37 us
    ppermute x4, waiting for transfers between devices, local(): theirs = [lax.ppermute(piece, 'grp', pair_plan) for piece in own]  5.71 us
    ppermute x4, starting transfers between devices, local(): theirs = [lax.ppermute(piece, 'grp', pair_plan) for piece in own]  4.18 us
    ppermute x1, starting transfers between devices, local(): other = lax.ppermute(sent, 'grp', pair_plan)  1.58 us
  transfers between devices with their start and end apart: 24, of which 15 were waited for; matrix products, arithmetic and copies ran while one was open for 0% of the time, Pallas kernels for 17%

profile of v6, /device:TPU:0, one launch (start us, length us, event | category | flops | bytes accessed | tf_op | source)
XLA Modules:
  0.0 78.1 jit_solution(9408352973125557893)
XLA Ops:
  0.6 1.7 %shard_map.77 = (bf16[384,512]{1,0:T(8,128)(2,1)S(1)}, f32[512,384]{1,0:T(8,128)S(1)}, f32[128,128]{1,0:T(8,128)S(1)}, f32[96,384]{1,0:T(8,128)S(1)}, f32[96,384]{1,0:T(8,128)S(1)}, /*index=5*/f32[96,384]{1,0:T(8,128)S(1)}) custom-call(s32[4,96]{1,0:T(4,128)} %bitcast.15, f32[512,384]{1,0:T(8,128)} %bitcast.14, f32[512,128]{1,0:T(8,128)} %bitcast.9), custom_call_target="tpu_custom_call" | custom-call | flops 301989888 | bytes 3145728 | tf_op jit(solution)/shard_map/pallas_call | solution.py:35
  2.4 3.0 %collective-permute-start = (f32[96,384]{1,0:T(8,128)S(1)}, f32[96,384]{1,0:T(8,128)S(1)}, u32[]{:S(2)}, u32[]{:S(2)}) collective-permute-start(f32[96,384]{1,0:T(8,128)S(1)} %get-tuple-element.65), channel_id=1, source_target_pairs={{0,16},{4,20},{8,24},{12,28},{16,0},{20,4},{24,8},{28,12},{1,17},{... | collective-permute-start | bytes 442376 | tf_op jit(solution)/shard_map/ppermute | solution.py:316
  5.4 0.6 collective-permute-start.1
  6.0 1.0 %collective-permute-start.2 = (f32[96,384]{1,0:T(8,128)S(1)}, f32[96,384]{1,0:T(8,128)S(1)}, u32[]{:S(2)}, u32[]{:S(2)}) collective-permute-start(f32[96,384]{1,0:T(8,128)S(1)} %get-tuple-element.67), channel_id=1, source_target_pairs={{0,4},{4,0},{8,12},{12,8},{16,20},{20,16},{24,28},{28,24},{1,5},{5... | collective-permute-start | bytes 442376 | tf_op jit(solution)/shard_map/ppermute | solution.py:316
  7.0 1.6 %collective-permute-start.4 = (f32[128,128]{1,0:T(8,128)S(1)}, f32[128,128]{1,0:T(8,128)S(1)}, u32[]{:S(2)}, u32[]{:S(2)}) collective-permute-start(f32[128,128]{1,0:T(8,128)S(1)} %get-tuple-element.70), channel_id=1, source_target_pairs={{0,1},{1,0},{2,3},{3,2},{4,5},{5,4},{6,7},{7,6},{8,9},{9,8},{10,11... | collective-permute-start | bytes 196616 | tf_op jit(solution)/shard_map/ppermute | solution.py:337
  8.6 1.6 %shard_map.78 = (bf16[512,512]{1,0:T(8,128)(2,1)S(1)}, bf16[512,512]{1,0:T(8,128)(2,1)S(1)}, bf16[512,128]{1,0:T(8,128)(2,1)S(1)}, bf16[512,128]{1,0:T(8,128)(2,...) custom-call(bf16[384,512]{1,0:T(8,128)(2,1)S(1)} %get-tuple-element., ...), custom_call_target="tpu_custom_call" | custom-call | flops 402653184 | bytes 4718592 | tf_op jit(solution)/shard_map/pallas_call | solution.py:35
  10.2 1.4 %collective-permute-done.1.refs_4_ = f32[96,384]{1,0:T(8,128)S(1)} collective-permute-done((f32[96,384]{1,0:T(8,128)S(1)}, f32[96,384]{1,0:T(8,128)S(1)}, u32[]{:S(2)}, u32[]{:S(2)}) %collective-permute-start.1) | collective-permute-done | bytes 147488 | tf_op jit(solution)/shard_map/ppermute | solution.py:316
  11.5 0.4 shard_map.79
  11.9 1.6 %collective-permute-start.3 = (f32[128,128]{1,0:T(8,128)S(1)}, f32[128,128]{1,0:T(8,128)S(1)}, u32[]{:S(2)}, u32[]{:S(2)}) collective-permute-start(f32[128,128]{1,0:T(8,128)S(1)} %get-tuple-element.69.refs_2_.refs_0_), channel_id=1, source_target_pairs={{0,1},{1,0},{2,3},{3,2},{4,5},{5,4},{6,7},{7,6},{8,9},{9,8},{10,11... | collective-permute-start | bytes 196616 | tf_op jit(solution)/shard_map/ppermute | solution.py:352
  13.5 0.5 collective-permute-start.6
  14.1 2.5 %collective-permute-done.3.refs_1_ = f32[128,128]{1,0:T(8,128)S(1)} collective-permute-done((f32[128,128]{1,0:T(8,128)S(1)}, f32[128,128]{1,0:T(8,128)S(1)}, u32[]{:S(2)}, u32[]{:S(2)}) %collective-permute-start.3) | collective-permute-done | bytes 65568 | tf_op jit(solution)/shard_map/ppermute | solution.py:352
  16.9 2.6 %collective-permute-start.5 = (f32[128,128]{1,0:T(8,128)S(1)}, f32[128,128]{1,0:T(8,128)S(1)}, u32[]{:S(2)}, u32[]{:S(2)}) collective-permute-start(f32[128,128]{1,0:T(8,128)S(1)} %get-tuple-element.74.refs_4_), channel_id=1, source_target_pairs={{0,2},{1,3},{2,0},{3,1},{4,6},{5,7},{6,4},{7,5},{8,10},{9,11},{10,... | collective-permute-start | bytes 196616 | tf_op jit(solution)/shard_map/ppermute | solution.py:362
  20.0 2.6 %collective-permute-start.7 = (f32[128,256]{1,0:T(8,128)S(1)}, f32[128,256]{1,0:T(8,128)S(1)}, u32[]{:S(2)}, u32[]{:S(2)}) collective-permute-start(f32[128,256]{1,0:T(8,128)S(1)} %get-tuple-element.77.refs_2_), channel_id=1, source_target_pairs={{0,2},{1,3},{2,0},{3,1},{4,6},{5,7},{6,4},{7,5},{8,10},{9,11},{10,... | collective-permute-start | bytes 393224 | tf_op jit(solution)/shard_map/ppermute | solution.py:362
  22.7 1.3 %shard_map.83 = (bf16[512,512]{1,0:T(8,128)(2,1)S(1)}, bf16[512,512]{1,0:T(8,128)(2,1)S(1)}) custom-call(bf16[512,512]{1,0:T(8,128)(2,1)S(1)} %get-tuple-element.68.refs_6_.refs_0_, f32[512,512]{1,0:T(8,128)S(1)} %bitcast.11, f32[128,256]{1,0:T(8,128)S(1)} %get-tuple-element.77.refs_2_), custom_call_target="tpu_custom_call" | custom-call | flops 1073741824 | bytes 2359296 | tf_op jit(solution)/shard_map/pallas_call | solution.py:35
  24.0 1.0 %shard_map.84.refs_2_.refs_5_ = f32[512,384]{1,0:T(8,128)S(1)} custom-call(f32[512,384]{1,0:T(8,128)S(1)} %get-tuple-element.75.refs_0_.refs_2_.refs_3_, bf16[512,512]{1,0:T(8,128)(2,1)S(1)} %get-tuple-element.78.refs_1_.refs_6_, bf16[512,512]{1,0:T(8,128)(2,1)S(1)} %get-tuple-element.79.refs_2_, f32[96,384]{1,0:T(8,128)S(1)} %collective-permute-done.refs_3_, ...), custom_call_target="tpu_custom_call" | custom-call | flops 9663676416 | bytes 37748736 | tf_op jit(solution)/shard_map/pallas_call | solution.py:35
  25.3 3.2 %collective-permute-done.7.refs_1_ = f32[128,256]{1,0:T(8,128)S(1)} collective-permute-done((f32[128,256]{1,0:T(8,128)S(1)}, f32[128,256]{1,0:T(8,128)S(1)}, u32[]{:S(2)}, u32[]{:S(2)}) %collective-permute-start.7) | collective-permute-done | bytes 131104 | tf_op jit(solution)/shard_map/ppermute | solution.py:362
  29.0 1.4 %collective-permute-start.9 = (f32[96,384]{1,0:T(8,128)S(1)}, f32[96,384]{1,0:T(8,128)S(1)}, u32[]{:S(2)}, u32[]{:S(2)}) collective-permute-start(f32[96,384]{1,0:T(8,128)S(1)} %get-tuple-element.89), channel_id=1, source_target_pairs={{0,28},{4,8},{8,4},{12,16},{16,12},{20,24},{24,20},{28,0},{1,29},{... | collective-permute-start | bytes 442376 | tf_op jit(solution)/shard_map/ppermute | solution.py:316
  30.4 1.4 %collective-permute-start.10 = (f32[96,384]{1,0:T(8,128)S(1)}, f32[96,384]{1,0:T(8,128)S(1)}, u32[]{:S(2)}, u32[]{:S(2)}) collective-permute-start(f32[96,384]{1,0:T(8,128)S(1)} %get-tuple-element.90), channel_id=1, source_target_pairs={{0,4},{4,0},{8,12},{12,8},{16,20},{20,16},{24,28},{28,24},{1,5},{5... | collective-permute-start | bytes 442376 | tf_op jit(solution)/shard_map/ppermute | solution.py:316
  31.8 1.3 %shard_map.87 = (bf16[512,512]{1,0:T(8,128)(2,1)S(1)}, bf16[512,512]{1,0:T(8,128)(2,1)S(1)}) custom-call(bf16[512,512]{1,0:T(8,128)(2,1)S(1)} %get-tuple-element.68.refs_6_.refs_0_, bf16[512,512]{1,0:T(8,128)(2,1)S(1)} %get-tuple-element.61.refs_1_.refs_0_, f32[512,512]{1,0:T(8,128)S(1)} %bitcast.12, f32[512,256]{1,0:T(8,128)S(1)} %get-tuple-element.83.refs_3_.refs_1_), custom_call_target="tpu_custom_call" | custom-call | flops 1073741824 | bytes 2359296 | tf_op jit(solution)/shard_map/pallas_call | solution.py:35
  33.1 1.0 %shard_map.88 = (f32[512,384]{1,0:T(8,128)S(1)}, f32[512,384]{1,0:T(8,128)S(1)}) custom-call(f32[512,128]{1,0:T(8,128)S(1)} %shard_map.85.refs_5_.refs_6_.refs_0_, f32[512,256]{1,0:T(8,128)S(1)} %get-tuple-element.83.refs_3_.refs_1_, f32[512,384]{1,0:T(8,128)S(1)} %get-tuple-element.75.refs_0_.refs_2_.refs_3_, ...), custom_call_target="tpu_custom_call" | custom-call | flops 603979776 | bytes 3145728 | tf_op jit(solution)/shard_map/pallas_call | solution.py:35
  34.1 1.5 %collective-permute-done.8.refs_3_.refs_4_ = f32[96,384]{1,0:T(8,128)S(1)} collective-permute-done((f32[96,384]{1,0:T(8,128)S(1)}, f32[96,384]{1,0:T(8,128)S(1)}, u32[]{:S(2)}, u32[]{:S(2)}) %collective-permute-start.8) | collective-permute-done | bytes 147488 | tf_op jit(solution)/shard_map/ppermute | solution.py:316
  35.9 0.6 shard_map.89
  36.5 2.1 %collective-permute-start.11 = (f32[96,384]{1,0:T(8,128)S(1)}, f32[96,384]{1,0:T(8,128)S(1)}, u32[]{:S(2)}, u32[]{:S(2)}) collective-permute-start(f32[96,384]{1,0:T(8,128)S(1)} %get-tuple-element.91.refs_7_.refs_12_), channel_id=1, source_target_pairs={{0,16},{4,20},{8,24},{12,28},{16,0},{20,4},{24,8},{28,12},{1,17},{... | collective-permute-start | bytes 442376 | tf_op jit(solution)/shard_map/ppermute | solution.py:316
  38.5 0.5 collective-permute-start.12
  39.0 0.4 collective-permute-start.13
  39.4 0.9 %shard_map.90 = (f32[128,384]{1,0:T(8,128)S(1)}, f32[512,384]{1,0:T(8,128)S(1)}, f32[512,384]{1,0:T(8,128)S(1)}) custom-call(f32[512,384]{1,0:T(8,128)S(1)} %get-tuple-element.86.refs_0_.refs_6_, f32[512,384]{1,0:T(8,128)S(1)} %get-tuple-element.87.refs_1_, bf16[512,512]{1,0:T(8,128)(2,1)S(1)} %get-tuple-element.84.refs_3_.refs_5_.refs_1_.refs_2_.refs_4_, ...), custom_call_target="tpu_custom_call" | custom-call | flops 301989888 | bytes 3145728 | tf_op jit(solution)/shard_map/pallas_call | solution.py:35
  40.2 2.3 %collective-permute-done.11.refs_3_ = f32[96,384]{1,0:T(8,128)S(1)} collective-permute-done((f32[96,384]{1,0:T(8,128)S(1)}, f32[96,384]{1,0:T(8,128)S(1)}, u32[]{:S(2)}, u32[]{:S(2)}) %collective-permute-start.11) | collective-permute-done | bytes 147488 | tf_op jit(solution)/shard_map/ppermute | solution.py:316
  42.5 1.7 %collective-permute-done.12.refs_4_ = f32[96,384]{1,0:T(8,128)S(1)} collective-permute-done((f32[96,384]{1,0:T(8,128)S(1)}, f32[96,384]{1,0:T(8,128)S(1)}, u32[]{:S(2)}, u32[]{:S(2)}) %collective-permute-start.12) | collective-permute-done | bytes 147488 | tf_op jit(solution)/shard_map/ppermute | solution.py:316
  44.9 1.8 %collective-permute-start.16 = (f32[128,256]{1,0:T(8,128)S(1)}, f32[128,256]{1,0:T(8,128)S(1)}, u32[]{:S(2)}, u32[]{:S(2)}) collective-permute-start(f32[128,256]{1,0:T(8,128)S(1)} %get-tuple-element.99.refs_0_), channel_id=1, source_target_pairs={{0,1},{1,0},{2,3},{3,2},{4,5},{5,4},{6,7},{7,6},{8,9},{9,8},{10,11... | collective-permute-start | bytes 393224 | tf_op jit(solution)/shard_map/ppermute | solution.py:352
  46.7 3.0 %collective-permute-done.14.refs_1_ = f32[128,128]{1,0:T(8,128)S(1)} collective-permute-done((f32[128,128]{1,0:T(8,128)S(1)}, f32[128,128]{1,0:T(8,128)S(1)}, u32[]{:S(2)}, u32[]{:S(2)}) %collective-permute-start.14) | collective-permute-done | bytes 65568 | tf_op jit(solution)/shard_map/ppermute | solution.py:352
  49.9 1.6 %collective-permute-start.15 = (f32[128,128]{1,0:T(8,128)S(1)}, f32[128,128]{1,0:T(8,128)S(1)}, u32[]{:S(2)}, u32[]{:S(2)}) collective-permute-start(f32[128,128]{1,0:T(8,128)S(1)} %get-tuple-element.97.refs_4_), channel_id=1, source_target_pairs={{0,2},{1,3},{2,0},{3,1},{4,6},{5,7},{6,4},{7,5},{8,10},{9,11},{10,... | collective-permute-start | bytes 196616 | tf_op jit(solution)/shard_map/ppermute | solution.py:362
  51.9 2.4 %collective-permute-start.17 = (f32[128,256]{1,0:T(8,128)S(1)}, f32[128,256]{1,0:T(8,128)S(1)}, u32[]{:S(2)}, u32[]{:S(2)}) collective-permute-start(f32[128,256]{1,0:T(8,128)S(1)} %get-tuple-element.100.refs_6_), channel_id=1, source_target_pairs={{0,2},{1,3},{2,0},{3,1},{4,6},{5,7},{6,4},{7,5},{8,10},{9,11},{10,... | collective-permute-start | bytes 393224 | tf_op jit(solution)/shard_map/ppermute | solution.py:362
  54.2 1.0 %shard_map.94.refs_2_.refs_5_ = f32[512,384]{1,0:T(8,128)S(1)} custom-call(f32[512,384]{1,0:T(8,128)S(1)} %get-tuple-element.98.refs_0_, bf16[512,512]{1,0:T(8,128)(2,1)S(1)} %get-tuple-element.78.refs_1_.refs_6_, bf16[512,512]{1,0:T(8,128)(2,1)S(1)} %get-tuple-element.79.refs_2_, f32[96,384]{1,0:T(8,128)S(1)} %collective-permute-done.11.refs_3_, ...), custom_call_target="tpu_custom_call" | custom-call | flops 9663676416 | bytes 37748736 | tf_op jit(solution)/shard_map/pallas_call | solution.py:35
  55.2 3.8 %collective-permute-done.15.refs_1_ = f32[128,128]{1,0:T(8,128)S(1)} collective-permute-done((f32[128,128]{1,0:T(8,128)S(1)}, f32[128,128]{1,0:T(8,128)S(1)}, u32[]{:S(2)}, u32[]{:S(2)}) %collective-permute-start.15) | collective-permute-done | bytes 65568 | tf_op jit(solution)/shard_map/ppermute | solution.py:362
  59.3 1.3 %collective-permute-done.17.refs_1_ = f32[128,256]{1,0:T(8,128)S(1)} collective-permute-done((f32[128,256]{1,0:T(8,128)S(1)}, f32[128,256]{1,0:T(8,128)S(1)}, u32[]{:S(2)}, u32[]{:S(2)}) %collective-permute-start.17) | collective-permute-done | bytes 131104 | tf_op jit(solution)/shard_map/ppermute | solution.py:362
  61.1 1.6 %collective-permute-start.19 = (f32[96,384]{1,0:T(8,128)S(1)}, f32[96,384]{1,0:T(8,128)S(1)}, u32[]{:S(2)}, u32[]{:S(2)}) collective-permute-start(f32[96,384]{1,0:T(8,128)S(1)} %get-tuple-element.107), channel_id=1, source_target_pairs={{0,28},{4,8},{8,4},{12,16},{16,12},{20,24},{24,20},{28,0},{1,29},{... | collective-permute-start | bytes 442376 | tf_op jit(solution)/shard_map/ppermute | solution.py:316
  62.7 1.0 %collective-permute-start.20 = (f32[96,384]{1,0:T(8,128)S(1)}, f32[96,384]{1,0:T(8,128)S(1)}, u32[]{:S(2)}, u32[]{:S(2)}) collective-permute-start(f32[96,384]{1,0:T(8,128)S(1)} %get-tuple-element.108), channel_id=1, source_target_pairs={{0,4},{4,0},{8,12},{12,8},{16,20},{20,16},{24,28},{28,24},{1,5},{5... | collective-permute-start | bytes 442376 | tf_op jit(solution)/shard_map/ppermute | solution.py:316
  63.7 1.0 %shard_map.97 = (f32[512,384]{1,0:T(8,128)S(1)}, f32[512,384]{1,0:T(8,128)S(1)}) custom-call(f32[512,128]{1,0:T(8,128)S(1)} %shard_map.95.refs_5_.refs_6_.refs_0_, f32[512,256]{1,0:T(8,128)S(1)} %get-tuple-element.102.refs_1_.refs_6_, f32[512,384]{1,0:T(8,128)S(1)} %get-tuple-element.103.refs_2_, f32[512,384]{1,0:T(8,128)S(1)} %get-tuple-element.75.refs_0_.refs_2_.refs_3_, ...), custom_call_target="tpu_custom_call" | custom-call | flops 603979776 | bytes 3145728 | tf_op jit(solution)/shard_map/pallas_call | solution.py:35
  64.7 3.0 %collective-permute-done.18.refs_3_.refs_4_ = f32[96,384]{1,0:T(8,128)S(1)} collective-permute-done((f32[96,384]{1,0:T(8,128)S(1)}, f32[96,384]{1,0:T(8,128)S(1)}, u32[]{:S(2)}, u32[]{:S(2)}) %collective-permute-start.18) | collective-permute-done | bytes 147488 | tf_op jit(solution)/shard_map/ppermute | solution.py:316
  67.9 0.8 shard_map.98
  68.7 1.9 %collective-permute-start.21 = (f32[96,384]{1,0:T(8,128)S(1)}, f32[96,384]{1,0:T(8,128)S(1)}, u32[]{:S(2)}, u32[]{:S(2)}) collective-permute-start(f32[96,384]{1,0:T(8,128)S(1)} %get-tuple-element.109.refs_7_.refs_10_), channel_id=1, source_target_pairs={{0,16},{4,20},{8,24},{12,28},{16,0},{20,4},{24,8},{28,12},{1,17},{... | collective-permute-start | bytes 442376 | tf_op jit(solution)/shard_map/ppermute | solution.py:316
  70.6 0.9 %collective-permute-start.22 = (f32[96,384]{1,0:T(8,128)S(1)}, f32[96,384]{1,0:T(8,128)S(1)}, u32[]{:S(2)}, u32[]{:S(2)}) collective-permute-start(f32[96,384]{1,0:T(8,128)S(1)} %get-tuple-element.110.refs_8_), channel_id=1, source_target_pairs={{0,28},{4,8},{8,4},{12,16},{16,12},{20,24},{24,20},{28,0},{1,29},{... | collective-permute-start | bytes 442376 | tf_op jit(solution)/shard_map/ppermute | solution.py:316
  71.5 0.4 collective-permute-start.23
  71.9 0.5 shard_map.99
  72.4 1.6 %shard_map.100 = (f32[512,384]{1,0:T(8,128)S(1)}, f32[512,384]{1,0:T(8,128)}) custom-call(bf16[512,512]{1,0:T(8,128)(2,1)S(1)} %get-tuple-element.61.refs_1_.refs_0_, f32[512,384]{1,0:T(8,128)S(1)} %get-tuple-element.112.refs_1_, f32[512,384]{1,0:T(8,128)S(1)} %get-tuple-element.113.refs_2_.refs_3_, f32[512,384]{1,0:T(8,128)S(1)} %get-tuple-element.113.refs_2_.refs_3_), custom_call_target="tpu_custom_call" | custom-call | flops 805306368 | bytes 1966080 | tf_op jit(solution)/shard_map/pallas_call | solution.py:35
  74.0 0.7 collective-permute-done.21.refs_2_
  74.7 1.8 %collective-permute-done.22.refs_3_ = f32[96,384]{1,0:T(8,128)S(1)} collective-permute-done((f32[96,384]{1,0:T(8,128)S(1)}, f32[96,384]{1,0:T(8,128)S(1)}, u32[]{:S(2)}, u32[]{:S(2)}) %collective-permute-start.22) | collective-permute-done | bytes 147488 | tf_op jit(solution)/shard_map/ppermute | solution.py:316
  76.5 1.5 %shard_map.101 = f32[512,384]{1,0:T(8,128)} custom-call(bf16[512,512]{1,0:T(8,128)(2,1)S(1)} %get-tuple-element.61.refs_1_.refs_0_, f32[512,384]{1,0:T(8,128)S(1)} %get-tuple-element.115.refs_1_.refs_5_, f32[96,384]{1,0:T(8,128)S(1)} %collective-permute-done.21.refs_2_, f32[96,384]{1,0:T(8,128)S(1)} %collective-permute-done.22.refs_3_, ...), custom_call_target="tpu_custom_call" | custom-call | flops 402653184 | bytes 1966080 | tf_op jit(solution)/shard_map/pallas_call | solution.py:35
  (33 shorter events, 3.9 us)
Async XLA Ops:
  0.6 8.0 %copy-start = (f32[1,1,512,128]{3,2,1,0:T(8,128)S(1)}, f32[1,1,512,128]{3,2,1,0:T(8,128)}, u32[]{:S(2)}) copy-start(f32[1,1,512,128]{3,2,1,0:T(8,128)} %param.9) | copy-start | bytes 786436
  2.4 7.8 %collective-permute-start = (f32[96,384]{1,0:T(8,128)S(1)}, f32[96,384]{1,0:T(8,128)S(1)}, u32[]{:S(2)}, u32[]{:S(2)}) collective-permute-start(f32[96,384]{1,0:T(8,128)S(1)} %get-tuple-element.65), channel_id=1, source_target_pairs={{0,16},{4,20},{8,24},{12,28},{16,0},{20,4},{24,8},{28,12},{1,17},{... | collective-permute-start | bytes 442376 | tf_op jit(solution)/shard_map/ppermute | solution.py:316
  5.4 6.1 %collective-permute-start.1 = (f32[96,384]{1,0:T(8,128)S(1)}, f32[96,384]{1,0:T(8,128)S(1)}, u32[]{:S(2)}, u32[]{:S(2)}) collective-permute-start(f32[96,384]{1,0:T(8,128)S(1)} %get-tuple-element.66), channel_id=1, source_target_pairs={{0,28},{4,8},{8,4},{12,16},{16,12},{20,24},{24,20},{28,0},{1,29},{... | collective-permute-start | bytes 442376 | tf_op jit(solution)/shard_map/ppermute | solution.py:316
  6.0 5.5 %collective-permute-start.2 = (f32[96,384]{1,0:T(8,128)S(1)}, f32[96,384]{1,0:T(8,128)S(1)}, u32[]{:S(2)}, u32[]{:S(2)}) collective-permute-start(f32[96,384]{1,0:T(8,128)S(1)} %get-tuple-element.67), channel_id=1, source_target_pairs={{0,4},{4,0},{8,12},{12,8},{16,20},{20,16},{24,28},{28,24},{1,5},{5... | collective-permute-start | bytes 442376 | tf_op jit(solution)/shard_map/ppermute | solution.py:316
  7.0 7.0 %collective-permute-start.4 = (f32[128,128]{1,0:T(8,128)S(1)}, f32[128,128]{1,0:T(8,128)S(1)}, u32[]{:S(2)}, u32[]{:S(2)}) collective-permute-start(f32[128,128]{1,0:T(8,128)S(1)} %get-tuple-element.70), channel_id=1, source_target_pairs={{0,1},{1,0},{2,3},{3,2},{4,5},{5,4},{6,7},{7,6},{8,9},{9,8},{10,11... | collective-permute-start | bytes 196616 | tf_op jit(solution)/shard_map/ppermute | solution.py:337
  11.5 2.5 %copy-start.1 = (f32[1,512,128]{2,1,0:T(8,128)S(1)}, f32[1,512,128]{2,1,0:T(8,128)}, u32[]{:S(2)}) copy-start(f32[1,512,128]{2,1,0:T(8,128)} %param.10) | copy-start | bytes 786436
  11.9 4.7 %collective-permute-start.3 = (f32[128,128]{1,0:T(8,128)S(1)}, f32[128,128]{1,0:T(8,128)S(1)}, u32[]{:S(2)}, u32[]{:S(2)}) collective-permute-start(f32[128,128]{1,0:T(8,128)S(1)} %get-tuple-element.69.refs_2_.refs_0_), channel_id=1, source_target_pairs={{0,1},{1,0},{2,3},{3,2},{4,5},{5,4},{6,7},{7,6},{8,9},{9,8},{10,11... | collective-permute-start | bytes 196616 | tf_op jit(solution)/shard_map/ppermute | solution.py:352
  13.5 6.2 %collective-permute-start.6 = (f32[128,256]{1,0:T(8,128)S(1)}, f32[128,256]{1,0:T(8,128)S(1)}, u32[]{:S(2)}, u32[]{:S(2)}) collective-permute-start(f32[128,256]{1,0:T(8,128)S(1)} %get-tuple-element.76.refs_0_), channel_id=1, source_target_pairs={{0,1},{1,0},{2,3},{3,2},{4,5},{5,4},{6,7},{7,6},{8,9},{9,8},{10,11... | collective-permute-start | bytes 393224 | tf_op jit(solution)/shard_map/ppermute | solution.py:352
  16.9 5.8 %copy-start.2 = (f32[1,1,512,512]{3,2,1,0:T(8,128)S(1)}, f32[1,1,512,512]{3,2,1,0:T(8,128)}, u32[]{:S(2)}) copy-start(f32[1,1,512,512]{3,2,1,0:T(8,128)} %param.8) | copy-start | bytes 3145732
  16.9 8.1 %collective-permute-start.5 = (f32[128,128]{1,0:T(8,128)S(1)}, f32[128,128]{1,0:T(8,128)S(1)}, u32[]{:S(2)}, u32[]{:S(2)}) collective-permute-start(f32[128,128]{1,0:T(8,128)S(1)} %get-tuple-element.74.refs_4_), channel_id=1, source_target_pairs={{0,2},{1,3},{2,0},{3,1},{4,6},{5,7},{6,4},{7,5},{8,10},{9,11},{10,... | collective-permute-start | bytes 196616 | tf_op jit(solution)/shard_map/ppermute | solution.py:362
  20.0 8.5 %collective-permute-start.7 = (f32[128,256]{1,0:T(8,128)S(1)}, f32[128,256]{1,0:T(8,128)S(1)}, u32[]{:S(2)}, u32[]{:S(2)}) collective-permute-start(f32[128,256]{1,0:T(8,128)S(1)} %get-tuple-element.77.refs_2_), channel_id=1, source_target_pairs={{0,2},{1,3},{2,0},{3,1},{4,6},{5,7},{6,4},{7,5},{8,10},{9,11},{10,... | collective-permute-start | bytes 393224 | tf_op jit(solution)/shard_map/ppermute | solution.py:362
  25.3 6.5 %copy-start.3 = (f32[1,1,512,512]{3,2,1,0:T(8,128)S(1)}, f32[1,1,512,512]{3,2,1,0:T(8,128)}, u32[]{:S(2)}) copy-start(f32[1,1,512,512]{3,2,1,0:T(8,128)} %param.7) | copy-start | bytes 3145732
  28.9 6.7 %collective-permute-start.8 = (f32[96,384]{1,0:T(8,128)S(1)}, f32[96,384]{1,0:T(8,128)S(1)}, u32[]{:S(2)}, u32[]{:S(2)}) collective-permute-start(f32[96,384]{1,0:T(8,128)S(1)} %get-tuple-element.88), channel_id=1, source_target_pairs={{0,16},{4,20},{8,24},{12,28},{16,0},{20,4},{24,8},{28,12},{1,17},{... | collective-permute-start | bytes 442376 | tf_op jit(solution)/shard_map/ppermute | solution.py:316
  29.0 6.9 %collective-permute-start.9 = (f32[96,384]{1,0:T(8,128)S(1)}, f32[96,384]{1,0:T(8,128)S(1)}, u32[]{:S(2)}, u32[]{:S(2)}) collective-permute-start(f32[96,384]{1,0:T(8,128)S(1)} %get-tuple-element.89), channel_id=1, source_target_pairs={{0,28},{4,8},{8,4},{12,16},{16,12},{20,24},{24,20},{28,0},{1,29},{... | collective-permute-start | bytes 442376 | tf_op jit(solution)/shard_map/ppermute | solution.py:316
  30.4 5.5 %collective-permute-start.10 = (f32[96,384]{1,0:T(8,128)S(1)}, f32[96,384]{1,0:T(8,128)S(1)}, u32[]{:S(2)}, u32[]{:S(2)}) collective-permute-start(f32[96,384]{1,0:T(8,128)S(1)} %get-tuple-element.90), channel_id=1, source_target_pairs={{0,4},{4,0},{8,12},{12,8},{16,20},{20,16},{24,28},{28,24},{1,5},{5... | collective-permute-start | bytes 442376 | tf_op jit(solution)/shard_map/ppermute | solution.py:316
  36.5 6.1 %collective-permute-start.11 = (f32[96,384]{1,0:T(8,128)S(1)}, f32[96,384]{1,0:T(8,128)S(1)}, u32[]{:S(2)}, u32[]{:S(2)}) collective-permute-start(f32[96,384]{1,0:T(8,128)S(1)} %get-tuple-element.91.refs_7_.refs_12_), channel_id=1, source_target_pairs={{0,16},{4,20},{8,24},{12,28},{16,0},{20,4},{24,8},{28,12},{1,17},{... | collective-permute-start | bytes 442376 | tf_op jit(solution)/shard_map/ppermute | solution.py:316
  38.5 5.7 %collective-permute-start.12 = (f32[96,384]{1,0:T(8,128)S(1)}, f32[96,384]{1,0:T(8,128)S(1)}, u32[]{:S(2)}, u32[]{:S(2)}) collective-permute-start(f32[96,384]{1,0:T(8,128)S(1)} %get-tuple-element.92.refs_8_), channel_id=1, source_target_pairs={{0,28},{4,8},{8,4},{12,16},{16,12},{20,24},{24,20},{28,0},{1,29},{... | collective-permute-start | bytes 442376 | tf_op jit(solution)/shard_map/ppermute | solution.py:316
  39.0 5.3 %collective-permute-start.13 = (f32[96,384]{1,0:T(8,128)S(1)}, f32[96,384]{1,0:T(8,128)S(1)}, u32[]{:S(2)}, u32[]{:S(2)}) collective-permute-start(f32[96,384]{1,0:T(8,128)S(1)} %get-tuple-element.93.refs_9_), channel_id=1, source_target_pairs={{0,4},{4,0},{8,12},{12,8},{16,20},{20,16},{24,28},{28,24},{1,5},{5... | collective-permute-start | bytes 442376 | tf_op jit(solution)/shard_map/ppermute | solution.py:316
  44.6 5.1 %collective-permute-start.14 = (f32[128,128]{1,0:T(8,128)S(1)}, f32[128,128]{1,0:T(8,128)S(1)}, u32[]{:S(2)}, u32[]{:S(2)}) collective-permute-start(f32[128,128]{1,0:T(8,128)S(1)} %get-tuple-element.95.refs_0_.refs_4_), channel_id=1, source_target_pairs={{0,1},{1,0},{2,3},{3,2},{4,5},{5,4},{6,7},{7,6},{8,9},{9,8},{10,11... | collective-permute-start | bytes 196616 | tf_op jit(solution)/shard_map/ppermute | solution.py:352
  44.9 6.7 %collective-permute-start.16 = (f32[128,256]{1,0:T(8,128)S(1)}, f32[128,256]{1,0:T(8,128)S(1)}, u32[]{:S(2)}, u32[]{:S(2)}) collective-permute-start(f32[128,256]{1,0:T(8,128)S(1)} %get-tuple-element.99.refs_0_), channel_id=1, source_target_pairs={{0,1},{1,0},{2,3},{3,2},{4,5},{5,4},{6,7},{7,6},{8,9},{9,8},{10,11... | collective-permute-start | bytes 393224 | tf_op jit(solution)/shard_map/ppermute | solution.py:352
  49.9 9.1 %collective-permute-start.15 = (f32[128,128]{1,0:T(8,128)S(1)}, f32[128,128]{1,0:T(8,128)S(1)}, u32[]{:S(2)}, u32[]{:S(2)}) collective-permute-start(f32[128,128]{1,0:T(8,128)S(1)} %get-tuple-element.97.refs_4_), channel_id=1, source_target_pairs={{0,2},{1,3},{2,0},{3,1},{4,6},{5,7},{6,4},{7,5},{8,10},{9,11},{10,... | collective-permute-start | bytes 196616 | tf_op jit(solution)/shard_map/ppermute | solution.py:362
  51.9 8.8 %collective-permute-start.17 = (f32[128,256]{1,0:T(8,128)S(1)}, f32[128,256]{1,0:T(8,128)S(1)}, u32[]{:S(2)}, u32[]{:S(2)}) collective-permute-start(f32[128,256]{1,0:T(8,128)S(1)} %get-tuple-element.100.refs_6_), channel_id=1, source_target_pairs={{0,2},{1,3},{2,0},{3,1},{4,6},{5,7},{6,4},{7,5},{8,10},{9,11},{10,... | collective-permute-start | bytes 393224 | tf_op jit(solution)/shard_map/ppermute | solution.py:362
  61.0 6.7 %collective-permute-start.18 = (f32[96,384]{1,0:T(8,128)S(1)}, f32[96,384]{1,0:T(8,128)S(1)}, u32[]{:S(2)}, u32[]{:S(2)}) collective-permute-start(f32[96,384]{1,0:T(8,128)S(1)} %get-tuple-element.106), channel_id=1, source_target_pairs={{0,16},{4,20},{8,24},{12,28},{16,0},{20,4},{24,8},{28,12},{1,17},{... | collective-permute-start | bytes 442376 | tf_op jit(solution)/shard_map/ppermute | solution.py:316
  61.1 6.8 %collective-permute-start.19 = (f32[96,384]{1,0:T(8,128)S(1)}, f32[96,384]{1,0:T(8,128)S(1)}, u32[]{:S(2)}, u32[]{:S(2)}) collective-permute-start(f32[96,384]{1,0:T(8,128)S(1)} %get-tuple-element.107), channel_id=1, source_target_pairs={{0,28},{4,8},{8,4},{12,16},{16,12},{20,24},{24,20},{28,0},{1,29},{... | collective-permute-start | bytes 442376 | tf_op jit(solution)/shard_map/ppermute | solution.py:316
  62.7 5.2 %collective-permute-start.20 = (f32[96,384]{1,0:T(8,128)S(1)}, f32[96,384]{1,0:T(8,128)S(1)}, u32[]{:S(2)}, u32[]{:S(2)}) collective-permute-start(f32[96,384]{1,0:T(8,128)S(1)} %get-tuple-element.108), channel_id=1, source_target_pairs={{0,4},{4,0},{8,12},{12,8},{16,20},{20,16},{24,28},{28,24},{1,5},{5... | collective-permute-start | bytes 442376 | tf_op jit(solution)/shard_map/ppermute | solution.py:316
  68.7 6.0 %collective-permute-start.21 = (f32[96,384]{1,0:T(8,128)S(1)}, f32[96,384]{1,0:T(8,128)S(1)}, u32[]{:S(2)}, u32[]{:S(2)}) collective-permute-start(f32[96,384]{1,0:T(8,128)S(1)} %get-tuple-element.109.refs_7_.refs_10_), channel_id=1, source_target_pairs={{0,16},{4,20},{8,24},{12,28},{16,0},{20,4},{24,8},{28,12},{1,17},{... | collective-permute-start | bytes 442376 | tf_op jit(solution)/shard_map/ppermute | solution.py:316
  70.6 5.9 %collective-permute-start.22 = (f32[96,384]{1,0:T(8,128)S(1)}, f32[96,384]{1,0:T(8,128)S(1)}, u32[]{:S(2)}, u32[]{:S(2)}) collective-permute-start(f32[96,384]{1,0:T(8,128)S(1)} %get-tuple-element.110.refs_8_), channel_id=1, source_target_pairs={{0,28},{4,8},{8,4},{12,16},{16,12},{20,24},{24,20},{28,0},{1,29},{... | collective-permute-start | bytes 442376 | tf_op jit(solution)/shard_map/ppermute | solution.py:316
  71.5 4.9 %collective-permute-start.23 = (f32[96,384]{1,0:T(8,128)S(1)}, f32[96,384]{1,0:T(8,128)S(1)}, u32[]{:S(2)}, u32[]{:S(2)}) collective-permute-start(f32[96,384]{1,0:T(8,128)S(1)} %get-tuple-element.111.refs_9_), channel_id=1, source_target_pairs={{0,4},{4,0},{8,12},{12,8},{16,20},{20,16},{24,28},{28,24},{1,5},{5... | collective-permute-start | bytes 442376 | tf_op jit(solution)/shard_map/ppermute | solution.py:316

commit v7 on v5

--- a/solution.py
+++ b/solution.py
@@ -9,8 +9,7 @@
 ROW_SUBS = 4
 RELAX = 0.5
 GROUPS = 4
-HIDE = 16
-PIECES = (128, 256)
+PIECES = (128, 128, 128)
 f32 = jnp.float32
 bf16 = jnp.bfloat16
 NN = (((1,), (0,)), ((), ()))
@@ -98,7 +97,7 @@
 def listed_body(subs, count, blocks_hbm, load_hbm, columns_hbm, listed_ref, load_ref, sent_ref, *refs):
     *shared_refs, blocks_ref, load_sems, blocks_sem, sent_sem = refs
     modes = sent_ref.shape[0]
-    wanted = pl.multiple_of((3 - (lax.axis_index("grp") ^ 1)) * modes, modes)
+    wanted = pl.multiple_of((lax.axis_index("grp") ^ 2) * modes, modes)
     sent_copy = pltpu.make_async_copy(columns_hbm.at[pl.ds(wanted, modes), :], sent_ref, sent_sem)
     half = load_ref.shape[0] // 2
     halves = [slice(0, half), slice(half, 2 * half)]
@@ -183,8 +182,8 @@
 
 def blend_body(columns_ref, other_ref, mix_high, mix_low):
     grp = lax.axis_index("grp")
-    away = jnp.concatenate([rows_of(columns_ref, 3 - grp), other_ref[...]], axis=1)
-    kept = jnp.concatenate([rows_of(columns_ref, grp), rows_of(columns_ref, grp ^ 1).T], axis=1)
+    away = jnp.concatenate([rows_of(columns_ref, grp ^ 1), other_ref[...]], axis=1)
+    kept = jnp.concatenate([rows_of(columns_ref, grp), rows_of(columns_ref, grp ^ 3).T], axis=1)
     mix_high[...], mix_low[...] = split(jnp.concatenate([away, kept], axis=0) * RELAX)
 
 
@@ -334,7 +333,7 @@
         + [pltpu.SemaphoreType.DMA] * 2,
     )
     arrived = exchange(parts)
-    other = lax.ppermute(sent, "grp", pair_plan)
+    other = lax.ppermute(sent, "grp", mirror_plan)
     chooser, flipped, basis_high, basis_low, test_high, test_low, ahead, ordered = run(
         lambda *refs: order_body(subs, *refs),
         [whole(rows, bf16)] * 2 + [whole(modes, bf16)] * 2 + [((modes, rows), bf16)] * 2
@@ -349,24 +348,24 @@
             lambda *refs: project_body(subs, count, *refs), shapes, 6 * modes * size, 12 * size,
             ahead, test_high, test_low, *arrived,
         )
-        theirs = [lax.ppermute(piece, "grp", pair_plan) for piece in own]
+        theirs = [lax.ppermute(piece, "grp", mirror_plan) for piece in own]
         if first:
             mixers = run(blend_body, [((2 * modes, 2 * modes), bf16)] * 2, size, size, columns, other)
         kept, came = [], []
         for place, width in enumerate(PIECES):
             away, keep = run(
-                mix_body, [((modes, width), f32)] * 2, HIDE * 24 * modes * modes * width, HIDE * 4 * rows * width,
+                mix_body, [((modes, width), f32)] * 2, 24 * modes * modes * width, 4 * rows * width,
                 own[place], theirs[place], *mixers,
             )
             kept.append(keep)
-            came.append(lax.ppermute(away, "grp", mirror_plan))
+            came.append(lax.ppermute(away, "grp", pair_plan))
         if first:
             solve_high, solve_low = run(
                 lambda *refs: solver_body(subs, listed, *refs), [whole(rows, bf16)] * 2, 8 * rows**3, 12 * size,
                 chooser, local_inverse[0, 0],
             )
         (fine,) = run(
-            lambda *refs: solve_body(subs, *refs), [whole(loads)], HIDE * 6 * rows * size, HIDE * 12 * size,
+            lambda *refs: solve_body(subs, *refs), [whole(loads)], 6 * rows * size, 12 * size,
             value, solve_high, solve_low, *arrived,
         )
         steps = []

time: 75.6 us -> 77.2 us (1.021)
  starting transfers between devices: 27.8 us -> 34.2 us
  waiting for transfers between devices: 27.7 us -> 22.3 us
    ppermute x9 -> x13, starting transfers between devices: 15.3 us -> 20.8 us  [the longest x6 12.7 us: local(): theirs = [lax.ppermute(piece, 'grp', mirror_plan) for piece in own]]
    ppermute x9 -> x13, waiting for transfers between devices: 11.1 us -> 7.82 us  [the longest x6 5.27 us: local(): theirs = [lax.ppermute(piece, 'grp', mirror_plan) for piece in own]]
    ppermute x15, waiting for transfers between devices: 16.6 us -> 14.4 us  [exchange(): return [lax.ppermute(part, 'sub', plan) for part, plan in zip(parts, plans)]]
    ppermute x15, starting transfers between devices: 12.4 us -> 13.4 us  [exchange(): return [lax.ppermute(part, 'sub', plan) for part, plan in zip(parts, plans)]]
    pallas_call x25 -> x29, Pallas kernels: 18.7 us -> 19.4 us  [__call__(): pl.pallas_call(whole_body, out_shape=[jax.ShapeDtypeStruct(shape, kind) f...]
  transfers between devices with their start and end apart: 24 -> 28, of which waited for: 14 -> 15; matrix products, arithmetic and copies ran while one was open for 0% -> 0% of each run, Pallas kernels for 17% -> 18%
where the time goes in v7:
time: 77.2 us; the launch traced here: 77 us
  starting transfers between devices  34.2 us (44%)
  waiting for transfers between devices  22.3 us (29%)
  Pallas kernels  19.4 us (25%)
  between operations  1.1 us (1%)
    pallas_call x29, Pallas kernels, __call__(): pl.pallas_call(whole_body, out_shape=[jax.ShapeDtypeStruct(shape, kind) f...  19.4 us
    ppermute x15, waiting for transfers between devices, exchange(): return [lax.ppermute(part, 'sub', plan) for part, plan in zip(parts, plans)]  14.4 us
    ppermute x15, starting transfers between devices, exchange(): return [lax.ppermute(part, 'sub', plan) for part, plan in zip(parts, plans)]  13.4 us
    ppermute x6, starting transfers between devices, local(): theirs = [lax.ppermute(piece, 'grp', mirror_plan) for piece in own]  12.7 us
    ppermute x6, waiting for transfers between devices, local(): theirs = [lax.ppermute(piece, 'grp', mirror_plan) for piece in own]  5.27 us
    ppermute x6, starting transfers between devices, local(): came.append(lax.ppermute(away, 'grp', pair_plan))  4.49 us
    ppermute x1, starting transfers between devices, local(): other = lax.ppermute(sent, 'grp', mirror_plan)  3.59 us
    ppermute x6, waiting for transfers between devices, local(): came.append(lax.ppermute(away, 'grp', pair_plan))  2.54 us
  transfers between devices with their start and end apart: 28, of which 15 were waited for; matrix products, arithmetic and copies ran while one was open for 0% of the time, Pallas kernels for 18%

profile of v7, /device:TPU:0, one launch (start us, length us, event | category | flops | bytes accessed | tf_op | source)
XLA Modules:
  0.0 77.0 jit_solution(426001236680895908)
XLA Ops:
  0.6 1.7 %shard_map.77 = (bf16[384,512]{1,0:T(8,128)(2,1)S(1)}, f32[512,384]{1,0:T(8,128)S(1)}, f32[128,128]{1,0:T(8,128)S(1)}, f32[96,384]{1,0:T(8,128)S(1)}, f32[96,384]{1,0:T(8,128)S(1)}, /*index=5*/f32[96,384]{1,0:T(8,128)S(1)}) custom-call(s32[4,96]{1,0:T(4,128)} %bitcast.15, f32[512,384]{1,0:T(8,128)} %bitcast.14, f32[512,128]{1,0:T(8,128)} %bitcast.9), custom_call_target="tpu_custom_call" | custom-call | flops 301989888 | bytes 3145728 | tf_op jit(solution)/shard_map/pallas_call | solution.py:34
  2.4 3.0 %collective-permute-start = (f32[96,384]{1,0:T(8,128)S(1)}, f32[96,384]{1,0:T(8,128)S(1)}, u32[]{:S(2)}, u32[]{:S(2)}) collective-permute-start(f32[96,384]{1,0:T(8,128)S(1)} %get-tuple-element.71), channel_id=1, source_target_pairs={{0,16},{4,20},{8,24},{12,28},{16,0},{20,4},{24,8},{28,12},{1,17},{... | collective-permute-start | bytes 442376 | tf_op jit(solution)/shard_map/ppermute | solution.py:315
  5.4 0.6 collective-permute-start.1
  6.0 1.0 %collective-permute-start.2 = (f32[96,384]{1,0:T(8,128)S(1)}, f32[96,384]{1,0:T(8,128)S(1)}, u32[]{:S(2)}, u32[]{:S(2)}) collective-permute-start(f32[96,384]{1,0:T(8,128)S(1)} %get-tuple-element.73), channel_id=1, source_target_pairs={{0,4},{4,0},{8,12},{12,8},{16,20},{20,16},{24,28},{28,24},{1,5},{5... | collective-permute-start | bytes 442376 | tf_op jit(solution)/shard_map/ppermute | solution.py:315
  7.0 3.6 %collective-permute-start.4 = (f32[128,128]{1,0:T(8,128)S(1)}, f32[128,128]{1,0:T(8,128)S(1)}, u32[]{:S(2)}, u32[]{:S(2)}) collective-permute-start(f32[128,128]{1,0:T(8,128)S(1)} %get-tuple-element.76), channel_id=1, source_target_pairs={{0,3},{3,0},{1,2},{2,1},{4,7},{7,4},{5,6},{6,5},{8,11},{11,8},{9,1... | collective-permute-start | bytes 196616 | tf_op jit(solution)/shard_map/ppermute | solution.py:336
  10.6 1.6 %shard_map.78 = (bf16[512,512]{1,0:T(8,128)(2,1)S(1)}, bf16[512,512]{1,0:T(8,128)(2,1)S(1)}, bf16[512,128]{1,0:T(8,128)(2,1)S(1)}, bf16[512,128]{1,0:T(8,128)(2,...) custom-call(bf16[384,512]{1,0:T(8,128)(2,1)S(1)} %get-tuple-element., ...), custom_call_target="tpu_custom_call" | custom-call | flops 402653184 | bytes 4718592 | tf_op jit(solution)/shard_map/pallas_call | solution.py:34
  12.6 3.0 %collective-permute-start.3 = (f32[128,128]{1,0:T(8,128)S(1)}, f32[128,128]{1,0:T(8,128)S(1)}, u32[]{:S(2)}, u32[]{:S(2)}) collective-permute-start(f32[128,128]{1,0:T(8,128)S(1)} %get-tuple-element.75.refs_2_.refs_0_), channel_id=1, source_target_pairs={{0,3},{3,0},{1,2},{2,1},{4,7},{7,4},{5,6},{6,5},{8,11},{11,8},{9,1... | collective-permute-start | bytes 196616 | tf_op jit(solution)/shard_map/ppermute | solution.py:351
  15.6 0.9 %collective-permute-start.7 = (f32[128,128]{1,0:T(8,128)S(1)}, f32[128,128]{1,0:T(8,128)S(1)}, u32[]{:S(2)}, u32[]{:S(2)}) collective-permute-start(f32[128,128]{1,0:T(8,128)S(1)} %get-tuple-element.83.refs_0_), channel_id=1, source_target_pairs={{0,3},{3,0},{1,2},{2,1},{4,7},{7,4},{5,6},{6,5},{8,11},{11,8},{9,1... | collective-permute-start | bytes 196616 | tf_op jit(solution)/shard_map/ppermute | solution.py:351
  16.5 2.9 %collective-permute-start.6 = (f32[128,128]{1,0:T(8,128)S(1)}, f32[128,128]{1,0:T(8,128)S(1)}, u32[]{:S(2)}, u32[]{:S(2)}) collective-permute-start(f32[128,128]{1,0:T(8,128)S(1)} %get-tuple-element.82.refs_0_), channel_id=1, source_target_pairs={{0,3},{3,0},{1,2},{2,1},{4,7},{7,4},{5,6},{6,5},{8,11},{11,8},{9,1... | collective-permute-start | bytes 196616 | tf_op jit(solution)/shard_map/ppermute | solution.py:351
  19.9 2.1 %collective-permute-done.7.refs_1_ = f32[128,128]{1,0:T(8,128)S(1)} collective-permute-done((f32[128,128]{1,0:T(8,128)S(1)}, f32[128,128]{1,0:T(8,128)S(1)}, u32[]{:S(2)}, u32[]{:S(2)}) %collective-permute-start.7) | collective-permute-done | bytes 65568 | tf_op jit(solution)/shard_map/ppermute | solution.py:351
  22.3 1.7 %collective-permute-start.8 = (f32[128,128]{1,0:T(8,128)S(1)}, f32[128,128]{1,0:T(8,128)S(1)}, u32[]{:S(2)}, u32[]{:S(2)}) collective-permute-start(f32[128,128]{1,0:T(8,128)S(1)} %get-tuple-element.84.refs_4_), channel_id=1, source_target_pairs={{0,1},{1,0},{2,3},{3,2},{4,5},{5,4},{6,7},{7,6},{8,9},{9,8},{10,11... | collective-permute-start | bytes 196616 | tf_op jit(solution)/shard_map/ppermute | solution.py:361
  24.2 1.0 %collective-permute-start.9 = (f32[128,128]{1,0:T(8,128)S(1)}, f32[128,128]{1,0:T(8,128)S(1)}, u32[]{:S(2)}, u32[]{:S(2)}) collective-permute-start(f32[128,128]{1,0:T(8,128)S(1)} %get-tuple-element.85.refs_2_), channel_id=1, source_target_pairs={{0,1},{1,0},{2,3},{3,2},{4,5},{5,4},{6,7},{7,6},{8,9},{9,8},{10,11... | collective-permute-start | bytes 196616 | tf_op jit(solution)/shard_map/ppermute | solution.py:361
  25.2 1.3 %shard_map.84 = (bf16[512,512]{1,0:T(8,128)(2,1)S(1)}, bf16[512,512]{1,0:T(8,128)(2,1)S(1)}) custom-call(bf16[512,512]{1,0:T(8,128)(2,1)S(1)} %get-tuple-element.74.refs_6_.refs_0_, f32[512,512]{1,0:T(8,128)S(1)} %bitcast.11, f32[128,128]{1,0:T(8,128)S(1)} %get-tuple-element.85.refs_2_), custom_call_target="tpu_custom_call" | custom-call | flops 1073741824 | bytes 2359296 | tf_op jit(solution)/shard_map/pallas_call | solution.py:34
  26.5 1.0 %shard_map.85.refs_2_.refs_5_ = f32[512,384]{1,0:T(8,128)S(1)} custom-call(f32[512,384]{1,0:T(8,128)S(1)} %get-tuple-element.81.refs_0_.refs_3_.refs_4_, bf16[512,512]{1,0:T(8,128)(2,1)S(1)} %get-tuple-element.86.refs_1_.refs_6_, bf16[512,512]{1,0:T(8,128)(2,1)S(1)} %get-tuple-element.87.refs_2_, f32[96,384]{1,0:T(8,128)S(1)} %collective-permute-done.refs_3_, ...), custom_call_target="tpu_custom_call" | custom-call | flops 603979776 | bytes 2359296 | tf_op jit(solution)/shard_map/pallas_call | solution.py:34
  28.8 0.5 collective-permute-start.10
  29.8 1.9 %collective-permute-start.12 = (f32[96,384]{1,0:T(8,128)S(1)}, f32[96,384]{1,0:T(8,128)S(1)}, u32[]{:S(2)}, u32[]{:S(2)}) collective-permute-start(f32[96,384]{1,0:T(8,128)S(1)} %get-tuple-element.99), channel_id=1, source_target_pairs={{0,4},{4,0},{8,12},{12,8},{16,20},{20,16},{24,28},{28,24},{1,5},{5... | collective-permute-start | bytes 442376 | tf_op jit(solution)/shard_map/ppermute | solution.py:315
  31.7 1.3 %shard_map.89 = (bf16[512,512]{1,0:T(8,128)(2,1)S(1)}, bf16[512,512]{1,0:T(8,128)(2,1)S(1)}) custom-call(bf16[512,512]{1,0:T(8,128)(2,1)S(1)} %get-tuple-element.74.refs_6_.refs_0_, bf16[512,512]{1,0:T(8,128)(2,1)S(1)} %get-tuple-element.67.refs_1_.refs_0_, f32[512,512]{1,0:T(8,128)S(1)} %bitcast.12, f32[512,128]{1,0:T(8,128)S(1)} %get-tuple-element.92.refs_3_.refs_2_), custom_call_target="tpu_custom_call" | custom-call | flops 1073741824 | bytes 2359296 | tf_op jit(solution)/shard_map/pallas_call | solution.py:34
  33.0 1.0 %shard_map.90 = (f32[512,384]{1,0:T(8,128)S(1)}, f32[512,384]{1,0:T(8,128)S(1)}) custom-call(f32[512,128]{1,0:T(8,128)S(1)} %shard_map.86.refs_5_.refs_0_, f32[512,128]{1,0:T(8,128)S(1)} %shard_map.87.refs_6_.refs_7_.refs_1_, f32[512,128]{1,0:T(8,128)S(1)} %get-tuple-element.92.refs_3_.refs_2_, f32[512,384]{1,0:T(8,128)S(1)} %get-tuple-element.81.refs_0_.refs_3_.refs_4_, ...), custom_call_target="tpu_custom_call" | custom-call | flops 603979776 | bytes 3145728 | tf_op jit(solution)/shard_map/pallas_call | solution.py:34
  34.0 0.9 %collective-permute-done.10.refs_3_.refs_4_ = f32[96,384]{1,0:T(8,128)S(1)} collective-permute-done((f32[96,384]{1,0:T(8,128)S(1)}, f32[96,384]{1,0:T(8,128)S(1)}, u32[]{:S(2)}, u32[]{:S(2)}) %collective-permute-start.10) | collective-permute-done | bytes 147488 | tf_op jit(solution)/shard_map/ppermute | solution.py:315
  34.8 1.5 %collective-permute-done.11.refs_4_.refs_5_ = f32[96,384]{1,0:T(8,128)S(1)} collective-permute-done((f32[96,384]{1,0:T(8,128)S(1)}, f32[96,384]{1,0:T(8,128)S(1)}, u32[]{:S(2)}, u32[]{:S(2)}) %collective-permute-start.11) | collective-permute-done | bytes 147488 | tf_op jit(solution)/shard_map/ppermute | solution.py:315
  36.3 0.6 shard_map.91
  36.9 1.5 %collective-permute-start.13 = (f32[96,384]{1,0:T(8,128)S(1)}, f32[96,384]{1,0:T(8,128)S(1)}, u32[]{:S(2)}, u32[]{:S(2)}) collective-permute-start(f32[96,384]{1,0:T(8,128)S(1)} %get-tuple-element.100.refs_7_.refs_12_), channel_id=1, source_target_pairs={{0,16},{4,20},{8,24},{12,28},{16,0},{20,4},{24,8},{28,12},{1,17},{... | collective-permute-start | bytes 442376 | tf_op jit(solution)/shard_map/ppermute | solution.py:315
  38.8 0.9 %shard_map.92 = (f32[128,384]{1,0:T(8,128)S(1)}, f32[512,384]{1,0:T(8,128)S(1)}, f32[512,384]{1,0:T(8,128)S(1)}) custom-call(f32[512,384]{1,0:T(8,128)S(1)} %get-tuple-element.95.refs_0_.refs_6_, f32[512,384]{1,0:T(8,128)S(1)} %get-tuple-element.96.refs_1_, bf16[512,512]{1,0:T(8,128)(2,1)S(1)} %get-tuple-element.93.refs_4_.refs_6_.refs_1_.refs_2_.refs_5_, ...), custom_call_target="tpu_custom_call" | custom-call | flops 301989888 | bytes 3145728 | tf_op jit(solution)/shard_map/pallas_call | solution.py:34
  39.6 3.3 %collective-permute-done.13.refs_3_ = f32[96,384]{1,0:T(8,128)S(1)} collective-permute-done((f32[96,384]{1,0:T(8,128)S(1)}, f32[96,384]{1,0:T(8,128)S(1)}, u32[]{:S(2)}, u32[]{:S(2)}) %collective-permute-start.13) | collective-permute-done | bytes 147488 | tf_op jit(solution)/shard_map/ppermute | solution.py:315
  42.9 1.4 %collective-permute-done.14.refs_4_ = f32[96,384]{1,0:T(8,128)S(1)} collective-permute-done((f32[96,384]{1,0:T(8,128)S(1)}, f32[96,384]{1,0:T(8,128)S(1)}, u32[]{:S(2)}, u32[]{:S(2)}) %collective-permute-start.14) | collective-permute-done | bytes 147488 | tf_op jit(solution)/shard_map/ppermute | solution.py:315
  44.7 2.1 %collective-permute-start.16 = (f32[128,128]{1,0:T(8,128)S(1)}, f32[128,128]{1,0:T(8,128)S(1)}, u32[]{:S(2)}, u32[]{:S(2)}) collective-permute-start(f32[128,128]{1,0:T(8,128)S(1)} %get-tuple-element.104.refs_0_.refs_4_), channel_id=1, source_target_pairs={{0,3},{3,0},{1,2},{2,1},{4,7},{7,4},{5,6},{6,5},{8,11},{11,8},{9,1... | collective-permute-start | bytes 196616 | tf_op jit(solution)/shard_map/ppermute | solution.py:351
  46.8 1.8 %collective-permute-start.19 = (f32[128,128]{1,0:T(8,128)S(1)}, f32[128,128]{1,0:T(8,128)S(1)}, u32[]{:S(2)}, u32[]{:S(2)}) collective-permute-start(f32[128,128]{1,0:T(8,128)S(1)} %get-tuple-element.109.refs_0_), channel_id=1, source_target_pairs={{0,3},{3,0},{1,2},{2,1},{4,7},{7,4},{5,6},{6,5},{8,11},{11,8},{9,1... | collective-permute-start | bytes 196616 | tf_op jit(solution)/shard_map/ppermute | solution.py:351
  48.6 2.0 %collective-permute-start.18 = (f32[128,128]{1,0:T(8,128)S(1)}, f32[128,128]{1,0:T(8,128)S(1)}, u32[]{:S(2)}, u32[]{:S(2)}) collective-permute-start(f32[128,128]{1,0:T(8,128)S(1)} %get-tuple-element.108.refs_0_), channel_id=1, source_target_pairs={{0,3},{3,0},{1,2},{2,1},{4,7},{7,4},{5,6},{6,5},{8,11},{11,8},{9,1... | collective-permute-start | bytes 196616 | tf_op jit(solution)/shard_map/ppermute | solution.py:351
  50.6 1.0 %collective-permute-done.16.refs_1_ = f32[128,128]{1,0:T(8,128)S(1)} collective-permute-done((f32[128,128]{1,0:T(8,128)S(1)}, f32[128,128]{1,0:T(8,128)S(1)}, u32[]{:S(2)}, u32[]{:S(2)}) %collective-permute-start.16) | collective-permute-done | bytes 65568 | tf_op jit(solution)/shard_map/ppermute | solution.py:351
  52.0 1.7 %collective-permute-done.19.refs_1_ = f32[128,128]{1,0:T(8,128)S(1)} collective-permute-done((f32[128,128]{1,0:T(8,128)S(1)}, f32[128,128]{1,0:T(8,128)S(1)}, u32[]{:S(2)}, u32[]{:S(2)}) %collective-permute-start.19) | collective-permute-done | bytes 65568 | tf_op jit(solution)/shard_map/ppermute | solution.py:351
  53.9 1.0 %collective-permute-start.20 = (f32[128,128]{1,0:T(8,128)S(1)}, f32[128,128]{1,0:T(8,128)S(1)}, u32[]{:S(2)}, u32[]{:S(2)}) collective-permute-start(f32[128,128]{1,0:T(8,128)S(1)} %get-tuple-element.110.refs_4_), channel_id=1, source_target_pairs={{0,1},{1,0},{2,3},{3,2},{4,5},{5,4},{6,7},{7,6},{8,9},{9,8},{10,11... | collective-permute-start | bytes 196616 | tf_op jit(solution)/shard_map/ppermute | solution.py:361
  54.8 0.5 collective-permute-done.18.refs_1_
  55.6 0.7 collective-permute-start.21
  56.3 1.0 %shard_map.97.refs_2_.refs_5_ = f32[512,384]{1,0:T(8,128)S(1)} custom-call(f32[512,384]{1,0:T(8,128)S(1)} %get-tuple-element.107.refs_0_, bf16[512,512]{1,0:T(8,128)(2,1)S(1)} %get-tuple-element.86.refs_1_.refs_6_, bf16[512,512]{1,0:T(8,128)(2,1)S(1)} %get-tuple-element.87.refs_2_, f32[96,384]{1,0:T(8,128)S(1)} %collective-permute-done.13.refs_3_, ...), custom_call_target="tpu_custom_call" | custom-call | flops 603979776 | bytes 2359296 | tf_op jit(solution)/shard_map/pallas_call | solution.py:34
  57.6 0.7 collective-permute-done.20.refs_1_
  58.5 1.4 %collective-permute-done.21.refs_1_ = f32[128,128]{1,0:T(8,128)S(1)} collective-permute-done((f32[128,128]{1,0:T(8,128)S(1)}, f32[128,128]{1,0:T(8,128)S(1)}, u32[]{:S(2)}, u32[]{:S(2)}) %collective-permute-start.21) | collective-permute-done | bytes 65568 | tf_op jit(solution)/shard_map/ppermute | solution.py:361
  60.2 0.8 %collective-permute-start.22 = (f32[96,384]{1,0:T(8,128)S(1)}, f32[96,384]{1,0:T(8,128)S(1)}, u32[]{:S(2)}, u32[]{:S(2)}) collective-permute-start(f32[96,384]{1,0:T(8,128)S(1)} %get-tuple-element.118), channel_id=1, source_target_pairs={{0,16},{4,20},{8,24},{12,28},{16,0},{20,4},{24,8},{28,12},{1,17},{... | collective-permute-start | bytes 442376 | tf_op jit(solution)/shard_map/ppermute | solution.py:315
  61.0 1.9 %collective-permute-start.24 = (f32[96,384]{1,0:T(8,128)S(1)}, f32[96,384]{1,0:T(8,128)S(1)}, u32[]{:S(2)}, u32[]{:S(2)}) collective-permute-start(f32[96,384]{1,0:T(8,128)S(1)} %get-tuple-element.120), channel_id=1, source_target_pairs={{0,4},{4,0},{8,12},{12,8},{16,20},{20,16},{24,28},{28,24},{1,5},{5... | collective-permute-start | bytes 442376 | tf_op jit(solution)/shard_map/ppermute | solution.py:315
  62.9 1.2 %shard_map.101 = (f32[512,384]{1,0:T(8,128)S(1)}, f32[512,384]{1,0:T(8,128)S(1)}) custom-call(f32[512,128]{1,0:T(8,128)S(1)} %shard_map.98.refs_5_.refs_0_, f32[512,128]{1,0:T(8,128)S(1)} %shard_map.99.refs_6_.refs_7_.refs_1_, f32[512,128]{1,0:T(8,128)S(1)} %get-tuple-element.114.refs_2_.refs_7_, f32[512,384]{1,0:T(8,128)S(1)} %get-tuple-element.115.refs_3_, ...), custom_call_target="tpu_custom_call" | custom-call | flops 603979776 | bytes 3145728 | tf_op jit(solution)/shard_map/pallas_call | solution.py:34
  64.0 1.9 %collective-permute-done.22.refs_3_.refs_4_ = f32[96,384]{1,0:T(8,128)S(1)} collective-permute-done((f32[96,384]{1,0:T(8,128)S(1)}, f32[96,384]{1,0:T(8,128)S(1)}, u32[]{:S(2)}, u32[]{:S(2)}) %collective-permute-start.22) | collective-permute-done | bytes 147488 | tf_op jit(solution)/shard_map/ppermute | solution.py:315
  65.9 2.1 %collective-permute-done.23.refs_4_.refs_5_ = f32[96,384]{1,0:T(8,128)S(1)} collective-permute-done((f32[96,384]{1,0:T(8,128)S(1)}, f32[96,384]{1,0:T(8,128)S(1)}, u32[]{:S(2)}, u32[]{:S(2)}) %collective-permute-start.23) | collective-permute-done | bytes 147488 | tf_op jit(solution)/shard_map/ppermute | solution.py:315
  68.0 0.6 shard_map.102
  68.6 1.0 %collective-permute-start.25 = (f32[96,384]{1,0:T(8,128)S(1)}, f32[96,384]{1,0:T(8,128)S(1)}, u32[]{:S(2)}, u32[]{:S(2)}) collective-permute-start(f32[96,384]{1,0:T(8,128)S(1)} %get-tuple-element.121.refs_7_.refs_10_), channel_id=1, source_target_pairs={{0,16},{4,20},{8,24},{12,28},{16,0},{20,4},{24,8},{28,12},{1,17},{... | collective-permute-start | bytes 442376 | tf_op jit(solution)/shard_map/ppermute | solution.py:315
  69.9 0.5 shard_map.103
  70.4 1.6 %shard_map.104 = (f32[512,384]{1,0:T(8,128)S(1)}, f32[512,384]{1,0:T(8,128)}) custom-call(bf16[512,512]{1,0:T(8,128)(2,1)S(1)} %get-tuple-element.67.refs_1_.refs_0_, f32[512,384]{1,0:T(8,128)S(1)} %get-tuple-element.124.refs_1_, f32[512,384]{1,0:T(8,128)S(1)} %get-tuple-element.125.refs_2_.refs_3_, f32[512,384]{1,0:T(8,128)S(1)} %get-tuple-element.125.refs_2_.refs_3_), custom_call_target="tpu_custom_call" | custom-call | flops 805306368 | bytes 1966080 | tf_op jit(solution)/shard_map/pallas_call | solution.py:34
  72.0 2.1 %collective-permute-done.25.refs_2_ = f32[96,384]{1,0:T(8,128)S(1)} collective-permute-done((f32[96,384]{1,0:T(8,128)S(1)}, f32[96,384]{1,0:T(8,128)S(1)}, u32[]{:S(2)}, u32[]{:S(2)}) %collective-permute-start.25) | collective-permute-done | bytes 147488 | tf_op jit(solution)/shard_map/ppermute | solution.py:315
  74.1 1.3 %collective-permute-done.26.refs_3_ = f32[96,384]{1,0:T(8,128)S(1)} collective-permute-done((f32[96,384]{1,0:T(8,128)S(1)}, f32[96,384]{1,0:T(8,128)S(1)}, u32[]{:S(2)}, u32[]{:S(2)}) %collective-permute-start.26) | collective-permute-done | bytes 147488 | tf_op jit(solution)/shard_map/ppermute | solution.py:315
  75.4 1.5 %shard_map.105 = f32[512,384]{1,0:T(8,128)} custom-call(bf16[512,512]{1,0:T(8,128)(2,1)S(1)} %get-tuple-element.67.refs_1_.refs_0_, f32[512,384]{1,0:T(8,128)S(1)} %get-tuple-element.127.refs_1_.refs_5_, f32[96,384]{1,0:T(8,128)S(1)} %collective-permute-done.25.refs_2_, f32[96,384]{1,0:T(8,128)S(1)} %collective-permute-done.26.refs_3_, ...), custom_call_target="tpu_custom_call" | custom-call | flops 402653184 | bytes 1966080 | tf_op jit(solution)/shard_map/pallas_call | solution.py:34
  (45 shorter events, 5.7 us)
Async XLA Ops:
  0.6 10.0 %copy-start = (f32[1,1,512,128]{3,2,1,0:T(8,128)S(1)}, f32[1,1,512,128]{3,2,1,0:T(8,128)}, u32[]{:S(2)}) copy-start(f32[1,1,512,128]{3,2,1,0:T(8,128)} %param.9) | copy-start | bytes 786436
  2.4 9.8 %collective-permute-start = (f32[96,384]{1,0:T(8,128)S(1)}, f32[96,384]{1,0:T(8,128)S(1)}, u32[]{:S(2)}, u32[]{:S(2)}) collective-permute-start(f32[96,384]{1,0:T(8,128)S(1)} %get-tuple-element.71), channel_id=1, source_target_pairs={{0,16},{4,20},{8,24},{12,28},{16,0},{20,4},{24,8},{28,12},{1,17},{... | collective-permute-start | bytes 442376 | tf_op jit(solution)/shard_map/ppermute | solution.py:315
  5.4 6.8 %collective-permute-start.1 = (f32[96,384]{1,0:T(8,128)S(1)}, f32[96,384]{1,0:T(8,128)S(1)}, u32[]{:S(2)}, u32[]{:S(2)}) collective-permute-start(f32[96,384]{1,0:T(8,128)S(1)} %get-tuple-element.72), channel_id=1, source_target_pairs={{0,28},{4,8},{8,4},{12,16},{16,12},{20,24},{24,20},{28,0},{1,29},{... | collective-permute-start | bytes 442376 | tf_op jit(solution)/shard_map/ppermute | solution.py:315
  6.0 6.2 %collective-permute-start.2 = (f32[96,384]{1,0:T(8,128)S(1)}, f32[96,384]{1,0:T(8,128)S(1)}, u32[]{:S(2)}, u32[]{:S(2)}) collective-permute-start(f32[96,384]{1,0:T(8,128)S(1)} %get-tuple-element.73), channel_id=1, source_target_pairs={{0,4},{4,0},{8,12},{12,8},{16,20},{20,16},{24,28},{28,24},{1,5},{5... | collective-permute-start | bytes 442376 | tf_op jit(solution)/shard_map/ppermute | solution.py:315
  7.0 12.4 %collective-permute-start.4 = (f32[128,128]{1,0:T(8,128)S(1)}, f32[128,128]{1,0:T(8,128)S(1)}, u32[]{:S(2)}, u32[]{:S(2)}) collective-permute-start(f32[128,128]{1,0:T(8,128)S(1)} %get-tuple-element.76), channel_id=1, source_target_pairs={{0,3},{3,0},{1,2},{2,1},{4,7},{7,4},{5,6},{6,5},{8,11},{11,8},{9,1... | collective-permute-start | bytes 196616 | tf_op jit(solution)/shard_map/ppermute | solution.py:336
  12.2 7.2 %copy-start.1 = (f32[1,512,128]{2,1,0:T(8,128)S(1)}, f32[1,512,128]{2,1,0:T(8,128)}, u32[]{:S(2)}) copy-start(f32[1,512,128]{2,1,0:T(8,128)} %param.10) | copy-start | bytes 786436
  12.6 12.6 %copy-start.2 = (f32[1,1,512,512]{3,2,1,0:T(8,128)S(1)}, f32[1,1,512,512]{3,2,1,0:T(8,128)}, u32[]{:S(2)}) copy-start(f32[1,1,512,512]{3,2,1,0:T(8,128)} %param.8) | copy-start | bytes 3145732
  12.6 6.9 %collective-permute-start.3 = (f32[128,128]{1,0:T(8,128)S(1)}, f32[128,128]{1,0:T(8,128)S(1)}, u32[]{:S(2)}, u32[]{:S(2)}) collective-permute-start(f32[128,128]{1,0:T(8,128)S(1)} %get-tuple-element.75.refs_2_.refs_0_), channel_id=1, source_target_pairs={{0,3},{3,0},{1,2},{2,1},{4,7},{7,4},{5,6},{6,5},{8,11},{11,8},{9,1... | collective-permute-start | bytes 196616 | tf_op jit(solution)/shard_map/ppermute | solution.py:351
  15.6 6.4 %collective-permute-start.7 = (f32[128,128]{1,0:T(8,128)S(1)}, f32[128,128]{1,0:T(8,128)S(1)}, u32[]{:S(2)}, u32[]{:S(2)}) collective-permute-start(f32[128,128]{1,0:T(8,128)S(1)} %get-tuple-element.83.refs_0_), channel_id=1, source_target_pairs={{0,3},{3,0},{1,2},{2,1},{4,7},{7,4},{5,6},{6,5},{8,11},{11,8},{9,1... | collective-permute-start | bytes 196616 | tf_op jit(solution)/shard_map/ppermute | solution.py:351
  16.5 7.5 %collective-permute-start.6 = (f32[128,128]{1,0:T(8,128)S(1)}, f32[128,128]{1,0:T(8,128)S(1)}, u32[]{:S(2)}, u32[]{:S(2)}) collective-permute-start(f32[128,128]{1,0:T(8,128)S(1)} %get-tuple-element.82.refs_0_), channel_id=1, source_target_pairs={{0,3},{3,0},{1,2},{2,1},{4,7},{7,4},{5,6},{6,5},{8,11},{11,8},{9,1... | collective-permute-start | bytes 196616 | tf_op jit(solution)/shard_map/ppermute | solution.py:351
  19.8 7.7 %collective-permute-start.5 = (f32[128,128]{1,0:T(8,128)S(1)}, f32[128,128]{1,0:T(8,128)S(1)}, u32[]{:S(2)}, u32[]{:S(2)}) collective-permute-start(f32[128,128]{1,0:T(8,128)S(1)} %get-tuple-element.80.refs_4_), channel_id=1, source_target_pairs={{0,1},{1,0},{2,3},{3,2},{4,5},{5,4},{6,7},{7,6},{8,9},{9,8},{10,11... | collective-permute-start | bytes 196616 | tf_op jit(solution)/shard_map/ppermute | solution.py:361
  22.3 5.5 %collective-permute-start.8 = (f32[128,128]{1,0:T(8,128)S(1)}, f32[128,128]{1,0:T(8,128)S(1)}, u32[]{:S(2)}, u32[]{:S(2)}) collective-permute-start(f32[128,128]{1,0:T(8,128)S(1)} %get-tuple-element.84.refs_4_), channel_id=1, source_target_pairs={{0,1},{1,0},{2,3},{3,2},{4,5},{5,4},{6,7},{7,6},{8,9},{9,8},{10,11... | collective-permute-start | bytes 196616 | tf_op jit(solution)/shard_map/ppermute | solution.py:361
  24.2 4.3 %collective-permute-start.9 = (f32[128,128]{1,0:T(8,128)S(1)}, f32[128,128]{1,0:T(8,128)S(1)}, u32[]{:S(2)}, u32[]{:S(2)}) collective-permute-start(f32[128,128]{1,0:T(8,128)S(1)} %get-tuple-element.85.refs_2_), channel_id=1, source_target_pairs={{0,1},{1,0},{2,3},{3,2},{4,5},{5,4},{6,7},{7,6},{8,9},{9,8},{10,11... | collective-permute-start | bytes 196616 | tf_op jit(solution)/shard_map/ppermute | solution.py:361
  28.1 3.6 %copy-start.3 = (f32[1,1,512,512]{3,2,1,0:T(8,128)S(1)}, f32[1,1,512,512]{3,2,1,0:T(8,128)}, u32[]{:S(2)}) copy-start(f32[1,1,512,512]{3,2,1,0:T(8,128)} %param.7) | copy-start | bytes 3145732
  28.8 6.0 %collective-permute-start.10 = (f32[96,384]{1,0:T(8,128)S(1)}, f32[96,384]{1,0:T(8,128)S(1)}, u32[]{:S(2)}, u32[]{:S(2)}) collective-permute-start(f32[96,384]{1,0:T(8,128)S(1)} %get-tuple-element.97), channel_id=1, source_target_pairs={{0,16},{4,20},{8,24},{12,28},{16,0},{20,4},{24,8},{28,12},{1,17},{... | collective-permute-start | bytes 442376 | tf_op jit(solution)/shard_map/ppermute | solution.py:315
  29.3 7.0 %collective-permute-start.11 = (f32[96,384]{1,0:T(8,128)S(1)}, f32[96,384]{1,0:T(8,128)S(1)}, u32[]{:S(2)}, u32[]{:S(2)}) collective-permute-start(f32[96,384]{1,0:T(8,128)S(1)} %get-tuple-element.98), channel_id=1, source_target_pairs={{0,28},{4,8},{8,4},{12,16},{16,12},{20,24},{24,20},{28,0},{1,29},{... | collective-permute-start | bytes 442376 | tf_op jit(solution)/shard_map/ppermute | solution.py:315
  29.8 6.5 %collective-permute-start.12 = (f32[96,384]{1,0:T(8,128)S(1)}, f32[96,384]{1,0:T(8,128)S(1)}, u32[]{:S(2)}, u32[]{:S(2)}) collective-permute-start(f32[96,384]{1,0:T(8,128)S(1)} %get-tuple-element.99), channel_id=1, source_target_pairs={{0,4},{4,0},{8,12},{12,8},{16,20},{20,16},{24,28},{28,24},{1,5},{5... | collective-permute-start | bytes 442376 | tf_op jit(solution)/shard_map/ppermute | solution.py:315
  36.9 6.0 %collective-permute-start.13 = (f32[96,384]{1,0:T(8,128)S(1)}, f32[96,384]{1,0:T(8,128)S(1)}, u32[]{:S(2)}, u32[]{:S(2)}) collective-permute-start(f32[96,384]{1,0:T(8,128)S(1)} %get-tuple-element.100.refs_7_.refs_12_), channel_id=1, source_target_pairs={{0,16},{4,20},{8,24},{12,28},{16,0},{20,4},{24,8},{28,12},{1,17},{... | collective-permute-start | bytes 442376 | tf_op jit(solution)/shard_map/ppermute | solution.py:315
  38.4 6.0 %collective-permute-start.14 = (f32[96,384]{1,0:T(8,128)S(1)}, f32[96,384]{1,0:T(8,128)S(1)}, u32[]{:S(2)}, u32[]{:S(2)}) collective-permute-start(f32[96,384]{1,0:T(8,128)S(1)} %get-tuple-element.101.refs_8_), channel_id=1, source_target_pairs={{0,28},{4,8},{8,4},{12,16},{16,12},{20,24},{24,20},{28,0},{1,29},{... | collective-permute-start | bytes 442376 | tf_op jit(solution)/shard_map/ppermute | solution.py:315
  38.4 6.0 %collective-permute-start.15 = (f32[96,384]{1,0:T(8,128)S(1)}, f32[96,384]{1,0:T(8,128)S(1)}, u32[]{:S(2)}, u32[]{:S(2)}) collective-permute-start(f32[96,384]{1,0:T(8,128)S(1)} %get-tuple-element.102.refs_9_), channel_id=1, source_target_pairs={{0,4},{4,0},{8,12},{12,8},{16,20},{20,16},{24,28},{28,24},{1,5},{5... | collective-permute-start | bytes 442376 | tf_op jit(solution)/shard_map/ppermute | solution.py:315
  44.7 6.9 %collective-permute-start.16 = (f32[128,128]{1,0:T(8,128)S(1)}, f32[128,128]{1,0:T(8,128)S(1)}, u32[]{:S(2)}, u32[]{:S(2)}) collective-permute-start(f32[128,128]{1,0:T(8,128)S(1)} %get-tuple-element.104.refs_0_.refs_4_), channel_id=1, source_target_pairs={{0,3},{3,0},{1,2},{2,1},{4,7},{7,4},{5,6},{6,5},{8,11},{11,8},{9,1... | collective-permute-start | bytes 196616 | tf_op jit(solution)/shard_map/ppermute | solution.py:351
  46.8 6.8 %collective-permute-start.19 = (f32[128,128]{1,0:T(8,128)S(1)}, f32[128,128]{1,0:T(8,128)S(1)}, u32[]{:S(2)}, u32[]{:S(2)}) collective-permute-start(f32[128,128]{1,0:T(8,128)S(1)} %get-tuple-element.109.refs_0_), channel_id=1, source_target_pairs={{0,3},{3,0},{1,2},{2,1},{4,7},{7,4},{5,6},{6,5},{8,11},{11,8},{9,1... | collective-permute-start | bytes 196616 | tf_op jit(solution)/shard_map/ppermute | solution.py:351
  48.6 6.7 %collective-permute-start.18 = (f32[128,128]{1,0:T(8,128)S(1)}, f32[128,128]{1,0:T(8,128)S(1)}, u32[]{:S(2)}, u32[]{:S(2)}) collective-permute-start(f32[128,128]{1,0:T(8,128)S(1)} %get-tuple-element.108.refs_0_), channel_id=1, source_target_pairs={{0,3},{3,0},{1,2},{2,1},{4,7},{7,4},{5,6},{6,5},{8,11},{11,8},{9,1... | collective-permute-start | bytes 196616 | tf_op jit(solution)/shard_map/ppermute | solution.py:351
  51.9 5.4 %collective-permute-start.17 = (f32[128,128]{1,0:T(8,128)S(1)}, f32[128,128]{1,0:T(8,128)S(1)}, u32[]{:S(2)}, u32[]{:S(2)}) collective-permute-start(f32[128,128]{1,0:T(8,128)S(1)} %get-tuple-element.106.refs_4_), channel_id=1, source_target_pairs={{0,1},{1,0},{2,3},{3,2},{4,5},{5,4},{6,7},{7,6},{8,9},{9,8},{10,11... | collective-permute-start | bytes 196616 | tf_op jit(solution)/shard_map/ppermute | solution.py:361
  53.9 4.3 %collective-permute-start.20 = (f32[128,128]{1,0:T(8,128)S(1)}, f32[128,128]{1,0:T(8,128)S(1)}, u32[]{:S(2)}, u32[]{:S(2)}) collective-permute-start(f32[128,128]{1,0:T(8,128)S(1)} %get-tuple-element.110.refs_4_), channel_id=1, source_target_pairs={{0,1},{1,0},{2,3},{3,2},{4,5},{5,4},{6,7},{7,6},{8,9},{9,8},{10,11... | collective-permute-start | bytes 196616 | tf_op jit(solution)/shard_map/ppermute | solution.py:361
  55.6 4.3 %collective-permute-start.21 = (f32[128,128]{1,0:T(8,128)S(1)}, f32[128,128]{1,0:T(8,128)S(1)}, u32[]{:S(2)}, u32[]{:S(2)}) collective-permute-start(f32[128,128]{1,0:T(8,128)S(1)} %get-tuple-element.111.refs_6_), channel_id=1, source_target_pairs={{0,1},{1,0},{2,3},{3,2},{4,5},{5,4},{6,7},{7,6},{8,9},{9,8},{10,11... | collective-permute-start | bytes 196616 | tf_op jit(solution)/shard_map/ppermute | solution.py:361
  60.2 5.7 %collective-permute-start.22 = (f32[96,384]{1,0:T(8,128)S(1)}, f32[96,384]{1,0:T(8,128)S(1)}, u32[]{:S(2)}, u32[]{:S(2)}) collective-permute-start(f32[96,384]{1,0:T(8,128)S(1)} %get-tuple-element.118), channel_id=1, source_target_pairs={{0,16},{4,20},{8,24},{12,28},{16,0},{20,4},{24,8},{28,12},{1,17},{... | collective-permute-start | bytes 442376 | tf_op jit(solution)/shard_map/ppermute | solution.py:315
  61.0 7.0 %collective-permute-start.23 = (f32[96,384]{1,0:T(8,128)S(1)}, f32[96,384]{1,0:T(8,128)S(1)}, u32[]{:S(2)}, u32[]{:S(2)}) collective-permute-start(f32[96,384]{1,0:T(8,128)S(1)} %get-tuple-element.119), channel_id=1, source_target_pairs={{0,28},{4,8},{8,4},{12,16},{16,12},{20,24},{24,20},{28,0},{1,29},{... | collective-permute-start | bytes 442376 | tf_op jit(solution)/shard_map/ppermute | solution.py:315
  61.0 7.0 %collective-permute-start.24 = (f32[96,384]{1,0:T(8,128)S(1)}, f32[96,384]{1,0:T(8,128)S(1)}, u32[]{:S(2)}, u32[]{:S(2)}) collective-permute-start(f32[96,384]{1,0:T(8,128)S(1)} %get-tuple-element.120), channel_id=1, source_target_pairs={{0,4},{4,0},{8,12},{12,8},{16,20},{20,16},{24,28},{28,24},{1,5},{5... | collective-permute-start | bytes 442376 | tf_op jit(solution)/shard_map/ppermute | solution.py:315
  68.6 5.5 %collective-permute-start.25 = (f32[96,384]{1,0:T(8,128)S(1)}, f32[96,384]{1,0:T(8,128)S(1)}, u32[]{:S(2)}, u32[]{:S(2)}) collective-permute-start(f32[96,384]{1,0:T(8,128)S(1)} %get-tuple-element.121.refs_7_.refs_10_), channel_id=1, source_target_pairs={{0,16},{4,20},{8,24},{12,28},{16,0},{20,4},{24,8},{28,12},{1,17},{... | collective-permute-start | bytes 442376 | tf_op jit(solution)/shard_map/ppermute | solution.py:315
  69.6 5.8 %collective-permute-start.26 = (f32[96,384]{1,0:T(8,128)S(1)}, f32[96,384]{1,0:T(8,128)S(1)}, u32[]{:S(2)}, u32[]{:S(2)}) collective-permute-start(f32[96,384]{1,0:T(8,128)S(1)} %get-tuple-element.122.refs_8_), channel_id=1, source_target_pairs={{0,28},{4,8},{8,4},{12,16},{16,12},{20,24},{24,20},{28,0},{1,29},{... | collective-permute-start | bytes 442376 | tf_op jit(solution)/shard_map/ppermute | solution.py:315
  69.6 5.8 %collective-permute-start.27 = (f32[96,384]{1,0:T(8,128)S(1)}, f32[96,384]{1,0:T(8,128)S(1)}, u32[]{:S(2)}, u32[]{:S(2)}) collective-permute-start(f32[96,384]{1,0:T(8,128)S(1)} %get-tuple-element.123.refs_9_), channel_id=1, source_target_pairs={{0,4},{4,0},{8,12},{12,8},{16,20},{20,16},{24,28},{28,24},{1,5},{5... | collective-permute-start | bytes 442376 | tf_op jit(solution)/shard_map/ppermute | solution.py:315

commit v8 on v5

--- a/solution.py
+++ b/solution.py
@@ -56,6 +56,14 @@
 
 def dot3(left, right):
     return dot(left[0], right[0]) + (dot(left[0], right[1]) + dot(left[1], right[0]))
+
+
+def join_left(halves):
+    return jnp.concatenate([halves[0], halves[0], halves[1]], axis=1)
+
+
+def join_right(halves):
+    return jnp.concatenate([halves[0], halves[1], halves[0]], axis=0)
 
 
 def pick(chooser, value):
@@ -132,8 +140,8 @@
     sent_copy.wait()
 
 
-def order_body(subs, listed_ref, load_ref, basis_ref,
-               chooser_ref, flipped_ref, basis_high, basis_low, test_high, test_low, ahead_ref, ordered_ref):
+def order_body(subs, count, listed_ref, load_ref, basis_ref, chooser_ref, flipped_ref, twice_ref,
+               basis_wide, test_high, test_low, test_wide, ahead_ref, ordered_ref):
     listed, total = listed_ref.shape
     first = listed_ref[...].astype(f32)
     unlisted = 1.0 - jnp.sum(first, axis=0, keepdims=True)
@@ -151,10 +159,14 @@
     chooser_ref[...] = chooser
     ordered = pick(chooser, load_ref[...])
     ordered_ref[...] = ordered
-    for part, out, turned in zip(split(basis_ref[...]), (basis_high, basis_low), (test_high, test_low)):
-        placed = dot(weighted, part)
-        out[...] = placed.astype(bf16)
-        turned[...] = placed.T.astype(bf16)
+    size = count * listed // 4
+    shared = flipped_ref[:, :size]
+    twice_ref[...] = jnp.concatenate([shared, shared], axis=1)
+    placed = [dot(weighted, part) for part in split(basis_ref[...])]
+    basis_wide[...] = join_left([part.astype(bf16) for part in placed])
+    for part, turned in zip(placed, (test_high, test_low)):
+        turned[...] = part.T.astype(bf16)
+    test_wide[...] = join_left([test_high[:, :size], test_low[:, :size]])
     ahead_ref[...] = dot3((test_high[...], test_low[...]), split(ordered))
 
 
@@ -175,10 +187,12 @@
         out[...] = dot(dot(weighted, part).astype(bf16), weighted, NT).astype(bf16)
 
 
-def schur_body(chooser_ref, flipped_ref, schur_ref, schur_high, schur_low):
+def schur_body(chooser_ref, flipped_ref, schur_ref, schur_high, schur_low, schur_wide):
     chooser, flipped = chooser_ref[...], flipped_ref[...]
+    size = schur_wide.shape[0]
     for part, out in zip(split(schur_ref[...]), (schur_high, schur_low)):
         out[...] = dot(dot(chooser, part).astype(bf16), flipped).astype(bf16)
+    schur_wide[...] = join_left([schur_high[:size, :size], schur_low[:size, :size]])
 
 
 def blend_body(columns_ref, other_ref, mix_high, mix_low):
@@ -192,10 +206,9 @@
     return [(sum(PIECES[:place]), width) for place, width in enumerate(PIECES)]
 
 
-def project_body(subs, count, ahead_ref, test_high, test_low, *refs):
-    came = came_in(subs, refs[:count])
-    size = came.shape[0]
-    projected = ahead_ref[...] + dot3((test_high[:, :size], test_low[:, :size]), split(came))
+def project_body(subs, count, ahead_ref, test_wide, *refs):
+    halves = split(came_in(subs, refs[:count]))
+    projected = ahead_ref[...] + dot(test_wide[...], join_right(halves))
     for ref, (start, width) in zip(refs[count:], cut()):
         ref[...] = projected[:, start : start + width]
 
@@ -213,11 +226,11 @@
     kept_ref[...] = mixed[modes:]
 
 
-def correct_body(kept_ref, came_ref, fine_ref, basis_high, basis_low, place, *refs):
+def correct_body(kept_ref, came_ref, fine_ref, basis_wide, place, *refs):
     coarse = kept_ref[...] + came_ref[...]
     start, width = cut()[place]
     fine = fine_ref[:, start : start + width]
-    step = fine + dot3((basis_high[...], basis_low[...]), split(coarse))
+    step = fine + dot(basis_wide[...], join_right(split(coarse)))
     formers = place if len(refs) > 1 else 0
     former_refs, out_ref = refs[:formers], refs[formers]
     out_ref[...] = step
@@ -238,10 +251,10 @@
     base_ref[...] = load_ref[...] - dot3((schur_high[...], schur_low[...]), split(total))
 
 
-def product_body(subs, count, base_ref, schur_high, schur_low, *refs):
+def product_body(subs, count, base_ref, schur_wide, *refs):
     came = came_in(subs, refs[:count])
     size = came.shape[0]
-    part = dot3((schur_high[:size, :size], schur_low[:size, :size]), split(came))
+    part = dot(schur_wide[...], join_right(split(came)))
     put_shared(base_ref[:size] - part, refs[count:])
 
 
@@ -265,10 +278,10 @@
     base_ref[...] = pick(flipped, value_ref[...])
 
 
-def finish_body(subs, flipped_ref, base_ref, *refs):
+def finish_body(subs, twice_ref, base_ref, *refs):
     *arrived, out_hbm, out_ref, sems = refs
     came = came_in(subs, arrived)
-    total = base_ref[...] + pick(flipped_ref[:, : came.shape[0]], came)
+    total = base_ref[...] + dot(twice_ref[...], jnp.concatenate(split(came), axis=0))
     copies = []
     size = out_ref.shape[0] // 4
     for step in range(4):
@@ -324,6 +337,7 @@
     outside = pl.BlockSpec(memory_space=pltpu.HBM)
     pieces = len(PIECES)
     size = rows * loads
+    sent_rows = count * shared_rows
     run = Chain()
 
     one_hot, load_near, sent, *parts = run(
@@ -335,10 +349,10 @@
     )
     arrived = exchange(parts)
     other = lax.ppermute(sent, "grp", pair_plan)
-    chooser, flipped, basis_high, basis_low, test_high, test_low, ahead, ordered = run(
-        lambda *refs: order_body(subs, *refs),
-        [whole(rows, bf16)] * 2 + [whole(modes, bf16)] * 2 + [((modes, rows), bf16)] * 2
-        + [((modes, loads), f32), whole(loads)],
+    chooser, flipped, twice, basis_wide, test_high, test_low, test_wide, ahead, ordered = run(
+        lambda *refs: order_body(subs, count, *refs),
+        [whole(rows, bf16)] * 2 + [whole(2 * sent_rows, bf16), whole(3 * modes, bf16)]
+        + [((modes, rows), bf16)] * 2 + [((modes, 3 * sent_rows), bf16), ((modes, loads), f32), whole(loads)],
         4 * rows * size, 24 * size, one_hot, load_near, basis,
     )
     value, iterate = ordered, None
@@ -347,7 +361,7 @@
         shapes = [((modes, width), f32) for width in PIECES]
         own = run(
             lambda *refs: project_body(subs, count, *refs), shapes, 6 * modes * size, 12 * size,
-            ahead, test_high, test_low, *arrived,
+            ahead, test_wide, *arrived,
         )
         theirs = [lax.ppermute(piece, "grp", pair_plan) for piece in own]
         if first:
@@ -373,15 +387,15 @@
         for place, width in enumerate(PIECES):
             final = place == pieces - 1
             step, *parts = run(
-                lambda kept, came, fine, high, low, *refs: correct_body(kept, came, fine, high, low, place, *refs),
+                lambda kept, came, fine, wide, *refs: correct_body(kept, came, fine, wide, place, *refs),
                 [whole(width)] + (shared if final else []), 6 * modes * rows * width, 12 * rows * width,
-                kept[place], came[place], fine, basis_high, basis_low, *(steps if final else []),
+                kept[place], came[place], fine, basis_wide, *(steps if final else []),
             )
             steps.append(step)
         arrived = exchange(parts)
         if first:
-            schur_high, schur_low = run(
-                schur_body, [whole(rows, bf16)] * 2, 8 * rows**3, 12 * size, chooser, flipped, schur_matrix[0, 0],
+            schur_high, schur_low, schur_wide = run(
+                schur_body, [whole(rows, bf16)] * 2 + [((sent_rows, 3 * sent_rows), bf16)], 8 * rows**3, 12 * size, chooser, flipped, schur_matrix[0, 0],
             )
         base, total = run(
             lambda *refs: ahead_body(pieces, first, *refs), [whole(loads)] * 2, 6 * rows * size, 16 * size,
@@ -389,7 +403,7 @@
         )
         parts = run(
             lambda *refs: product_body(subs, count, *refs), shared, 2 * rows * size, 12 * size,
-            base, schur_high, schur_low, *arrived,
+            base, schur_wide, *arrived,
         )
         before, arrived = arrived, exchange(parts)
         *projected, iterate, value = run(
@@ -403,7 +417,7 @@
     )
     (residual_rows,) = run(
         lambda *refs: finish_body(subs, *refs), [whole(loads)], 4 * rows * size, 10 * size,
-        flipped, near, *arrived, places=[outside],
+        twice, near, *arrived, places=[outside],
         scratch=[pltpu.VMEM((rows, loads), f32), pltpu.SemaphoreType.DMA((4,))],
     )
     return (solution_rows[None, None], residual_rows[None, None])

time: 75.6 us -> 74.8 us (0.989)
  transfers between devices with their start and end apart: 24 -> 24, of which waited for: 14 -> 14; matrix products, arithmetic and copies ran while one was open for 0% -> 0% of each run, Pallas kernels for 17% -> 18%
where the time goes in v8:
time: 74.8 us; the launch traced here: 74.4 us
  starting transfers between devices  27.8 us (37%)
  waiting for transfers between devices  27.4 us (37%)
  Pallas kernels  18.2 us (24%)
  between operations  0.85 us (1%)
    pallas_call x25, Pallas kernels, __call__(): pl.pallas_call(whole_body, out_shape=[jax.ShapeDtypeStruct(shape, kind) f...  18.2 us
    ppermute x15, waiting for transfers between devices, exchange(): return [lax.ppermute(part, 'sub', plan) for part, plan in zip(parts, plans)]  16.4 us
    ppermute x15, starting transfers between devices, exchange(): return [lax.ppermute(part, 'sub', plan) for part, plan in zip(parts, plans)]  12.5 us
    ppermute x4, starting transfers between devices, local(): came.append(lax.ppermute(away, 'grp', mirror_plan))  9.62 us
    ppermute x4, waiting for transfers between devices, local(): came.append(lax.ppermute(away, 'grp', mirror_plan))  5.98 us
    ppermute x4, waiting for transfers between devices, local(): theirs = [lax.ppermute(piece, 'grp', pair_plan) for piece in own]  5.03 us
    ppermute x4, starting transfers between devices, local(): theirs = [lax.ppermute(piece, 'grp', pair_plan) for piece in own]  4.18 us
    ppermute x1, starting transfers between devices, local(): other = lax.ppermute(sent, 'grp', pair_plan)  1.56 us
  transfers between devices with their start and end apart: 24, of which 14 were waited for; matrix products, arithmetic and copies ran while one was open for 0% of the time, Pallas kernels for 18%

profile of v8, /device:TPU:0, one launch (start us, length us, event | category | flops | bytes accessed | tf_op | source)
XLA Modules:
  0.0 74.4 jit_solution(12200649753203716992)
XLA Ops:
  0.6 1.7 %shard_map.77 = (bf16[384,512]{1,0:T(8,128)(2,1)S(1)}, f32[512,384]{1,0:T(8,128)S(1)}, f32[128,128]{1,0:T(8,128)S(1)}, f32[96,384]{1,0:T(8,128)S(1)}, f32[96,384]{1,0:T(8,128)S(1)}, /*index=5*/f32[96,384]{1,0:T(8,128)S(1)}) custom-call(s32[4,96]{1,0:T(4,128)} %bitcast.15, f32[512,384]{1,0:T(8,128)} %bitcast.14, f32[512,128]{1,0:T(8,128)} %bitcast.9), custom_call_target="tpu_custom_call" | custom-call | flops 301989888 | bytes 3145728 | tf_op jit(solution)/shard_map/pallas_call | solution.py:35
  2.4 3.0 %collective-permute-start = (f32[96,384]{1,0:T(8,128)S(1)}, f32[96,384]{1,0:T(8,128)S(1)}, u32[]{:S(2)}, u32[]{:S(2)}) collective-permute-start(f32[96,384]{1,0:T(8,128)S(1)} %get-tuple-element.66), channel_id=1, source_target_pairs={{0,16},{4,20},{8,24},{12,28},{16,0},{20,4},{24,8},{28,12},{1,17},{... | collective-permute-start | bytes 442376 | tf_op jit(solution)/shard_map/ppermute | solution.py:329
  5.4 0.6 collective-permute-start.1
  6.0 1.0 %collective-permute-start.2 = (f32[96,384]{1,0:T(8,128)S(1)}, f32[96,384]{1,0:T(8,128)S(1)}, u32[]{:S(2)}, u32[]{:S(2)}) collective-permute-start(f32[96,384]{1,0:T(8,128)S(1)} %get-tuple-element.68), channel_id=1, source_target_pairs={{0,4},{4,0},{8,12},{12,8},{16,20},{20,16},{24,28},{28,24},{1,5},{5... | collective-permute-start | bytes 442376 | tf_op jit(solution)/shard_map/ppermute | solution.py:329
  7.0 1.6 %collective-permute-start.4 = (f32[128,128]{1,0:T(8,128)S(1)}, f32[128,128]{1,0:T(8,128)S(1)}, u32[]{:S(2)}, u32[]{:S(2)}) collective-permute-start(f32[128,128]{1,0:T(8,128)S(1)} %get-tuple-element.71), channel_id=1, source_target_pairs={{0,1},{1,0},{2,3},{3,2},{4,5},{5,4},{6,7},{7,6},{8,9},{9,8},{10,11... | collective-permute-start | bytes 196616 | tf_op jit(solution)/shard_map/ppermute | solution.py:351
  8.6 1.6 %shard_map.78 = (bf16[512,512]{1,0:T(8,128)(2,1)S(1)}, bf16[512,512]{1,0:T(8,128)(2,1)S(1)}, bf16[512,576]{1,0:T(8,128)(2,1)S(1)}, bf16[512,384]{1,0:T(8,128)(2,...) custom-call(bf16[384,512]{1,0:T(8,128)(2,1)S(1)} %get-tuple-element., ...), custom_call_target="tpu_custom_call" | custom-call | flops 402653184 | bytes 4718592 | tf_op jit(solution)/shard_map/pallas_call | solution.py:35
  10.2 1.3 %collective-permute-done.1.refs_3_.refs_4_ = f32[96,384]{1,0:T(8,128)S(1)} collective-permute-done((f32[96,384]{1,0:T(8,128)S(1)}, f32[96,384]{1,0:T(8,128)S(1)}, u32[]{:S(2)}, u32[]{:S(2)}) %collective-permute-start.1) | collective-permute-done | bytes 147488 | tf_op jit(solution)/shard_map/ppermute | solution.py:329
  11.5 0.3 shard_map.79
  11.8 1.7 %collective-permute-start.3 = (f32[128,128]{1,0:T(8,128)S(1)}, f32[128,128]{1,0:T(8,128)S(1)}, u32[]{:S(2)}, u32[]{:S(2)}) collective-permute-start(f32[128,128]{1,0:T(8,128)S(1)} %get-tuple-element.70.refs_2_.refs_0_), channel_id=1, source_target_pairs={{0,1},{1,0},{2,3},{3,2},{4,5},{5,4},{6,7},{7,6},{8,9},{9,8},{10,11... | collective-permute-start | bytes 196616 | tf_op jit(solution)/shard_map/ppermute | solution.py:366
  13.5 0.4 collective-permute-start.6
  14.1 2.5 %collective-permute-done.3.refs_1_ = f32[128,128]{1,0:T(8,128)S(1)} collective-permute-done((f32[128,128]{1,0:T(8,128)S(1)}, f32[128,128]{1,0:T(8,128)S(1)}, u32[]{:S(2)}, u32[]{:S(2)}) %collective-permute-start.3) | collective-permute-done | bytes 65568 | tf_op jit(solution)/shard_map/ppermute | solution.py:366
  16.8 4.0 %collective-permute-start.5 = (f32[128,128]{1,0:T(8,128)S(1)}, f32[128,128]{1,0:T(8,128)S(1)}, u32[]{:S(2)}, u32[]{:S(2)}) collective-permute-start(f32[128,128]{1,0:T(8,128)S(1)} %get-tuple-element.75.refs_4_), channel_id=1, source_target_pairs={{0,3},{3,0},{1,2},{2,1},{4,7},{7,4},{5,6},{6,5},{8,11},{11,8},{9,1... | collective-permute-start | bytes 196616 | tf_op jit(solution)/shard_map/ppermute | solution.py:376
  21.1 1.7 %collective-permute-start.7 = (f32[128,256]{1,0:T(8,128)S(1)}, f32[128,256]{1,0:T(8,128)S(1)}, u32[]{:S(2)}, u32[]{:S(2)}) collective-permute-start(f32[128,256]{1,0:T(8,128)S(1)} %get-tuple-element.78.refs_2_), channel_id=1, source_target_pairs={{0,3},{3,0},{1,2},{2,1},{4,7},{7,4},{5,6},{6,5},{8,11},{11,8},{9,1... | collective-permute-start | bytes 393224 | tf_op jit(solution)/shard_map/ppermute | solution.py:376
  22.8 1.3 %shard_map.83 = (bf16[512,512]{1,0:T(8,128)(2,1)S(1)}, bf16[512,512]{1,0:T(8,128)(2,1)S(1)}) custom-call(bf16[512,512]{1,0:T(8,128)(2,1)S(1)} %get-tuple-element.69.refs_5_.refs_0_, f32[512,512]{1,0:T(8,128)S(1)} %bitcast.11, f32[128,256]{1,0:T(8,128)S(1)} %get-tuple-element.78.refs_2_), custom_call_target="tpu_custom_call" | custom-call | flops 1073741824 | bytes 2359296 | tf_op jit(solution)/shard_map/pallas_call | solution.py:35
  24.1 1.0 %shard_map.84.refs_2_.refs_4_ = f32[512,384]{1,0:T(8,128)S(1)} custom-call(f32[512,384]{1,0:T(8,128)S(1)} %get-tuple-element.76.refs_0_.refs_2_.refs_3_, bf16[512,512]{1,0:T(8,128)(2,1)S(1)} %get-tuple-element.79.refs_1_.refs_6_, bf16[512,512]{1,0:T(8,128)(2,1)S(1)} %get-tuple-element.80.refs_2_, f32[96,384]{1,0:T(8,128)S(1)} %collective-permute-done.refs_2_.refs_3_, ...), custom_call_target="tpu_custom_call" | custom-call | flops 9663676416 | bytes 37748736 | tf_op jit(solution)/shard_map/pallas_call | solution.py:35
  25.4 2.6 %collective-permute-done.7.refs_1_ = f32[128,256]{1,0:T(8,128)S(1)} collective-permute-done((f32[128,256]{1,0:T(8,128)S(1)}, f32[128,256]{1,0:T(8,128)S(1)}, u32[]{:S(2)}, u32[]{:S(2)}) %collective-permute-start.7) | collective-permute-done | bytes 131104 | tf_op jit(solution)/shard_map/ppermute | solution.py:376
  28.3 0.6 collective-permute-start.8
  28.9 2.2 %collective-permute-start.10 = (f32[96,384]{1,0:T(8,128)S(1)}, f32[96,384]{1,0:T(8,128)S(1)}, u32[]{:S(2)}, u32[]{:S(2)}) collective-permute-start(f32[96,384]{1,0:T(8,128)S(1)} %get-tuple-element.90), channel_id=1, source_target_pairs={{0,4},{4,0},{8,12},{12,8},{16,20},{20,16},{24,28},{28,24},{1,5},{5... | collective-permute-start | bytes 442376 | tf_op jit(solution)/shard_map/ppermute | solution.py:329
  31.1 1.3 %shard_map.87 = (bf16[512,512]{1,0:T(8,128)(2,1)S(1)}, bf16[512,512]{1,0:T(8,128)(2,1)S(1)}, bf16[288,864]{1,0:T(8,128)(2,1)S(1)}) custom-call(bf16[512,512]{1,0:T(8,128)(2,1)S(1)} %get-tuple-element.69.refs_5_.refs_0_, bf16[512,512]{1,0:T(8,128)(2,1)S(1)} %get-tuple-element.63.refs_1_.refs_0_, f32[512,512]{1,0:T(8,128)S(1)} %bitcast.12, ...), custom_call_target="tpu_custom_call" | custom-call | flops 1073741824 | bytes 2359296 | tf_op jit(solution)/shard_map/pallas_call | solution.py:35
  32.4 1.0 %shard_map.88 = (f32[512,384]{1,0:T(8,128)S(1)}, f32[512,384]{1,0:T(8,128)S(1)}) custom-call(f32[512,128]{1,0:T(8,128)S(1)} %shard_map.85.refs_4_.refs_5_.refs_0_, f32[512,256]{1,0:T(8,128)S(1)} %get-tuple-element.83.refs_3_.refs_1_, f32[512,384]{1,0:T(8,128)S(1)} %get-tuple-element.76.refs_0_.refs_2_.refs_3_, ...), custom_call_target="tpu_custom_call" | custom-call | flops 603979776 | bytes 3145728 | tf_op jit(solution)/shard_map/pallas_call | solution.py:35
  33.4 0.8 %collective-permute-done.8.refs_2_.refs_4_ = f32[96,384]{1,0:T(8,128)S(1)} collective-permute-done((f32[96,384]{1,0:T(8,128)S(1)}, f32[96,384]{1,0:T(8,128)S(1)}, u32[]{:S(2)}, u32[]{:S(2)}) %collective-permute-start.8) | collective-permute-done | bytes 147488 | tf_op jit(solution)/shard_map/ppermute | solution.py:329
  34.2 1.5 %collective-permute-done.9.refs_3_.refs_5_ = f32[96,384]{1,0:T(8,128)S(1)} collective-permute-done((f32[96,384]{1,0:T(8,128)S(1)}, f32[96,384]{1,0:T(8,128)S(1)}, u32[]{:S(2)}, u32[]{:S(2)}) %collective-permute-start.9) | collective-permute-done | bytes 147488 | tf_op jit(solution)/shard_map/ppermute | solution.py:329
  35.7 0.5 shard_map.89
  36.3 1.5 %collective-permute-start.11 = (f32[96,384]{1,0:T(8,128)S(1)}, f32[96,384]{1,0:T(8,128)S(1)}, u32[]{:S(2)}, u32[]{:S(2)}) collective-permute-start(f32[96,384]{1,0:T(8,128)S(1)} %get-tuple-element.92.refs_7_.refs_12_), channel_id=1, source_target_pairs={{0,16},{4,20},{8,24},{12,28},{16,0},{20,4},{24,8},{28,12},{1,17},{... | collective-permute-start | bytes 442376 | tf_op jit(solution)/shard_map/ppermute | solution.py:329
  37.8 0.9 %shard_map.90 = (f32[128,384]{1,0:T(8,128)S(1)}, f32[512,384]{1,0:T(8,128)S(1)}, f32[512,384]{1,0:T(8,128)S(1)}) custom-call(f32[512,384]{1,0:T(8,128)S(1)} %get-tuple-element.86.refs_0_.refs_5_, f32[512,384]{1,0:T(8,128)S(1)} %get-tuple-element.87.refs_1_, bf16[512,512]{1,0:T(8,128)(2,1)S(1)} %get-tuple-element.84.refs_3_.refs_5_.refs_2_.refs_4_, ...), custom_call_target="tpu_custom_call" | custom-call | flops 301989888 | bytes 3145728 | tf_op jit(solution)/shard_map/pallas_call | solution.py:35
  38.7 3.3 %collective-permute-done.11.refs_2_.refs_3_ = f32[96,384]{1,0:T(8,128)S(1)} collective-permute-done((f32[96,384]{1,0:T(8,128)S(1)}, f32[96,384]{1,0:T(8,128)S(1)}, u32[]{:S(2)}, u32[]{:S(2)}) %collective-permute-start.11) | collective-permute-done | bytes 147488 | tf_op jit(solution)/shard_map/ppermute | solution.py:329
  42.0 1.6 %collective-permute-done.12.refs_3_.refs_4_ = f32[96,384]{1,0:T(8,128)S(1)} collective-permute-done((f32[96,384]{1,0:T(8,128)S(1)}, f32[96,384]{1,0:T(8,128)S(1)}, u32[]{:S(2)}, u32[]{:S(2)}) %collective-permute-start.12) | collective-permute-done | bytes 147488 | tf_op jit(solution)/shard_map/ppermute | solution.py:329
  43.9 1.4 %collective-permute-start.14 = (f32[128,128]{1,0:T(8,128)S(1)}, f32[128,128]{1,0:T(8,128)S(1)}, u32[]{:S(2)}, u32[]{:S(2)}) collective-permute-start(f32[128,128]{1,0:T(8,128)S(1)} %get-tuple-element.98.refs_0_.refs_4_), channel_id=1, source_target_pairs={{0,1},{1,0},{2,3},{3,2},{4,5},{5,4},{6,7},{7,6},{8,9},{9,8},{10,11... | collective-permute-start | bytes 196616 | tf_op jit(solution)/shard_map/ppermute | solution.py:366
  45.3 0.7 collective-permute-start.16
  46.0 2.5 %collective-permute-done.14.refs_1_ = f32[128,128]{1,0:T(8,128)S(1)} collective-permute-done((f32[128,128]{1,0:T(8,128)S(1)}, f32[128,128]{1,0:T(8,128)S(1)}, u32[]{:S(2)}, u32[]{:S(2)}) %collective-permute-start.14) | collective-permute-done | bytes 65568 | tf_op jit(solution)/shard_map/ppermute | solution.py:366
  48.8 1.7 %collective-permute-start.15 = (f32[128,128]{1,0:T(8,128)S(1)}, f32[128,128]{1,0:T(8,128)S(1)}, u32[]{:S(2)}, u32[]{:S(2)}) collective-permute-start(f32[128,128]{1,0:T(8,128)S(1)} %get-tuple-element.100.refs_4_), channel_id=1, source_target_pairs={{0,3},{3,0},{1,2},{2,1},{4,7},{7,4},{5,6},{6,5},{8,11},{11,8},{9,1... | collective-permute-start | bytes 196616 | tf_op jit(solution)/shard_map/ppermute | solution.py:376
  50.8 2.3 %collective-permute-start.17 = (f32[128,256]{1,0:T(8,128)S(1)}, f32[128,256]{1,0:T(8,128)S(1)}, u32[]{:S(2)}, u32[]{:S(2)}) collective-permute-start(f32[128,256]{1,0:T(8,128)S(1)} %get-tuple-element.103.refs_6_), channel_id=1, source_target_pairs={{0,3},{3,0},{1,2},{2,1},{4,7},{7,4},{5,6},{6,5},{8,11},{11,8},{9,1... | collective-permute-start | bytes 393224 | tf_op jit(solution)/shard_map/ppermute | solution.py:376
  53.0 1.0 %shard_map.94.refs_2_.refs_4_ = f32[512,384]{1,0:T(8,128)S(1)} custom-call(f32[512,384]{1,0:T(8,128)S(1)} %get-tuple-element.101.refs_0_, bf16[512,512]{1,0:T(8,128)(2,1)S(1)} %get-tuple-element.79.refs_1_.refs_6_, bf16[512,512]{1,0:T(8,128)(2,1)S(1)} %get-tuple-element.80.refs_2_, f32[96,384]{1,0:T(8,128)S(1)} %collective-permute-done.11.refs_2_.refs_3_, ...), custom_call_target="tpu_custom_call" | custom-call | flops 9663676416 | bytes 37748736 | tf_op jit(solution)/shard_map/pallas_call | solution.py:35
  54.1 1.6 %collective-permute-done.15.refs_1_ = f32[128,128]{1,0:T(8,128)S(1)} collective-permute-done((f32[128,128]{1,0:T(8,128)S(1)}, f32[128,128]{1,0:T(8,128)S(1)}, u32[]{:S(2)}, u32[]{:S(2)}) %collective-permute-start.15) | collective-permute-done | bytes 65568 | tf_op jit(solution)/shard_map/ppermute | solution.py:376
  55.9 1.8 %collective-permute-done.17.refs_1_ = f32[128,256]{1,0:T(8,128)S(1)} collective-permute-done((f32[128,256]{1,0:T(8,128)S(1)}, f32[128,256]{1,0:T(8,128)S(1)}, u32[]{:S(2)}, u32[]{:S(2)}) %collective-permute-start.17) | collective-permute-done | bytes 131104 | tf_op jit(solution)/shard_map/ppermute | solution.py:376
  58.0 1.2 %collective-permute-start.18 = (f32[96,384]{1,0:T(8,128)S(1)}, f32[96,384]{1,0:T(8,128)S(1)}, u32[]{:S(2)}, u32[]{:S(2)}) collective-permute-start(f32[96,384]{1,0:T(8,128)S(1)} %get-tuple-element.109), channel_id=1, source_target_pairs={{0,16},{4,20},{8,24},{12,28},{16,0},{20,4},{24,8},{28,12},{1,17},{... | collective-permute-start | bytes 442376 | tf_op jit(solution)/shard_map/ppermute | solution.py:329
  59.2 1.0 %collective-permute-start.20 = (f32[96,384]{1,0:T(8,128)S(1)}, f32[96,384]{1,0:T(8,128)S(1)}, u32[]{:S(2)}, u32[]{:S(2)}) collective-permute-start(f32[96,384]{1,0:T(8,128)S(1)} %get-tuple-element.111), channel_id=1, source_target_pairs={{0,4},{4,0},{8,12},{12,8},{16,20},{20,16},{24,28},{28,24},{1,5},{5... | collective-permute-start | bytes 442376 | tf_op jit(solution)/shard_map/ppermute | solution.py:329
  60.2 1.0 %shard_map.97 = (f32[512,384]{1,0:T(8,128)S(1)}, f32[512,384]{1,0:T(8,128)S(1)}) custom-call(f32[512,128]{1,0:T(8,128)S(1)} %shard_map.95.refs_4_.refs_5_.refs_0_, f32[512,256]{1,0:T(8,128)S(1)} %get-tuple-element.105.refs_1_.refs_6_, f32[512,384]{1,0:T(8,128)S(1)} %get-tuple-element.106.refs_2_, f32[512,384]{1,0:T(8,128)S(1)} %get-tuple-element.76.refs_0_.refs_2_.refs_3_, ...), custom_call_target="tpu_custom_call" | custom-call | flops 603979776 | bytes 3145728 | tf_op jit(solution)/shard_map/pallas_call | solution.py:35
  61.2 2.2 %collective-permute-done.18.refs_2_.refs_4_ = f32[96,384]{1,0:T(8,128)S(1)} collective-permute-done((f32[96,384]{1,0:T(8,128)S(1)}, f32[96,384]{1,0:T(8,128)S(1)}, u32[]{:S(2)}, u32[]{:S(2)}) %collective-permute-start.18) | collective-permute-done | bytes 147488 | tf_op jit(solution)/shard_map/ppermute | solution.py:329
  63.4 2.3 %collective-permute-done.19.refs_3_.refs_5_ = f32[96,384]{1,0:T(8,128)S(1)} collective-permute-done((f32[96,384]{1,0:T(8,128)S(1)}, f32[96,384]{1,0:T(8,128)S(1)}, u32[]{:S(2)}, u32[]{:S(2)}) %collective-permute-start.19) | collective-permute-done | bytes 147488 | tf_op jit(solution)/shard_map/ppermute | solution.py:329
  65.7 0.5 shard_map.98
  66.2 0.6 collective-permute-start.21
  66.8 0.7 collective-permute-start.23
  67.5 0.5 shard_map.99
  68.0 1.6 %shard_map.100 = (f32[512,384]{1,0:T(8,128)S(1)}, f32[512,384]{1,0:T(8,128)}) custom-call(bf16[512,512]{1,0:T(8,128)(2,1)S(1)} %get-tuple-element.63.refs_1_.refs_0_, f32[512,384]{1,0:T(8,128)S(1)} %get-tuple-element.115.refs_1_, f32[512,384]{1,0:T(8,128)S(1)} %get-tuple-element.116.refs_2_.refs_3_, f32[512,384]{1,0:T(8,128)S(1)} %get-tuple-element.116.refs_2_.refs_3_), custom_call_target="tpu_custom_call" | custom-call | flops 805306368 | bytes 1966080 | tf_op jit(solution)/shard_map/pallas_call | solution.py:35
  69.6 2.5 %collective-permute-done.21.refs_2_ = f32[96,384]{1,0:T(8,128)S(1)} collective-permute-done((f32[96,384]{1,0:T(8,128)S(1)}, f32[96,384]{1,0:T(8,128)S(1)}, u32[]{:S(2)}, u32[]{:S(2)}) %collective-permute-start.21) | collective-permute-done | bytes 147488 | tf_op jit(solution)/shard_map/ppermute | solution.py:329
  72.1 0.8 %collective-permute-done.22.refs_3_ = f32[96,384]{1,0:T(8,128)S(1)} collective-permute-done((f32[96,384]{1,0:T(8,128)S(1)}, f32[96,384]{1,0:T(8,128)S(1)}, u32[]{:S(2)}, u32[]{:S(2)}) %collective-permute-start.22) | collective-permute-done | bytes 147488 | tf_op jit(solution)/shard_map/ppermute | solution.py:329
  73.0 1.4 %shard_map.101 = f32[512,384]{1,0:T(8,128)} custom-call(bf16[512,576]{1,0:T(8,128)(2,1)S(1)} %get-tuple-element.118.refs_0_, f32[512,384]{1,0:T(8,128)S(1)} %get-tuple-element.119.refs_1_.refs_5_, f32[96,384]{1,0:T(8,128)S(1)} %collective-permute-done.21.refs_2_, f32[96,384]{1,0:T(8,128)S(1)} %collective-permute-done.22.refs_3_, ...), custom_call_target="tpu_custom_call" | custom-call | flops 402653184 | bytes 1966080 | tf_op jit(solution)/shard_map/pallas_call | solution.py:35
  (33 shorter events, 2.7 us)
Async XLA Ops:
  0.6 7.9 %copy-start = (f32[1,1,512,128]{3,2,1,0:T(8,128)S(1)}, f32[1,1,512,128]{3,2,1,0:T(8,128)}, u32[]{:S(2)}) copy-start(f32[1,1,512,128]{3,2,1,0:T(8,128)} %param.9) | copy-start | bytes 786436
  2.4 7.8 %collective-permute-start = (f32[96,384]{1,0:T(8,128)S(1)}, f32[96,384]{1,0:T(8,128)S(1)}, u32[]{:S(2)}, u32[]{:S(2)}) collective-permute-start(f32[96,384]{1,0:T(8,128)S(1)} %get-tuple-element.66), channel_id=1, source_target_pairs={{0,16},{4,20},{8,24},{12,28},{16,0},{20,4},{24,8},{28,12},{1,17},{... | collective-permute-start | bytes 442376 | tf_op jit(solution)/shard_map/ppermute | solution.py:329
  5.4 6.1 %collective-permute-start.1 = (f32[96,384]{1,0:T(8,128)S(1)}, f32[96,384]{1,0:T(8,128)S(1)}, u32[]{:S(2)}, u32[]{:S(2)}) collective-permute-start(f32[96,384]{1,0:T(8,128)S(1)} %get-tuple-element.67), channel_id=1, source_target_pairs={{0,28},{4,8},{8,4},{12,16},{16,12},{20,24},{24,20},{28,0},{1,29},{... | collective-permute-start | bytes 442376 | tf_op jit(solution)/shard_map/ppermute | solution.py:329
  6.0 5.5 %collective-permute-start.2 = (f32[96,384]{1,0:T(8,128)S(1)}, f32[96,384]{1,0:T(8,128)S(1)}, u32[]{:S(2)}, u32[]{:S(2)}) collective-permute-start(f32[96,384]{1,0:T(8,128)S(1)} %get-tuple-element.68), channel_id=1, source_target_pairs={{0,4},{4,0},{8,12},{12,8},{16,20},{20,16},{24,28},{28,24},{1,5},{5... | collective-permute-start | bytes 442376 | tf_op jit(solution)/shard_map/ppermute | solution.py:329
  7.0 6.9 %collective-permute-start.4 = (f32[128,128]{1,0:T(8,128)S(1)}, f32[128,128]{1,0:T(8,128)S(1)}, u32[]{:S(2)}, u32[]{:S(2)}) collective-permute-start(f32[128,128]{1,0:T(8,128)S(1)} %get-tuple-element.71), channel_id=1, source_target_pairs={{0,1},{1,0},{2,3},{3,2},{4,5},{5,4},{6,7},{7,6},{8,9},{9,8},{10,11... | collective-permute-start | bytes 196616 | tf_op jit(solution)/shard_map/ppermute | solution.py:351
  11.5 2.4 %copy-start.1 = (f32[1,512,128]{2,1,0:T(8,128)S(1)}, f32[1,512,128]{2,1,0:T(8,128)}, u32[]{:S(2)}) copy-start(f32[1,512,128]{2,1,0:T(8,128)} %param.10) | copy-start | bytes 786436
  11.8 4.7 %collective-permute-start.3 = (f32[128,128]{1,0:T(8,128)S(1)}, f32[128,128]{1,0:T(8,128)S(1)}, u32[]{:S(2)}, u32[]{:S(2)}) collective-permute-start(f32[128,128]{1,0:T(8,128)S(1)} %get-tuple-element.70.refs_2_.refs_0_), channel_id=1, source_target_pairs={{0,1},{1,0},{2,3},{3,2},{4,5},{5,4},{6,7},{7,6},{8,9},{9,8},{10,11... | collective-permute-start | bytes 196616 | tf_op jit(solution)/shard_map/ppermute | solution.py:366
  13.5 7.3 %collective-permute-start.6 = (f32[128,256]{1,0:T(8,128)S(1)}, f32[128,256]{1,0:T(8,128)S(1)}, u32[]{:S(2)}, u32[]{:S(2)}) collective-permute-start(f32[128,256]{1,0:T(8,128)S(1)} %get-tuple-element.77.refs_0_), channel_id=1, source_target_pairs={{0,1},{1,0},{2,3},{3,2},{4,5},{5,4},{6,7},{7,6},{8,9},{9,8},{10,11... | collective-permute-start | bytes 393224 | tf_op jit(solution)/shard_map/ppermute | solution.py:366
  16.8 6.0 %copy-start.2 = (f32[1,1,512,512]{3,2,1,0:T(8,128)S(1)}, f32[1,1,512,512]{3,2,1,0:T(8,128)}, u32[]{:S(2)}) copy-start(f32[1,1,512,512]{3,2,1,0:T(8,128)} %param.8) | copy-start | bytes 3145732
  16.8 8.3 %collective-permute-start.5 = (f32[128,128]{1,0:T(8,128)S(1)}, f32[128,128]{1,0:T(8,128)S(1)}, u32[]{:S(2)}, u32[]{:S(2)}) collective-permute-start(f32[128,128]{1,0:T(8,128)S(1)} %get-tuple-element.75.refs_4_), channel_id=1, source_target_pairs={{0,3},{3,0},{1,2},{2,1},{4,7},{7,4},{5,6},{6,5},{8,11},{11,8},{9,1... | collective-permute-start | bytes 196616 | tf_op jit(solution)/shard_map/ppermute | solution.py:376
  21.1 6.9 %collective-permute-start.7 = (f32[128,256]{1,0:T(8,128)S(1)}, f32[128,256]{1,0:T(8,128)S(1)}, u32[]{:S(2)}, u32[]{:S(2)}) collective-permute-start(f32[128,256]{1,0:T(8,128)S(1)} %get-tuple-element.78.refs_2_), channel_id=1, source_target_pairs={{0,3},{3,0},{1,2},{2,1},{4,7},{7,4},{5,6},{6,5},{8,11},{11,8},{9,1... | collective-permute-start | bytes 393224 | tf_op jit(solution)/shard_map/ppermute | solution.py:376
  25.4 5.7 %copy-start.3 = (f32[1,1,512,512]{3,2,1,0:T(8,128)S(1)}, f32[1,1,512,512]{3,2,1,0:T(8,128)}, u32[]{:S(2)}) copy-start(f32[1,1,512,512]{3,2,1,0:T(8,128)} %param.7) | copy-start | bytes 3145732
  28.3 5.9 %collective-permute-start.8 = (f32[96,384]{1,0:T(8,128)S(1)}, f32[96,384]{1,0:T(8,128)S(1)}, u32[]{:S(2)}, u32[]{:S(2)}) collective-permute-start(f32[96,384]{1,0:T(8,128)S(1)} %get-tuple-element.88), channel_id=1, source_target_pairs={{0,16},{4,20},{8,24},{12,28},{16,0},{20,4},{24,8},{28,12},{1,17},{... | collective-permute-start | bytes 442376 | tf_op jit(solution)/shard_map/ppermute | solution.py:329
  28.9 6.8 %collective-permute-start.9 = (f32[96,384]{1,0:T(8,128)S(1)}, f32[96,384]{1,0:T(8,128)S(1)}, u32[]{:S(2)}, u32[]{:S(2)}) collective-permute-start(f32[96,384]{1,0:T(8,128)S(1)} %get-tuple-element.89), channel_id=1, source_target_pairs={{0,28},{4,8},{8,4},{12,16},{16,12},{20,24},{24,20},{28,0},{1,29},{... | collective-permute-start | bytes 442376 | tf_op jit(solution)/shard_map/ppermute | solution.py:329
  28.9 6.8 %collective-permute-start.10 = (f32[96,384]{1,0:T(8,128)S(1)}, f32[96,384]{1,0:T(8,128)S(1)}, u32[]{:S(2)}, u32[]{:S(2)}) collective-permute-start(f32[96,384]{1,0:T(8,128)S(1)} %get-tuple-element.90), channel_id=1, source_target_pairs={{0,4},{4,0},{8,12},{12,8},{16,20},{20,16},{24,28},{28,24},{1,5},{5... | collective-permute-start | bytes 442376 | tf_op jit(solution)/shard_map/ppermute | solution.py:329
  36.3 5.7 %collective-permute-start.11 = (f32[96,384]{1,0:T(8,128)S(1)}, f32[96,384]{1,0:T(8,128)S(1)}, u32[]{:S(2)}, u32[]{:S(2)}) collective-permute-start(f32[96,384]{1,0:T(8,128)S(1)} %get-tuple-element.92.refs_7_.refs_12_), channel_id=1, source_target_pairs={{0,16},{4,20},{8,24},{12,28},{16,0},{20,4},{24,8},{28,12},{1,17},{... | collective-permute-start | bytes 442376 | tf_op jit(solution)/shard_map/ppermute | solution.py:329
  37.7 5.9 %collective-permute-start.12 = (f32[96,384]{1,0:T(8,128)S(1)}, f32[96,384]{1,0:T(8,128)S(1)}, u32[]{:S(2)}, u32[]{:S(2)}) collective-permute-start(f32[96,384]{1,0:T(8,128)S(1)} %get-tuple-element.93.refs_8_), channel_id=1, source_target_pairs={{0,28},{4,8},{8,4},{12,16},{16,12},{20,24},{24,20},{28,0},{1,29},{... | collective-permute-start | bytes 442376 | tf_op jit(solution)/shard_map/ppermute | solution.py:329
  37.7 5.9 %collective-permute-start.13 = (f32[96,384]{1,0:T(8,128)S(1)}, f32[96,384]{1,0:T(8,128)S(1)}, u32[]{:S(2)}, u32[]{:S(2)}) collective-permute-start(f32[96,384]{1,0:T(8,128)S(1)} %get-tuple-element.94.refs_9_), channel_id=1, source_target_pairs={{0,4},{4,0},{8,12},{12,8},{16,20},{20,16},{24,28},{28,24},{1,5},{5... | collective-permute-start | bytes 442376 | tf_op jit(solution)/shard_map/ppermute | solution.py:329
  43.9 4.6 %collective-permute-start.14 = (f32[128,128]{1,0:T(8,128)S(1)}, f32[128,128]{1,0:T(8,128)S(1)}, u32[]{:S(2)}, u32[]{:S(2)}) collective-permute-start(f32[128,128]{1,0:T(8,128)S(1)} %get-tuple-element.98.refs_0_.refs_4_), channel_id=1, source_target_pairs={{0,1},{1,0},{2,3},{3,2},{4,5},{5,4},{6,7},{7,6},{8,9},{9,8},{10,11... | collective-permute-start | bytes 196616 | tf_op jit(solution)/shard_map/ppermute | solution.py:366
  45.3 5.2 %collective-permute-start.16 = (f32[128,256]{1,0:T(8,128)S(1)}, f32[128,256]{1,0:T(8,128)S(1)}, u32[]{:S(2)}, u32[]{:S(2)}) collective-permute-start(f32[128,256]{1,0:T(8,128)S(1)} %get-tuple-element.102.refs_0_), channel_id=1, source_target_pairs={{0,1},{1,0},{2,3},{3,2},{4,5},{5,4},{6,7},{7,6},{8,9},{9,8},{10,11... | collective-permute-start | bytes 393224 | tf_op jit(solution)/shard_map/ppermute | solution.py:366
  48.8 6.8 %collective-permute-start.15 = (f32[128,128]{1,0:T(8,128)S(1)}, f32[128,128]{1,0:T(8,128)S(1)}, u32[]{:S(2)}, u32[]{:S(2)}) collective-permute-start(f32[128,128]{1,0:T(8,128)S(1)} %get-tuple-element.100.refs_4_), channel_id=1, source_target_pairs={{0,3},{3,0},{1,2},{2,1},{4,7},{7,4},{5,6},{6,5},{8,11},{11,8},{9,1... | collective-permute-start | bytes 196616 | tf_op jit(solution)/shard_map/ppermute | solution.py:376
  50.8 6.9 %collective-permute-start.17 = (f32[128,256]{1,0:T(8,128)S(1)}, f32[128,256]{1,0:T(8,128)S(1)}, u32[]{:S(2)}, u32[]{:S(2)}) collective-permute-start(f32[128,256]{1,0:T(8,128)S(1)} %get-tuple-element.103.refs_6_), channel_id=1, source_target_pairs={{0,3},{3,0},{1,2},{2,1},{4,7},{7,4},{5,6},{6,5},{8,11},{11,8},{9,1... | collective-permute-start | bytes 393224 | tf_op jit(solution)/shard_map/ppermute | solution.py:376
  58.0 5.4 %collective-permute-start.18 = (f32[96,384]{1,0:T(8,128)S(1)}, f32[96,384]{1,0:T(8,128)S(1)}, u32[]{:S(2)}, u32[]{:S(2)}) collective-permute-start(f32[96,384]{1,0:T(8,128)S(1)} %get-tuple-element.109), channel_id=1, source_target_pairs={{0,16},{4,20},{8,24},{12,28},{16,0},{20,4},{24,8},{28,12},{1,17},{... | collective-permute-start | bytes 442376 | tf_op jit(solution)/shard_map/ppermute | solution.py:329
  59.2 6.5 %collective-permute-start.19 = (f32[96,384]{1,0:T(8,128)S(1)}, f32[96,384]{1,0:T(8,128)S(1)}, u32[]{:S(2)}, u32[]{:S(2)}) collective-permute-start(f32[96,384]{1,0:T(8,128)S(1)} %get-tuple-element.110), channel_id=1, source_target_pairs={{0,28},{4,8},{8,4},{12,16},{16,12},{20,24},{24,20},{28,0},{1,29},{... | collective-permute-start | bytes 442376 | tf_op jit(solution)/shard_map/ppermute | solution.py:329
  59.2 6.5 %collective-permute-start.20 = (f32[96,384]{1,0:T(8,128)S(1)}, f32[96,384]{1,0:T(8,128)S(1)}, u32[]{:S(2)}, u32[]{:S(2)}) collective-permute-start(f32[96,384]{1,0:T(8,128)S(1)} %get-tuple-element.111), channel_id=1, source_target_pairs={{0,4},{4,0},{8,12},{12,8},{16,20},{20,16},{24,28},{28,24},{1,5},{5... | collective-permute-start | bytes 442376 | tf_op jit(solution)/shard_map/ppermute | solution.py:329
  66.2 5.9 %collective-permute-start.21 = (f32[96,384]{1,0:T(8,128)S(1)}, f32[96,384]{1,0:T(8,128)S(1)}, u32[]{:S(2)}, u32[]{:S(2)}) collective-permute-start(f32[96,384]{1,0:T(8,128)S(1)} %get-tuple-element.112.refs_7_.refs_10_), channel_id=1, source_target_pairs={{0,16},{4,20},{8,24},{12,28},{16,0},{20,4},{24,8},{28,12},{1,17},{... | collective-permute-start | bytes 442376 | tf_op jit(solution)/shard_map/ppermute | solution.py:329
  66.8 6.2 %collective-permute-start.22 = (f32[96,384]{1,0:T(8,128)S(1)}, f32[96,384]{1,0:T(8,128)S(1)}, u32[]{:S(2)}, u32[]{:S(2)}) collective-permute-start(f32[96,384]{1,0:T(8,128)S(1)} %get-tuple-element.113.refs_8_), channel_id=1, source_target_pairs={{0,28},{4,8},{8,4},{12,16},{16,12},{20,24},{24,20},{28,0},{1,29},{... | collective-permute-start | bytes 442376 | tf_op jit(solution)/shard_map/ppermute | solution.py:329
  66.8 6.2 %collective-permute-start.23 = (f32[96,384]{1,0:T(8,128)S(1)}, f32[96,384]{1,0:T(8,128)S(1)}, u32[]{:S(2)}, u32[]{:S(2)}) collective-permute-start(f32[96,384]{1,0:T(8,128)S(1)} %get-tuple-element.114.refs_9_), channel_id=1, source_target_pairs={{0,4},{4,0},{8,12},{12,8},{16,20},{20,16},{24,28},{28,24},{1,5},{5... | collective-permute-start | bytes 442376 | tf_op jit(solution)/shard_map/ppermute | solution.py:329

commit v9 on v8

--- a/solution.py
+++ b/solution.py
@@ -180,9 +180,10 @@
     return columns_ref[pl.ds(pl.multiple_of(place * modes, modes), modes), :]
 
 
-def solver_body(subs, listed, chooser_ref, solve_ref, solve_high, solve_low):
+def solver_body(subs, listed, chooser_ref, solve_ref, later_ref, solve_high, solve_low, passed_ref):
     chooser = chooser_ref[...]
     weighted = (chooser.astype(f32) * weight_column(subs, listed // 4, chooser.shape[0])).astype(bf16)
+    passed_ref[...] = later_ref[...]
     for part, out in zip(split(solve_ref[...] * RELAX), (solve_high, solve_low)):
         out[...] = dot(dot(weighted, part).astype(bf16), weighted, NT).astype(bf16)
 
@@ -359,10 +360,15 @@
     for iteration in range(ITERS):
         first, last = iteration == 0, iteration == ITERS - 1
         shapes = [((modes, width), f32) for width in PIECES]
-        own = run(
+        own = list(run(
             lambda *refs: project_body(subs, count, *refs), shapes, 6 * modes * size, 12 * size,
             ahead, test_wide, *arrived,
-        )
+        ))
+        if first:
+            solve_high, solve_low, own[1] = run(
+                lambda *refs: solver_body(subs, listed, *refs), [whole(rows, bf16)] * 2 + [shapes[1]],
+                8 * rows**3, 12 * size, chooser, local_inverse[0, 0], own[1],
+            )
         theirs = [lax.ppermute(piece, "grp", pair_plan) for piece in own]
         if first:
             mixers = run(blend_body, [((2 * modes, 2 * modes), bf16)] * 2, size, size, columns, other)
@@ -374,11 +380,6 @@
             )
             kept.append(keep)
             came.append(lax.ppermute(away, "grp", mirror_plan))
-        if first:
-            solve_high, solve_low = run(
-                lambda *refs: solver_body(subs, listed, *refs), [whole(rows, bf16)] * 2, 8 * rows**3, 12 * size,
-                chooser, local_inverse[0, 0],
-            )
         (fine,) = run(
             lambda *refs: solve_body(subs, *refs), [whole(loads)], HIDE * 6 * rows * size, HIDE * 12 * size,
             value, solve_high, solve_low, *arrived,

time: 74.8 us -> 74.9 us (level)
  starting transfers between devices: 27.8 us -> 30.5 us
  waiting for transfers between devices: 27.4 us -> 25.2 us
    ppermute x15, starting transfers between devices: 12.5 us -> 14.5 us  [exchange(): return [lax.ppermute(part, 'sub', plan) for part, plan in zip(parts, plans)]]
    ppermute x15, waiting for transfers between devices: 16.4 us -> 14.6 us  [exchange(): return [lax.ppermute(part, 'sub', plan) for part, plan in zip(parts, plans)]]
    ppermute x4, waiting for transfers between devices: 5.03 us -> 3.6 us  [local(): theirs = [lax.ppermute(piece, 'grp', pair_plan) for piece in own]]
    ppermute x4, waiting for transfers between devices: 5.98 us -> 6.99 us  [local(): came.append(lax.ppermute(away, 'grp', mirror_plan))]
  transfers between devices with their start and end apart: 24 -> 24, of which waited for: 14 -> 13; matrix products, arithmetic and copies ran while one was open for 0% -> 0% of each run, Pallas kernels for 18% -> 18%
where the time goes in v9:
time: 74.9 us; the launch traced here: 74.7 us
  starting transfers between devices  30.5 us (41%)
  waiting for transfers between devices  25.2 us (34%)
  Pallas kernels  18.2 us (24%)
  between operations  0.86 us (1%)
    pallas_call x25, Pallas kernels, __call__(): pl.pallas_call(whole_body, out_shape=[jax.ShapeDtypeStruct(shape, kind) f...  18.2 us
    ppermute x15, waiting for transfers between devices, exchange(): return [lax.ppermute(part, 'sub', plan) for part, plan in zip(parts, plans)]  14.6 us
    ppermute x15, starting transfers between devices, exchange(): return [lax.ppermute(part, 'sub', plan) for part, plan in zip(parts, plans)]  14.5 us
    ppermute x4, starting transfers between devices, local(): came.append(lax.ppermute(away, 'grp', mirror_plan))  10.2 us
    ppermute x4, waiting for transfers between devices, local(): came.append(lax.ppermute(away, 'grp', mirror_plan))  6.99 us
    ppermute x4, starting transfers between devices, local(): theirs = [lax.ppermute(piece, 'grp', pair_plan) for piece in own]  4.25 us
    ppermute x4, waiting for transfers between devices, local(): theirs = [lax.ppermute(piece, 'grp', pair_plan) for piece in own]  3.6 us
    ppermute x1, starting transfers between devices, local(): other = lax.ppermute(sent, 'grp', pair_plan)  1.56 us
  transfers between devices with their start and end apart: 24, of which 13 were waited for; matrix products, arithmetic and copies ran while one was open for 0% of the time, Pallas kernels for 18%

profile of v9, /device:TPU:0, one launch (start us, length us, event | category | flops | bytes accessed | tf_op | source)
XLA Modules:
  0.0 74.7 jit_solution(16113841066586920660)
XLA Ops:
  0.6 1.7 %shard_map.77 = (bf16[384,512]{1,0:T(8,128)(2,1)S(1)}, f32[512,384]{1,0:T(8,128)S(1)}, f32[128,128]{1,0:T(8,128)S(1)}, f32[96,384]{1,0:T(8,128)S(1)}, f32[96,384]{1,0:T(8,128)S(1)}, /*index=5*/f32[96,384]{1,0:T(8,128)S(1)}) custom-call(s32[4,96]{1,0:T(4,128)} %bitcast.15, f32[512,384]{1,0:T(8,128)} %bitcast.14, f32[512,128]{1,0:T(8,128)} %bitcast.9), custom_call_target="tpu_custom_call" | custom-call | flops 301989888 | bytes 3145728 | tf_op jit(solution)/shard_map/pallas_call | solution.py:35
  2.4 3.0 %collective-permute-start = (f32[96,384]{1,0:T(8,128)S(1)}, f32[96,384]{1,0:T(8,128)S(1)}, u32[]{:S(2)}, u32[]{:S(2)}) collective-permute-start(f32[96,384]{1,0:T(8,128)S(1)} %get-tuple-element.67), channel_id=1, source_target_pairs={{0,16},{4,20},{8,24},{12,28},{16,0},{20,4},{24,8},{28,12},{1,17},{... | collective-permute-start | bytes 442376 | tf_op jit(solution)/shard_map/ppermute | solution.py:330
  5.4 0.6 collective-permute-start.1
  6.0 1.0 %collective-permute-start.2 = (f32[96,384]{1,0:T(8,128)S(1)}, f32[96,384]{1,0:T(8,128)S(1)}, u32[]{:S(2)}, u32[]{:S(2)}) collective-permute-start(f32[96,384]{1,0:T(8,128)S(1)} %get-tuple-element.69), channel_id=1, source_target_pairs={{0,4},{4,0},{8,12},{12,8},{16,20},{20,16},{24,28},{28,24},{1,5},{5... | collective-permute-start | bytes 442376 | tf_op jit(solution)/shard_map/ppermute | solution.py:330
  7.0 1.6 %collective-permute-start.4 = (f32[128,128]{1,0:T(8,128)S(1)}, f32[128,128]{1,0:T(8,128)S(1)}, u32[]{:S(2)}, u32[]{:S(2)}) collective-permute-start(f32[128,128]{1,0:T(8,128)S(1)} %get-tuple-element.72), channel_id=1, source_target_pairs={{0,1},{1,0},{2,3},{3,2},{4,5},{5,4},{6,7},{7,6},{8,9},{9,8},{10,11... | collective-permute-start | bytes 196616 | tf_op jit(solution)/shard_map/ppermute | solution.py:352
  8.6 1.6 %shard_map.78 = (bf16[512,512]{1,0:T(8,128)(2,1)S(1)}, bf16[512,512]{1,0:T(8,128)(2,1)S(1)}, bf16[512,576]{1,0:T(8,128)(2,1)S(1)}, bf16[512,384]{1,0:T(8,128)(2,...) custom-call(bf16[384,512]{1,0:T(8,128)(2,1)S(1)} %get-tuple-element., ...), custom_call_target="tpu_custom_call" | custom-call | flops 402653184 | bytes 4718592 | tf_op jit(solution)/shard_map/pallas_call | solution.py:35
  10.2 1.3 %collective-permute-done.1.refs_3_.refs_4_ = f32[96,384]{1,0:T(8,128)S(1)} collective-permute-done((f32[96,384]{1,0:T(8,128)S(1)}, f32[96,384]{1,0:T(8,128)S(1)}, u32[]{:S(2)}, u32[]{:S(2)}) %collective-permute-start.1) | collective-permute-done | bytes 147488 | tf_op jit(solution)/shard_map/ppermute | solution.py:330
  11.5 0.3 shard_map.79
  11.8 1.7 %collective-permute-start.3 = (f32[128,128]{1,0:T(8,128)S(1)}, f32[128,128]{1,0:T(8,128)S(1)}, u32[]{:S(2)}, u32[]{:S(2)}) collective-permute-start(f32[128,128]{1,0:T(8,128)S(1)} %get-tuple-element.71.refs_3_.refs_0_), channel_id=1, source_target_pairs={{0,1},{1,0},{2,3},{3,2},{4,5},{5,4},{6,7},{7,6},{8,9},{9,8},{10,11... | collective-permute-start | bytes 196616 | tf_op jit(solution)/shard_map/ppermute | solution.py:372
  13.5 1.3 %shard_map.80 = (bf16[512,512]{1,0:T(8,128)(2,1)S(1)}, bf16[512,512]{1,0:T(8,128)(2,1)S(1)}, f32[128,256]{1,0:T(8,128)S(1)}) custom-call(bf16[512,512]{1,0:T(8,128)(2,1)S(1)} %get-tuple-element.70.refs_5_.refs_0_, f32[512,512]{1,0:T(8,128)S(1)} %bitcast.11, f32[128,256]{1,0:T(8,128)S(1)} %get-tuple-element.73.refs_2_, ...), custom_call_target="tpu_custom_call" | custom-call | flops 1073741824 | bytes 2359296 | tf_op jit(solution)/shard_map/pallas_call | solution.py:35
  14.9 0.5 collective-permute-start.6
  15.5 0.7 collective-permute-done.3.refs_1_
  16.4 3.7 %collective-permute-start.5 = (f32[128,128]{1,0:T(8,128)S(1)}, f32[128,128]{1,0:T(8,128)S(1)}, u32[]{:S(2)}, u32[]{:S(2)}) collective-permute-start(f32[128,128]{1,0:T(8,128)S(1)} %get-tuple-element.78.refs_4_), channel_id=1, source_target_pairs={{0,3},{3,0},{1,2},{2,1},{4,7},{7,4},{5,6},{6,5},{8,11},{11,8},{9,1... | collective-permute-start | bytes 196616 | tf_op jit(solution)/shard_map/ppermute | solution.py:382
  20.4 2.5 %collective-permute-start.7 = (f32[128,256]{1,0:T(8,128)S(1)}, f32[128,256]{1,0:T(8,128)S(1)}, u32[]{:S(2)}, u32[]{:S(2)}) collective-permute-start(f32[128,256]{1,0:T(8,128)S(1)} %get-tuple-element.82.refs_6_), channel_id=1, source_target_pairs={{0,3},{3,0},{1,2},{2,1},{4,7},{7,4},{5,6},{6,5},{8,11},{11,8},{9,1... | collective-permute-start | bytes 393224 | tf_op jit(solution)/shard_map/ppermute | solution.py:382
  22.9 1.0 %shard_map.84.refs_2_.refs_4_ = f32[512,384]{1,0:T(8,128)S(1)} custom-call(f32[512,384]{1,0:T(8,128)S(1)} %get-tuple-element.79.refs_0_.refs_2_.refs_3_, bf16[512,512]{1,0:T(8,128)(2,1)S(1)} %get-tuple-element.74.refs_2_.refs_1_, bf16[512,512]{1,0:T(8,128)(2,1)S(1)} %get-tuple-element.80.refs_2_, f32[96,384]{1,0:T(8,128)S(1)} %collective-permute-done.refs_2_.refs_3_, ...), custom_call_target="tpu_custom_call" | custom-call | flops 9663676416 | bytes 37748736 | tf_op jit(solution)/shard_map/pallas_call | solution.py:35
  24.2 3.1 %collective-permute-done.7.refs_1_ = f32[128,256]{1,0:T(8,128)S(1)} collective-permute-done((f32[128,256]{1,0:T(8,128)S(1)}, f32[128,256]{1,0:T(8,128)S(1)}, u32[]{:S(2)}, u32[]{:S(2)}) %collective-permute-start.7) | collective-permute-done | bytes 131104 | tf_op jit(solution)/shard_map/ppermute | solution.py:382
  27.6 1.9 %collective-permute-start.8 = (f32[96,384]{1,0:T(8,128)S(1)}, f32[96,384]{1,0:T(8,128)S(1)}, u32[]{:S(2)}, u32[]{:S(2)}) collective-permute-start(f32[96,384]{1,0:T(8,128)S(1)} %get-tuple-element.90), channel_id=1, source_target_pairs={{0,16},{4,20},{8,24},{12,28},{16,0},{20,4},{24,8},{28,12},{1,17},{... | collective-permute-start | bytes 442376 | tf_op jit(solution)/shard_map/ppermute | solution.py:330
  29.5 1.3 %collective-permute-start.10 = (f32[96,384]{1,0:T(8,128)S(1)}, f32[96,384]{1,0:T(8,128)S(1)}, u32[]{:S(2)}, u32[]{:S(2)}) collective-permute-start(f32[96,384]{1,0:T(8,128)S(1)} %get-tuple-element.92), channel_id=1, source_target_pairs={{0,4},{4,0},{8,12},{12,8},{16,20},{20,16},{24,28},{28,24},{1,5},{5... | collective-permute-start | bytes 442376 | tf_op jit(solution)/shard_map/ppermute | solution.py:330
  30.8 1.3 %shard_map.87 = (bf16[512,512]{1,0:T(8,128)(2,1)S(1)}, bf16[512,512]{1,0:T(8,128)(2,1)S(1)}, bf16[288,864]{1,0:T(8,128)(2,1)S(1)}) custom-call(bf16[512,512]{1,0:T(8,128)(2,1)S(1)} %get-tuple-element.70.refs_5_.refs_0_, bf16[512,512]{1,0:T(8,128)(2,1)S(1)} %get-tuple-element.64.refs_1_.refs_0_, f32[512,512]{1,0:T(8,128)S(1)} %bitcast.12, ...), custom_call_target="tpu_custom_call" | custom-call | flops 1073741824 | bytes 2359296 | tf_op jit(solution)/shard_map/pallas_call | solution.py:35
  32.1 1.0 %shard_map.88 = (f32[512,384]{1,0:T(8,128)S(1)}, f32[512,384]{1,0:T(8,128)S(1)}) custom-call(f32[512,128]{1,0:T(8,128)S(1)} %shard_map.85.refs_4_.refs_5_.refs_0_, f32[512,256]{1,0:T(8,128)S(1)} %get-tuple-element.85.refs_3_.refs_1_, f32[512,384]{1,0:T(8,128)S(1)} %get-tuple-element.79.refs_0_.refs_2_.refs_3_, ...), custom_call_target="tpu_custom_call" | custom-call | flops 603979776 | bytes 3145728 | tf_op jit(solution)/shard_map/pallas_call | solution.py:35
  33.1 1.9 %collective-permute-done.9.refs_3_.refs_5_ = f32[96,384]{1,0:T(8,128)S(1)} collective-permute-done((f32[96,384]{1,0:T(8,128)S(1)}, f32[96,384]{1,0:T(8,128)S(1)}, u32[]{:S(2)}, u32[]{:S(2)}) %collective-permute-start.9) | collective-permute-done | bytes 147488 | tf_op jit(solution)/shard_map/ppermute | solution.py:330
  35.1 0.5 shard_map.89
  35.6 1.7 %collective-permute-start.11 = (f32[96,384]{1,0:T(8,128)S(1)}, f32[96,384]{1,0:T(8,128)S(1)}, u32[]{:S(2)}, u32[]{:S(2)}) collective-permute-start(f32[96,384]{1,0:T(8,128)S(1)} %get-tuple-element.94.refs_7_.refs_12_), channel_id=1, source_target_pairs={{0,16},{4,20},{8,24},{12,28},{16,0},{20,4},{24,8},{28,12},{1,17},{... | collective-permute-start | bytes 442376 | tf_op jit(solution)/shard_map/ppermute | solution.py:330
  37.3 0.8 %collective-permute-start.13 = (f32[96,384]{1,0:T(8,128)S(1)}, f32[96,384]{1,0:T(8,128)S(1)}, u32[]{:S(2)}, u32[]{:S(2)}) collective-permute-start(f32[96,384]{1,0:T(8,128)S(1)} %get-tuple-element.96.refs_9_), channel_id=1, source_target_pairs={{0,4},{4,0},{8,12},{12,8},{16,20},{20,16},{24,28},{28,24},{1,5},{5... | collective-permute-start | bytes 442376 | tf_op jit(solution)/shard_map/ppermute | solution.py:330
  38.1 0.9 %shard_map.90 = (f32[128,384]{1,0:T(8,128)S(1)}, f32[512,384]{1,0:T(8,128)S(1)}, f32[512,384]{1,0:T(8,128)S(1)}) custom-call(f32[512,384]{1,0:T(8,128)S(1)} %get-tuple-element.88.refs_0_.refs_5_, f32[512,384]{1,0:T(8,128)S(1)} %get-tuple-element.89.refs_1_, bf16[512,512]{1,0:T(8,128)(2,1)S(1)} %get-tuple-element.86.refs_3_.refs_5_.refs_2_.refs_4_, ...), custom_call_target="tpu_custom_call" | custom-call | flops 301989888 | bytes 3145728 | tf_op jit(solution)/shard_map/pallas_call | solution.py:35
  39.0 2.9 %collective-permute-done.11.refs_2_.refs_3_ = f32[96,384]{1,0:T(8,128)S(1)} collective-permute-done((f32[96,384]{1,0:T(8,128)S(1)}, f32[96,384]{1,0:T(8,128)S(1)}, u32[]{:S(2)}, u32[]{:S(2)}) %collective-permute-start.11) | collective-permute-done | bytes 147488 | tf_op jit(solution)/shard_map/ppermute | solution.py:330
  41.8 1.4 %collective-permute-done.12.refs_3_.refs_4_ = f32[96,384]{1,0:T(8,128)S(1)} collective-permute-done((f32[96,384]{1,0:T(8,128)S(1)}, f32[96,384]{1,0:T(8,128)S(1)}, u32[]{:S(2)}, u32[]{:S(2)}) %collective-permute-start.12) | collective-permute-done | bytes 147488 | tf_op jit(solution)/shard_map/ppermute | solution.py:330
  43.3 0.3 shard_map.91
  43.6 1.8 %collective-permute-start.14 = (f32[128,128]{1,0:T(8,128)S(1)}, f32[128,128]{1,0:T(8,128)S(1)}, u32[]{:S(2)}, u32[]{:S(2)}) collective-permute-start(f32[128,128]{1,0:T(8,128)S(1)} %get-tuple-element.100.refs_0_.refs_4_), channel_id=1, source_target_pairs={{0,1},{1,0},{2,3},{3,2},{4,5},{5,4},{6,7},{7,6},{8,9},{9,8},{10,11... | collective-permute-start | bytes 196616 | tf_op jit(solution)/shard_map/ppermute | solution.py:372
  45.7 2.9 %collective-permute-done.14.refs_1_ = f32[128,128]{1,0:T(8,128)S(1)} collective-permute-done((f32[128,128]{1,0:T(8,128)S(1)}, f32[128,128]{1,0:T(8,128)S(1)}, u32[]{:S(2)}, u32[]{:S(2)}) %collective-permute-start.14) | collective-permute-done | bytes 65568 | tf_op jit(solution)/shard_map/ppermute | solution.py:372
  48.8 2.2 %collective-permute-start.15 = (f32[128,128]{1,0:T(8,128)S(1)}, f32[128,128]{1,0:T(8,128)S(1)}, u32[]{:S(2)}, u32[]{:S(2)}) collective-permute-start(f32[128,128]{1,0:T(8,128)S(1)} %get-tuple-element.102.refs_4_), channel_id=1, source_target_pairs={{0,3},{3,0},{1,2},{2,1},{4,7},{7,4},{5,6},{6,5},{8,11},{11,8},{9,1... | collective-permute-start | bytes 196616 | tf_op jit(solution)/shard_map/ppermute | solution.py:382
  51.3 1.8 %collective-permute-start.17 = (f32[128,256]{1,0:T(8,128)S(1)}, f32[128,256]{1,0:T(8,128)S(1)}, u32[]{:S(2)}, u32[]{:S(2)}) collective-permute-start(f32[128,256]{1,0:T(8,128)S(1)} %get-tuple-element.105.refs_6_), channel_id=1, source_target_pairs={{0,3},{3,0},{1,2},{2,1},{4,7},{7,4},{5,6},{6,5},{8,11},{11,8},{9,1... | collective-permute-start | bytes 393224 | tf_op jit(solution)/shard_map/ppermute | solution.py:382
  53.1 1.0 %shard_map.94.refs_2_.refs_4_ = f32[512,384]{1,0:T(8,128)S(1)} custom-call(f32[512,384]{1,0:T(8,128)S(1)} %get-tuple-element.103.refs_0_, bf16[512,512]{1,0:T(8,128)(2,1)S(1)} %get-tuple-element.74.refs_2_.refs_1_, bf16[512,512]{1,0:T(8,128)(2,1)S(1)} %get-tuple-element.80.refs_2_, f32[96,384]{1,0:T(8,128)S(1)} %collective-permute-done.11.refs_2_.refs_3_, ...), custom_call_target="tpu_custom_call" | custom-call | flops 9663676416 | bytes 37748736 | tf_op jit(solution)/shard_map/pallas_call | solution.py:35
  54.1 1.6 %collective-permute-done.15.refs_1_ = f32[128,128]{1,0:T(8,128)S(1)} collective-permute-done((f32[128,128]{1,0:T(8,128)S(1)}, f32[128,128]{1,0:T(8,128)S(1)}, u32[]{:S(2)}, u32[]{:S(2)}) %collective-permute-start.15) | collective-permute-done | bytes 65568 | tf_op jit(solution)/shard_map/ppermute | solution.py:382
  55.9 2.3 %collective-permute-done.17.refs_1_ = f32[128,256]{1,0:T(8,128)S(1)} collective-permute-done((f32[128,256]{1,0:T(8,128)S(1)}, f32[128,256]{1,0:T(8,128)S(1)}, u32[]{:S(2)}, u32[]{:S(2)}) %collective-permute-start.17) | collective-permute-done | bytes 131104 | tf_op jit(solution)/shard_map/ppermute | solution.py:382
  58.6 1.3 %collective-permute-start.18 = (f32[96,384]{1,0:T(8,128)S(1)}, f32[96,384]{1,0:T(8,128)S(1)}, u32[]{:S(2)}, u32[]{:S(2)}) collective-permute-start(f32[96,384]{1,0:T(8,128)S(1)} %get-tuple-element.111), channel_id=1, source_target_pairs={{0,16},{4,20},{8,24},{12,28},{16,0},{20,4},{24,8},{28,12},{1,17},{... | collective-permute-start | bytes 442376 | tf_op jit(solution)/shard_map/ppermute | solution.py:330
  59.8 1.0 %collective-permute-start.20 = (f32[96,384]{1,0:T(8,128)S(1)}, f32[96,384]{1,0:T(8,128)S(1)}, u32[]{:S(2)}, u32[]{:S(2)}) collective-permute-start(f32[96,384]{1,0:T(8,128)S(1)} %get-tuple-element.113), channel_id=1, source_target_pairs={{0,4},{4,0},{8,12},{12,8},{16,20},{20,16},{24,28},{28,24},{1,5},{5... | collective-permute-start | bytes 442376 | tf_op jit(solution)/shard_map/ppermute | solution.py:330
  60.8 1.0 %shard_map.97 = (f32[512,384]{1,0:T(8,128)S(1)}, f32[512,384]{1,0:T(8,128)S(1)}) custom-call(f32[512,128]{1,0:T(8,128)S(1)} %shard_map.95.refs_4_.refs_5_.refs_0_, f32[512,256]{1,0:T(8,128)S(1)} %get-tuple-element.107.refs_1_.refs_6_, f32[512,384]{1,0:T(8,128)S(1)} %get-tuple-element.108.refs_2_, f32[512,384]{1,0:T(8,128)S(1)} %get-tuple-element.79.refs_0_.refs_2_.refs_3_, ...), custom_call_target="tpu_custom_call" | custom-call | flops 603979776 | bytes 3145728 | tf_op jit(solution)/shard_map/pallas_call | solution.py:35
  61.8 2.0 %collective-permute-done.18.refs_2_.refs_4_ = f32[96,384]{1,0:T(8,128)S(1)} collective-permute-done((f32[96,384]{1,0:T(8,128)S(1)}, f32[96,384]{1,0:T(8,128)S(1)}, u32[]{:S(2)}, u32[]{:S(2)}) %collective-permute-start.18) | collective-permute-done | bytes 147488 | tf_op jit(solution)/shard_map/ppermute | solution.py:330
  63.8 1.9 %collective-permute-done.19.refs_3_.refs_5_ = f32[96,384]{1,0:T(8,128)S(1)} collective-permute-done((f32[96,384]{1,0:T(8,128)S(1)}, f32[96,384]{1,0:T(8,128)S(1)}, u32[]{:S(2)}, u32[]{:S(2)}) %collective-permute-start.19) | collective-permute-done | bytes 147488 | tf_op jit(solution)/shard_map/ppermute | solution.py:330
  65.7 0.5 shard_map.98
  66.2 1.2 %collective-permute-start.21 = (f32[96,384]{1,0:T(8,128)S(1)}, f32[96,384]{1,0:T(8,128)S(1)}, u32[]{:S(2)}, u32[]{:S(2)}) collective-permute-start(f32[96,384]{1,0:T(8,128)S(1)} %get-tuple-element.114.refs_7_.refs_10_), channel_id=1, source_target_pairs={{0,16},{4,20},{8,24},{12,28},{16,0},{20,4},{24,8},{28,12},{1,17},{... | collective-permute-start | bytes 442376 | tf_op jit(solution)/shard_map/ppermute | solution.py:330
  67.7 0.4 collective-permute-start.23
  68.1 0.5 shard_map.99
  68.6 1.6 %shard_map.100 = (f32[512,384]{1,0:T(8,128)S(1)}, f32[512,384]{1,0:T(8,128)}) custom-call(bf16[512,512]{1,0:T(8,128)(2,1)S(1)} %get-tuple-element.64.refs_1_.refs_0_, f32[512,384]{1,0:T(8,128)S(1)} %get-tuple-element.117.refs_1_, f32[512,384]{1,0:T(8,128)S(1)} %get-tuple-element.118.refs_2_.refs_3_, f32[512,384]{1,0:T(8,128)S(1)} %get-tuple-element.118.refs_2_.refs_3_), custom_call_target="tpu_custom_call" | custom-call | flops 805306368 | bytes 1966080 | tf_op jit(solution)/shard_map/pallas_call | solution.py:35
  70.2 1.3 %collective-permute-done.21.refs_2_ = f32[96,384]{1,0:T(8,128)S(1)} collective-permute-done((f32[96,384]{1,0:T(8,128)S(1)}, f32[96,384]{1,0:T(8,128)S(1)}, u32[]{:S(2)}, u32[]{:S(2)}) %collective-permute-start.21) | collective-permute-done | bytes 147488 | tf_op jit(solution)/shard_map/ppermute | solution.py:330
  71.5 1.8 %collective-permute-done.22.refs_3_ = f32[96,384]{1,0:T(8,128)S(1)} collective-permute-done((f32[96,384]{1,0:T(8,128)S(1)}, f32[96,384]{1,0:T(8,128)S(1)}, u32[]{:S(2)}, u32[]{:S(2)}) %collective-permute-start.22) | collective-permute-done | bytes 147488 | tf_op jit(solution)/shard_map/ppermute | solution.py:330
  73.3 1.4 %shard_map.101 = f32[512,384]{1,0:T(8,128)} custom-call(bf16[512,576]{1,0:T(8,128)(2,1)S(1)} %get-tuple-element.120.refs_0_, f32[512,384]{1,0:T(8,128)S(1)} %get-tuple-element.121.refs_1_.refs_5_, f32[96,384]{1,0:T(8,128)S(1)} %collective-permute-done.21.refs_2_, f32[96,384]{1,0:T(8,128)S(1)} %collective-permute-done.22.refs_3_, ...), custom_call_target="tpu_custom_call" | custom-call | flops 402653184 | bytes 1966080 | tf_op jit(solution)/shard_map/pallas_call | solution.py:35
  (33 shorter events, 2.8 us)
Async XLA Ops:
  0.6 7.9 %copy-start = (f32[1,1,512,128]{3,2,1,0:T(8,128)S(1)}, f32[1,1,512,128]{3,2,1,0:T(8,128)}, u32[]{:S(2)}) copy-start(f32[1,1,512,128]{3,2,1,0:T(8,128)} %param.9) | copy-start | bytes 786436
  2.4 7.8 %collective-permute-start = (f32[96,384]{1,0:T(8,128)S(1)}, f32[96,384]{1,0:T(8,128)S(1)}, u32[]{:S(2)}, u32[]{:S(2)}) collective-permute-start(f32[96,384]{1,0:T(8,128)S(1)} %get-tuple-element.67), channel_id=1, source_target_pairs={{0,16},{4,20},{8,24},{12,28},{16,0},{20,4},{24,8},{28,12},{1,17},{... | collective-permute-start | bytes 442376 | tf_op jit(solution)/shard_map/ppermute | solution.py:330
  5.4 6.1 %collective-permute-start.1 = (f32[96,384]{1,0:T(8,128)S(1)}, f32[96,384]{1,0:T(8,128)S(1)}, u32[]{:S(2)}, u32[]{:S(2)}) collective-permute-start(f32[96,384]{1,0:T(8,128)S(1)} %get-tuple-element.68), channel_id=1, source_target_pairs={{0,28},{4,8},{8,4},{12,16},{16,12},{20,24},{24,20},{28,0},{1,29},{... | collective-permute-start | bytes 442376 | tf_op jit(solution)/shard_map/ppermute | solution.py:330
  6.0 5.5 %collective-permute-start.2 = (f32[96,384]{1,0:T(8,128)S(1)}, f32[96,384]{1,0:T(8,128)S(1)}, u32[]{:S(2)}, u32[]{:S(2)}) collective-permute-start(f32[96,384]{1,0:T(8,128)S(1)} %get-tuple-element.69), channel_id=1, source_target_pairs={{0,4},{4,0},{8,12},{12,8},{16,20},{20,16},{24,28},{28,24},{1,5},{5... | collective-permute-start | bytes 442376 | tf_op jit(solution)/shard_map/ppermute | solution.py:330
  7.0 8.4 %collective-permute-start.4 = (f32[128,128]{1,0:T(8,128)S(1)}, f32[128,128]{1,0:T(8,128)S(1)}, u32[]{:S(2)}, u32[]{:S(2)}) collective-permute-start(f32[128,128]{1,0:T(8,128)S(1)} %get-tuple-element.72), channel_id=1, source_target_pairs={{0,1},{1,0},{2,3},{3,2},{4,5},{5,4},{6,7},{7,6},{8,9},{9,8},{10,11... | collective-permute-start | bytes 196616 | tf_op jit(solution)/shard_map/ppermute | solution.py:352
  10.2 3.3 %copy-start.2 = (f32[1,1,512,512]{3,2,1,0:T(8,128)S(1)}, f32[1,1,512,512]{3,2,1,0:T(8,128)}, u32[]{:S(2)}) copy-start(f32[1,1,512,512]{3,2,1,0:T(8,128)} %param.8) | copy-start | bytes 3145732
  11.8 4.3 %collective-permute-start.3 = (f32[128,128]{1,0:T(8,128)S(1)}, f32[128,128]{1,0:T(8,128)S(1)}, u32[]{:S(2)}, u32[]{:S(2)}) collective-permute-start(f32[128,128]{1,0:T(8,128)S(1)} %get-tuple-element.71.refs_3_.refs_0_), channel_id=1, source_target_pairs={{0,1},{1,0},{2,3},{3,2},{4,5},{5,4},{6,7},{7,6},{8,9},{9,8},{10,11... | collective-permute-start | bytes 196616 | tf_op jit(solution)/shard_map/ppermute | solution.py:372
  13.5 1.9 %copy-start.1 = (f32[1,512,128]{2,1,0:T(8,128)S(1)}, f32[1,512,128]{2,1,0:T(8,128)}, u32[]{:S(2)}) copy-start(f32[1,512,128]{2,1,0:T(8,128)} %param.10) | copy-start | bytes 786436
  14.9 5.3 %collective-permute-start.6 = (f32[128,256]{1,0:T(8,128)S(1)}, f32[128,256]{1,0:T(8,128)S(1)}, u32[]{:S(2)}, u32[]{:S(2)}) collective-permute-start(f32[128,256]{1,0:T(8,128)S(1)} %get-tuple-element.81.refs_0_), channel_id=1, source_target_pairs={{0,1},{1,0},{2,3},{3,2},{4,5},{5,4},{6,7},{7,6},{8,9},{9,8},{10,11... | collective-permute-start | bytes 393224 | tf_op jit(solution)/shard_map/ppermute | solution.py:372
  16.4 7.5 %collective-permute-start.5 = (f32[128,128]{1,0:T(8,128)S(1)}, f32[128,128]{1,0:T(8,128)S(1)}, u32[]{:S(2)}, u32[]{:S(2)}) collective-permute-start(f32[128,128]{1,0:T(8,128)S(1)} %get-tuple-element.78.refs_4_), channel_id=1, source_target_pairs={{0,3},{3,0},{1,2},{2,1},{4,7},{7,4},{5,6},{6,5},{8,11},{11,8},{9,1... | collective-permute-start | bytes 196616 | tf_op jit(solution)/shard_map/ppermute | solution.py:382
  20.4 6.9 %collective-permute-start.7 = (f32[128,256]{1,0:T(8,128)S(1)}, f32[128,256]{1,0:T(8,128)S(1)}, u32[]{:S(2)}, u32[]{:S(2)}) collective-permute-start(f32[128,256]{1,0:T(8,128)S(1)} %get-tuple-element.82.refs_6_), channel_id=1, source_target_pairs={{0,3},{3,0},{1,2},{2,1},{4,7},{7,4},{5,6},{6,5},{8,11},{11,8},{9,1... | collective-permute-start | bytes 393224 | tf_op jit(solution)/shard_map/ppermute | solution.py:382
  24.2 6.6 %copy-start.3 = (f32[1,1,512,512]{3,2,1,0:T(8,128)S(1)}, f32[1,1,512,512]{3,2,1,0:T(8,128)}, u32[]{:S(2)}) copy-start(f32[1,1,512,512]{3,2,1,0:T(8,128)} %param.7) | copy-start | bytes 3145732
  27.6 5.5 %collective-permute-start.8 = (f32[96,384]{1,0:T(8,128)S(1)}, f32[96,384]{1,0:T(8,128)S(1)}, u32[]{:S(2)}, u32[]{:S(2)}) collective-permute-start(f32[96,384]{1,0:T(8,128)S(1)} %get-tuple-element.90), channel_id=1, source_target_pairs={{0,16},{4,20},{8,24},{12,28},{16,0},{20,4},{24,8},{28,12},{1,17},{... | collective-permute-start | bytes 442376 | tf_op jit(solution)/shard_map/ppermute | solution.py:330
  29.5 5.6 %collective-permute-start.9 = (f32[96,384]{1,0:T(8,128)S(1)}, f32[96,384]{1,0:T(8,128)S(1)}, u32[]{:S(2)}, u32[]{:S(2)}) collective-permute-start(f32[96,384]{1,0:T(8,128)S(1)} %get-tuple-element.91), channel_id=1, source_target_pairs={{0,28},{4,8},{8,4},{12,16},{16,12},{20,24},{24,20},{28,0},{1,29},{... | collective-permute-start | bytes 442376 | tf_op jit(solution)/shard_map/ppermute | solution.py:330
  29.5 5.6 %collective-permute-start.10 = (f32[96,384]{1,0:T(8,128)S(1)}, f32[96,384]{1,0:T(8,128)S(1)}, u32[]{:S(2)}, u32[]{:S(2)}) collective-permute-start(f32[96,384]{1,0:T(8,128)S(1)} %get-tuple-element.92), channel_id=1, source_target_pairs={{0,4},{4,0},{8,12},{12,8},{16,20},{20,16},{24,28},{28,24},{1,5},{5... | collective-permute-start | bytes 442376 | tf_op jit(solution)/shard_map/ppermute | solution.py:330
  35.6 6.3 %collective-permute-start.11 = (f32[96,384]{1,0:T(8,128)S(1)}, f32[96,384]{1,0:T(8,128)S(1)}, u32[]{:S(2)}, u32[]{:S(2)}) collective-permute-start(f32[96,384]{1,0:T(8,128)S(1)} %get-tuple-element.94.refs_7_.refs_12_), channel_id=1, source_target_pairs={{0,16},{4,20},{8,24},{12,28},{16,0},{20,4},{24,8},{28,12},{1,17},{... | collective-permute-start | bytes 442376 | tf_op jit(solution)/shard_map/ppermute | solution.py:330
  37.3 6.0 %collective-permute-start.12 = (f32[96,384]{1,0:T(8,128)S(1)}, f32[96,384]{1,0:T(8,128)S(1)}, u32[]{:S(2)}, u32[]{:S(2)}) collective-permute-start(f32[96,384]{1,0:T(8,128)S(1)} %get-tuple-element.95.refs_8_), channel_id=1, source_target_pairs={{0,28},{4,8},{8,4},{12,16},{16,12},{20,24},{24,20},{28,0},{1,29},{... | collective-permute-start | bytes 442376 | tf_op jit(solution)/shard_map/ppermute | solution.py:330
  37.3 6.0 %collective-permute-start.13 = (f32[96,384]{1,0:T(8,128)S(1)}, f32[96,384]{1,0:T(8,128)S(1)}, u32[]{:S(2)}, u32[]{:S(2)}) collective-permute-start(f32[96,384]{1,0:T(8,128)S(1)} %get-tuple-element.96.refs_9_), channel_id=1, source_target_pairs={{0,4},{4,0},{8,12},{12,8},{16,20},{20,16},{24,28},{28,24},{1,5},{5... | collective-permute-start | bytes 442376 | tf_op jit(solution)/shard_map/ppermute | solution.py:330
  43.6 5.0 %collective-permute-start.14 = (f32[128,128]{1,0:T(8,128)S(1)}, f32[128,128]{1,0:T(8,128)S(1)}, u32[]{:S(2)}, u32[]{:S(2)}) collective-permute-start(f32[128,128]{1,0:T(8,128)S(1)} %get-tuple-element.100.refs_0_.refs_4_), channel_id=1, source_target_pairs={{0,1},{1,0},{2,3},{3,2},{4,5},{5,4},{6,7},{7,6},{8,9},{9,8},{10,11... | collective-permute-start | bytes 196616 | tf_op jit(solution)/shard_map/ppermute | solution.py:372
  45.4 5.6 %collective-permute-start.16 = (f32[128,256]{1,0:T(8,128)S(1)}, f32[128,256]{1,0:T(8,128)S(1)}, u32[]{:S(2)}, u32[]{:S(2)}) collective-permute-start(f32[128,256]{1,0:T(8,128)S(1)} %get-tuple-element.104.refs_0_), channel_id=1, source_target_pairs={{0,1},{1,0},{2,3},{3,2},{4,5},{5,4},{6,7},{7,6},{8,9},{9,8},{10,11... | collective-permute-start | bytes 393224 | tf_op jit(solution)/shard_map/ppermute | solution.py:372
  48.8 6.8 %collective-permute-start.15 = (f32[128,128]{1,0:T(8,128)S(1)}, f32[128,128]{1,0:T(8,128)S(1)}, u32[]{:S(2)}, u32[]{:S(2)}) collective-permute-start(f32[128,128]{1,0:T(8,128)S(1)} %get-tuple-element.102.refs_4_), channel_id=1, source_target_pairs={{0,3},{3,0},{1,2},{2,1},{4,7},{7,4},{5,6},{6,5},{8,11},{11,8},{9,1... | collective-permute-start | bytes 196616 | tf_op jit(solution)/shard_map/ppermute | solution.py:382
  51.3 6.9 %collective-permute-start.17 = (f32[128,256]{1,0:T(8,128)S(1)}, f32[128,256]{1,0:T(8,128)S(1)}, u32[]{:S(2)}, u32[]{:S(2)}) collective-permute-start(f32[128,256]{1,0:T(8,128)S(1)} %get-tuple-element.105.refs_6_), channel_id=1, source_target_pairs={{0,3},{3,0},{1,2},{2,1},{4,7},{7,4},{5,6},{6,5},{8,11},{11,8},{9,1... | collective-permute-start | bytes 393224 | tf_op jit(solution)/shard_map/ppermute | solution.py:382
  58.6 5.2 %collective-permute-start.18 = (f32[96,384]{1,0:T(8,128)S(1)}, f32[96,384]{1,0:T(8,128)S(1)}, u32[]{:S(2)}, u32[]{:S(2)}) collective-permute-start(f32[96,384]{1,0:T(8,128)S(1)} %get-tuple-element.111), channel_id=1, source_target_pairs={{0,16},{4,20},{8,24},{12,28},{16,0},{20,4},{24,8},{28,12},{1,17},{... | collective-permute-start | bytes 442376 | tf_op jit(solution)/shard_map/ppermute | solution.py:330
  59.8 5.9 %collective-permute-start.19 = (f32[96,384]{1,0:T(8,128)S(1)}, f32[96,384]{1,0:T(8,128)S(1)}, u32[]{:S(2)}, u32[]{:S(2)}) collective-permute-start(f32[96,384]{1,0:T(8,128)S(1)} %get-tuple-element.112), channel_id=1, source_target_pairs={{0,28},{4,8},{8,4},{12,16},{16,12},{20,24},{24,20},{28,0},{1,29},{... | collective-permute-start | bytes 442376 | tf_op jit(solution)/shard_map/ppermute | solution.py:330
  59.8 5.9 %collective-permute-start.20 = (f32[96,384]{1,0:T(8,128)S(1)}, f32[96,384]{1,0:T(8,128)S(1)}, u32[]{:S(2)}, u32[]{:S(2)}) collective-permute-start(f32[96,384]{1,0:T(8,128)S(1)} %get-tuple-element.113), channel_id=1, source_target_pairs={{0,4},{4,0},{8,12},{12,8},{16,20},{20,16},{24,28},{28,24},{1,5},{5... | collective-permute-start | bytes 442376 | tf_op jit(solution)/shard_map/ppermute | solution.py:330
  66.2 5.3 %collective-permute-start.21 = (f32[96,384]{1,0:T(8,128)S(1)}, f32[96,384]{1,0:T(8,128)S(1)}, u32[]{:S(2)}, u32[]{:S(2)}) collective-permute-start(f32[96,384]{1,0:T(8,128)S(1)} %get-tuple-element.114.refs_7_.refs_10_), channel_id=1, source_target_pairs={{0,16},{4,20},{8,24},{12,28},{16,0},{20,4},{24,8},{28,12},{1,17},{... | collective-permute-start | bytes 442376 | tf_op jit(solution)/shard_map/ppermute | solution.py:330
  67.4 5.9 %collective-permute-start.22 = (f32[96,384]{1,0:T(8,128)S(1)}, f32[96,384]{1,0:T(8,128)S(1)}, u32[]{:S(2)}, u32[]{:S(2)}) collective-permute-start(f32[96,384]{1,0:T(8,128)S(1)} %get-tuple-element.115.refs_8_), channel_id=1, source_target_pairs={{0,28},{4,8},{8,4},{12,16},{16,12},{20,24},{24,20},{28,0},{1,29},{... | collective-permute-start | bytes 442376 | tf_op jit(solution)/shard_map/ppermute | solution.py:330
  67.7 5.6 %collective-permute-start.23 = (f32[96,384]{1,0:T(8,128)S(1)}, f32[96,384]{1,0:T(8,128)S(1)}, u32[]{:S(2)}, u32[]{:S(2)}) collective-permute-start(f32[96,384]{1,0:T(8,128)S(1)} %get-tuple-element.116.refs_9_), channel_id=1, source_target_pairs={{0,4},{4,0},{8,12},{12,8},{16,20},{20,16},{24,28},{28,24},{1,5},{5... | collective-permute-start | bytes 442376 | tf_op jit(solution)/shard_map/ppermute | solution.py:330

commit v10 on v9

--- a/solution.py
+++ b/solution.py
@@ -79,8 +79,8 @@
     over, under = sub < subs - ROW_SUBS, sub >= ROW_SUBS
     return [
         (low_row, 3, 2, jnp.where(low_row, over, under)),
+        (low_side, 1, 0, jnp.where(low_side, up, down)),
         (low_side, 0, 1, jnp.where(low_side, down, up)),
-        (low_side, 1, 0, jnp.where(low_side, up, down)),
         (low_row, 2, 3, jnp.where(low_row, under, over)),
     ]
 
@@ -322,7 +322,7 @@
     if lax.axis_size("grp") != GROUPS or sum(PIECES) != loads:
         raise ValueError("unexpected sizes")
 
-    plans = [swaps(subs, ROW_SUBS, 0), swaps(subs, 1, 1), swaps(subs, 1, 0), swaps(subs, ROW_SUBS, 1)]
+    plans = [swaps(subs, ROW_SUBS, 0), swaps(subs, 1, 0), swaps(subs, 1, 1), swaps(subs, ROW_SUBS, 1)]
     plans = [plan for plan in plans if plan]
     count = len(plans)
 

time: 74.9 us -> 77.4 us (1.033)
  waiting for transfers between devices: 25.2 us -> 28.8 us
  starting transfers between devices: 30.5 us -> 29.4 us
    ppermute x15, waiting for transfers between devices: 14.6 us -> 17.6 us  [exchange(): return [lax.ppermute(part, 'sub', plan) for part, plan in zip(parts, plans)]]
    ppermute x15, starting transfers between devices: 14.5 us -> 12.6 us  [exchange(): return [lax.ppermute(part, 'sub', plan) for part, plan in zip(parts, plans)]]
    ppermute x4, starting transfers between devices: 10.2 us -> 11 us  [local(): came.append(lax.ppermute(away, 'grp', mirror_plan))]
  transfers between devices with their start and end apart: 24 -> 24, of which waited for: 13 -> 12; matrix products, arithmetic and copies ran while one was open for 0% -> 0% of each run, Pallas kernels for 18% -> 17%
where the time goes in v10:
time: 77.4 us; the launch traced here: 77.3 us
  starting transfers between devices  29.4 us (38%)
  waiting for transfers between devices  28.8 us (37%)
  Pallas kernels  18.2 us (24%)
  between operations  0.88 us (1%)
    pallas_call x25, Pallas kernels, __call__(): pl.pallas_call(whole_body, out_shape=[jax.ShapeDtypeStruct(shape, kind) f...  18.2 us
    ppermute x15, waiting for transfers between devices, exchange(): return [lax.ppermute(part, 'sub', plan) for part, plan in zip(parts, plans)]  17.6 us
    ppermute x15, starting transfers between devices, exchange(): return [lax.ppermute(part, 'sub', plan) for part, plan in zip(parts, plans)]  12.6 us
    ppermute x4, starting transfers between devices, local(): came.append(lax.ppermute(away, 'grp', mirror_plan))  11 us
    ppermute x4, waiting for transfers between devices, local(): came.append(lax.ppermute(away, 'grp', mirror_plan))  7.34 us
    ppermute x4, starting transfers between devices, local(): theirs = [lax.ppermute(piece, 'grp', pair_plan) for piece in own]  4.26 us
    ppermute x4, waiting for transfers between devices, local(): theirs = [lax.ppermute(piece, 'grp', pair_plan) for piece in own]  3.82 us
    ppermute x1, starting transfers between devices, local(): other = lax.ppermute(sent, 'grp', pair_plan)  1.59 us
  transfers between devices with their start and end apart: 24, of which 12 were waited for; matrix products, arithmetic and copies ran while one was open for 0% of the time, Pallas kernels for 17%

profile of v10, /device:TPU:0, one launch (start us, length us, event | category | flops | bytes accessed | tf_op | source)
XLA Modules:
  0.0 77.3 jit_solution(7550020952802369730)
XLA Ops:
  0.6 1.7 %shard_map.77 = (bf16[384,512]{1,0:T(8,128)(2,1)S(1)}, f32[512,384]{1,0:T(8,128)S(1)}, f32[128,128]{1,0:T(8,128)S(1)}, f32[96,384]{1,0:T(8,128)S(1)}, f32[96,384]{1,0:T(8,128)S(1)}, /*index=5*/f32[96,384]{1,0:T(8,128)S(1)}) custom-call(s32[4,96]{1,0:T(4,128)} %bitcast.15, f32[512,384]{1,0:T(8,128)} %bitcast.14, f32[512,128]{1,0:T(8,128)} %bitcast.9), custom_call_target="tpu_custom_call" | custom-call | flops 301989888 | bytes 3145728 | tf_op jit(solution)/shard_map/pallas_call | solution.py:35
  2.4 3.0 %collective-permute-start = (f32[96,384]{1,0:T(8,128)S(1)}, f32[96,384]{1,0:T(8,128)S(1)}, u32[]{:S(2)}, u32[]{:S(2)}) collective-permute-start(f32[96,384]{1,0:T(8,128)S(1)} %get-tuple-element.67), channel_id=1, source_target_pairs={{0,16},{4,20},{8,24},{12,28},{16,0},{20,4},{24,8},{28,12},{1,17},{... | collective-permute-start | bytes 442376 | tf_op jit(solution)/shard_map/ppermute | solution.py:330
  5.4 1.5 %collective-permute-start.2 = (f32[96,384]{1,0:T(8,128)S(1)}, f32[96,384]{1,0:T(8,128)S(1)}, u32[]{:S(2)}, u32[]{:S(2)}) collective-permute-start(f32[96,384]{1,0:T(8,128)S(1)} %get-tuple-element.69), channel_id=1, source_target_pairs={{0,28},{4,8},{8,4},{12,16},{16,12},{20,24},{24,20},{28,0},{1,29},{... | collective-permute-start | bytes 442376 | tf_op jit(solution)/shard_map/ppermute | solution.py:330
  6.9 1.6 %collective-permute-start.4 = (f32[128,128]{1,0:T(8,128)S(1)}, f32[128,128]{1,0:T(8,128)S(1)}, u32[]{:S(2)}, u32[]{:S(2)}) collective-permute-start(f32[128,128]{1,0:T(8,128)S(1)} %get-tuple-element.72), channel_id=1, source_target_pairs={{0,1},{1,0},{2,3},{3,2},{4,5},{5,4},{6,7},{7,6},{8,9},{9,8},{10,11... | collective-permute-start | bytes 196616 | tf_op jit(solution)/shard_map/ppermute | solution.py:352
  8.5 1.6 %shard_map.78 = (bf16[512,512]{1,0:T(8,128)(2,1)S(1)}, bf16[512,512]{1,0:T(8,128)(2,1)S(1)}, bf16[512,576]{1,0:T(8,128)(2,1)S(1)}, bf16[512,384]{1,0:T(8,128)(2,...) custom-call(bf16[384,512]{1,0:T(8,128)(2,1)S(1)} %get-tuple-element., ...), custom_call_target="tpu_custom_call" | custom-call | flops 402653184 | bytes 4718592 | tf_op jit(solution)/shard_map/pallas_call | solution.py:35
  10.2 1.6 %collective-permute-done.2.refs_4_.refs_5_ = f32[96,384]{1,0:T(8,128)S(1)} collective-permute-done((f32[96,384]{1,0:T(8,128)S(1)}, f32[96,384]{1,0:T(8,128)S(1)}, u32[]{:S(2)}, u32[]{:S(2)}) %collective-permute-start.2) | collective-permute-done | bytes 147488 | tf_op jit(solution)/shard_map/ppermute | solution.py:330
  11.8 0.3 shard_map.79
  12.1 2.1 %collective-permute-start.3 = (f32[128,128]{1,0:T(8,128)S(1)}, f32[128,128]{1,0:T(8,128)S(1)}, u32[]{:S(2)}, u32[]{:S(2)}) collective-permute-start(f32[128,128]{1,0:T(8,128)S(1)} %get-tuple-element.71.refs_3_.refs_0_), channel_id=1, source_target_pairs={{0,1},{1,0},{2,3},{3,2},{4,5},{5,4},{6,7},{7,6},{8,9},{9,8},{10,11... | collective-permute-start | bytes 196616 | tf_op jit(solution)/shard_map/ppermute | solution.py:372
  14.1 1.3 %shard_map.80 = (bf16[512,512]{1,0:T(8,128)(2,1)S(1)}, bf16[512,512]{1,0:T(8,128)(2,1)S(1)}, f32[128,256]{1,0:T(8,128)S(1)}) custom-call(bf16[512,512]{1,0:T(8,128)(2,1)S(1)} %get-tuple-element.70.refs_5_.refs_0_, f32[512,512]{1,0:T(8,128)S(1)} %bitcast.11, f32[128,256]{1,0:T(8,128)S(1)} %get-tuple-element.73.refs_2_, ...), custom_call_target="tpu_custom_call" | custom-call | flops 1073741824 | bytes 2359296 | tf_op jit(solution)/shard_map/pallas_call | solution.py:35
  15.7 0.9 %collective-permute-done.3.refs_1_ = f32[128,128]{1,0:T(8,128)S(1)} collective-permute-done((f32[128,128]{1,0:T(8,128)S(1)}, f32[128,128]{1,0:T(8,128)S(1)}, u32[]{:S(2)}, u32[]{:S(2)}) %collective-permute-start.3) | collective-permute-done | bytes 65568 | tf_op jit(solution)/shard_map/ppermute | solution.py:372
  16.9 4.5 %collective-permute-start.5 = (f32[128,128]{1,0:T(8,128)S(1)}, f32[128,128]{1,0:T(8,128)S(1)}, u32[]{:S(2)}, u32[]{:S(2)}) collective-permute-start(f32[128,128]{1,0:T(8,128)S(1)} %get-tuple-element.78.refs_4_), channel_id=1, source_target_pairs={{0,3},{3,0},{1,2},{2,1},{4,7},{7,4},{5,6},{6,5},{8,11},{11,8},{9,1... | collective-permute-start | bytes 196616 | tf_op jit(solution)/shard_map/ppermute | solution.py:382
  21.4 0.3 shard_map.83
  21.7 1.9 %collective-permute-start.7 = (f32[128,256]{1,0:T(8,128)S(1)}, f32[128,256]{1,0:T(8,128)S(1)}, u32[]{:S(2)}, u32[]{:S(2)}) collective-permute-start(f32[128,256]{1,0:T(8,128)S(1)} %get-tuple-element.82.refs_6_), channel_id=1, source_target_pairs={{0,3},{3,0},{1,2},{2,1},{4,7},{7,4},{5,6},{6,5},{8,11},{11,8},{9,1... | collective-permute-start | bytes 393224 | tf_op jit(solution)/shard_map/ppermute | solution.py:382
  23.6 1.0 %shard_map.84.refs_2_.refs_4_ = f32[512,384]{1,0:T(8,128)S(1)} custom-call(f32[512,384]{1,0:T(8,128)S(1)} %get-tuple-element.79.refs_0_.refs_2_.refs_3_, bf16[512,512]{1,0:T(8,128)(2,1)S(1)} %get-tuple-element.74.refs_2_.refs_1_, bf16[512,512]{1,0:T(8,128)(2,1)S(1)} %get-tuple-element.80.refs_2_, f32[96,384]{1,0:T(8,128)S(1)} %collective-permute-done.refs_2_.refs_3_, ...), custom_call_target="tpu_custom_call" | custom-call | flops 9663676416 | bytes 37748736 | tf_op jit(solution)/shard_map/pallas_call | solution.py:35
  24.6 0.3 shard_map.85.refs_4_.refs_5_.refs_0_
  24.9 3.7 %collective-permute-done.7.refs_1_ = f32[128,256]{1,0:T(8,128)S(1)} collective-permute-done((f32[128,256]{1,0:T(8,128)S(1)}, f32[128,256]{1,0:T(8,128)S(1)}, u32[]{:S(2)}, u32[]{:S(2)}) %collective-permute-start.7) | collective-permute-done | bytes 131104 | tf_op jit(solution)/shard_map/ppermute | solution.py:382
  28.6 0.3 shard_map.86
  29.1 1.5 %collective-permute-start.10 = (f32[96,384]{1,0:T(8,128)S(1)}, f32[96,384]{1,0:T(8,128)S(1)}, u32[]{:S(2)}, u32[]{:S(2)}) collective-permute-start(f32[96,384]{1,0:T(8,128)S(1)} %get-tuple-element.92), channel_id=1, source_target_pairs={{0,28},{4,8},{8,4},{12,16},{16,12},{20,24},{24,20},{28,0},{1,29},{... | collective-permute-start | bytes 442376 | tf_op jit(solution)/shard_map/ppermute | solution.py:330
  30.5 1.3 %shard_map.87 = (bf16[512,512]{1,0:T(8,128)(2,1)S(1)}, bf16[512,512]{1,0:T(8,128)(2,1)S(1)}, bf16[288,864]{1,0:T(8,128)(2,1)S(1)}) custom-call(bf16[512,512]{1,0:T(8,128)(2,1)S(1)} %get-tuple-element.70.refs_5_.refs_0_, bf16[512,512]{1,0:T(8,128)(2,1)S(1)} %get-tuple-element.64.refs_1_.refs_0_, f32[512,512]{1,0:T(8,128)S(1)} %bitcast.12, ...), custom_call_target="tpu_custom_call" | custom-call | flops 1073741824 | bytes 2359296 | tf_op jit(solution)/shard_map/pallas_call | solution.py:35
  31.9 1.0 %shard_map.88 = (f32[512,384]{1,0:T(8,128)S(1)}, f32[512,384]{1,0:T(8,128)S(1)}) custom-call(f32[512,128]{1,0:T(8,128)S(1)} %shard_map.85.refs_4_.refs_5_.refs_0_, f32[512,256]{1,0:T(8,128)S(1)} %get-tuple-element.85.refs_3_.refs_1_, f32[512,384]{1,0:T(8,128)S(1)} %get-tuple-element.79.refs_0_.refs_2_.refs_3_, ...), custom_call_target="tpu_custom_call" | custom-call | flops 603979776 | bytes 3145728 | tf_op jit(solution)/shard_map/pallas_call | solution.py:35
  32.9 2.8 %collective-permute-done.8.refs_2_.refs_4_ = f32[96,384]{1,0:T(8,128)S(1)} collective-permute-done((f32[96,384]{1,0:T(8,128)S(1)}, f32[96,384]{1,0:T(8,128)S(1)}, u32[]{:S(2)}, u32[]{:S(2)}) %collective-permute-start.8) | collective-permute-done | bytes 147488 | tf_op jit(solution)/shard_map/ppermute | solution.py:330
  35.7 0.5 shard_map.89
  36.2 1.7 %collective-permute-start.11 = (f32[96,384]{1,0:T(8,128)S(1)}, f32[96,384]{1,0:T(8,128)S(1)}, u32[]{:S(2)}, u32[]{:S(2)}) collective-permute-start(f32[96,384]{1,0:T(8,128)S(1)} %get-tuple-element.94.refs_7_.refs_12_), channel_id=1, source_target_pairs={{0,16},{4,20},{8,24},{12,28},{16,0},{20,4},{24,8},{28,12},{1,17},{... | collective-permute-start | bytes 442376 | tf_op jit(solution)/shard_map/ppermute | solution.py:330
  37.9 1.1 %collective-permute-start.13 = (f32[96,384]{1,0:T(8,128)S(1)}, f32[96,384]{1,0:T(8,128)S(1)}, u32[]{:S(2)}, u32[]{:S(2)}) collective-permute-start(f32[96,384]{1,0:T(8,128)S(1)} %get-tuple-element.96.refs_9_), channel_id=1, source_target_pairs={{0,28},{4,8},{8,4},{12,16},{16,12},{20,24},{24,20},{28,0},{1,29},{... | collective-permute-start | bytes 442376 | tf_op jit(solution)/shard_map/ppermute | solution.py:330
  39.0 0.9 %shard_map.90 = (f32[128,384]{1,0:T(8,128)S(1)}, f32[512,384]{1,0:T(8,128)S(1)}, f32[512,384]{1,0:T(8,128)S(1)}) custom-call(f32[512,384]{1,0:T(8,128)S(1)} %get-tuple-element.88.refs_0_.refs_5_, f32[512,384]{1,0:T(8,128)S(1)} %get-tuple-element.89.refs_1_, bf16[512,512]{1,0:T(8,128)(2,1)S(1)} %get-tuple-element.86.refs_3_.refs_5_.refs_2_.refs_4_, ...), custom_call_target="tpu_custom_call" | custom-call | flops 301989888 | bytes 3145728 | tf_op jit(solution)/shard_map/pallas_call | solution.py:35
  39.9 2.5 %collective-permute-done.11.refs_2_.refs_3_ = f32[96,384]{1,0:T(8,128)S(1)} collective-permute-done((f32[96,384]{1,0:T(8,128)S(1)}, f32[96,384]{1,0:T(8,128)S(1)}, u32[]{:S(2)}, u32[]{:S(2)}) %collective-permute-start.11) | collective-permute-done | bytes 147488 | tf_op jit(solution)/shard_map/ppermute | solution.py:330
  42.4 2.2 %collective-permute-done.13.refs_4_.refs_5_ = f32[96,384]{1,0:T(8,128)S(1)} collective-permute-done((f32[96,384]{1,0:T(8,128)S(1)}, f32[96,384]{1,0:T(8,128)S(1)}, u32[]{:S(2)}, u32[]{:S(2)}) %collective-permute-start.13) | collective-permute-done | bytes 147488 | tf_op jit(solution)/shard_map/ppermute | solution.py:330
  44.6 0.3 shard_map.91
  44.9 1.8 %collective-permute-start.14 = (f32[128,128]{1,0:T(8,128)S(1)}, f32[128,128]{1,0:T(8,128)S(1)}, u32[]{:S(2)}, u32[]{:S(2)}) collective-permute-start(f32[128,128]{1,0:T(8,128)S(1)} %get-tuple-element.100.refs_0_.refs_4_), channel_id=1, source_target_pairs={{0,1},{1,0},{2,3},{3,2},{4,5},{5,4},{6,7},{7,6},{8,9},{9,8},{10,11... | collective-permute-start | bytes 196616 | tf_op jit(solution)/shard_map/ppermute | solution.py:372
  46.7 0.3 collective-permute-start.16
  47.0 2.9 %collective-permute-done.14.refs_1_ = f32[128,128]{1,0:T(8,128)S(1)} collective-permute-done((f32[128,128]{1,0:T(8,128)S(1)}, f32[128,128]{1,0:T(8,128)S(1)}, u32[]{:S(2)}, u32[]{:S(2)}) %collective-permute-start.14) | collective-permute-done | bytes 65568 | tf_op jit(solution)/shard_map/ppermute | solution.py:372
  50.2 2.5 %collective-permute-start.15 = (f32[128,128]{1,0:T(8,128)S(1)}, f32[128,128]{1,0:T(8,128)S(1)}, u32[]{:S(2)}, u32[]{:S(2)}) collective-permute-start(f32[128,128]{1,0:T(8,128)S(1)} %get-tuple-element.102.refs_4_), channel_id=1, source_target_pairs={{0,3},{3,0},{1,2},{2,1},{4,7},{7,4},{5,6},{6,5},{8,11},{11,8},{9,1... | collective-permute-start | bytes 196616 | tf_op jit(solution)/shard_map/ppermute | solution.py:382
  53.0 2.1 %collective-permute-start.17 = (f32[128,256]{1,0:T(8,128)S(1)}, f32[128,256]{1,0:T(8,128)S(1)}, u32[]{:S(2)}, u32[]{:S(2)}) collective-permute-start(f32[128,256]{1,0:T(8,128)S(1)} %get-tuple-element.105.refs_6_), channel_id=1, source_target_pairs={{0,3},{3,0},{1,2},{2,1},{4,7},{7,4},{5,6},{6,5},{8,11},{11,8},{9,1... | collective-permute-start | bytes 393224 | tf_op jit(solution)/shard_map/ppermute | solution.py:382
  55.0 1.0 %shard_map.94.refs_2_.refs_4_ = f32[512,384]{1,0:T(8,128)S(1)} custom-call(f32[512,384]{1,0:T(8,128)S(1)} %get-tuple-element.103.refs_0_, bf16[512,512]{1,0:T(8,128)(2,1)S(1)} %get-tuple-element.74.refs_2_.refs_1_, bf16[512,512]{1,0:T(8,128)(2,1)S(1)} %get-tuple-element.80.refs_2_, f32[96,384]{1,0:T(8,128)S(1)} %collective-permute-done.11.refs_2_.refs_3_, ...), custom_call_target="tpu_custom_call" | custom-call | flops 9663676416 | bytes 37748736 | tf_op jit(solution)/shard_map/pallas_call | solution.py:35
  56.0 0.8 %collective-permute-done.15.refs_1_ = f32[128,128]{1,0:T(8,128)S(1)} collective-permute-done((f32[128,128]{1,0:T(8,128)S(1)}, f32[128,128]{1,0:T(8,128)S(1)}, u32[]{:S(2)}, u32[]{:S(2)}) %collective-permute-start.15) | collective-permute-done | bytes 65568 | tf_op jit(solution)/shard_map/ppermute | solution.py:382
  56.9 0.3 shard_map.95.refs_4_.refs_5_.refs_0_
  57.2 2.7 %collective-permute-done.17.refs_1_ = f32[128,256]{1,0:T(8,128)S(1)} collective-permute-done((f32[128,256]{1,0:T(8,128)S(1)}, f32[128,256]{1,0:T(8,128)S(1)}, u32[]{:S(2)}, u32[]{:S(2)}) %collective-permute-start.17) | collective-permute-done | bytes 131104 | tf_op jit(solution)/shard_map/ppermute | solution.py:382
  59.9 0.3 shard_map.96
  60.4 1.5 %collective-permute-start.20 = (f32[96,384]{1,0:T(8,128)S(1)}, f32[96,384]{1,0:T(8,128)S(1)}, u32[]{:S(2)}, u32[]{:S(2)}) collective-permute-start(f32[96,384]{1,0:T(8,128)S(1)} %get-tuple-element.113), channel_id=1, source_target_pairs={{0,28},{4,8},{8,4},{12,16},{16,12},{20,24},{24,20},{28,0},{1,29},{... | collective-permute-start | bytes 442376 | tf_op jit(solution)/shard_map/ppermute | solution.py:330
  61.9 1.0 %shard_map.97 = (f32[512,384]{1,0:T(8,128)S(1)}, f32[512,384]{1,0:T(8,128)S(1)}) custom-call(f32[512,128]{1,0:T(8,128)S(1)} %shard_map.95.refs_4_.refs_5_.refs_0_, f32[512,256]{1,0:T(8,128)S(1)} %get-tuple-element.107.refs_1_.refs_6_, f32[512,384]{1,0:T(8,128)S(1)} %get-tuple-element.108.refs_2_, f32[512,384]{1,0:T(8,128)S(1)} %get-tuple-element.79.refs_0_.refs_2_.refs_3_, ...), custom_call_target="tpu_custom_call" | custom-call | flops 603979776 | bytes 3145728 | tf_op jit(solution)/shard_map/pallas_call | solution.py:35
  62.9 4.1 %collective-permute-done.18.refs_2_.refs_4_ = f32[96,384]{1,0:T(8,128)S(1)} collective-permute-done((f32[96,384]{1,0:T(8,128)S(1)}, f32[96,384]{1,0:T(8,128)S(1)}, u32[]{:S(2)}, u32[]{:S(2)}) %collective-permute-start.18) | collective-permute-done | bytes 147488 | tf_op jit(solution)/shard_map/ppermute | solution.py:330
  67.0 0.5 shard_map.98
  67.5 1.7 %collective-permute-start.21 = (f32[96,384]{1,0:T(8,128)S(1)}, f32[96,384]{1,0:T(8,128)S(1)}, u32[]{:S(2)}, u32[]{:S(2)}) collective-permute-start(f32[96,384]{1,0:T(8,128)S(1)} %get-tuple-element.114.refs_7_.refs_10_), channel_id=1, source_target_pairs={{0,16},{4,20},{8,24},{12,28},{16,0},{20,4},{24,8},{28,12},{1,17},{... | collective-permute-start | bytes 442376 | tf_op jit(solution)/shard_map/ppermute | solution.py:330
  69.5 0.5 shard_map.99
  70.0 1.6 %shard_map.100 = (f32[512,384]{1,0:T(8,128)S(1)}, f32[512,384]{1,0:T(8,128)}) custom-call(bf16[512,512]{1,0:T(8,128)(2,1)S(1)} %get-tuple-element.64.refs_1_.refs_0_, f32[512,384]{1,0:T(8,128)S(1)} %get-tuple-element.117.refs_1_, f32[512,384]{1,0:T(8,128)S(1)} %get-tuple-element.118.refs_2_.refs_3_, f32[512,384]{1,0:T(8,128)S(1)} %get-tuple-element.118.refs_2_.refs_3_), custom_call_target="tpu_custom_call" | custom-call | flops 805306368 | bytes 1966080 | tf_op jit(solution)/shard_map/pallas_call | solution.py:35
  71.6 2.1 %collective-permute-done.21.refs_2_ = f32[96,384]{1,0:T(8,128)S(1)} collective-permute-done((f32[96,384]{1,0:T(8,128)S(1)}, f32[96,384]{1,0:T(8,128)S(1)}, u32[]{:S(2)}, u32[]{:S(2)}) %collective-permute-start.21) | collective-permute-done | bytes 147488 | tf_op jit(solution)/shard_map/ppermute | solution.py:330
  73.7 2.2 %collective-permute-done.23.refs_4_ = f32[96,384]{1,0:T(8,128)S(1)} collective-permute-done((f32[96,384]{1,0:T(8,128)S(1)}, f32[96,384]{1,0:T(8,128)S(1)}, u32[]{:S(2)}, u32[]{:S(2)}) %collective-permute-start.23) | collective-permute-done | bytes 147488 | tf_op jit(solution)/shard_map/ppermute | solution.py:330
  75.9 1.4 %shard_map.101 = f32[512,384]{1,0:T(8,128)} custom-call(bf16[512,576]{1,0:T(8,128)(2,1)S(1)} %get-tuple-element.120.refs_0_, f32[512,384]{1,0:T(8,128)S(1)} %get-tuple-element.121.refs_1_.refs_5_, f32[96,384]{1,0:T(8,128)S(1)} %collective-permute-done.21.refs_2_, f32[96,384]{1,0:T(8,128)S(1)} %collective-permute-done.22.refs_3_, ...), custom_call_target="tpu_custom_call" | custom-call | flops 402653184 | bytes 1966080 | tf_op jit(solution)/shard_map/pallas_call | solution.py:35
  (33 shorter events, 1.6 us)
Async XLA Ops:
  0.6 7.9 %copy-start = (f32[1,1,512,128]{3,2,1,0:T(8,128)S(1)}, f32[1,1,512,128]{3,2,1,0:T(8,128)}, u32[]{:S(2)}) copy-start(f32[1,1,512,128]{3,2,1,0:T(8,128)} %param.9) | copy-start | bytes 786436
  2.4 7.8 %collective-permute-start = (f32[96,384]{1,0:T(8,128)S(1)}, f32[96,384]{1,0:T(8,128)S(1)}, u32[]{:S(2)}, u32[]{:S(2)}) collective-permute-start(f32[96,384]{1,0:T(8,128)S(1)} %get-tuple-element.67), channel_id=1, source_target_pairs={{0,16},{4,20},{8,24},{12,28},{16,0},{20,4},{24,8},{28,12},{1,17},{... | collective-permute-start | bytes 442376 | tf_op jit(solution)/shard_map/ppermute | solution.py:330
  5.4 4.7 %collective-permute-start.1 = (f32[96,384]{1,0:T(8,128)S(1)}, f32[96,384]{1,0:T(8,128)S(1)}, u32[]{:S(2)}, u32[]{:S(2)}) collective-permute-start(f32[96,384]{1,0:T(8,128)S(1)} %get-tuple-element.68), channel_id=1, source_target_pairs={{0,4},{4,0},{8,12},{12,8},{16,20},{20,16},{24,28},{28,24},{1,5},{5... | collective-permute-start | bytes 442376 | tf_op jit(solution)/shard_map/ppermute | solution.py:330
  5.4 6.3 %collective-permute-start.2 = (f32[96,384]{1,0:T(8,128)S(1)}, f32[96,384]{1,0:T(8,128)S(1)}, u32[]{:S(2)}, u32[]{:S(2)}) collective-permute-start(f32[96,384]{1,0:T(8,128)S(1)} %get-tuple-element.69), channel_id=1, source_target_pairs={{0,28},{4,8},{8,4},{12,16},{16,12},{20,24},{24,20},{28,0},{1,29},{... | collective-permute-start | bytes 442376 | tf_op jit(solution)/shard_map/ppermute | solution.py:330
  6.9 8.7 %collective-permute-start.4 = (f32[128,128]{1,0:T(8,128)S(1)}, f32[128,128]{1,0:T(8,128)S(1)}, u32[]{:S(2)}, u32[]{:S(2)}) collective-permute-start(f32[128,128]{1,0:T(8,128)S(1)} %get-tuple-element.72), channel_id=1, source_target_pairs={{0,1},{1,0},{2,3},{3,2},{4,5},{5,4},{6,7},{7,6},{8,9},{9,8},{10,11... | collective-permute-start | bytes 196616 | tf_op jit(solution)/shard_map/ppermute | solution.py:352
  10.1 4.0 %copy-start.2 = (f32[1,1,512,512]{3,2,1,0:T(8,128)S(1)}, f32[1,1,512,512]{3,2,1,0:T(8,128)}, u32[]{:S(2)}) copy-start(f32[1,1,512,512]{3,2,1,0:T(8,128)} %param.8) | copy-start | bytes 3145732
  12.1 4.6 %collective-permute-start.3 = (f32[128,128]{1,0:T(8,128)S(1)}, f32[128,128]{1,0:T(8,128)S(1)}, u32[]{:S(2)}, u32[]{:S(2)}) collective-permute-start(f32[128,128]{1,0:T(8,128)S(1)} %get-tuple-element.71.refs_3_.refs_0_), channel_id=1, source_target_pairs={{0,1},{1,0},{2,3},{3,2},{4,5},{5,4},{6,7},{7,6},{8,9},{9,8},{10,11... | collective-permute-start | bytes 196616 | tf_op jit(solution)/shard_map/ppermute | solution.py:372
  14.1 1.5 %copy-start.1 = (f32[1,512,128]{2,1,0:T(8,128)S(1)}, f32[1,512,128]{2,1,0:T(8,128)}, u32[]{:S(2)}) copy-start(f32[1,512,128]{2,1,0:T(8,128)} %param.10) | copy-start | bytes 786436
  15.5 5.9 %collective-permute-start.6 = (f32[128,256]{1,0:T(8,128)S(1)}, f32[128,256]{1,0:T(8,128)S(1)}, u32[]{:S(2)}, u32[]{:S(2)}) collective-permute-start(f32[128,256]{1,0:T(8,128)S(1)} %get-tuple-element.81.refs_0_), channel_id=1, source_target_pairs={{0,1},{1,0},{2,3},{3,2},{4,5},{5,4},{6,7},{7,6},{8,9},{9,8},{10,11... | collective-permute-start | bytes 393224 | tf_op jit(solution)/shard_map/ppermute | solution.py:372
  16.9 7.7 %collective-permute-start.5 = (f32[128,128]{1,0:T(8,128)S(1)}, f32[128,128]{1,0:T(8,128)S(1)}, u32[]{:S(2)}, u32[]{:S(2)}) collective-permute-start(f32[128,128]{1,0:T(8,128)S(1)} %get-tuple-element.78.refs_4_), channel_id=1, source_target_pairs={{0,3},{3,0},{1,2},{2,1},{4,7},{7,4},{5,6},{6,5},{8,11},{11,8},{9,1... | collective-permute-start | bytes 196616 | tf_op jit(solution)/shard_map/ppermute | solution.py:382
  21.7 6.9 %collective-permute-start.7 = (f32[128,256]{1,0:T(8,128)S(1)}, f32[128,256]{1,0:T(8,128)S(1)}, u32[]{:S(2)}, u32[]{:S(2)}) collective-permute-start(f32[128,256]{1,0:T(8,128)S(1)} %get-tuple-element.82.refs_6_), channel_id=1, source_target_pairs={{0,3},{3,0},{1,2},{2,1},{4,7},{7,4},{5,6},{6,5},{8,11},{11,8},{9,1... | collective-permute-start | bytes 393224 | tf_op jit(solution)/shard_map/ppermute | solution.py:382
  24.9 5.7 %copy-start.3 = (f32[1,1,512,512]{3,2,1,0:T(8,128)S(1)}, f32[1,1,512,512]{3,2,1,0:T(8,128)}, u32[]{:S(2)}) copy-start(f32[1,1,512,512]{3,2,1,0:T(8,128)} %param.7) | copy-start | bytes 3145732
  28.9 6.8 %collective-permute-start.8 = (f32[96,384]{1,0:T(8,128)S(1)}, f32[96,384]{1,0:T(8,128)S(1)}, u32[]{:S(2)}, u32[]{:S(2)}) collective-permute-start(f32[96,384]{1,0:T(8,128)S(1)} %get-tuple-element.90), channel_id=1, source_target_pairs={{0,16},{4,20},{8,24},{12,28},{16,0},{20,4},{24,8},{28,12},{1,17},{... | collective-permute-start | bytes 442376 | tf_op jit(solution)/shard_map/ppermute | solution.py:330
  29.0 6.7 %collective-permute-start.9 = (f32[96,384]{1,0:T(8,128)S(1)}, f32[96,384]{1,0:T(8,128)S(1)}, u32[]{:S(2)}, u32[]{:S(2)}) collective-permute-start(f32[96,384]{1,0:T(8,128)S(1)} %get-tuple-element.91), channel_id=1, source_target_pairs={{0,4},{4,0},{8,12},{12,8},{16,20},{20,16},{24,28},{28,24},{1,5},{5... | collective-permute-start | bytes 442376 | tf_op jit(solution)/shard_map/ppermute | solution.py:330
  29.1 6.6 %collective-permute-start.10 = (f32[96,384]{1,0:T(8,128)S(1)}, f32[96,384]{1,0:T(8,128)S(1)}, u32[]{:S(2)}, u32[]{:S(2)}) collective-permute-start(f32[96,384]{1,0:T(8,128)S(1)} %get-tuple-element.92), channel_id=1, source_target_pairs={{0,28},{4,8},{8,4},{12,16},{16,12},{20,24},{24,20},{28,0},{1,29},{... | collective-permute-start | bytes 442376 | tf_op jit(solution)/shard_map/ppermute | solution.py:330
  36.2 6.1 %collective-permute-start.11 = (f32[96,384]{1,0:T(8,128)S(1)}, f32[96,384]{1,0:T(8,128)S(1)}, u32[]{:S(2)}, u32[]{:S(2)}) collective-permute-start(f32[96,384]{1,0:T(8,128)S(1)} %get-tuple-element.94.refs_7_.refs_12_), channel_id=1, source_target_pairs={{0,16},{4,20},{8,24},{12,28},{16,0},{20,4},{24,8},{28,12},{1,17},{... | collective-permute-start | bytes 442376 | tf_op jit(solution)/shard_map/ppermute | solution.py:330
  37.9 4.4 %collective-permute-start.12 = (f32[96,384]{1,0:T(8,128)S(1)}, f32[96,384]{1,0:T(8,128)S(1)}, u32[]{:S(2)}, u32[]{:S(2)}) collective-permute-start(f32[96,384]{1,0:T(8,128)S(1)} %get-tuple-element.95.refs_8_), channel_id=1, source_target_pairs={{0,4},{4,0},{8,12},{12,8},{16,20},{20,16},{24,28},{28,24},{1,5},{5... | collective-permute-start | bytes 442376 | tf_op jit(solution)/shard_map/ppermute | solution.py:330
  37.9 6.7 %collective-permute-start.13 = (f32[96,384]{1,0:T(8,128)S(1)}, f32[96,384]{1,0:T(8,128)S(1)}, u32[]{:S(2)}, u32[]{:S(2)}) collective-permute-start(f32[96,384]{1,0:T(8,128)S(1)} %get-tuple-element.96.refs_9_), channel_id=1, source_target_pairs={{0,28},{4,8},{8,4},{12,16},{16,12},{20,24},{24,20},{28,0},{1,29},{... | collective-permute-start | bytes 442376 | tf_op jit(solution)/shard_map/ppermute | solution.py:330
  44.9 5.0 %collective-permute-start.14 = (f32[128,128]{1,0:T(8,128)S(1)}, f32[128,128]{1,0:T(8,128)S(1)}, u32[]{:S(2)}, u32[]{:S(2)}) collective-permute-start(f32[128,128]{1,0:T(8,128)S(1)} %get-tuple-element.100.refs_0_.refs_4_), channel_id=1, source_target_pairs={{0,1},{1,0},{2,3},{3,2},{4,5},{5,4},{6,7},{7,6},{8,9},{9,8},{10,11... | collective-permute-start | bytes 196616 | tf_op jit(solution)/shard_map/ppermute | solution.py:372
  46.7 6.0 %collective-permute-start.16 = (f32[128,256]{1,0:T(8,128)S(1)}, f32[128,256]{1,0:T(8,128)S(1)}, u32[]{:S(2)}, u32[]{:S(2)}) collective-permute-start(f32[128,256]{1,0:T(8,128)S(1)} %get-tuple-element.104.refs_0_), channel_id=1, source_target_pairs={{0,1},{1,0},{2,3},{3,2},{4,5},{5,4},{6,7},{7,6},{8,9},{9,8},{10,11... | collective-permute-start | bytes 393224 | tf_op jit(solution)/shard_map/ppermute | solution.py:372
  50.2 6.7 %collective-permute-start.15 = (f32[128,128]{1,0:T(8,128)S(1)}, f32[128,128]{1,0:T(8,128)S(1)}, u32[]{:S(2)}, u32[]{:S(2)}) collective-permute-start(f32[128,128]{1,0:T(8,128)S(1)} %get-tuple-element.102.refs_4_), channel_id=1, source_target_pairs={{0,3},{3,0},{1,2},{2,1},{4,7},{7,4},{5,6},{6,5},{8,11},{11,8},{9,1... | collective-permute-start | bytes 196616 | tf_op jit(solution)/shard_map/ppermute | solution.py:382
  53.0 6.9 %collective-permute-start.17 = (f32[128,256]{1,0:T(8,128)S(1)}, f32[128,256]{1,0:T(8,128)S(1)}, u32[]{:S(2)}, u32[]{:S(2)}) collective-permute-start(f32[128,256]{1,0:T(8,128)S(1)} %get-tuple-element.105.refs_6_), channel_id=1, source_target_pairs={{0,3},{3,0},{1,2},{2,1},{4,7},{7,4},{5,6},{6,5},{8,11},{11,8},{9,1... | collective-permute-start | bytes 393224 | tf_op jit(solution)/shard_map/ppermute | solution.py:382
  60.2 6.8 %collective-permute-start.18 = (f32[96,384]{1,0:T(8,128)S(1)}, f32[96,384]{1,0:T(8,128)S(1)}, u32[]{:S(2)}, u32[]{:S(2)}) collective-permute-start(f32[96,384]{1,0:T(8,128)S(1)} %get-tuple-element.111), channel_id=1, source_target_pairs={{0,16},{4,20},{8,24},{12,28},{16,0},{20,4},{24,8},{28,12},{1,17},{... | collective-permute-start | bytes 442376 | tf_op jit(solution)/shard_map/ppermute | solution.py:330
  60.3 6.7 %collective-permute-start.19 = (f32[96,384]{1,0:T(8,128)S(1)}, f32[96,384]{1,0:T(8,128)S(1)}, u32[]{:S(2)}, u32[]{:S(2)}) collective-permute-start(f32[96,384]{1,0:T(8,128)S(1)} %get-tuple-element.112), channel_id=1, source_target_pairs={{0,4},{4,0},{8,12},{12,8},{16,20},{20,16},{24,28},{28,24},{1,5},{5... | collective-permute-start | bytes 442376 | tf_op jit(solution)/shard_map/ppermute | solution.py:330
  60.4 6.6 %collective-permute-start.20 = (f32[96,384]{1,0:T(8,128)S(1)}, f32[96,384]{1,0:T(8,128)S(1)}, u32[]{:S(2)}, u32[]{:S(2)}) collective-permute-start(f32[96,384]{1,0:T(8,128)S(1)} %get-tuple-element.113), channel_id=1, source_target_pairs={{0,28},{4,8},{8,4},{12,16},{16,12},{20,24},{24,20},{28,0},{1,29},{... | collective-permute-start | bytes 442376 | tf_op jit(solution)/shard_map/ppermute | solution.py:330
  67.5 6.1 %collective-permute-start.21 = (f32[96,384]{1,0:T(8,128)S(1)}, f32[96,384]{1,0:T(8,128)S(1)}, u32[]{:S(2)}, u32[]{:S(2)}) collective-permute-start(f32[96,384]{1,0:T(8,128)S(1)} %get-tuple-element.114.refs_7_.refs_10_), channel_id=1, source_target_pairs={{0,16},{4,20},{8,24},{12,28},{16,0},{20,4},{24,8},{28,12},{1,17},{... | collective-permute-start | bytes 442376 | tf_op jit(solution)/shard_map/ppermute | solution.py:330
  69.2 4.4 %collective-permute-start.22 = (f32[96,384]{1,0:T(8,128)S(1)}, f32[96,384]{1,0:T(8,128)S(1)}, u32[]{:S(2)}, u32[]{:S(2)}) collective-permute-start(f32[96,384]{1,0:T(8,128)S(1)} %get-tuple-element.115.refs_8_), channel_id=1, source_target_pairs={{0,4},{4,0},{8,12},{12,8},{16,20},{20,16},{24,28},{28,24},{1,5},{5... | collective-permute-start | bytes 442376 | tf_op jit(solution)/shard_map/ppermute | solution.py:330
  69.2 6.7 %collective-permute-start.23 = (f32[96,384]{1,0:T(8,128)S(1)}, f32[96,384]{1,0:T(8,128)S(1)}, u32[]{:S(2)}, u32[]{:S(2)}) collective-permute-start(f32[96,384]{1,0:T(8,128)S(1)} %get-tuple-element.116.refs_9_), channel_id=1, source_target_pairs={{0,28},{4,8},{8,4},{12,16},{16,12},{20,24},{24,20},{28,0},{1,29},{... | collective-permute-start | bytes 442376 | tf_op jit(solution)/shard_map/ppermute | solution.py:330

commit v11 on v9

--- a/solution.py
+++ b/solution.py
@@ -92,8 +92,13 @@
 
 
 def came_in(subs, shared_refs):
+    always = (subs % (2 * ROW_SUBS) == 0, False, subs % 2 == 0, False)
     return jnp.concatenate(
-        [ref[...] * jnp.where(here, 1.0, 0.0) for ref, (_, _, _, here) in zip(shared_refs, sides(subs))], axis=0
+        [
+            ref[...] if whole else ref[...] * jnp.where(here, 1.0, 0.0)
+            for ref, (_, _, _, here), whole in zip(shared_refs, sides(subs), always)
+        ],
+        axis=0,
     )
 
 

time: 74.9 us -> 74.8 us (level)
  no operation moved by 1% of the time
where the time goes in v11:
time: 74.8 us; the launch traced here: 74.6 us
  starting transfers between devices  30.4 us (41%)
  waiting for transfers between devices  25.2 us (34%)
  Pallas kernels  18.1 us (24%)
  between operations  0.86 us (1%)
    pallas_call x25, Pallas kernels, __call__(): pl.pallas_call(whole_body, out_shape=[jax.ShapeDtypeStruct(shape, kind) f...  18.1 us
    ppermute x15, waiting for transfers between devices, exchange(): return [lax.ppermute(part, 'sub', plan) for part, plan in zip(parts, plans)]  14.6 us
    ppermute x15, starting transfers between devices, exchange(): return [lax.ppermute(part, 'sub', plan) for part, plan in zip(parts, plans)]  14.4 us
    ppermute x4, starting transfers between devices, local(): came.append(lax.ppermute(away, 'grp', mirror_plan))  10.2 us
    ppermute x4, waiting for transfers between devices, local(): came.append(lax.ppermute(away, 'grp', mirror_plan))  7.01 us
    ppermute x4, starting transfers between devices, local(): theirs = [lax.ppermute(piece, 'grp', pair_plan) for piece in own]  4.25 us
    ppermute x4, waiting for transfers between devices, local(): theirs = [lax.ppermute(piece, 'grp', pair_plan) for piece in own]  3.6 us
    ppermute x1, starting transfers between devices, local(): other = lax.ppermute(sent, 'grp', pair_plan)  1.56 us
  transfers between devices with their start and end apart: 24, of which 13 were waited for; matrix products, arithmetic and copies ran while one was open for 0% of the time, Pallas kernels for 18%

profile of v11, /device:TPU:0, one launch (start us, length us, event | category | flops | bytes accessed | tf_op | source)
XLA Modules:
  0.0 74.6 jit_solution(7235664657455703977)
XLA Ops:
  0.6 1.7 %shard_map.77 = (bf16[384,512]{1,0:T(8,128)(2,1)S(1)}, f32[512,384]{1,0:T(8,128)S(1)}, f32[128,128]{1,0:T(8,128)S(1)}, f32[96,384]{1,0:T(8,128)S(1)}, f32[96,384]{1,0:T(8,128)S(1)}, /*index=5*/f32[96,384]{1,0:T(8,128)S(1)}) custom-call(s32[4,96]{1,0:T(4,128)} %bitcast.15, f32[512,384]{1,0:T(8,128)} %bitcast.14, f32[512,128]{1,0:T(8,128)} %bitcast.9), custom_call_target="tpu_custom_call" | custom-call | flops 301989888 | bytes 3145728 | tf_op jit(solution)/shard_map/pallas_call | solution.py:35
  2.4 3.0 %collective-permute-start = (f32[96,384]{1,0:T(8,128)S(1)}, f32[96,384]{1,0:T(8,128)S(1)}, u32[]{:S(2)}, u32[]{:S(2)}) collective-permute-start(f32[96,384]{1,0:T(8,128)S(1)} %get-tuple-element.67), channel_id=1, source_target_pairs={{0,16},{4,20},{8,24},{12,28},{16,0},{20,4},{24,8},{28,12},{1,17},{... | collective-permute-start | bytes 442376 | tf_op jit(solution)/shard_map/ppermute | solution.py:335
  5.4 0.6 collective-permute-start.1
  6.0 1.0 %collective-permute-start.2 = (f32[96,384]{1,0:T(8,128)S(1)}, f32[96,384]{1,0:T(8,128)S(1)}, u32[]{:S(2)}, u32[]{:S(2)}) collective-permute-start(f32[96,384]{1,0:T(8,128)S(1)} %get-tuple-element.69), channel_id=1, source_target_pairs={{0,4},{4,0},{8,12},{12,8},{16,20},{20,16},{24,28},{28,24},{1,5},{5... | collective-permute-start | bytes 442376 | tf_op jit(solution)/shard_map/ppermute | solution.py:335
  7.0 1.6 %collective-permute-start.4 = (f32[128,128]{1,0:T(8,128)S(1)}, f32[128,128]{1,0:T(8,128)S(1)}, u32[]{:S(2)}, u32[]{:S(2)}) collective-permute-start(f32[128,128]{1,0:T(8,128)S(1)} %get-tuple-element.72), channel_id=1, source_target_pairs={{0,1},{1,0},{2,3},{3,2},{4,5},{5,4},{6,7},{7,6},{8,9},{9,8},{10,11... | collective-permute-start | bytes 196616 | tf_op jit(solution)/shard_map/ppermute | solution.py:357
  8.6 1.6 %shard_map.78 = (bf16[512,512]{1,0:T(8,128)(2,1)S(1)}, bf16[512,512]{1,0:T(8,128)(2,1)S(1)}, bf16[512,576]{1,0:T(8,128)(2,1)S(1)}, bf16[512,384]{1,0:T(8,128)(2,...) custom-call(bf16[384,512]{1,0:T(8,128)(2,1)S(1)} %get-tuple-element., ...), custom_call_target="tpu_custom_call" | custom-call | flops 402653184 | bytes 4718592 | tf_op jit(solution)/shard_map/pallas_call | solution.py:35
  10.2 1.3 %collective-permute-done.1.refs_3_.refs_4_ = f32[96,384]{1,0:T(8,128)S(1)} collective-permute-done((f32[96,384]{1,0:T(8,128)S(1)}, f32[96,384]{1,0:T(8,128)S(1)}, u32[]{:S(2)}, u32[]{:S(2)}) %collective-permute-start.1) | collective-permute-done | bytes 147488 | tf_op jit(solution)/shard_map/ppermute | solution.py:335
  11.5 0.3 shard_map.79
  11.8 1.7 %collective-permute-start.3 = (f32[128,128]{1,0:T(8,128)S(1)}, f32[128,128]{1,0:T(8,128)S(1)}, u32[]{:S(2)}, u32[]{:S(2)}) collective-permute-start(f32[128,128]{1,0:T(8,128)S(1)} %get-tuple-element.71.refs_3_.refs_0_), channel_id=1, source_target_pairs={{0,1},{1,0},{2,3},{3,2},{4,5},{5,4},{6,7},{7,6},{8,9},{9,8},{10,11... | collective-permute-start | bytes 196616 | tf_op jit(solution)/shard_map/ppermute | solution.py:377
  13.5 1.3 %shard_map.80 = (bf16[512,512]{1,0:T(8,128)(2,1)S(1)}, bf16[512,512]{1,0:T(8,128)(2,1)S(1)}, f32[128,256]{1,0:T(8,128)S(1)}) custom-call(bf16[512,512]{1,0:T(8,128)(2,1)S(1)} %get-tuple-element.70.refs_5_.refs_0_, f32[512,512]{1,0:T(8,128)S(1)} %bitcast.11, f32[128,256]{1,0:T(8,128)S(1)} %get-tuple-element.73.refs_2_, ...), custom_call_target="tpu_custom_call" | custom-call | flops 1073741824 | bytes 2359296 | tf_op jit(solution)/shard_map/pallas_call | solution.py:35
  14.8 0.5 collective-permute-start.6
  15.5 0.7 collective-permute-done.3.refs_1_
  16.4 3.7 %collective-permute-start.5 = (f32[128,128]{1,0:T(8,128)S(1)}, f32[128,128]{1,0:T(8,128)S(1)}, u32[]{:S(2)}, u32[]{:S(2)}) collective-permute-start(f32[128,128]{1,0:T(8,128)S(1)} %get-tuple-element.78.refs_4_), channel_id=1, source_target_pairs={{0,3},{3,0},{1,2},{2,1},{4,7},{7,4},{5,6},{6,5},{8,11},{11,8},{9,1... | collective-permute-start | bytes 196616 | tf_op jit(solution)/shard_map/ppermute | solution.py:387
  20.4 2.5 %collective-permute-start.7 = (f32[128,256]{1,0:T(8,128)S(1)}, f32[128,256]{1,0:T(8,128)S(1)}, u32[]{:S(2)}, u32[]{:S(2)}) collective-permute-start(f32[128,256]{1,0:T(8,128)S(1)} %get-tuple-element.82.refs_6_), channel_id=1, source_target_pairs={{0,3},{3,0},{1,2},{2,1},{4,7},{7,4},{5,6},{6,5},{8,11},{11,8},{9,1... | collective-permute-start | bytes 393224 | tf_op jit(solution)/shard_map/ppermute | solution.py:387
  22.9 1.0 %shard_map.84.refs_2_.refs_4_ = f32[512,384]{1,0:T(8,128)S(1)} custom-call(f32[512,384]{1,0:T(8,128)S(1)} %get-tuple-element.79.refs_0_.refs_2_.refs_3_, bf16[512,512]{1,0:T(8,128)(2,1)S(1)} %get-tuple-element.74.refs_2_.refs_1_, bf16[512,512]{1,0:T(8,128)(2,1)S(1)} %get-tuple-element.80.refs_2_, f32[96,384]{1,0:T(8,128)S(1)} %collective-permute-done.refs_2_.refs_3_, ...), custom_call_target="tpu_custom_call" | custom-call | flops 9663676416 | bytes 37748736 | tf_op jit(solution)/shard_map/pallas_call | solution.py:35
  24.2 3.1 %collective-permute-done.7.refs_1_ = f32[128,256]{1,0:T(8,128)S(1)} collective-permute-done((f32[128,256]{1,0:T(8,128)S(1)}, f32[128,256]{1,0:T(8,128)S(1)}, u32[]{:S(2)}, u32[]{:S(2)}) %collective-permute-start.7) | collective-permute-done | bytes 131104 | tf_op jit(solution)/shard_map/ppermute | solution.py:387
  27.6 1.9 %collective-permute-start.8 = (f32[96,384]{1,0:T(8,128)S(1)}, f32[96,384]{1,0:T(8,128)S(1)}, u32[]{:S(2)}, u32[]{:S(2)}) collective-permute-start(f32[96,384]{1,0:T(8,128)S(1)} %get-tuple-element.90), channel_id=1, source_target_pairs={{0,16},{4,20},{8,24},{12,28},{16,0},{20,4},{24,8},{28,12},{1,17},{... | collective-permute-start | bytes 442376 | tf_op jit(solution)/shard_map/ppermute | solution.py:335
  29.5 1.3 %collective-permute-start.10 = (f32[96,384]{1,0:T(8,128)S(1)}, f32[96,384]{1,0:T(8,128)S(1)}, u32[]{:S(2)}, u32[]{:S(2)}) collective-permute-start(f32[96,384]{1,0:T(8,128)S(1)} %get-tuple-element.92), channel_id=1, source_target_pairs={{0,4},{4,0},{8,12},{12,8},{16,20},{20,16},{24,28},{28,24},{1,5},{5... | collective-permute-start | bytes 442376 | tf_op jit(solution)/shard_map/ppermute | solution.py:335
  30.8 1.3 %shard_map.87 = (bf16[512,512]{1,0:T(8,128)(2,1)S(1)}, bf16[512,512]{1,0:T(8,128)(2,1)S(1)}, bf16[288,864]{1,0:T(8,128)(2,1)S(1)}) custom-call(bf16[512,512]{1,0:T(8,128)(2,1)S(1)} %get-tuple-element.70.refs_5_.refs_0_, bf16[512,512]{1,0:T(8,128)(2,1)S(1)} %get-tuple-element.64.refs_1_.refs_0_, f32[512,512]{1,0:T(8,128)S(1)} %bitcast.12, ...), custom_call_target="tpu_custom_call" | custom-call | flops 1073741824 | bytes 2359296 | tf_op jit(solution)/shard_map/pallas_call | solution.py:35
  32.1 1.0 %shard_map.88 = (f32[512,384]{1,0:T(8,128)S(1)}, f32[512,384]{1,0:T(8,128)S(1)}) custom-call(f32[512,128]{1,0:T(8,128)S(1)} %shard_map.85.refs_4_.refs_5_.refs_0_, f32[512,256]{1,0:T(8,128)S(1)} %get-tuple-element.85.refs_3_.refs_1_, f32[512,384]{1,0:T(8,128)S(1)} %get-tuple-element.79.refs_0_.refs_2_.refs_3_, ...), custom_call_target="tpu_custom_call" | custom-call | flops 603979776 | bytes 3145728 | tf_op jit(solution)/shard_map/pallas_call | solution.py:35
  33.1 1.9 %collective-permute-done.9.refs_3_.refs_5_ = f32[96,384]{1,0:T(8,128)S(1)} collective-permute-done((f32[96,384]{1,0:T(8,128)S(1)}, f32[96,384]{1,0:T(8,128)S(1)}, u32[]{:S(2)}, u32[]{:S(2)}) %collective-permute-start.9) | collective-permute-done | bytes 147488 | tf_op jit(solution)/shard_map/ppermute | solution.py:335
  35.0 0.5 shard_map.89
  35.5 1.7 %collective-permute-start.11 = (f32[96,384]{1,0:T(8,128)S(1)}, f32[96,384]{1,0:T(8,128)S(1)}, u32[]{:S(2)}, u32[]{:S(2)}) collective-permute-start(f32[96,384]{1,0:T(8,128)S(1)} %get-tuple-element.94.refs_7_.refs_12_), channel_id=1, source_target_pairs={{0,16},{4,20},{8,24},{12,28},{16,0},{20,4},{24,8},{28,12},{1,17},{... | collective-permute-start | bytes 442376 | tf_op jit(solution)/shard_map/ppermute | solution.py:335
  37.2 0.8 %collective-permute-start.13 = (f32[96,384]{1,0:T(8,128)S(1)}, f32[96,384]{1,0:T(8,128)S(1)}, u32[]{:S(2)}, u32[]{:S(2)}) collective-permute-start(f32[96,384]{1,0:T(8,128)S(1)} %get-tuple-element.96.refs_9_), channel_id=1, source_target_pairs={{0,4},{4,0},{8,12},{12,8},{16,20},{20,16},{24,28},{28,24},{1,5},{5... | collective-permute-start | bytes 442376 | tf_op jit(solution)/shard_map/ppermute | solution.py:335
  38.1 0.9 %shard_map.90 = (f32[128,384]{1,0:T(8,128)S(1)}, f32[512,384]{1,0:T(8,128)S(1)}, f32[512,384]{1,0:T(8,128)S(1)}) custom-call(f32[512,384]{1,0:T(8,128)S(1)} %get-tuple-element.88.refs_0_.refs_5_, f32[512,384]{1,0:T(8,128)S(1)} %get-tuple-element.89.refs_1_, bf16[512,512]{1,0:T(8,128)(2,1)S(1)} %get-tuple-element.86.refs_3_.refs_5_.refs_2_.refs_4_, ...), custom_call_target="tpu_custom_call" | custom-call | flops 301989888 | bytes 3145728 | tf_op jit(solution)/shard_map/pallas_call | solution.py:35
  38.9 2.9 %collective-permute-done.11.refs_2_.refs_3_ = f32[96,384]{1,0:T(8,128)S(1)} collective-permute-done((f32[96,384]{1,0:T(8,128)S(1)}, f32[96,384]{1,0:T(8,128)S(1)}, u32[]{:S(2)}, u32[]{:S(2)}) %collective-permute-start.11) | collective-permute-done | bytes 147488 | tf_op jit(solution)/shard_map/ppermute | solution.py:335
  41.8 1.4 %collective-permute-done.12.refs_3_.refs_4_ = f32[96,384]{1,0:T(8,128)S(1)} collective-permute-done((f32[96,384]{1,0:T(8,128)S(1)}, f32[96,384]{1,0:T(8,128)S(1)}, u32[]{:S(2)}, u32[]{:S(2)}) %collective-permute-start.12) | collective-permute-done | bytes 147488 | tf_op jit(solution)/shard_map/ppermute | solution.py:335
  43.2 0.3 shard_map.91
  43.5 1.8 %collective-permute-start.14 = (f32[128,128]{1,0:T(8,128)S(1)}, f32[128,128]{1,0:T(8,128)S(1)}, u32[]{:S(2)}, u32[]{:S(2)}) collective-permute-start(f32[128,128]{1,0:T(8,128)S(1)} %get-tuple-element.100.refs_0_.refs_4_), channel_id=1, source_target_pairs={{0,1},{1,0},{2,3},{3,2},{4,5},{5,4},{6,7},{7,6},{8,9},{9,8},{10,11... | collective-permute-start | bytes 196616 | tf_op jit(solution)/shard_map/ppermute | solution.py:377
  45.6 2.9 %collective-permute-done.14.refs_1_ = f32[128,128]{1,0:T(8,128)S(1)} collective-permute-done((f32[128,128]{1,0:T(8,128)S(1)}, f32[128,128]{1,0:T(8,128)S(1)}, u32[]{:S(2)}, u32[]{:S(2)}) %collective-permute-start.14) | collective-permute-done | bytes 65568 | tf_op jit(solution)/shard_map/ppermute | solution.py:377
  48.8 2.2 %collective-permute-start.15 = (f32[128,128]{1,0:T(8,128)S(1)}, f32[128,128]{1,0:T(8,128)S(1)}, u32[]{:S(2)}, u32[]{:S(2)}) collective-permute-start(f32[128,128]{1,0:T(8,128)S(1)} %get-tuple-element.102.refs_4_), channel_id=1, source_target_pairs={{0,3},{3,0},{1,2},{2,1},{4,7},{7,4},{5,6},{6,5},{8,11},{11,8},{9,1... | collective-permute-start | bytes 196616 | tf_op jit(solution)/shard_map/ppermute | solution.py:387
  51.3 1.8 %collective-permute-start.17 = (f32[128,256]{1,0:T(8,128)S(1)}, f32[128,256]{1,0:T(8,128)S(1)}, u32[]{:S(2)}, u32[]{:S(2)}) collective-permute-start(f32[128,256]{1,0:T(8,128)S(1)} %get-tuple-element.105.refs_6_), channel_id=1, source_target_pairs={{0,3},{3,0},{1,2},{2,1},{4,7},{7,4},{5,6},{6,5},{8,11},{11,8},{9,1... | collective-permute-start | bytes 393224 | tf_op jit(solution)/shard_map/ppermute | solution.py:387
  53.0 1.0 %shard_map.94.refs_2_.refs_4_ = f32[512,384]{1,0:T(8,128)S(1)} custom-call(f32[512,384]{1,0:T(8,128)S(1)} %get-tuple-element.103.refs_0_, bf16[512,512]{1,0:T(8,128)(2,1)S(1)} %get-tuple-element.74.refs_2_.refs_1_, bf16[512,512]{1,0:T(8,128)(2,1)S(1)} %get-tuple-element.80.refs_2_, f32[96,384]{1,0:T(8,128)S(1)} %collective-permute-done.11.refs_2_.refs_3_, ...), custom_call_target="tpu_custom_call" | custom-call | flops 9663676416 | bytes 37748736 | tf_op jit(solution)/shard_map/pallas_call | solution.py:35
  54.0 1.5 %collective-permute-done.15.refs_1_ = f32[128,128]{1,0:T(8,128)S(1)} collective-permute-done((f32[128,128]{1,0:T(8,128)S(1)}, f32[128,128]{1,0:T(8,128)S(1)}, u32[]{:S(2)}, u32[]{:S(2)}) %collective-permute-start.15) | collective-permute-done | bytes 65568 | tf_op jit(solution)/shard_map/ppermute | solution.py:387
  55.9 2.3 %collective-permute-done.17.refs_1_ = f32[128,256]{1,0:T(8,128)S(1)} collective-permute-done((f32[128,256]{1,0:T(8,128)S(1)}, f32[128,256]{1,0:T(8,128)S(1)}, u32[]{:S(2)}, u32[]{:S(2)}) %collective-permute-start.17) | collective-permute-done | bytes 131104 | tf_op jit(solution)/shard_map/ppermute | solution.py:387
  58.5 1.3 %collective-permute-start.18 = (f32[96,384]{1,0:T(8,128)S(1)}, f32[96,384]{1,0:T(8,128)S(1)}, u32[]{:S(2)}, u32[]{:S(2)}) collective-permute-start(f32[96,384]{1,0:T(8,128)S(1)} %get-tuple-element.111), channel_id=1, source_target_pairs={{0,16},{4,20},{8,24},{12,28},{16,0},{20,4},{24,8},{28,12},{1,17},{... | collective-permute-start | bytes 442376 | tf_op jit(solution)/shard_map/ppermute | solution.py:335
  59.8 0.9 %collective-permute-start.20 = (f32[96,384]{1,0:T(8,128)S(1)}, f32[96,384]{1,0:T(8,128)S(1)}, u32[]{:S(2)}, u32[]{:S(2)}) collective-permute-start(f32[96,384]{1,0:T(8,128)S(1)} %get-tuple-element.113), channel_id=1, source_target_pairs={{0,4},{4,0},{8,12},{12,8},{16,20},{20,16},{24,28},{28,24},{1,5},{5... | collective-permute-start | bytes 442376 | tf_op jit(solution)/shard_map/ppermute | solution.py:335
  60.7 1.0 %shard_map.97 = (f32[512,384]{1,0:T(8,128)S(1)}, f32[512,384]{1,0:T(8,128)S(1)}) custom-call(f32[512,128]{1,0:T(8,128)S(1)} %shard_map.95.refs_4_.refs_5_.refs_0_, f32[512,256]{1,0:T(8,128)S(1)} %get-tuple-element.107.refs_1_.refs_6_, f32[512,384]{1,0:T(8,128)S(1)} %get-tuple-element.108.refs_2_, f32[512,384]{1,0:T(8,128)S(1)} %get-tuple-element.79.refs_0_.refs_2_.refs_3_, ...), custom_call_target="tpu_custom_call" | custom-call | flops 603979776 | bytes 3145728 | tf_op jit(solution)/shard_map/pallas_call | solution.py:35
  61.7 2.0 %collective-permute-done.18.refs_2_.refs_4_ = f32[96,384]{1,0:T(8,128)S(1)} collective-permute-done((f32[96,384]{1,0:T(8,128)S(1)}, f32[96,384]{1,0:T(8,128)S(1)}, u32[]{:S(2)}, u32[]{:S(2)}) %collective-permute-start.18) | collective-permute-done | bytes 147488 | tf_op jit(solution)/shard_map/ppermute | solution.py:335
  63.7 1.9 %collective-permute-done.19.refs_3_.refs_5_ = f32[96,384]{1,0:T(8,128)S(1)} collective-permute-done((f32[96,384]{1,0:T(8,128)S(1)}, f32[96,384]{1,0:T(8,128)S(1)}, u32[]{:S(2)}, u32[]{:S(2)}) %collective-permute-start.19) | collective-permute-done | bytes 147488 | tf_op jit(solution)/shard_map/ppermute | solution.py:335
  65.6 0.5 shard_map.98
  66.1 1.2 %collective-permute-start.21 = (f32[96,384]{1,0:T(8,128)S(1)}, f32[96,384]{1,0:T(8,128)S(1)}, u32[]{:S(2)}, u32[]{:S(2)}) collective-permute-start(f32[96,384]{1,0:T(8,128)S(1)} %get-tuple-element.114.refs_7_.refs_10_), channel_id=1, source_target_pairs={{0,16},{4,20},{8,24},{12,28},{16,0},{20,4},{24,8},{28,12},{1,17},{... | collective-permute-start | bytes 442376 | tf_op jit(solution)/shard_map/ppermute | solution.py:335
  67.6 0.4 collective-permute-start.23
  68.0 0.5 shard_map.99
  68.5 1.6 %shard_map.100 = (f32[512,384]{1,0:T(8,128)S(1)}, f32[512,384]{1,0:T(8,128)}) custom-call(bf16[512,512]{1,0:T(8,128)(2,1)S(1)} %get-tuple-element.64.refs_1_.refs_0_, f32[512,384]{1,0:T(8,128)S(1)} %get-tuple-element.117.refs_1_, f32[512,384]{1,0:T(8,128)S(1)} %get-tuple-element.118.refs_2_.refs_3_, f32[512,384]{1,0:T(8,128)S(1)} %get-tuple-element.118.refs_2_.refs_3_), custom_call_target="tpu_custom_call" | custom-call | flops 805306368 | bytes 1966080 | tf_op jit(solution)/shard_map/pallas_call | solution.py:35
  70.1 1.3 %collective-permute-done.21.refs_2_ = f32[96,384]{1,0:T(8,128)S(1)} collective-permute-done((f32[96,384]{1,0:T(8,128)S(1)}, f32[96,384]{1,0:T(8,128)S(1)}, u32[]{:S(2)}, u32[]{:S(2)}) %collective-permute-start.21) | collective-permute-done | bytes 147488 | tf_op jit(solution)/shard_map/ppermute | solution.py:335
  71.4 1.8 %collective-permute-done.22.refs_3_ = f32[96,384]{1,0:T(8,128)S(1)} collective-permute-done((f32[96,384]{1,0:T(8,128)S(1)}, f32[96,384]{1,0:T(8,128)S(1)}, u32[]{:S(2)}, u32[]{:S(2)}) %collective-permute-start.22) | collective-permute-done | bytes 147488 | tf_op jit(solution)/shard_map/ppermute | solution.py:335
  73.2 1.4 %shard_map.101 = f32[512,384]{1,0:T(8,128)} custom-call(bf16[512,576]{1,0:T(8,128)(2,1)S(1)} %get-tuple-element.120.refs_0_, f32[512,384]{1,0:T(8,128)S(1)} %get-tuple-element.121.refs_1_.refs_5_, f32[96,384]{1,0:T(8,128)S(1)} %collective-permute-done.21.refs_2_, f32[96,384]{1,0:T(8,128)S(1)} %collective-permute-done.22.refs_3_, ...), custom_call_target="tpu_custom_call" | custom-call | flops 402653184 | bytes 1966080 | tf_op jit(solution)/shard_map/pallas_call | solution.py:35
  (33 shorter events, 2.8 us)
Async XLA Ops:
  0.6 7.9 %copy-start = (f32[1,1,512,128]{3,2,1,0:T(8,128)S(1)}, f32[1,1,512,128]{3,2,1,0:T(8,128)}, u32[]{:S(2)}) copy-start(f32[1,1,512,128]{3,2,1,0:T(8,128)} %param.9) | copy-start | bytes 786436
  2.4 7.8 %collective-permute-start = (f32[96,384]{1,0:T(8,128)S(1)}, f32[96,384]{1,0:T(8,128)S(1)}, u32[]{:S(2)}, u32[]{:S(2)}) collective-permute-start(f32[96,384]{1,0:T(8,128)S(1)} %get-tuple-element.67), channel_id=1, source_target_pairs={{0,16},{4,20},{8,24},{12,28},{16,0},{20,4},{24,8},{28,12},{1,17},{... | collective-permute-start | bytes 442376 | tf_op jit(solution)/shard_map/ppermute | solution.py:335
  5.4 6.1 %collective-permute-start.1 = (f32[96,384]{1,0:T(8,128)S(1)}, f32[96,384]{1,0:T(8,128)S(1)}, u32[]{:S(2)}, u32[]{:S(2)}) collective-permute-start(f32[96,384]{1,0:T(8,128)S(1)} %get-tuple-element.68), channel_id=1, source_target_pairs={{0,28},{4,8},{8,4},{12,16},{16,12},{20,24},{24,20},{28,0},{1,29},{... | collective-permute-start | bytes 442376 | tf_op jit(solution)/shard_map/ppermute | solution.py:335
  6.0 5.5 %collective-permute-start.2 = (f32[96,384]{1,0:T(8,128)S(1)}, f32[96,384]{1,0:T(8,128)S(1)}, u32[]{:S(2)}, u32[]{:S(2)}) collective-permute-start(f32[96,384]{1,0:T(8,128)S(1)} %get-tuple-element.69), channel_id=1, source_target_pairs={{0,4},{4,0},{8,12},{12,8},{16,20},{20,16},{24,28},{28,24},{1,5},{5... | collective-permute-start | bytes 442376 | tf_op jit(solution)/shard_map/ppermute | solution.py:335
  7.0 8.3 %collective-permute-start.4 = (f32[128,128]{1,0:T(8,128)S(1)}, f32[128,128]{1,0:T(8,128)S(1)}, u32[]{:S(2)}, u32[]{:S(2)}) collective-permute-start(f32[128,128]{1,0:T(8,128)S(1)} %get-tuple-element.72), channel_id=1, source_target_pairs={{0,1},{1,0},{2,3},{3,2},{4,5},{5,4},{6,7},{7,6},{8,9},{9,8},{10,11... | collective-permute-start | bytes 196616 | tf_op jit(solution)/shard_map/ppermute | solution.py:357
  10.2 3.3 %copy-start.2 = (f32[1,1,512,512]{3,2,1,0:T(8,128)S(1)}, f32[1,1,512,512]{3,2,1,0:T(8,128)}, u32[]{:S(2)}) copy-start(f32[1,1,512,512]{3,2,1,0:T(8,128)} %param.8) | copy-start | bytes 3145732
  11.8 4.3 %collective-permute-start.3 = (f32[128,128]{1,0:T(8,128)S(1)}, f32[128,128]{1,0:T(8,128)S(1)}, u32[]{:S(2)}, u32[]{:S(2)}) collective-permute-start(f32[128,128]{1,0:T(8,128)S(1)} %get-tuple-element.71.refs_3_.refs_0_), channel_id=1, source_target_pairs={{0,1},{1,0},{2,3},{3,2},{4,5},{5,4},{6,7},{7,6},{8,9},{9,8},{10,11... | collective-permute-start | bytes 196616 | tf_op jit(solution)/shard_map/ppermute | solution.py:377
  13.5 1.9 %copy-start.1 = (f32[1,512,128]{2,1,0:T(8,128)S(1)}, f32[1,512,128]{2,1,0:T(8,128)}, u32[]{:S(2)}) copy-start(f32[1,512,128]{2,1,0:T(8,128)} %param.10) | copy-start | bytes 786436
  14.8 5.3 %collective-permute-start.6 = (f32[128,256]{1,0:T(8,128)S(1)}, f32[128,256]{1,0:T(8,128)S(1)}, u32[]{:S(2)}, u32[]{:S(2)}) collective-permute-start(f32[128,256]{1,0:T(8,128)S(1)} %get-tuple-element.81.refs_0_), channel_id=1, source_target_pairs={{0,1},{1,0},{2,3},{3,2},{4,5},{5,4},{6,7},{7,6},{8,9},{9,8},{10,11... | collective-permute-start | bytes 393224 | tf_op jit(solution)/shard_map/ppermute | solution.py:377
  16.4 7.5 %collective-permute-start.5 = (f32[128,128]{1,0:T(8,128)S(1)}, f32[128,128]{1,0:T(8,128)S(1)}, u32[]{:S(2)}, u32[]{:S(2)}) collective-permute-start(f32[128,128]{1,0:T(8,128)S(1)} %get-tuple-element.78.refs_4_), channel_id=1, source_target_pairs={{0,3},{3,0},{1,2},{2,1},{4,7},{7,4},{5,6},{6,5},{8,11},{11,8},{9,1... | collective-permute-start | bytes 196616 | tf_op jit(solution)/shard_map/ppermute | solution.py:387
  20.4 6.9 %collective-permute-start.7 = (f32[128,256]{1,0:T(8,128)S(1)}, f32[128,256]{1,0:T(8,128)S(1)}, u32[]{:S(2)}, u32[]{:S(2)}) collective-permute-start(f32[128,256]{1,0:T(8,128)S(1)} %get-tuple-element.82.refs_6_), channel_id=1, source_target_pairs={{0,3},{3,0},{1,2},{2,1},{4,7},{7,4},{5,6},{6,5},{8,11},{11,8},{9,1... | collective-permute-start | bytes 393224 | tf_op jit(solution)/shard_map/ppermute | solution.py:387
  24.2 6.6 %copy-start.3 = (f32[1,1,512,512]{3,2,1,0:T(8,128)S(1)}, f32[1,1,512,512]{3,2,1,0:T(8,128)}, u32[]{:S(2)}) copy-start(f32[1,1,512,512]{3,2,1,0:T(8,128)} %param.7) | copy-start | bytes 3145732
  27.6 5.5 %collective-permute-start.8 = (f32[96,384]{1,0:T(8,128)S(1)}, f32[96,384]{1,0:T(8,128)S(1)}, u32[]{:S(2)}, u32[]{:S(2)}) collective-permute-start(f32[96,384]{1,0:T(8,128)S(1)} %get-tuple-element.90), channel_id=1, source_target_pairs={{0,16},{4,20},{8,24},{12,28},{16,0},{20,4},{24,8},{28,12},{1,17},{... | collective-permute-start | bytes 442376 | tf_op jit(solution)/shard_map/ppermute | solution.py:335
  29.5 5.5 %collective-permute-start.9 = (f32[96,384]{1,0:T(8,128)S(1)}, f32[96,384]{1,0:T(8,128)S(1)}, u32[]{:S(2)}, u32[]{:S(2)}) collective-permute-start(f32[96,384]{1,0:T(8,128)S(1)} %get-tuple-element.91), channel_id=1, source_target_pairs={{0,28},{4,8},{8,4},{12,16},{16,12},{20,24},{24,20},{28,0},{1,29},{... | collective-permute-start | bytes 442376 | tf_op jit(solution)/shard_map/ppermute | solution.py:335
  29.5 5.5 %collective-permute-start.10 = (f32[96,384]{1,0:T(8,128)S(1)}, f32[96,384]{1,0:T(8,128)S(1)}, u32[]{:S(2)}, u32[]{:S(2)}) collective-permute-start(f32[96,384]{1,0:T(8,128)S(1)} %get-tuple-element.92), channel_id=1, source_target_pairs={{0,4},{4,0},{8,12},{12,8},{16,20},{20,16},{24,28},{28,24},{1,5},{5... | collective-permute-start | bytes 442376 | tf_op jit(solution)/shard_map/ppermute | solution.py:335
  35.5 6.3 %collective-permute-start.11 = (f32[96,384]{1,0:T(8,128)S(1)}, f32[96,384]{1,0:T(8,128)S(1)}, u32[]{:S(2)}, u32[]{:S(2)}) collective-permute-start(f32[96,384]{1,0:T(8,128)S(1)} %get-tuple-element.94.refs_7_.refs_12_), channel_id=1, source_target_pairs={{0,16},{4,20},{8,24},{12,28},{16,0},{20,4},{24,8},{28,12},{1,17},{... | collective-permute-start | bytes 442376 | tf_op jit(solution)/shard_map/ppermute | solution.py:335
  37.2 6.0 %collective-permute-start.12 = (f32[96,384]{1,0:T(8,128)S(1)}, f32[96,384]{1,0:T(8,128)S(1)}, u32[]{:S(2)}, u32[]{:S(2)}) collective-permute-start(f32[96,384]{1,0:T(8,128)S(1)} %get-tuple-element.95.refs_8_), channel_id=1, source_target_pairs={{0,28},{4,8},{8,4},{12,16},{16,12},{20,24},{24,20},{28,0},{1,29},{... | collective-permute-start | bytes 442376 | tf_op jit(solution)/shard_map/ppermute | solution.py:335
  37.2 6.0 %collective-permute-start.13 = (f32[96,384]{1,0:T(8,128)S(1)}, f32[96,384]{1,0:T(8,128)S(1)}, u32[]{:S(2)}, u32[]{:S(2)}) collective-permute-start(f32[96,384]{1,0:T(8,128)S(1)} %get-tuple-element.96.refs_9_), channel_id=1, source_target_pairs={{0,4},{4,0},{8,12},{12,8},{16,20},{20,16},{24,28},{28,24},{1,5},{5... | collective-permute-start | bytes 442376 | tf_op jit(solution)/shard_map/ppermute | solution.py:335
  43.5 5.0 %collective-permute-start.14 = (f32[128,128]{1,0:T(8,128)S(1)}, f32[128,128]{1,0:T(8,128)S(1)}, u32[]{:S(2)}, u32[]{:S(2)}) collective-permute-start(f32[128,128]{1,0:T(8,128)S(1)} %get-tuple-element.100.refs_0_.refs_4_), channel_id=1, source_target_pairs={{0,1},{1,0},{2,3},{3,2},{4,5},{5,4},{6,7},{7,6},{8,9},{9,8},{10,11... | collective-permute-start | bytes 196616 | tf_op jit(solution)/shard_map/ppermute | solution.py:377
  45.4 5.6 %collective-permute-start.16 = (f32[128,256]{1,0:T(8,128)S(1)}, f32[128,256]{1,0:T(8,128)S(1)}, u32[]{:S(2)}, u32[]{:S(2)}) collective-permute-start(f32[128,256]{1,0:T(8,128)S(1)} %get-tuple-element.104.refs_0_), channel_id=1, source_target_pairs={{0,1},{1,0},{2,3},{3,2},{4,5},{5,4},{6,7},{7,6},{8,9},{9,8},{10,11... | collective-permute-start | bytes 393224 | tf_op jit(solution)/shard_map/ppermute | solution.py:377
  48.8 6.8 %collective-permute-start.15 = (f32[128,128]{1,0:T(8,128)S(1)}, f32[128,128]{1,0:T(8,128)S(1)}, u32[]{:S(2)}, u32[]{:S(2)}) collective-permute-start(f32[128,128]{1,0:T(8,128)S(1)} %get-tuple-element.102.refs_4_), channel_id=1, source_target_pairs={{0,3},{3,0},{1,2},{2,1},{4,7},{7,4},{5,6},{6,5},{8,11},{11,8},{9,1... | collective-permute-start | bytes 196616 | tf_op jit(solution)/shard_map/ppermute | solution.py:387
  51.3 6.9 %collective-permute-start.17 = (f32[128,256]{1,0:T(8,128)S(1)}, f32[128,256]{1,0:T(8,128)S(1)}, u32[]{:S(2)}, u32[]{:S(2)}) collective-permute-start(f32[128,256]{1,0:T(8,128)S(1)} %get-tuple-element.105.refs_6_), channel_id=1, source_target_pairs={{0,3},{3,0},{1,2},{2,1},{4,7},{7,4},{5,6},{6,5},{8,11},{11,8},{9,1... | collective-permute-start | bytes 393224 | tf_op jit(solution)/shard_map/ppermute | solution.py:387
  58.5 5.2 %collective-permute-start.18 = (f32[96,384]{1,0:T(8,128)S(1)}, f32[96,384]{1,0:T(8,128)S(1)}, u32[]{:S(2)}, u32[]{:S(2)}) collective-permute-start(f32[96,384]{1,0:T(8,128)S(1)} %get-tuple-element.111), channel_id=1, source_target_pairs={{0,16},{4,20},{8,24},{12,28},{16,0},{20,4},{24,8},{28,12},{1,17},{... | collective-permute-start | bytes 442376 | tf_op jit(solution)/shard_map/ppermute | solution.py:335
  59.8 5.8 %collective-permute-start.19 = (f32[96,384]{1,0:T(8,128)S(1)}, f32[96,384]{1,0:T(8,128)S(1)}, u32[]{:S(2)}, u32[]{:S(2)}) collective-permute-start(f32[96,384]{1,0:T(8,128)S(1)} %get-tuple-element.112), channel_id=1, source_target_pairs={{0,28},{4,8},{8,4},{12,16},{16,12},{20,24},{24,20},{28,0},{1,29},{... | collective-permute-start | bytes 442376 | tf_op jit(solution)/shard_map/ppermute | solution.py:335
  59.8 5.8 %collective-permute-start.20 = (f32[96,384]{1,0:T(8,128)S(1)}, f32[96,384]{1,0:T(8,128)S(1)}, u32[]{:S(2)}, u32[]{:S(2)}) collective-permute-start(f32[96,384]{1,0:T(8,128)S(1)} %get-tuple-element.113), channel_id=1, source_target_pairs={{0,4},{4,0},{8,12},{12,8},{16,20},{20,16},{24,28},{28,24},{1,5},{5... | collective-permute-start | bytes 442376 | tf_op jit(solution)/shard_map/ppermute | solution.py:335
  66.1 5.3 %collective-permute-start.21 = (f32[96,384]{1,0:T(8,128)S(1)}, f32[96,384]{1,0:T(8,128)S(1)}, u32[]{:S(2)}, u32[]{:S(2)}) collective-permute-start(f32[96,384]{1,0:T(8,128)S(1)} %get-tuple-element.114.refs_7_.refs_10_), channel_id=1, source_target_pairs={{0,16},{4,20},{8,24},{12,28},{16,0},{20,4},{24,8},{28,12},{1,17},{... | collective-permute-start | bytes 442376 | tf_op jit(solution)/shard_map/ppermute | solution.py:335
  67.3 5.9 %collective-permute-start.22 = (f32[96,384]{1,0:T(8,128)S(1)}, f32[96,384]{1,0:T(8,128)S(1)}, u32[]{:S(2)}, u32[]{:S(2)}) collective-permute-start(f32[96,384]{1,0:T(8,128)S(1)} %get-tuple-element.115.refs_8_), channel_id=1, source_target_pairs={{0,28},{4,8},{8,4},{12,16},{16,12},{20,24},{24,20},{28,0},{1,29},{... | collective-permute-start | bytes 442376 | tf_op jit(solution)/shard_map/ppermute | solution.py:335
  67.6 5.6 %collective-permute-start.23 = (f32[96,384]{1,0:T(8,128)S(1)}, f32[96,384]{1,0:T(8,128)S(1)}, u32[]{:S(2)}, u32[]{:S(2)}) collective-permute-start(f32[96,384]{1,0:T(8,128)S(1)} %get-tuple-element.116.refs_9_), channel_id=1, source_target_pairs={{0,4},{4,0},{8,12},{12,8},{16,20},{20,16},{24,28},{28,24},{1,5},{5... | collective-permute-start | bytes 442376 | tf_op jit(solution)/shard_map/ppermute | solution.py:335
